TPU v7x, 256 devices: a whole 4x4x8 slice. The times are simulated.
256 devices in a mesh: seq: 16 (over y, z_lo, core), row: 4 (over z_hi), col: 4 (over x).
Axes of the slice: x: 4, y: 4, z: 8 (z_hi: 4, z_lo: 2; z = z_hi * 2 + z_lo), core: 2. Of those that a mesh axis runs over, the one named last changes fastest.
Arguments:
- tokens: bfloat16 [8192, 4096], P(('seq', 'row'), 'col'), may hold values from -6 to 6
- w_uvqk: bfloat16 [4096, 8192], P(('seq', 'row'), 'col'), may hold values from -0.09375 to 0.09375
- w_out: bfloat16 [2048, 4096], P('col', ('seq', 'row')), may hold values from -0.375 to 0.375
- rab_table: float32 [16, 32], replicated, may hold values from -4 to 4
- norm_gain: float32 [16, 128], replicated, may hold values from 0.5 to 2
- user_lengths: int32 [4], replicated, may hold values from 1 to 6144, 8192 in all
- bucket_ids: int32 [8192], P('seq'), may hold values from 0 to 8191, as said below
Outputs:
- layer_out: bfloat16 [8192, 4096], P(('seq', 'row'), 'col')
Inputs may be any that keep to these rules, and one draw needn't show every extreme that they name: bucket_ids never fall from one token to the next.
All inputs are finite; a program needn't handle non-finite values.
Results may differ from a plain program's by a relative error of at most 0.014.
Values may be sent and summed in bfloat16 or wider, within the bound.
No kernel may reach another device: no remote copies, remote signals or barrier semaphores. Data moves between devices by JAX's collectives and lax.ppermute only.
A program may use at most 64 MiB of HBM per device.

v0:
```python
import math

import jax
import jax.numpy as jnp
from jax import lax
from jax.sharding import PartitionSpec as P

DH = 128
NB = 32


norm_eps = 1e-05


def user_index(user_ends, positions):
    return jnp.sum((user_ends[None, :] <= positions[:, None]).astype(jnp.int32), axis=1)


def bucket_biases(table_rows, bucket_gap):
    one_hot = (bucket_gap[:, :, None] == jnp.arange(NB, dtype=jnp.int32)[None, None, :]).astype(
        jnp.float32
    )
    return jnp.einsum(
        "qkb,hb->hqk",
        one_hot,
        table_rows,
        precision=lax.Precision.HIGHEST,
        preferred_element_type=jnp.float32,
    )


def on_device(tokens, w_uvqk, w_out, rab_table, norm_gain, user_lengths, bucket_ids):
    feature_rows = lax.all_gather(tokens, "col", axis=1, tiled=True)
    local_rows = tokens.shape[0]
    width_cols = w_uvqk.shape[1]
    row_index = lax.axis_index("row")
    col_index = lax.axis_index("col")
    seq_index = lax.axis_index("seq")
    projected = jnp.dot(
        feature_rows,
        lax.all_gather(w_uvqk, ("seq", "row"), axis=0, tiled=True),
        preferred_element_type=jnp.float32,
    )
    local_heads = width_cols // (4 * DH)
    activated = jax.nn.silu(projected).astype(jnp.bfloat16).reshape(local_rows, local_heads, 4, DH)
    head_major = lax.all_to_all(activated, "row", split_axis=1, concat_axis=0, tiled=True)
    block_len = head_major.shape[0]
    per_device = head_major.shape[1]
    user_ends = jnp.cumsum(user_lengths)
    query_pos = seq_index * block_len + jnp.arange(block_len, dtype=jnp.int32)
    query_user = user_index(user_ends, query_pos)
    first_head = col_index * local_heads + row_index * per_device
    rab_rows = lax.dynamic_slice_in_dim(rab_table, first_head, per_device, 0)
    gain_rows = lax.dynamic_slice_in_dim(norm_gain, first_head, per_device, 0)
    queries = head_major[:, :, 2]
    key_value = head_major[:, :, 1:4:2]
    score_scale = DH ** (-0.5)
    running = jnp.zeros((block_len, per_device, DH), jnp.float32)
    kv_piece = lax.all_gather(key_value, "seq", axis=0, tiled=True)
    key_bucket = lax.all_gather(bucket_ids, "seq", axis=0, tiled=True)
    key_count = kv_piece.shape[0]
    sub_size = math.gcd(key_count, 256)
    sub_count = key_count // sub_size

    def sub_block(accum_in, sub_index):
        sub_first = sub_index * sub_size
        kv_sub = lax.dynamic_slice_in_dim(kv_piece, sub_first, sub_size, 0)
        bucket_sub = lax.dynamic_slice_in_dim(key_bucket, sub_first, sub_size, 0)
        key_pos = sub_first + jnp.arange(sub_size, dtype=jnp.int32)
        key_user = user_index(user_ends, key_pos)
        visible = (query_user[:, None] == key_user[None, :]) & (
            key_pos[None, :] <= query_pos[:, None]
        )
        bucket_gap = jnp.clip(bucket_ids[:, None] - bucket_sub[None, :], 0, NB - 1)
        biases = bucket_biases(rab_rows, bucket_gap)
        scores = (
            jnp.dot(queries[:, 0], kv_sub[:, 0, 1].T, preferred_element_type=jnp.float32)
            * score_scale
        )
        scores = scores + biases[0]
        weights = jnp.where(visible, jax.nn.silu(scores), jnp.float32(0.0)).astype(jnp.bfloat16)
        per_head = [jnp.dot(weights, kv_sub[:, 0, 0], preferred_element_type=jnp.float32)]
        accum_out = accum_in + jnp.stack(per_head, axis=1)
        return (accum_out, None)

    running, _ = lax.scan(sub_block, running, jnp.arange(sub_count, dtype=jnp.int32))
    head_mean = jnp.mean(running, axis=-1, keepdims=True)
    centered = running - head_mean
    head_var = jnp.mean(centered * centered, axis=-1, keepdims=True)
    normed = centered * lax.rsqrt(head_var + norm_eps) * gain_rows[None, :, :]
    gated = (normed * head_major[:, :, 0].astype(jnp.float32)).astype(jnp.bfloat16)
    token_major = lax.all_to_all(gated, "row", split_axis=0, concat_axis=1, tiled=True)
    gated_rows = token_major.reshape(local_rows, local_heads * DH)
    partials = jnp.dot(
        gated_rows,
        lax.all_gather(w_out, ("seq", "row"), axis=1, tiled=True),
        preferred_element_type=jnp.float32,
    )
    summed = lax.psum_scatter(
        partials.astype(jnp.bfloat16), "col", scatter_dimension=1, tiled=True
    ).astype(jnp.float32)
    return (tokens.astype(jnp.float32) + summed).astype(jnp.bfloat16)


def solution(mesh):
    placed = (
        P(("seq", "row"), "col"),
        P(("seq", "row"), "col"),
        P("col", ("seq", "row")),
        P(),
        P(),
        P(),
        P("seq"),
    )
    return jax.shard_map(
        on_device, mesh=mesh, in_specs=placed, out_specs=P(("seq", "row"), "col"), check_vma=False
    )
```

profile of v0, /device:TPU:32, one launch (start us, length us, event | category | flops | bytes accessed | tf_op | source)
XLA Modules:
  0.0 657.4 jit_solution(16882960967085766931)
XLA Ops:
  8.1 30.2 %all-gather.6.cloned.1.call-done = bf16[128,4096]{1,0:T(8,128)(2,1)} async-done(((bf16[128,1024]{1,0:T(8,128)(2,1)}), bf16[128,4096]{1,0:T(8,128)(2,1)}) %all-gather.6.cloned.1.call-update) | async-done | bytes 1048592 | tf_op jit(solution)/shard_map/all_gather | solution.py:33
  38.3 208.5 %all-gather.8.cloned.1.call-done = bf16[4096,2048]{1,0:T(8,128)(2,1)} async-done(((bf16[64,2048]{1,0:T(8,128)(2,1)}), bf16[4096,2048]{1,0:T(8,128)(2,1)}) %all-gather.8.cloned.1.call-update) | async-done | bytes 16777232 | tf_op jit(solution)/shard_map/all_gather | solution.py:41
  246.8 8.5 %multiply_convert_fusion = bf16[128,2048]{1,0:T(8,128)(2,1)S(1)} fusion(bf16[128,4096]{1,0:T(8,128)(2,1)} %all-gather.6.cloned.1.call-done, bf16[4096,2048]{1,0:T(8,128)(2,1)} %all-gather.8.cloned.1.call-done), kind=kOutput, calls=%fused_computation.33 | convolution fusion | flops 2148794368 | bytes 18350080 | tf_op jit(solution)/shard_map/dot_general | solution.py:39
  255.9 20.5 %all_to_all.33 = bf16[128,4,4,128]{3,2,0,1:T(4,128)(2,1)S(1)} all-to-all(bf16[128,4,4,128]{3,2,0,1:T(4,128)(2,1)S(1)} %copy.26), channel_id=1, replica_groups=mesh['seq'=16,'row'=4,'col'=4] {'row'}, dimensions={1} | all-to-all | bytes 1048576 | tf_op jit(solution)/shard_map/all_to_all | solution.py:46
  278.1 19.3 %all-gather = s32[16,1,512]{2,1,0:T(1,128)S(1)} all-gather(s32[1,1,512]{2,1,0:T(1,128)S(1)} %bitcast.80), channel_id=1, replica_groups=mesh['seq'=16,'row'=4,'col'=4] {'seq'}, dimensions={0}, use_global_device_ids=true | all-gather | bytes 34816 | tf_op jit(solution)/shard_map/all_gather | solution.py:60
  298.2 17.2 %all-gather.10.cloned.1.call-done = bf16[8192,1,2,128]{3,0,2,1:T(8,128)(2,1)} async-done(((bf16[512,1,2,128]{3,0,2,1:T(8,128)(2,1)}), bf16[8192,1,2,128]{3,0,2,1:T(8,128)(2,1)}) %all-gather.10.cloned.1.call-update) | async-done | bytes 4194320 | tf_op jit(solution)/shard_map/all_gather | solution.py:59
  315.4 289.0 %while.11 = (s32[]{:T(128)}, f32[512,1,128]{2,0,1:T(8,128)S(1)}, s32[512]{0:T(512)S(1)}, s32[4]{0:T(128)S(1)}, s32[32]{0:T(128)S(1)}, /*index=5*/bf16[8192,1,2,1...) while((s32[]{:T(128)}, f32[512,1,128]{2,0,1:T(8,128)S(1)}, ...), condition=%wide.region_4.5_spmd.clone, body=%wide.region_2.4_spmd.clone.sunk | while | flops 123473408 | bytes 3950976 | solution.py:86
  316.9 5.3 fusion.36
  325.9 5.3 fusion.36
  334.9 5.3 fusion.36
  344.0 5.3 fusion.36
  353.0 5.3 fusion.36
  362.0 5.3 fusion.36
  371.1 5.3 fusion.36
  380.1 5.3 fusion.36
  389.1 5.3 fusion.36
  398.2 5.3 fusion.36
  407.2 5.3 fusion.36
  416.2 5.3 fusion.36
  425.3 5.3 fusion.36
  434.3 5.3 fusion.36
  443.3 5.3 fusion.36
  452.4 5.3 fusion.36
  461.4 5.3 fusion.36
  470.4 5.3 fusion.36
  479.5 5.3 fusion.36
  488.5 5.3 fusion.36
  497.5 5.3 fusion.36
  506.6 5.3 fusion.36
  515.6 5.3 fusion.36
  606.3 15.3 %all_to_all.34 = bf16[4,2,8192]{2,1,0:T(2,128)(2,1)S(1)} all-to-all(bf16[4,2,8192]{2,1,0:T(2,128)(2,1)S(1)} %reshape.130), channel_id=1, replica_groups=mesh['seq'=16,'row'=4,'col'=4] {'row'}, dimensions={0} | all-to-all | bytes 262144 | tf_op jit(solution)/shard_map/all_to_all | solution.py:92
  626.6 22.5 %reduce-scatter.2.cloned.1.call-done = bf16[128,1024]{1,0:T(8,128)(2,1)} async-done(((bf16[128,4096]{1,0:T(8,128)(2,1)}), bf16[128,1024]{1,0:T(8,128)(2,1)}) %reduce-scatter.2.cloned.1.call-update) | async-done | bytes 262160 | tf_op jit(solution)/shard_map/reduce_scatter | solution.py:99
  (309 shorter events, 158.3 us)
Async XLA Ops:
  6.5 291.6 %copy-start = (f32[16,128]{1,0:T(8,128)S(1)}, f32[16,128]{1,0:T(8,128)}, u32[]{:S(2)}) copy-start(f32[16,128]{1,0:T(8,128)} %param.13) | copy-start | bytes 24580
  6.5 31.8 %all-gather.6.cloned.1.call-start = ((), (), s32[]{:S(2)}) async-start(), calls=%async_computation.3 | async-start | bytes 1310720 | tf_op jit(solution)/shard_map/all_gather | solution.py:33
  7.3 239.6 %all-gather.8.cloned.1.call-start = ((), (), s32[]{:S(2)}) async-start(), calls=%async_computation.4 | async-start | bytes 17039360 | tf_op jit(solution)/shard_map/all_gather | solution.py:41
  8.0 307.4 %all-gather.10.cloned.1.call-start = ((), (), s32[]{:S(2)}) async-start(), calls=%async_computation.5 | async-start | bytes 4456448 | tf_op jit(solution)/shard_map/all_gather | solution.py:59
  255.3 22.6 %copy-start.3 = (s32[4]{0:T(128)S(1)}, s32[4]{0:T(128)}, u32[]{:S(2)}) copy-start(s32[4]{0:T(128)} %param.14) | copy-start | bytes 52
  255.4 22.8 %copy-start.2 = (s32[512]{0:T(512)S(1)}, s32[512]{0:T(512)}, u32[]{:S(2)}) copy-start(s32[512]{0:T(512)} %param.15) | copy-start | bytes 6148
  277.3 344.6 %all-gather.12.cloned.1.call-start = ((), (), s32[]{:S(2)}) async-start(), calls=%async_computation.6 | async-start | bytes 4259840 | tf_op jit(solution)/shard_map/all_gather | solution.py:96
  277.8 371.3 %reduce-scatter.2.cloned.1.call-start = ((), (), s32[]{:S(2)}) async-start(), calls=%async_computation.7 | async-start | bytes 1310720 | tf_op jit(solution)/shard_map/reduce_scatter | solution.py:99
  605.0 44.1 %copy-start.1 = (bf16[128,1024]{1,0:T(8,128)(2,1)S(1)}, bf16[128,1024]{1,0:T(8,128)(2,1)}, u32[]{:S(2)}) copy-start(bf16[128,1024]{1,0:T(8,128)(2,1)} %param.9) | copy-start | bytes 786436
Sparse Core Ops, SparseCore 0:
  9.2 29.0 all-gather.5
  40.1 206.6 all-gather.7
  277.4 37.9 all-gather.9
  317.1 190.1 all-gather.11
  626.7 22.3 reduce-scatter.1
where the time goes:
time: 660 us; the launch traced here: 657 us
  waiting for transfers between devices  280 us (42%)
  matrix products  229 us (35%)
  blocking collectives  55.1 us (8%)
  local copies, waits for them, and re-layouts  45.7 us (7%)
  loops' own time  22.8 us (3%)
  between operations  13.3 us (2%)
  other arithmetic  11.2 us (2%)
    all_gather x1, waiting for transfers between devices, on_device(): lax.all_gather(w_uvqk, ('seq', 'row'), axis=0, tiled=True)  209 us
    dot_general x32, matrix products, bucket_biases(): jnp.einsum('qkb,hb->hqk', one_hot, table_rows, precision=lax.Precision.HI...  168 us
    dot_general x32, matrix products, sub_block(): jnp.dot(weights, kv_sub[:, 0, 0], preferred_element_type=jnp.float32)  47.3 us
    all_gather x1, waiting for transfers between devices, on_device(): feature_rows = lax.all_gather(tokens, 'col', axis=1, tiled=True)  30.2 us
    another operation x1, loops' own time, on_device(): lax.scan(sub_block, running, jnp.arange(sub_count, dtype=jnp.int32))  22.8 us
    reduce_scatter x1, waiting for transfers between devices, on_device(): lax.psum_scatter(partials.astype(jnp.bfloat16), 'col', scatter_dimension=...  22.5 us
    dot_general x32, local copies, waits for them, and re-layouts, bucket_biases(): jnp.einsum('qkb,hb->hqk', one_hot, table_rows, precision=lax.Precision.HI...  21.5 us
    all_to_all x1, blocking collectives, on_device(): lax.all_to_all(activated, 'row', split_axis=1, concat_axis=0, tiled=True)  20.5 us
  transfers between devices with their start and end apart: 5, of which 4 were waited for; matrix products, arithmetic and copies ran while one was open for 41% of the time, Pallas kernels for 0%

commit v1 on v0

v1 whole, which is shorter than its diff:
```python
import functools

import jax
import jax.numpy as jnp
from jax import lax
from jax.experimental import pallas as pl
from jax.experimental.pallas import tpu as pltpu
from jax.sharding import Mesh
from jax.sharding import PartitionSpec as P

DH = 128
NB = 32
RUN = 128
TILE = 512
NORM_EPS = 1e-05
SCALE = DH ** (-0.5)


def rotations(value, axis, size, step=1):
    return [value] + [
        lax.ppermute(value, axis, [(i, (i + step * k) % size) for i in range(size)])
        for k in range(1, size)
    ]


def z_shift(k):
    pairs = []
    for zl in range(2):
        for zh in range(4):
            to = (zh * 2 + zl + k) % 8
            pairs.append((zl * 4 + zh, (to % 2) * 4 + to // 2))
    return pairs


def project_kernel(place, t0, t1, t2, t3, mine, other, kv_ref, uq_ref, sorted_w, total):
    y, zl, core, zh, x = (place[i] for i in range(5))
    z = zh * 2 + zl
    for kx, chunk in enumerate((t0, t1, t2, t3)):
        ky = (y - (x - kx)) & 3
        for kz in range(8):
            z_from = (z - kz) & 7
            for c, source in enumerate((mine, other)):
                core_from = core if c == 0 else 1 - core
                piece = ((z_from & 1) * 2 + core_from) * 4 + (z_from >> 1)
                rows = pl.ds(pl.multiple_of(piece * 64, 64), 64)
                sorted_w[rows, :] = source[kz, ky]
        part = jnp.dot(chunk[...], sorted_w[...], preferred_element_type=jnp.float32)
        if kx == 0:
            total[...] = part
        else:
            total[...] += part
    half = 0.5 * total[...]
    act = (half + half * jnp.tanh(half)).astype(jnp.bfloat16)
    for r in range(4):
        rows = slice(r * RUN, (r + 1) * RUN)
        uq_ref[r, :, :DH] = act[rows, :DH]
        kv_ref[r, :, :DH] = act[rows, DH : 2 * DH]
        uq_ref[r, :, DH:] = act[rows, 2 * DH : 3 * DH]
        kv_ref[r, :, DH:] = act[rows, 3 * DH :]


def attend_kernel(
    place, lengths, q_edges, k_edges, biases, kv_ref, uq_ref, q_ids, k_ids, table, gain, out_ref, acc
):
    y, zl, core, zh = (place[i] for i in range(4))
    block = zl * 2 + core
    end0 = lengths[0]
    end1 = end0 + lengths[1]
    end2 = end1 + lengths[2]

    def user_start(pos):
        return jnp.where(pos >= end2, end2, jnp.where(pos >= end1, end1, jnp.where(pos >= end0, end0, 0)))

    table_rows = jnp.broadcast_to(table[...], (RUN, DH))
    for r in range(4):
        run_tile = ((y - r) & 3) * 4 + block
        first = run_tile * TILE + zh * RUN
        low_first, low_last = user_start(first), user_start(first + RUN - 1)
        queries = uq_ref[r, :, DH:]
        q_low, q_high = q_edges[r, 0], q_edges[r, 1]
        acc[...] = jnp.zeros_like(acc)

        def tile(kt, carry):
            ky, km = (y - (kt >> 2)) & 3, kt & 3
            pieces = pl.ds(km * 4, 4)
            keys = kv_ref[pieces, ky, :, DH:].reshape(TILE, DH)
            values = kv_ref[pieces, ky, :, :DH].reshape(TILE, DH)
            entry = ky * 4 + km
            gap_low = jnp.clip(q_low - k_edges[entry, 1], 0, NB - 1)
            gap_high = jnp.clip(q_high - k_edges[entry, 0], 0, NB - 1)
            plain = (kt < run_tile) & (kt * TILE >= low_last) & (gap_low == gap_high)
            scores = lax.dot_general(
                queries, keys, (((1,), (1,)), ((), ())), preferred_element_type=jnp.float32
            ) * (0.5 * SCALE)

            @pl.when(plain)
            def _():
                half = scores + 0.5 * biases[gap_low]
                weights = (half + half * jnp.tanh(half)).astype(jnp.bfloat16)
                acc[...] += jnp.dot(weights, values, preferred_element_type=jnp.float32)

            @pl.when(jnp.logical_not(plain))
            def _():
                gaps = jnp.clip(q_ids[r] - k_ids[ky, pl.ds(km, 1), :], 0, NB - 1)
                bias = jnp.concatenate(
                    [
                        jnp.take_along_axis(
                            table_rows,
                            gaps[:, c * DH : (c + 1) * DH],
                            axis=1,
                            mode="promise_in_bounds",
                        )
                        for c in range(TILE // DH)
                    ],
                    axis=1,
                )
                half = scores + 0.5 * bias
                silu = half + half * jnp.tanh(half)
                q_pos = first + lax.broadcasted_iota(jnp.int32, (RUN, TILE), 0)
                k_pos = kt * TILE + lax.broadcasted_iota(jnp.int32, (RUN, TILE), 1)
                seen = (k_pos <= q_pos) & (k_pos >= user_start(q_pos))
                weights = jnp.where(seen, silu, 0.0).astype(jnp.bfloat16)
                acc[...] += jnp.dot(weights, values, preferred_element_type=jnp.float32)

            return carry

        lax.fori_loop(low_first // TILE, run_tile + 1, tile, 0)
        attended = acc[...]
        mean = jnp.mean(attended, axis=-1, keepdims=True)
        centered = attended - mean
        var = jnp.mean(centered * centered, axis=-1, keepdims=True)
        normed = centered * lax.rsqrt(var + NORM_EPS) * gain[...]
        out_ref[r] = (normed * uq_ref[r, :, :DH].astype(jnp.float32)).astype(jnp.bfloat16)


def output_kernel(place, tokens, gated, w0, w1, w2, w3, out_ref, rows):
    y, x = place[0], place[4]
    for kx in range(4):
        for k in range(4):
            head = ((x - kx) & 3) * 4 + ((y + k) & 3)
            rows[:, pl.ds(pl.multiple_of(head * DH, DH), DH)] = gated[kx, :, k * DH : (k + 1) * DH]
    total = tokens[...].astype(jnp.float32)
    for ky, weight in enumerate((w0, w1, w2, w3)):
        source = (y - ky) & 3
        left = rows[:, pl.ds(pl.multiple_of(source * 512, 512), 512)]
        total += lax.dot_general(
            left, weight[...].reshape(1024, 512), (((1,), (1,)), ((), ())), preferred_element_type=jnp.float32
        )
    out_ref[...] = total.astype(jnp.bfloat16)


def call(kernel, shapes, n_smem, n_vmem, scratch, flops, moved, name):
    return pl.pallas_call(
        kernel,
        out_shape=shapes,
        in_specs=[pl.BlockSpec(memory_space=pltpu.SMEM)] * n_smem
        + [pl.BlockSpec(memory_space=pltpu.VMEM)] * n_vmem,
        out_specs=jax.tree.map(lambda _: pl.BlockSpec(memory_space=pltpu.VMEM), shapes),
        scratch_shapes=scratch,
        compiler_params=pltpu.CompilerParams(vmem_limit_bytes=40 * 2**20),
        cost_estimate=pl.CostEstimate(flops=flops, bytes_accessed=moved, transcendentals=0),
        name=name,
    )


def on_device(tokens, w_uvqk, w_out, rab_table, norm_gain, user_lengths, bucket_ids):
    bf16 = jnp.bfloat16
    y, zl, core, zh, x = (lax.axis_index(a) for a in ("y", "zl", "core", "zh", "x"))
    place = jnp.stack([y, zl, core, zh, x]).astype(jnp.int32)
    plane = ("zl", "core", "zh")

    swapped = lax.ppermute(w_out.T, ("y", "x"), [(b * 4 + a, a * 4 + b) for a in range(4) for b in range(4)])
    ids = jnp.stack([bucket_ids // 128, bucket_ids % 128]).astype(bf16)
    ids = jnp.concatenate(rotations(ids, "y", 4) + [jnp.zeros((8, TILE), bf16)], axis=0)
    wo_and_ids = lax.all_gather(jnp.concatenate([swapped, ids], axis=0), plane)

    def columns(owner):
        return lax.dynamic_slice_in_dim(w_uvqk, owner * 512, 512, 1)

    pieces = [columns(y)] + [
        lax.ppermute(columns((y + k) & 3), "y", [(i, (i + k) % 4) for i in range(4)])
        for k in range(1, 4)
    ]
    piece = jnp.stack(pieces)
    mine = jnp.stack([piece] + [lax.ppermute(piece, ("zl", "zh"), z_shift(k)) for k in range(1, 8)])
    other = lax.ppermute(mine, "core", [(0, 1), (1, 0)])

    runs = jnp.concatenate(rotations(tokens, "y", 4), axis=0)
    chunks = rotations(runs, "x", 4)

    kv, uq = call(
        project_kernel,
        [jax.ShapeDtypeStruct((4, RUN, 2 * DH), bf16)] * 2,
        1,
        6,
        [pltpu.VMEM((1024, 512), bf16), pltpu.VMEM((512, 512), jnp.float32)],
        2 * 512 * 512 * 4096,
        9 * 2**20,
        "project",
    )(place, *chunks, mine, other)

    kv_all = lax.all_gather(kv, plane)

    wo = rotations(wo_and_ids[:, :64], "y", 4)
    coded = wo_and_ids[::4, 64:72].astype(jnp.int32).reshape(4, 4, 2, TILE)
    k_ids = (coded[:, :, 0] * 128 + coded[:, :, 1]).transpose(1, 0, 2)
    q_ids = lax.dynamic_slice(k_ids, (0, zl * 2 + core, zh * RUN), (4, 1, RUN)).reshape(4, RUN, 1)
    q_edges = jnp.concatenate([q_ids[:, 0], q_ids[:, -1]], axis=1)
    k_edges = jnp.stack([k_ids[:, :, 0], k_ids[:, :, -1]], axis=-1).reshape(16, 2)
    head = x * 4 + y
    biases = lax.dynamic_slice(rab_table, (head, 0), (1, NB))
    gain = lax.dynamic_slice(norm_gain, (head, 0), (1, DH))
    table = jnp.pad(biases, ((0, 0), (0, DH - NB)))

    gated = call(
        attend_kernel,
        jax.ShapeDtypeStruct((4, RUN, DH), bf16),
        5,
        6,
        [pltpu.VMEM((RUN, DH), jnp.float32)],
        4 * 512 * 4096 * DH,
        5 * 2**20,
        "attend",
    )(place, user_lengths, q_edges, k_edges, biases[0], kv_all, uq, q_ids, k_ids, table, gain)

    own = [gated[0]] + [
        lax.ppermute(gated[k], "y", [(i, (i - k) % 4) for i in range(4)]) for k in range(1, 4)
    ]
    heads = jnp.stack(rotations(jnp.concatenate(own, axis=1), "x", 4))

    return call(
        output_kernel,
        jax.ShapeDtypeStruct((RUN, 1024), bf16),
        1,
        6,
        [pltpu.VMEM((RUN, 2048), bf16)],
        2 * RUN * 2048 * 1024,
        5 * 2**20,
        "project_out",
    )(place, tokens, heads, *wo)


def solution(mesh):
    fine = Mesh(mesh.devices.reshape(4, 2, 2, 4, 4), ("y", "zl", "core", "zh", "x"))
    every = ("y", "zl", "core", "zh")
    placed = (
        P(every, "x"),
        P(every, "x"),
        P("x", every),
        P(),
        P(),
        P(),
        P(("y", "zl", "core")),
    )
    return jax.shard_map(
        on_device, mesh=fine, in_specs=placed, out_specs=P(every, "x"), check_vma=False
    )
```

time: 660 us -> 320 us (0.48)
  matrix products: 229 us -> 0 us
  waiting for transfers between devices: 280 us -> 202 us
  starting transfers between devices: 0.16 us -> 62.5 us
  blocking collectives: 55.1 us -> 0 us
  local copies, waits for them, and re-layouts: 45.7 us -> 13 us
  Pallas kernels: 0 us -> 22.8 us
  loops' own time: 22.8 us -> 0 us
  other arithmetic: 11.2 us -> 1.79 us
    dot_general x66 -> x0, matrix products: 229 us -> none  [the longest x32 168 us: bucket_biases(): jnp.einsum('qkb,hb->hqk', one_hot, table_rows, precision=lax.Precision.HI...]
    all_gather x4 -> x2, waiting for transfers between devices: 256 us -> 87.5 us  [the longest x1 87.5 us: on_device(): kv_all = lax.all_gather(kv, plane)]
    ppermute x0 -> x30, waiting for transfers between devices: none -> 115 us  [the longest x15 59.5 us: rotations(): lax.ppermute(value, axis, [(i, (i + step * k) % size) for i in range(size)])]
    ppermute x0 -> x30, starting transfers between devices: none -> 62.5 us  [the longest x15 33.5 us: rotations(): lax.ppermute(value, axis, [(i, (i + step * k) % size) for i in range(size)])]
    all_to_all x2 -> x0, blocking collectives: 35.8 us -> none  [the longest x1 20.5 us: on_device(): lax.all_to_all(activated, 'row', split_axis=1, concat_axis=0, tiled=True)]
    pallas_call x0 -> x3, Pallas kernels: none -> 22.8 us  [the longest x1 13.5 us: on_device(): call(attend_kernel, jax.ShapeDtypeStruct((4, RUN, DH), bf16), 5, 6, [pltp...]
    another operation x1 -> x0, loops' own time: 22.8 us -> none  [on_device(): lax.scan(sub_block, running, jnp.arange(sub_count, dtype=jnp.int32))]
    reduce_scatter x1 -> x0, waiting for transfers between devices: 22.5 us -> none  [on_device(): lax.psum_scatter(partials.astype(jnp.bfloat16), 'col', scatter_dimension=...]
  transfers between devices with their start and end apart: 5 -> 32, of which waited for: 4 -> 17; matrix products, arithmetic and copies ran while one was open for 41% -> 3% of each run, Pallas kernels for 0% -> 6%
where the time goes in v1:
time: 320 us; the launch traced here: 316 us
  waiting for transfers between devices  202 us (63%)
  starting transfers between devices  62.5 us (20%)
  Pallas kernels  22.8 us (7%)
  between operations  13.7 us (4%)
  local copies, waits for them, and re-layouts  13 us (4%)
    all_gather x1, waiting for transfers between devices, on_device(): kv_all = lax.all_gather(kv, plane)  87.5 us
    ppermute x15, waiting for transfers between devices, rotations(): lax.ppermute(value, axis, [(i, (i + step * k) % size) for i in range(size)])  59.5 us
    ppermute x7, waiting for transfers between devices, on_device(): lax.ppermute(piece, ('zl', 'zh'), z_shift(k))  47.1 us
    ppermute x15, starting transfers between devices, rotations(): lax.ppermute(value, axis, [(i, (i + step * k) % size) for i in range(size)])  33.5 us
    ppermute x7, starting transfers between devices, on_device(): lax.ppermute(piece, ('zl', 'zh'), z_shift(k))  17 us
    pallas_call x1, Pallas kernels, on_device(): call(attend_kernel, jax.ShapeDtypeStruct((4, RUN, DH), bf16), 5, 6, [pltp...  13.5 us
    unnamed x23, local copies, waits for them, and re-layouts  6.87 us
  transfers between devices with their start and end apart: 32, of which 17 were waited for; matrix products, arithmetic and copies ran while one was open for 3% of the time, Pallas kernels for 6%

profile of v1, /device:TPU:32, one launch (start us, length us, event | category | flops | bytes accessed | tf_op | source)
XLA Modules:
  0.0 315.9 jit_solution(16186724381321016900)
XLA Ops:
  9.2 2.9 collective-permute-start.11
  13.4 1.9 collective-permute-done.11
  16.4 2.0 collective-permute-start.13
  19.5 3.7 %collective-permute-start.2 = (bf16[2,512]{1,0:T(2,128)(2,1)S(1)}, bf16[2,512]{1,0:T(2,128)(2,1)S(1)}, u32[]{:S(2)}, u32[]{:S(2)}) collective-permute-start(bf16[2,512]{1,0:T(2,128)(2,1)S(1)} %pad_maximum_fusion.3), channel_id=1, source_target_pairs={{0,128},{64,192},{128,0},{192,64},{1,129},{65,193},{129,1},{193,65... | collective-permute-start | bytes 6152 | tf_op jit(solution)/shard_map/ppermute | solution.py:21
  24.9 4.5 %collective-permute-start.14 = (bf16[4,64,512]{2,1,0:T(8,128)(2,1)S(1)}, bf16[4,64,512]{2,1,0:T(8,128)(2,1)S(1)}, u32[]{:S(2)}, u32[]{:S(2)}) collective-permute-start(bf16[4,64,512]{2,1,0:T(8,128)(2,1)S(1)} %pad_maximum_fusion.1), channel_id=1, source_target_pairs={{0,4},{4,8},{8,12},{12,0},{32,36},{36,40},{40,44},{44,32},{1,5},{5... | collective-permute-start | bytes 786440 | tf_op jit(solution)/shard_map/ppermute | solution.py:185
  29.4 2.0 collective-permute-start.15
  32.9 3.0 collective-permute-start.17
  35.9 1.8 concatenate.13
  37.9 2.5 collective-permute-start.18
  40.4 4.8 %collective-permute-done.14 = bf16[4,64,512]{2,1,0:T(8,128)(2,1)S(1)} collective-permute-done((bf16[4,64,512]{2,1,0:T(8,128)(2,1)S(1)}, bf16[4,64,512]{2,1,0:T(8,128)(2,1)S(1)}, u32[]{:S(2)}, u32[]{:S(2)}) %collective-permute-start.14) | collective-permute-done | bytes 262176 | tf_op jit(solution)/shard_map/ppermute | solution.py:185
  46.8 23.4 %collective-permute-done.15 = bf16[4,64,512]{2,1,0:T(8,128)(2,1)} collective-permute-done((bf16[4,64,512]{2,1,0:T(8,128)(2,1)S(1)}, bf16[4,64,512]{2,1,0:T(8,128)(2,1)}, u32[]{:S(2)}, u32[]{:S(2)}) %collective-permute-start.15) | collective-permute-done | bytes 262176 | tf_op jit(solution)/shard_map/ppermute | solution.py:185
  73.1 12.1 %collective-permute-done.18 = bf16[4,64,512]{2,1,0:T(8,128)(2,1)S(1)} collective-permute-done((bf16[4,64,512]{2,1,0:T(8,128)(2,1)S(1)}, bf16[4,64,512]{2,1,0:T(8,128)(2,1)S(1)}, u32[]{:S(2)}, u32[]{:S(2)}) %collective-permute-start.18) | collective-permute-done | bytes 262176 | tf_op jit(solution)/shard_map/ppermute | solution.py:185
  85.3 6.8 %collective-permute-done.19 = bf16[4,64,512]{2,1,0:T(8,128)(2,1)S(1)} collective-permute-done((bf16[4,64,512]{2,1,0:T(8,128)(2,1)S(1)}, bf16[4,64,512]{2,1,0:T(8,128)(2,1)S(1)}, u32[]{:S(2)}, u32[]{:S(2)}) %collective-permute-start.19) | collective-permute-done | bytes 262176 | tf_op jit(solution)/shard_map/ppermute | solution.py:185
  92.2 4.9 %collective-permute-start.4 = (bf16[128,1024]{1,0:T(8,128)(2,1)S(1)}, bf16[128,1024]{1,0:T(8,128)(2,1)S(1)}, u32[]{:S(2)}, u32[]{:S(2)}) collective-permute-start(bf16[128,1024]{1,0:T(8,128)(2,1)S(1)} %copy-done.2), channel_id=1, source_target_pairs={{0,64},{64,128},{128,192},{192,0},{1,65},{65,129},{129,193},{193,1... | collective-permute-start | bytes 786440 | tf_op jit(solution)/shard_map/ppermute | solution.py:21
  97.1 4.5 %collective-permute-start.5 = (bf16[128,1024]{1,0:T(8,128)(2,1)S(1)}, bf16[128,1024]{1,0:T(8,128)(2,1)S(1)}, u32[]{:S(2)}, u32[]{:S(2)}) collective-permute-start(bf16[128,1024]{1,0:T(8,128)(2,1)S(1)} %copy-done.2), channel_id=1, source_target_pairs={{0,128},{64,192},{128,0},{192,64},{1,129},{65,193},{129,1},{193,65... | collective-permute-start | bytes 786440 | tf_op jit(solution)/shard_map/ppermute | solution.py:21
  101.6 2.3 collective-permute-start.6
  103.9 3.1 collective-permute-done.4
  107.0 6.8 %collective-permute-done.5 = bf16[128,1024]{1,0:T(8,128)(2,1)S(1)} collective-permute-done((bf16[128,1024]{1,0:T(8,128)(2,1)S(1)}, bf16[128,1024]{1,0:T(8,128)(2,1)S(1)}, u32[]{:S(2)}, u32[]{:S(2)}) %collective-permute-start.5) | collective-permute-done | bytes 262176 | tf_op jit(solution)/shard_map/ppermute | solution.py:21
  113.9 2.6 collective-permute-start.7
  116.5 2.8 collective-permute-start.9
  119.4 43.2 %collective-permute-done.7.t1 = bf16[512,1024]{1,0:T(8,128)(2,1)} collective-permute-done((bf16[512,1024]{1,0:T(8,128)(2,1)S(1)}, bf16[512,1024]{1,0:T(8,128)(2,1)}, u32[]{:S(2)}, u32[]{:S(2)}) %collective-permute-start.7) | collective-permute-done | bytes 1048608 | tf_op jit(solution)/shard_map/ppermute | solution.py:21
  163.2 5.8 %project.1 = (bf16[4,128,256]{2,1,0:T(8,128)(2,1)}, bf16[4,128,256]{2,1,0:T(8,128)(2,1)S(1)}) custom-call(s32[5]{0:T(128)S(1)} %stack.95.place, bf16[512,1024]{1,0:T(8,128)(2,1)S(1)} %constant_dynamic-update-slice_fusion.t0, bf16[512,1024]{1,0:T(8,128)(2,1)} %collective-permute-done.7.t1, bf16[512,1024]{1,0:T(8,128)(2,1)} %collective-permute-done.8.t2, ...), custom_call_target="tpu_custom_call" | custom-call | flops 2147483648 | bytes 9437184 | tf_op jit(solution)/shard_map/project/pallas_call | solution.py:191
  173.5 3.1 collective-permute-start.28
  179.6 87.5 %all-gather.7.cloned.1.call-done = bf16[64,128,256]{2,1,0:T(8,128)(2,1)} async-done(((bf16[4,128,256]{2,1,0:T(8,128)(2,1)}), bf16[64,128,256]{2,1,0:T(8,128)(2,1)}) %all-gather.7.cloned.1.call-update) | async-done | bytes 4194320 | tf_op jit(solution)/shard_map/all_gather | solution.py:202
  267.1 2.2 copy-done.1
  270.3 13.5 %attend.1 = bf16[4,128,128]{2,1,0:T(8,128)(2,1)S(1)} custom-call(s32[5]{0:T(128)S(1)} %stack.95.place, s32[4]{0:T(128)S(1)} %copy-done.6, s32[4,2]{1,0:T(4,128)S(1)} %pad_add_fusion.1.q_edges, s32[16,2]{1,0:T(8,128)S(1)} %bitcast.56, f32[32]{0:T(128)S(1)} %fusion.6.biases, bf16[16,4,128,256]{3,2,1,0:T(8,128)(2,1)S(1)} %bitcast.53, ...), custom_call_target="tpu_custom_call" | custom-call | flops 1073741824 | bytes 5242880 | tf_op jit(solution)/shard_map/attend/pallas_call | solution.py:215
  283.8 2.4 collective-permute-start.21
  288.9 2.7 collective-permute-done.22
  295.1 2.5 collective-permute-start.25
  297.6 2.8 collective-permute-done.24
  300.4 2.0 collective-permute-start.26
  305.6 3.5 %project_out.1 = bf16[128,1024]{1,0:T(8,128)(2,1)} custom-call(s32[5]{0:T(128)S(1)} %stack.95.place, bf16[128,1024]{1,0:T(8,128)(2,1)S(1)} %copy-done.3, bf16[4,128,512]{2,1,0:T(8,128)(2,1)S(1)} %pad_maximum_fusion.gated, bf16[16,64,512]{2,1,0:T(8,128)(2,1)S(1)} %slice.56.w0, bf16[16,64,512]{2,1,0:T(8,128)(2,1)S(1)} %collective-permute-done.27.w1, ...), custom_call_target="tpu_custom_call" | custom-call | flops 536870912 | bytes 5242880 | tf_op jit(solution)/shard_map/project_out/pallas_call | solution.py:231
  (90 shorter events, 32.6 us)
Async XLA Ops:
  6.5 164.6 %all-gather.5.cloned.1.call-start = ((), (), s32[]{:S(2)}) async-start(), calls=%async_computation | async-start | bytes 1392640 | tf_op jit(solution)/shard_map/all_gather | solution.py:175
  7.5 5.9 %collective-permute-start.10 = (bf16[64,512]{1,0:T(8,128)(2,1)S(1)}, bf16[64,512]{1,0:T(8,128)(2,1)S(1)}, u32[]{:S(2)}, u32[]{:S(2)}) collective-permute-start(bf16[64,512]{1,0:T(8,128)(2,1)S(1)} %get-tuple-element.10), channel_id=1, source_target_pairs={{0,64},{64,128},{128,192},{192,0},{1,65},{65,129},{129,193},{193,1... | collective-permute-start | bytes 196616 | tf_op jit(solution)/shard_map/ppermute | solution.py:181
  9.2 6.1 %collective-permute-start.11 = (bf16[64,512]{1,0:T(8,128)(2,1)S(1)}, bf16[64,512]{1,0:T(8,128)(2,1)S(1)}, u32[]{:S(2)}, u32[]{:S(2)}) collective-permute-start(bf16[64,512]{1,0:T(8,128)(2,1)S(1)} %get-tuple-element.12), channel_id=1, source_target_pairs={{0,128},{64,192},{128,0},{192,64},{1,129},{65,193},{129,1},{193,65... | collective-permute-start | bytes 196616 | tf_op jit(solution)/shard_map/ppermute | solution.py:181
  12.1 4.3 %collective-permute-start.12 = (bf16[64,512]{1,0:T(8,128)(2,1)S(1)}, bf16[64,512]{1,0:T(8,128)(2,1)S(1)}, u32[]{:S(2)}, u32[]{:S(2)}) collective-permute-start(bf16[64,512]{1,0:T(8,128)(2,1)S(1)} %get-tuple-element.11), channel_id=1, source_target_pairs={{0,192},{64,0},{128,64},{192,128},{1,193},{65,1},{129,65},{193,129... | collective-permute-start | bytes 196616 | tf_op jit(solution)/shard_map/ppermute | solution.py:181
  16.4 21.5 %collective-permute-start.13 = (bf16[4,64,512]{2,1,0:T(8,128)(2,1)S(1)}, bf16[4,64,512]{2,1,0:T(8,128)(2,1)S(1)}, u32[]{:S(2)}, u32[]{:S(2)}) collective-permute-start(bf16[4,64,512]{2,1,0:T(8,128)(2,1)S(1)} %pad_maximum_fusion.1), channel_id=1, source_target_pairs={{0,32},{4,36},{8,40},{12,44},{32,4},{36,8},{40,12},{44,0},{1,33},{... | collective-permute-start | bytes 786440 | tf_op jit(solution)/shard_map/ppermute | solution.py:185
  19.1 5.8 %collective-permute-start.1 = (bf16[2,512]{1,0:T(2,128)(2,1)S(1)}, bf16[2,512]{1,0:T(2,128)(2,1)S(1)}, u32[]{:S(2)}, u32[]{:S(2)}) collective-permute-start(bf16[2,512]{1,0:T(2,128)(2,1)S(1)} %pad_maximum_fusion.3), channel_id=1, source_target_pairs={{0,64},{64,128},{128,192},{192,0},{1,65},{65,129},{129,193},{193,1... | collective-permute-start | bytes 6152 | tf_op jit(solution)/shard_map/ppermute | solution.py:21
  19.5 10.0 %collective-permute-start.2 = (bf16[2,512]{1,0:T(2,128)(2,1)S(1)}, bf16[2,512]{1,0:T(2,128)(2,1)S(1)}, u32[]{:S(2)}, u32[]{:S(2)}) collective-permute-start(bf16[2,512]{1,0:T(2,128)(2,1)S(1)} %pad_maximum_fusion.3), channel_id=1, source_target_pairs={{0,128},{64,192},{128,0},{192,64},{1,129},{65,193},{129,1},{193,65... | collective-permute-start | bytes 6152 | tf_op jit(solution)/shard_map/ppermute | solution.py:21
  23.2 8.3 %collective-permute-start.3 = (bf16[2,512]{1,0:T(2,128)(2,1)S(1)}, bf16[2,512]{1,0:T(2,128)(2,1)S(1)}, u32[]{:S(2)}, u32[]{:S(2)}) collective-permute-start(bf16[2,512]{1,0:T(2,128)(2,1)S(1)} %pad_maximum_fusion.3), channel_id=1, source_target_pairs={{0,192},{64,0},{128,64},{192,128},{1,193},{65,1},{129,65},{193,129... | collective-permute-start | bytes 6152 | tf_op jit(solution)/shard_map/ppermute | solution.py:21
  23.3 9.6 %collective-permute-start = (bf16[64,512]{1,0:T(8,128)(2,1)}, bf16[64,512]{1,0:T(8,128)(2,1)S(1)}, u32[]{:S(2)}, u32[]{:S(2)}) collective-permute-start(bf16[64,512]{1,0:T(8,128)(2,1)} %bitcast.70), channel_id=1, source_target_pairs={{0,0},{64,1},{128,2},{192,3},{1,64},{65,65},{129,66},{193,67},{2,1... | collective-permute-start | bytes 196616 | tf_op jit(solution)/shard_map/ppermute | solution.py:172
  24.9 20.3 %collective-permute-start.14 = (bf16[4,64,512]{2,1,0:T(8,128)(2,1)S(1)}, bf16[4,64,512]{2,1,0:T(8,128)(2,1)S(1)}, u32[]{:S(2)}, u32[]{:S(2)}) collective-permute-start(bf16[4,64,512]{2,1,0:T(8,128)(2,1)S(1)} %pad_maximum_fusion.1), channel_id=1, source_target_pairs={{0,4},{4,8},{8,12},{12,0},{32,36},{36,40},{40,44},{44,32},{1,5},{5... | collective-permute-start | bytes 786440 | tf_op jit(solution)/shard_map/ppermute | solution.py:185
  29.4 40.7 %collective-permute-start.15 = (bf16[4,64,512]{2,1,0:T(8,128)(2,1)S(1)}, bf16[4,64,512]{2,1,0:T(8,128)(2,1)}, u32[]{:S(2)}, u32[]{:S(2)}) collective-permute-start(bf16[4,64,512]{2,1,0:T(8,128)(2,1)S(1)} %pad_maximum_fusion.1), channel_id=1, source_target_pairs={{0,36},{4,40},{8,44},{12,32},{32,8},{36,12},{40,0},{44,4},{1,37},{... | collective-permute-start | bytes 786440 | tf_op jit(solution)/shard_map/ppermute | solution.py:185
  31.5 39.7 %collective-permute-start.16 = (bf16[4,64,512]{2,1,0:T(8,128)(2,1)S(1)}, bf16[4,64,512]{2,1,0:T(8,128)(2,1)}, u32[]{:S(2)}, u32[]{:S(2)}) collective-permute-start(bf16[4,64,512]{2,1,0:T(8,128)(2,1)S(1)} %pad_maximum_fusion.1), channel_id=1, source_target_pairs={{0,8},{4,12},{8,0},{12,4},{32,40},{36,44},{40,32},{44,36},{1,9},{5... | collective-permute-start | bytes 786440 | tf_op jit(solution)/shard_map/ppermute | solution.py:185
  32.9 39.2 %collective-permute-start.17 = (bf16[4,64,512]{2,1,0:T(8,128)(2,1)S(1)}, bf16[4,64,512]{2,1,0:T(8,128)(2,1)}, u32[]{:S(2)}, u32[]{:S(2)}) collective-permute-start(bf16[4,64,512]{2,1,0:T(8,128)(2,1)S(1)} %pad_maximum_fusion.1), channel_id=1, source_target_pairs={{0,40},{4,44},{8,32},{12,36},{32,12},{36,0},{40,4},{44,8},{1,41},{... | collective-permute-start | bytes 786440 | tf_op jit(solution)/shard_map/ppermute | solution.py:185
  37.8 229.3 %all-gather.7.cloned.1.call-start = ((), (), s32[]{:S(2)}) async-start(), calls=%async_computation.1 | async-start | bytes 4456448 | tf_op jit(solution)/shard_map/all_gather | solution.py:202
  37.9 47.4 %collective-permute-start.18 = (bf16[4,64,512]{2,1,0:T(8,128)(2,1)S(1)}, bf16[4,64,512]{2,1,0:T(8,128)(2,1)S(1)}, u32[]{:S(2)}, u32[]{:S(2)}) collective-permute-start(bf16[4,64,512]{2,1,0:T(8,128)(2,1)S(1)} %pad_maximum_fusion.1), channel_id=1, source_target_pairs={{0,12},{4,0},{8,4},{12,8},{32,44},{36,32},{40,36},{44,40},{1,13},{... | collective-permute-start | bytes 786440 | tf_op jit(solution)/shard_map/ppermute | solution.py:185
  45.2 46.8 %collective-permute-start.19 = (bf16[4,64,512]{2,1,0:T(8,128)(2,1)S(1)}, bf16[4,64,512]{2,1,0:T(8,128)(2,1)S(1)}, u32[]{:S(2)}, u32[]{:S(2)}) collective-permute-start(bf16[4,64,512]{2,1,0:T(8,128)(2,1)S(1)} %pad_maximum_fusion.1), channel_id=1, source_target_pairs={{0,44},{4,32},{8,36},{12,40},{32,0},{36,4},{40,8},{44,12},{1,45},{... | collective-permute-start | bytes 786440 | tf_op jit(solution)/shard_map/ppermute | solution.py:185
  92.1 71.1 %collective-permute-start.20 = (bf16[8,4,64,512]{3,2,1,0:T(8,128)(2,1)S(1)}, bf16[8,4,64,512]{3,2,1,0:T(8,128)(2,1)}, u32[]{:S(2)}, u32[]{:S(2)}) collective-permute-start(bf16[8,4,64,512]{3,2,1,0:T(8,128)(2,1)S(1)} %bitcast_dynamic-update-slice_fusion.mine), channel_id=1, source_target_pairs={{0,16},{16,0},{1,17},{17,1},{2,18},{18,2},{3,19},{19,3},{4,20},{20... | collective-permute-start | bytes 6291464 | tf_op jit(solution)/shard_map/ppermute | solution.py:186
  92.2 14.8 %collective-permute-start.4 = (bf16[128,1024]{1,0:T(8,128)(2,1)S(1)}, bf16[128,1024]{1,0:T(8,128)(2,1)S(1)}, u32[]{:S(2)}, u32[]{:S(2)}) collective-permute-start(bf16[128,1024]{1,0:T(8,128)(2,1)S(1)} %copy-done.2), channel_id=1, source_target_pairs={{0,64},{64,128},{128,192},{192,0},{1,65},{65,129},{129,193},{193,1... | collective-permute-start | bytes 786440 | tf_op jit(solution)/shard_map/ppermute | solution.py:21
  97.1 16.8 %collective-permute-start.5 = (bf16[128,1024]{1,0:T(8,128)(2,1)S(1)}, bf16[128,1024]{1,0:T(8,128)(2,1)S(1)}, u32[]{:S(2)}, u32[]{:S(2)}) collective-permute-start(bf16[128,1024]{1,0:T(8,128)(2,1)S(1)} %copy-done.2), channel_id=1, source_target_pairs={{0,128},{64,192},{128,0},{192,64},{1,129},{65,193},{129,1},{193,65... | collective-permute-start | bytes 786440 | tf_op jit(solution)/shard_map/ppermute | solution.py:21
  101.6 12.3 %collective-permute-start.6 = (bf16[128,1024]{1,0:T(8,128)(2,1)S(1)}, bf16[128,1024]{1,0:T(8,128)(2,1)S(1)}, u32[]{:S(2)}, u32[]{:S(2)}) collective-permute-start(bf16[128,1024]{1,0:T(8,128)(2,1)S(1)} %copy-done.2), channel_id=1, source_target_pairs={{0,192},{64,0},{128,64},{192,128},{1,193},{65,1},{129,65},{193,129... | collective-permute-start | bytes 786440 | tf_op jit(solution)/shard_map/ppermute | solution.py:21
  113.9 48.7 %collective-permute-start.7 = (bf16[512,1024]{1,0:T(8,128)(2,1)S(1)}, bf16[512,1024]{1,0:T(8,128)(2,1)}, u32[]{:S(2)}, u32[]{:S(2)}) collective-permute-start(bf16[512,1024]{1,0:T(8,128)(2,1)S(1)} %constant_dynamic-update-slice_fusion.t0), channel_id=1, source_target_pairs={{0,1},{1,2},{2,3},{3,0},{4,5},{5,6},{6,7},{7,4},{8,9},{9,10},{10,1... | collective-permute-start | bytes 3145736 | tf_op jit(solution)/shard_map/ppermute | solution.py:21
  116.5 46.0 %collective-permute-start.8 = (bf16[512,1024]{1,0:T(8,128)(2,1)S(1)}, bf16[512,1024]{1,0:T(8,128)(2,1)}, u32[]{:S(2)}, u32[]{:S(2)}) collective-permute-start(bf16[512,1024]{1,0:T(8,128)(2,1)S(1)} %constant_dynamic-update-slice_fusion.t0), channel_id=1, source_target_pairs={{0,2},{1,3},{2,0},{3,1},{4,6},{5,7},{6,4},{7,5},{8,10},{9,11},{10,... | collective-permute-start | bytes 3145736 | tf_op jit(solution)/shard_map/ppermute | solution.py:21
  116.5 46.7 %collective-permute-start.9 = (bf16[512,1024]{1,0:T(8,128)(2,1)S(1)}, bf16[512,1024]{1,0:T(8,128)(2,1)}, u32[]{:S(2)}, u32[]{:S(2)}) collective-permute-start(bf16[512,1024]{1,0:T(8,128)(2,1)S(1)} %constant_dynamic-update-slice_fusion.t0), channel_id=1, source_target_pairs={{0,3},{1,0},{2,1},{3,2},{4,7},{5,4},{6,5},{7,6},{8,11},{9,8},{10,9... | collective-permute-start | bytes 3145736 | tf_op jit(solution)/shard_map/ppermute | solution.py:21
  172.4 133.1 %collective-permute-start.27 = (bf16[16,64,512]{2,1,0:T(8,128)(2,1)S(1)}, bf16[16,64,512]{2,1,0:T(8,128)(2,1)S(1)}, u32[]{:S(2)}, u32[]{:S(2)}) collective-permute-start(bf16[16,64,512]{2,1,0:T(8,128)(2,1)S(1)} %slice.56.w0), channel_id=1, source_target_pairs={{0,64},{64,128},{128,192},{192,0},{1,65},{65,129},{129,193},{193,1... | collective-permute-start | bytes 3145736 | tf_op jit(solution)/shard_map/ppermute | solution.py:21
  173.5 132.0 %collective-permute-start.28 = (bf16[16,64,512]{2,1,0:T(8,128)(2,1)S(1)}, bf16[16,64,512]{2,1,0:T(8,128)(2,1)S(1)}, u32[]{:S(2)}, u32[]{:S(2)}) collective-permute-start(bf16[16,64,512]{2,1,0:T(8,128)(2,1)S(1)} %slice.56.w0), channel_id=1, source_target_pairs={{0,128},{64,192},{128,0},{192,64},{1,129},{65,193},{129,1},{193,65... | collective-permute-start | bytes 3145736 | tf_op jit(solution)/shard_map/ppermute | solution.py:21
  176.6 129.0 %collective-permute-start.29 = (bf16[16,64,512]{2,1,0:T(8,128)(2,1)S(1)}, bf16[16,64,512]{2,1,0:T(8,128)(2,1)}, u32[]{:S(2)}, u32[]{:S(2)}) collective-permute-start(bf16[16,64,512]{2,1,0:T(8,128)(2,1)S(1)} %slice.56.w0), channel_id=1, source_target_pairs={{0,192},{64,0},{128,64},{192,128},{1,193},{65,1},{129,65},{193,129... | collective-permute-start | bytes 3145736 | tf_op jit(solution)/shard_map/ppermute | solution.py:21
  283.8 4.0 %collective-permute-start.21 = (bf16[128,128]{1,0:T(8,128)(2,1)S(1)}, bf16[128,128]{1,0:T(8,128)(2,1)S(1)}, u32[]{:S(2)}, u32[]{:S(2)}) collective-permute-start(bf16[128,128]{1,0:T(8,128)(2,1)S(1)} %get-tuple-element.18), channel_id=1, source_target_pairs={{0,192},{64,0},{128,64},{192,128},{1,193},{65,1},{129,65},{193,129... | collective-permute-start | bytes 98312 | tf_op jit(solution)/shard_map/ppermute | solution.py:227
  286.2 5.4 %collective-permute-start.22 = (bf16[128,128]{1,0:T(8,128)(2,1)S(1)}, bf16[128,128]{1,0:T(8,128)(2,1)S(1)}, u32[]{:S(2)}, u32[]{:S(2)}) collective-permute-start(bf16[128,128]{1,0:T(8,128)(2,1)S(1)} %get-tuple-element.17), channel_id=1, source_target_pairs={{0,128},{64,192},{128,0},{192,64},{1,129},{65,193},{129,1},{193,65... | collective-permute-start | bytes 98312 | tf_op jit(solution)/shard_map/ppermute | solution.py:227
  287.8 5.4 %collective-permute-start.23 = (bf16[128,128]{1,0:T(8,128)(2,1)S(1)}, bf16[128,128]{1,0:T(8,128)(2,1)S(1)}, u32[]{:S(2)}, u32[]{:S(2)}) collective-permute-start(bf16[128,128]{1,0:T(8,128)(2,1)S(1)} %get-tuple-element.16), channel_id=1, source_target_pairs={{0,64},{64,128},{128,192},{192,0},{1,65},{65,129},{129,193},{193,1... | collective-permute-start | bytes 98312 | tf_op jit(solution)/shard_map/ppermute | solution.py:227
  293.3 7.1 %collective-permute-start.24 = (bf16[128,512]{1,0:T(8,128)(2,1)S(1)}, bf16[128,512]{1,0:T(8,128)(2,1)S(1)}, u32[]{:S(2)}, u32[]{:S(2)}) collective-permute-start(bf16[128,512]{1,0:T(8,128)(2,1)S(1)} %get-tuple-element.14), channel_id=1, source_target_pairs={{0,1},{1,2},{2,3},{3,0},{4,5},{5,6},{6,7},{7,4},{8,9},{9,10},{10,1... | collective-permute-start | bytes 393224 | tf_op jit(solution)/shard_map/ppermute | solution.py:21
  295.1 9.1 %collective-permute-start.25 = (bf16[128,512]{1,0:T(8,128)(2,1)S(1)}, bf16[128,512]{1,0:T(8,128)(2,1)S(1)}, u32[]{:S(2)}, u32[]{:S(2)}) collective-permute-start(bf16[128,512]{1,0:T(8,128)(2,1)S(1)} %get-tuple-element.14), channel_id=1, source_target_pairs={{0,2},{1,3},{2,0},{3,1},{4,6},{5,7},{6,4},{7,5},{8,10},{9,11},{10,... | collective-permute-start | bytes 393224 | tf_op jit(solution)/shard_map/ppermute | solution.py:21
  300.4 5.1 %collective-permute-start.26 = (bf16[128,512]{1,0:T(8,128)(2,1)S(1)}, bf16[128,512]{1,0:T(8,128)(2,1)S(1)}, u32[]{:S(2)}, u32[]{:S(2)}) collective-permute-start(bf16[128,512]{1,0:T(8,128)(2,1)S(1)} %get-tuple-element.14), channel_id=1, source_target_pairs={{0,3},{1,0},{2,1},{3,2},{4,7},{5,4},{6,5},{7,6},{8,11},{9,8},{10,9... | collective-permute-start | bytes 393224 | tf_op jit(solution)/shard_map/ppermute | solution.py:21
  (7 other events, 370.1 us)
Sparse Core Ops, SparseCore 0:
  37.9 84.2 all-gather.4
  169.8 97.3 all-gather.6

commit v2 on v1

v2 whole, which is shorter than its diff:
```python
import functools

import jax
import jax.numpy as jnp
from jax import lax
from jax.experimental import pallas as pl
from jax.experimental.pallas import tpu as pltpu
from jax.sharding import Mesh
from jax.sharding import PartitionSpec as P

DH = 128
NB = 32
RUN = 128
BLOCK = 512
PAIR = 256
NORM_EPS = 1e-05
SCALE = DH ** (-0.5)


def rotations(value, axis, size, step=1):
    return [value] + [
        lax.ppermute(value, axis, [(i, (i + step * k) % size) for i in range(size)])
        for k in range(1, size)
    ]


def swap(value, axis):
    return lax.ppermute(value, axis, [(0, 1), (1, 0)])


def project_kernel(place, a0, a1, a2, a3, b0, b1, b2, b3, weights, kv_ref, q_ref, u_ref, total):
    y, x = place[0], place[4]
    seconds = (b0, b1, b2, b3)
    for kx, first in enumerate((a0, a1, a2, a3)):
        ky = (y - (x - kx)) & 3
        second = jnp.concatenate([b[kx * RUN : (kx + 1) * RUN, :] for b in seconds], axis=0)
        for m in range(4):
            left = first[...] if m < 2 else second
            right = jnp.concatenate([weights[j * 4 + m, ky, :64, :] for j in range(4)], axis=0)
            part = jnp.dot(
                left[:, (m & 1) * 256 : (m & 1) * 256 + 256], right, preferred_element_type=jnp.float32
            )
            if kx == 0 and m == 0:
                total[...] = part
            else:
                total[...] += part
    half = 0.5 * total[...]
    act = (half + half * jnp.tanh(half)).astype(jnp.bfloat16)
    for r in range(4):
        rows = slice(r * RUN, (r + 1) * RUN)
        u_ref[r] = act[rows, :DH]
        kv_ref[r, :, :DH] = act[rows, DH : 2 * DH]
        q_ref[r] = act[rows, 2 * DH : 3 * DH]
        kv_ref[r, :, DH:] = act[rows, 3 * DH :]


def attend_kernel(
    place,
    lengths,
    q_edges,
    k_edges,
    biases,
    q0,
    q1,
    q2,
    q3,
    kv_near,
    kv_far,
    q_ids,
    k_ids,
    table,
    own_ref,
    send_ref,
    queries,
    acc,
):
    y, zl, core, zh = (place[i] for i in range(4))
    block = zl * 2 + core
    end0 = lengths[0]
    end1 = end0 + lengths[1]
    end2 = end1 + lengths[2]

    def user_start(pos):
        return jnp.where(
            pos >= end2, end2, jnp.where(pos >= end1, end1, jnp.where(pos >= end0, end0, 0))
        )

    for kz, source in enumerate((q0, q1, q2, q3)):
        rows = pl.ds(pl.multiple_of(((zh - kz) & 3) * RUN, RUN), RUN)
        for r in range(4):
            queries[r, rows, :] = source[r]
    table_rows = jnp.broadcast_to(table[...], (PAIR, DH))

    @pl.loop(0, 4)
    def _(r):
        group = (y - r) & 3
        first = group * 2048 + block * BLOCK
        start_low, start_high = user_start(first), user_start(first + BLOCK - 1)
        q_low, q_high = q_edges[r, 0], q_edges[r, 1]
        acc[...] = jnp.zeros_like(acc)

        def tile(t, carry):
            ky, zl_from = (y - (t >> 1)) & 3, t & 1
            zx = zl ^ zl_from
            near, far = kv_near[zx, ky], kv_far[zx, ky]
            keys = jnp.concatenate([near[:, DH:], far[:, DH:]], axis=0)
            values = jnp.concatenate([near[:, :DH], far[:, :DH]], axis=0)
            k_first = t * 1024 + zh * RUN
            k_last = k_first + BLOCK + RUN - 1
            gap_low = jnp.clip(q_low - k_edges[ky, zl_from * 2 + 1], 0, NB - 1)
            gap_high = jnp.clip(q_high - k_edges[ky, zl_from * 2], 0, NB - 1)
            plain = (k_last <= first) & (k_first >= start_high) & (gap_low == gap_high)

            def scores(part):
                rows = slice(part * PAIR, (part + 1) * PAIR)
                return rows, lax.dot_general(
                    queries[r, rows, :],
                    keys,
                    (((1,), (1,)), ((), ())),
                    preferred_element_type=jnp.float32,
                ) * (0.5 * SCALE)

            @pl.when(plain)
            def _():
                bias = 0.5 * biases[gap_low]
                for part in range(2):
                    rows, half = scores(part)
                    half = half + bias
                    weights = (half + half * jnp.tanh(half)).astype(jnp.bfloat16)
                    acc[rows, :] += jnp.dot(weights, values, preferred_element_type=jnp.float32)

            @pl.when(jnp.logical_not(plain))
            def _():
                k_row = k_ids[ky, pl.ds(zl_from, 1), :]
                column = lax.broadcasted_iota(jnp.int32, (1, PAIR), 1)
                k_pos = k_first + ((column >> 7) ^ core) * BLOCK + (column & (RUN - 1))
                for part in range(2):
                    rows, half = scores(part)
                    gaps = jnp.clip(q_ids[r, rows, :] - k_row, 0, NB - 1)
                    bias = jnp.concatenate(
                        [
                            jnp.take_along_axis(
                                table_rows,
                                gaps[:, c * DH : (c + 1) * DH],
                                axis=1,
                                mode="promise_in_bounds",
                            )
                            for c in range(PAIR // DH)
                        ],
                        axis=1,
                    )
                    half = half + 0.5 * bias
                    q_pos = first + part * PAIR + lax.broadcasted_iota(jnp.int32, (PAIR, 1), 0)
                    seen = (k_pos <= q_pos) & (k_pos >= user_start(q_pos))
                    silu = half + half * jnp.tanh(half)
                    weights = jnp.where(seen, silu, 0.0).astype(jnp.bfloat16)
                    acc[rows, :] += jnp.dot(weights, values, preferred_element_type=jnp.float32)

            return carry

        lowest = jnp.maximum((start_low - (BLOCK + RUN - 1) - zh * RUN + 1023) >> 10, 0)
        lax.fori_loop(lowest, group * 2 + zl + 1, tile, 0)
        own_ref[r] = acc[pl.ds(pl.multiple_of(zh * RUN, RUN), RUN), :]
        for k in range(1, 4):
            rows = pl.ds(pl.multiple_of(((zh + k) & 3) * RUN, RUN), RUN)
            send_ref[k - 1, r] = acc[rows, :].astype(jnp.bfloat16)


def gate_kernel(own, p1, p2, p3, u, gain, out_ref):
    attended = own[...]
    for part in (p1, p2, p3):
        attended += part[...].astype(jnp.float32)
    mean = jnp.mean(attended, axis=-1, keepdims=True)
    centered = attended - mean
    var = jnp.mean(centered * centered, axis=-1, keepdims=True)
    normed = centered * lax.rsqrt(var + NORM_EPS) * gain[...]
    out_ref[...] = (normed * u[...].astype(jnp.float32)).astype(jnp.bfloat16)


def output_kernel(place, tokens, gated, weights, out_ref, rows):
    y, x = place[0], place[4]
    for kx in range(4):
        for k in range(4):
            head = ((x - kx) & 3) * 4 + ((y + k) & 3)
            rows[:, pl.ds(pl.multiple_of(head * DH, DH), DH)] = gated[kx, :, k * DH : (k + 1) * DH]
    for m in range(4):
        columns = slice(m * 256, (m + 1) * 256)
        total = tokens[:, columns].astype(jnp.float32)
        for ky in range(4):
            source = (y - ky) & 3
            left = rows[:, pl.ds(pl.multiple_of(source * 512, 512), 512)]
            right = jnp.concatenate([weights[j * 4 + m, ky] for j in range(4)], axis=0)
            total += lax.dot_general(
                left, right, (((1,), (1,)), ((), ())), preferred_element_type=jnp.float32
            )
        out_ref[:, columns] = total.astype(jnp.bfloat16)


def call(kernel, shapes, n_smem, n_vmem, scratch, flops, moved, name):
    return pl.pallas_call(
        kernel,
        out_shape=shapes,
        in_specs=[pl.BlockSpec(memory_space=pltpu.SMEM)] * n_smem
        + [pl.BlockSpec(memory_space=pltpu.VMEM)] * n_vmem,
        out_specs=jax.tree.map(lambda _: pl.BlockSpec(memory_space=pltpu.VMEM), shapes),
        scratch_shapes=scratch,
        compiler_params=pltpu.CompilerParams(vmem_limit_bytes=40 * 2**20),
        cost_estimate=pl.CostEstimate(flops=flops, bytes_accessed=moved, transcendentals=0),
        name=name,
    )


def on_device(tokens, w_uvqk, w_out, rab_table, norm_gain, user_lengths, bucket_ids):
    bf16, f32 = jnp.bfloat16, jnp.float32
    y, zl, core, zh, x = (lax.axis_index(a) for a in ("y", "zl", "core", "zh", "x"))
    place = jnp.stack([y, zl, core, zh, x]).astype(jnp.int32)
    plane = ("zh", "zl", "core")

    ids = jnp.stack([bucket_ids // 128, bucket_ids % 128]).astype(bf16)
    ids = jnp.concatenate([ids, jnp.zeros((14, BLOCK), bf16)], axis=0)

    def columns(owner):
        part = lax.dynamic_slice_in_dim(w_uvqk, owner * 512, 512, 1)
        return jnp.concatenate([part, ids], axis=0)

    pieces = [columns(y)] + [
        lax.ppermute(columns((y + k) & 3), "y", [(i, (i + k) % 4) for i in range(4)])
        for k in range(1, 4)
    ]
    piece = jnp.stack(pieces)
    weights = lax.all_gather(piece, plane)

    first = jnp.concatenate(rotations(tokens[:, :512], "y", 4), axis=0)
    second = jnp.concatenate(rotations(tokens[:, 512:], "x", 4), axis=0)
    firsts = rotations(first, "x", 4)
    seconds = rotations(second, "y", 4)

    late, _ = lax.optimization_barrier((w_out.T, (first, second)))
    swapped = lax.ppermute(late, ("y", "x"), [(b * 4 + a, a * 4 + b) for a in range(4) for b in range(4)])
    wo = jnp.stack(rotations(swapped, "y", 4))

    kv, q, u = call(
        project_kernel,
        [
            jax.ShapeDtypeStruct((4, RUN, 2 * DH), bf16),
            jax.ShapeDtypeStruct((4, RUN, DH), bf16),
            jax.ShapeDtypeStruct((4, RUN, DH), bf16),
        ],
        1,
        9,
        [pltpu.VMEM((512, 512), f32)],
        2 * 512 * 512 * 4096,
        9 * 2**20,
        "project",
    )(place, *firsts, *seconds, weights)

    wo, _ = lax.optimization_barrier((wo, kv))
    wo_all = lax.all_gather(wo, plane)

    kv_near = jnp.stack([kv, swap(kv, "zl")])
    kv_far = swap(kv_near, "core")
    q_all = rotations(q, "zh", 4)

    coded = weights[:4, :, 64:66].astype(jnp.int32)
    all_ids = (coded[:, :, 0] * 128 + coded[:, :, 1]).transpose(1, 0, 2)
    q_ids = lax.dynamic_slice(all_ids, (0, zl * 2 + core, 0), (4, 1, BLOCK)).reshape(4, BLOCK, 1)
    k_ids = lax.dynamic_slice(all_ids, (0, 0, zh * RUN), (4, 4, RUN))
    q_edges = jnp.concatenate([q_ids[:, 0], q_ids[:, -1]], axis=1)
    k_edges = jnp.stack([k_ids[:, ::2, 0], k_ids[:, 1::2, -1]], axis=-1).reshape(4, 4)
    k_pairs = k_ids.reshape(4, 2, 2, RUN)
    k_pairs = jnp.where(core == 0, k_pairs, k_pairs[:, :, ::-1]).reshape(4, 2, PAIR)
    head = x * 4 + y
    biases = lax.dynamic_slice(rab_table, (head, 0), (1, NB))
    gain = lax.dynamic_slice(norm_gain, (head, 0), (1, DH))
    table = jnp.pad(biases, ((0, 0), (0, DH - NB)))

    own, parts = call(
        attend_kernel,
        [jax.ShapeDtypeStruct((4, RUN, DH), f32), jax.ShapeDtypeStruct((3, 4, RUN, DH), bf16)],
        5,
        9,
        [pltpu.VMEM((4, BLOCK, DH), bf16), pltpu.VMEM((BLOCK, DH), f32)],
        4 * 512 * 4096 * DH,
        5 * 2**20,
        "attend",
    )(place, user_lengths, q_edges, k_edges, biases[0], *q_all, kv_near, kv_far, q_ids, k_pairs, table)

    arrived = [
        lax.ppermute(parts[k - 1], "zh", [(i, (i + k) % 4) for i in range(4)]) for k in range(1, 4)
    ]
    gated = call(
        gate_kernel,
        jax.ShapeDtypeStruct((4, RUN, DH), bf16),
        0,
        6,
        [],
        20 * 512 * DH,
        2**20,
        "gate",
    )(own, *arrived, u, gain)

    owned = [gated[0]] + [
        lax.ppermute(gated[k], "y", [(i, (i - k) % 4) for i in range(4)]) for k in range(1, 4)
    ]
    heads = jnp.stack(rotations(jnp.concatenate(owned, axis=1), "x", 4))

    return call(
        output_kernel,
        jax.ShapeDtypeStruct((RUN, 1024), bf16),
        1,
        3,
        [pltpu.VMEM((RUN, 2048), bf16)],
        2 * RUN * 2048 * 1024,
        5 * 2**20,
        "project_out",
    )(place, tokens, heads, wo_all)


def solution(mesh):
    fine = Mesh(mesh.devices.reshape(4, 2, 2, 4, 4), ("y", "zl", "core", "zh", "x"))
    every = ("y", "zl", "core", "zh")
    placed = (
        P(every, "x"),
        P(every, "x"),
        P("x", every),
        P(),
        P(),
        P(),
        P(("y", "zl", "core")),
    )
    return jax.shard_map(
        on_device, mesh=fine, in_specs=placed, out_specs=P(every, "x"), check_vma=False
    )
```

time: 320 us -> 190 us (0.59)
  waiting for transfers between devices: 202 us -> 84.1 us
  starting transfers between devices: 62.5 us -> 57.6 us
  Pallas kernels: 22.8 us -> 19.5 us
    all_gather x2, waiting for transfers between devices: 87.5 us -> 0.03 us  [the longest x1 0.02 us: on_device(): wo_all = lax.all_gather(wo, plane)]
    ppermute x9 -> x6, waiting for transfers between devices: 47.1 us -> 28.3 us  [the longest x2 19.3 us: swap(): return lax.ppermute(value, axis, [(0, 1), (1, 0)])]
    ppermute x15 -> x21, waiting for transfers between devices: 59.5 us -> 46.2 us  [rotations(): lax.ppermute(value, axis, [(i, (i + step * k) % size) for i in range(size)])]
    ppermute x9 -> x6, starting transfers between devices: 18.7 us -> 7.39 us  [the longest x3 4.78 us: on_device(): lax.ppermute(parts[k - 1], 'zh', [(i, (i + k) % 4) for i in range(4)])]
    ppermute x15 -> x21, starting transfers between devices: 33.5 us -> 39.4 us  [rotations(): lax.ppermute(value, axis, [(i, (i + step * k) % size) for i in range(size)])]
    pallas_call x3 -> x4, Pallas kernels: 22.8 us -> 19.5 us  [the longest x1 12.9 us: on_device(): call(attend_kernel, [jax.ShapeDtypeStruct((4, RUN, DH), f32), jax.ShapeDt...]
    unnamed x23 -> x15, local copies, waits for them, and re-layouts: 6.87 us -> 6.23 us
  transfers between devices with their start and end apart: 32 -> 35, of which waited for: 17 -> 25; matrix products, arithmetic and copies ran while one was open for 3% -> 3% of each run, Pallas kernels for 6% -> 7%
where the time goes in v2:
time: 190 us; the launch traced here: 189 us
  waiting for transfers between devices  84.1 us (44%)
  starting transfers between devices  57.6 us (30%)
  Pallas kernels  19.5 us (10%)
  between operations  13.7 us (7%)
  local copies, waits for them, and re-layouts  10.6 us (6%)
  other arithmetic  3.67 us (2%)
    ppermute x21, waiting for transfers between devices, rotations(): lax.ppermute(value, axis, [(i, (i + step * k) % size) for i in range(size)])  46.2 us
    ppermute x21, starting transfers between devices, rotations(): lax.ppermute(value, axis, [(i, (i + step * k) % size) for i in range(size)])  39.4 us
    ppermute x2, waiting for transfers between devices, swap(): return lax.ppermute(value, axis, [(0, 1), (1, 0)])  19.3 us
    pallas_call x1, Pallas kernels, on_device(): call(attend_kernel, [jax.ShapeDtypeStruct((4, RUN, DH), f32), jax.ShapeDt...  12.9 us
    ppermute x3, waiting for transfers between devices, on_device(): lax.ppermute(parts[k - 1], 'zh', [(i, (i + k) % 4) for i in range(4)])  9.03 us
    unnamed x15, local copies, waits for them, and re-layouts  6.23 us
    ppermute x3, starting transfers between devices, on_device(): lax.ppermute(gated[k], 'y', [(i, (i - k) % 4) for i in range(4)])  6.05 us
    ppermute x3, waiting for transfers between devices, on_device(): lax.ppermute(columns(y + k & 3), 'y', [(i, (i + k) % 4) for i in range(4)])  5.56 us
  transfers between devices with their start and end apart: 35, of which 25 were waited for; matrix products, arithmetic and copies ran while one was open for 3% of the time, Pallas kernels for 7%

profile of v2, /device:TPU:32, one launch (start us, length us, event | category | flops | bytes accessed | tf_op | source)
XLA Modules:
  0.0 189.1 jit_solution(5724515200882898874)
XLA Ops:
  8.4 3.1 %collective-permute-start.2 = (bf16[80,512]{1,0:T(8,128)(2,1)S(1)}, bf16[80,512]{1,0:T(8,128)(2,1)S(1)}, u32[]{:S(2)}, u32[]{:S(2)}) collective-permute-start(bf16[80,512]{1,0:T(8,128)(2,1)S(1)} %get-tuple-element.41), channel_id=1, source_target_pairs={{0,192},{64,0},{128,64},{192,128},{1,193},{65,1},{129,65},{193,129... | collective-permute-start | bytes 245768 | tf_op jit(solution)/shard_map/ppermute | solution.py:227
  13.1 1.9 collective-permute-done.2
  15.0 2.9 %collective-permute-done.1 = bf16[80,512]{1,0:T(8,128)(2,1)S(1)} collective-permute-done((bf16[80,512]{1,0:T(8,128)(2,1)S(1)}, bf16[80,512]{1,0:T(8,128)(2,1)S(1)}, u32[]{:S(2)}, u32[]{:S(2)}) %collective-permute-start.1) | collective-permute-done | bytes 81952 | tf_op jit(solution)/shard_map/ppermute | solution.py:227
  22.9 3.8 %collective-permute-done.5 = bf16[128,512]{1,0:T(8,128)(2,1)S(1)} collective-permute-done((bf16[128,512]{1,0:T(8,128)(2,1)S(1)}, bf16[128,512]{1,0:T(8,128)(2,1)S(1)}, u32[]{:S(2)}, u32[]{:S(2)}) %collective-permute-start.5) | collective-permute-done | bytes 131104 | tf_op jit(solution)/shard_map/ppermute | solution.py:22
  26.7 2.2 %collective-permute-done.4 = bf16[128,512]{1,0:T(8,128)(2,1)S(1)} collective-permute-done((bf16[128,512]{1,0:T(8,128)(2,1)S(1)}, bf16[128,512]{1,0:T(8,128)(2,1)S(1)}, u32[]{:S(2)}, u32[]{:S(2)}) %collective-permute-start.4) | collective-permute-done | bytes 131104 | tf_op jit(solution)/shard_map/ppermute | solution.py:22
  29.8 1.6 collective-permute-start.6
  31.3 1.7 collective-permute-start.11
  33.1 1.8 collective-permute-start.10
  36.9 11.9 %collective-permute-done.10 = bf16[128,512]{1,0:T(8,128)(2,1)S(1)} collective-permute-done((bf16[128,512]{1,0:T(8,128)(2,1)S(1)}, bf16[128,512]{1,0:T(8,128)(2,1)S(1)}, u32[]{:S(2)}, u32[]{:S(2)}) %collective-permute-start.10) | collective-permute-done | bytes 131104 | tf_op jit(solution)/shard_map/ppermute | solution.py:22
  50.7 9.6 %collective-permute-start.32 = (bf16[64,512]{1,0:T(8,128)(2,1)S(1)}, bf16[64,512]{1,0:T(8,128)(2,1)S(1)}, u32[]{:S(2)}, u32[]{:S(2)}) collective-permute-start(bf16[64,512]{1,0:T(8,128)(2,1)S(1)} %collective-permute-done.29), channel_id=1, source_target_pairs={{0,192},{64,0},{128,64},{192,128},{1,193},{65,1},{129,65},{193,129... | collective-permute-start | bytes 196616 | tf_op jit(solution)/shard_map/ppermute | solution.py:22
  61.2 2.2 %collective-permute-start.7 = (bf16[512,512]{1,0:T(8,128)(2,1)S(1)}, bf16[512,512]{1,0:T(8,128)(2,1)S(1)}, u32[]{:S(2)}, u32[]{:S(2)}) collective-permute-start(bf16[512,512]{1,0:T(8,128)(2,1)S(1)} %pad_maximum_fusion.a0), channel_id=1, source_target_pairs={{0,2},{1,3},{2,0},{3,1},{4,6},{5,7},{6,4},{7,5},{8,10},{9,11},{10,... | collective-permute-start | bytes 1572872 | tf_op jit(solution)/shard_map/ppermute | solution.py:22
  64.7 2.1 %collective-permute-done.31 = bf16[64,512]{1,0:T(8,128)(2,1)S(1)} collective-permute-done((bf16[64,512]{1,0:T(8,128)(2,1)S(1)}, bf16[64,512]{1,0:T(8,128)(2,1)S(1)}, u32[]{:S(2)}, u32[]{:S(2)}) %collective-permute-start.31) | collective-permute-done | bytes 65568 | tf_op jit(solution)/shard_map/ppermute | solution.py:22
  67.2 1.7 collective-permute-start.13
  71.9 10.6 %collective-permute-done.8.a3 = bf16[512,512]{1,0:T(8,128)(2,1)S(1)} collective-permute-done((bf16[512,512]{1,0:T(8,128)(2,1)S(1)}, bf16[512,512]{1,0:T(8,128)(2,1)S(1)}, u32[]{:S(2)}, u32[]{:S(2)}) %collective-permute-start.8) | collective-permute-done | bytes 524320 | tf_op jit(solution)/shard_map/ppermute | solution.py:22
  82.5 6.0 %collective-permute-done.12.b1 = bf16[512,512]{1,0:T(8,128)(2,1)S(1)} collective-permute-done((bf16[512,512]{1,0:T(8,128)(2,1)S(1)}, bf16[512,512]{1,0:T(8,128)(2,1)S(1)}, u32[]{:S(2)}, u32[]{:S(2)}) %collective-permute-start.12) | collective-permute-done | bytes 524320 | tf_op jit(solution)/shard_map/ppermute | solution.py:22
  88.5 2.5 %copy-done.1 = bf16[64,80,512]{2,1,0:T(8,128)(2,1)S(1)} copy-done((bf16[64,80,512]{2,1,0:T(8,128)(2,1)S(1)}, bf16[64,80,512]{2,1,0:T(8,128)(2,1)}, u32[]{:S(2)}) %copy-start.1) | copy-done | bytes 5242904
  91.0 3.6 %project.1 = (bf16[4,128,256]{2,1,0:T(8,128)(2,1)S(1)}, bf16[4,128,128]{2,1,0:T(8,128)(2,1)S(1)}, bf16[4,128,128]{2,1,0:T(8,128)(2,1)S(1)}) custom-call(s32[5]{0:T(128)S(1)} %stack.90.place, bf16[512,512]{1,0:T(8,128)(2,1)S(1)} %pad_maximum_fusion.a0, bf16[512,512]{1,0:T(8,128)(2,1)S(1)} %collective-permute-done.6.a1, ...), custom_call_target="tpu_custom_call" | custom-call | flops 2147483648 | bytes 9437184 | tf_op jit(solution)/shard_map/project/pallas_call | solution.py:242
  96.7 3.3 %collective-permute-start.15 = (bf16[4,128,128]{2,1,0:T(8,128)(2,1)}, bf16[4,128,128]{2,1,0:T(8,128)(2,1)S(1)}, u32[]{:S(2)}, u32[]{:S(2)}) collective-permute-start(bf16[4,128,128]{2,1,0:T(8,128)(2,1)} %copy-done.4), channel_id=1, source_target_pairs={{0,4},{4,8},{8,12},{12,0},{1,5},{5,9},{9,13},{13,1},{2,6},{6,10},{... | collective-permute-start | bytes 393224 | tf_op jit(solution)/shard_map/ppermute | solution.py:22
  100.0 4.5 %collective-permute-start.16 = (bf16[4,128,128]{2,1,0:T(8,128)(2,1)}, bf16[4,128,128]{2,1,0:T(8,128)(2,1)S(1)}, u32[]{:S(2)}, u32[]{:S(2)}) collective-permute-start(bf16[4,128,128]{2,1,0:T(8,128)(2,1)} %copy-done.4), channel_id=1, source_target_pairs={{0,8},{4,12},{8,0},{12,4},{1,9},{5,13},{9,1},{13,5},{2,10},{6,14},... | collective-permute-start | bytes 393224 | tf_op jit(solution)/shard_map/ppermute | solution.py:22
  104.5 2.7 %collective-permute-start.17 = (bf16[4,128,128]{2,1,0:T(8,128)(2,1)}, bf16[4,128,128]{2,1,0:T(8,128)(2,1)S(1)}, u32[]{:S(2)}, u32[]{:S(2)}) collective-permute-start(bf16[4,128,128]{2,1,0:T(8,128)(2,1)} %copy-done.4), channel_id=1, source_target_pairs={{0,12},{4,0},{8,4},{12,8},{1,13},{5,1},{9,5},{13,9},{2,14},{6,2},{... | collective-permute-start | bytes 393224 | tf_op jit(solution)/shard_map/ppermute | solution.py:22
  109.3 18.3 %collective-permute-done.18 = bf16[4,128,256]{2,1,0:T(8,128)(2,1)S(1)} collective-permute-done((bf16[4,128,256]{2,1,0:T(8,128)(2,1)S(1)}, bf16[4,128,256]{2,1,0:T(8,128)(2,1)S(1)}, u32[]{:S(2)}, u32[]{:S(2)}) %collective-permute-start.18) | collective-permute-done | bytes 262176 | tf_op jit(solution)/shard_map/ppermute | solution.py:28
  130.5 12.9 %attend.1 = (f32[4,128,128]{2,1,0:T(8,128)S(1)}, bf16[3,4,128,128]{3,2,1,0:T(8,128)(2,1)S(1)}) custom-call(s32[5]{0:T(128)S(1)} %stack.90.place, s32[4]{0:T(128)S(1)} %copy-done.6, s32[4,2]{1,0:T(4,128)S(1)} %pad_add_fusion.1.q_edges, s32[4,4]{1,0:T(4,128)S(1)} %copy.25.k_edges, f32[32]{0:T(128)S(1)} %fusion.11.biases, bf16[4,128,128]{2,1,0:T(8,128)(2,1)S(1)} %copy-done.5, ...), custom_call_target="tpu_custom_call" | custom-call | flops 1073741824 | bytes 5242880 | tf_op jit(solution)/shard_map/attend/pallas_call | solution.py:277
  143.5 4.7 %collective-permute-start.21 = (bf16[4,128,128]{2,1,0:T(8,128)(2,1)S(1)}, bf16[4,128,128]{2,1,0:T(8,128)(2,1)S(1)}, u32[]{:S(2)}, u32[]{:S(2)}) collective-permute-start(bf16[4,128,128]{2,1,0:T(8,128)(2,1)S(1)} %get-tuple-element.20), channel_id=1, source_target_pairs={{0,8},{4,12},{8,0},{12,4},{1,9},{5,13},{9,1},{13,5},{2,10},{6,14},... | collective-permute-start | bytes 393224 | tf_op jit(solution)/shard_map/ppermute | solution.py:289
  148.2 3.0 %collective-permute-done.20.p1 = bf16[4,128,128]{2,1,0:T(8,128)(2,1)S(1)} collective-permute-done((bf16[4,128,128]{2,1,0:T(8,128)(2,1)S(1)}, bf16[4,128,128]{2,1,0:T(8,128)(2,1)S(1)}, u32[]{:S(2)}, u32[]{:S(2)}) %collective-permute-start.20) | collective-permute-done | bytes 131104 | tf_op jit(solution)/shard_map/ppermute | solution.py:289
  151.2 4.5 %collective-permute-done.21.p2 = bf16[4,128,128]{2,1,0:T(8,128)(2,1)S(1)} collective-permute-done((bf16[4,128,128]{2,1,0:T(8,128)(2,1)S(1)}, bf16[4,128,128]{2,1,0:T(8,128)(2,1)S(1)}, u32[]{:S(2)}, u32[]{:S(2)}) %collective-permute-start.21) | collective-permute-done | bytes 131104 | tf_op jit(solution)/shard_map/ppermute | solution.py:289
  157.5 3.1 %collective-permute-start.25 = (bf16[128,128]{1,0:T(8,128)(2,1)S(1)}, bf16[128,128]{1,0:T(8,128)(2,1)S(1)}, u32[]{:S(2)}, u32[]{:S(2)}) collective-permute-start(bf16[128,128]{1,0:T(8,128)(2,1)S(1)} %get-tuple-element.31), channel_id=1, source_target_pairs={{0,64},{64,128},{128,192},{192,0},{1,65},{65,129},{129,193},{193,1... | collective-permute-start | bytes 98312 | tf_op jit(solution)/shard_map/ppermute | solution.py:303
  160.6 2.9 %collective-permute-start.24 = (bf16[128,128]{1,0:T(8,128)(2,1)S(1)}, bf16[128,128]{1,0:T(8,128)(2,1)S(1)}, u32[]{:S(2)}, u32[]{:S(2)}) collective-permute-start(bf16[128,128]{1,0:T(8,128)(2,1)S(1)} %get-tuple-element.32), channel_id=1, source_target_pairs={{0,128},{64,192},{128,0},{192,64},{1,129},{65,193},{129,1},{193,65... | collective-permute-start | bytes 98312 | tf_op jit(solution)/shard_map/ppermute | solution.py:303
  164.0 2.1 %collective-permute-done.24 = bf16[128,128]{1,0:T(8,128)(2,1)S(1)} collective-permute-done((bf16[128,128]{1,0:T(8,128)(2,1)S(1)}, bf16[128,128]{1,0:T(8,128)(2,1)S(1)}, u32[]{:S(2)}, u32[]{:S(2)}) %collective-permute-start.24) | collective-permute-done | bytes 32800 | tf_op jit(solution)/shard_map/ppermute | solution.py:303
  167.5 1.8 collective-permute-start.28
  172.6 3.3 %collective-permute-done.27 = bf16[128,512]{1,0:T(8,128)(2,1)S(1)} collective-permute-done((bf16[128,512]{1,0:T(8,128)(2,1)S(1)}, bf16[128,512]{1,0:T(8,128)(2,1)S(1)}, u32[]{:S(2)}, u32[]{:S(2)}) %collective-permute-start.27) | collective-permute-done | bytes 131104 | tf_op jit(solution)/shard_map/ppermute | solution.py:22
  177.3 2.2 %copy-done.2 = bf16[64,64,512]{2,1,0:T(8,128)(2,1)S(1)} copy-done((bf16[64,64,512]{2,1,0:T(8,128)(2,1)S(1)}, bf16[64,64,512]{2,1,0:T(8,128)(2,1)}, u32[]{:S(2)}) %copy-start.2) | copy-done | bytes 4194328
  179.5 2.8 %project_out.1 = bf16[128,1024]{1,0:T(8,128)(2,1)} custom-call(s32[5]{0:T(128)S(1)} %stack.90.place, bf16[128,1024]{1,0:T(8,128)(2,1)S(1)} %copy-done.3, bf16[4,128,512]{2,1,0:T(8,128)(2,1)S(1)} %pad_maximum_fusion.3.gated, bf16[16,4,64,512]{3,2,1,0:T(8,128)(2,1)S(1)} %bitcast.55), custom_call_target="tpu_custom_call" | custom-call | flops 536870912 | bytes 5242880 | tf_op jit(solution)/shard_map/project_out/pallas_call | solution.py:307
  (96 shorter events, 34.3 us)
Async XLA Ops:
  6.5 82.0 %all-gather.5.cloned.1.call-start = ((), (), s32[]{:S(2)}) async-start(), calls=%async_computation | async-start | bytes 5570560 | tf_op jit(solution)/shard_map/all_gather | solution.py:231
  8.4 6.6 %collective-permute-start.2 = (bf16[80,512]{1,0:T(8,128)(2,1)S(1)}, bf16[80,512]{1,0:T(8,128)(2,1)S(1)}, u32[]{:S(2)}, u32[]{:S(2)}) collective-permute-start(bf16[80,512]{1,0:T(8,128)(2,1)S(1)} %get-tuple-element.41), channel_id=1, source_target_pairs={{0,192},{64,0},{128,64},{192,128},{1,193},{65,1},{129,65},{193,129... | collective-permute-start | bytes 245768 | tf_op jit(solution)/shard_map/ppermute | solution.py:227
  11.5 6.3 %collective-permute-start.1 = (bf16[80,512]{1,0:T(8,128)(2,1)S(1)}, bf16[80,512]{1,0:T(8,128)(2,1)S(1)}, u32[]{:S(2)}, u32[]{:S(2)}) collective-permute-start(bf16[80,512]{1,0:T(8,128)(2,1)S(1)} %get-tuple-element.40), channel_id=1, source_target_pairs={{0,128},{64,192},{128,0},{192,64},{1,129},{65,193},{129,1},{193,65... | collective-permute-start | bytes 245768 | tf_op jit(solution)/shard_map/ppermute | solution.py:227
  12.1 6.5 %collective-permute-start = (bf16[80,512]{1,0:T(8,128)(2,1)S(1)}, bf16[80,512]{1,0:T(8,128)(2,1)S(1)}, u32[]{:S(2)}, u32[]{:S(2)}) collective-permute-start(bf16[80,512]{1,0:T(8,128)(2,1)S(1)} %get-tuple-element.39), channel_id=1, source_target_pairs={{0,64},{64,128},{128,192},{192,0},{1,65},{65,129},{129,193},{193,1... | collective-permute-start | bytes 245768 | tf_op jit(solution)/shard_map/ppermute | solution.py:227
  19.5 157.8 %all-gather.7.cloned.1.call-start = ((), (), s32[]{:S(2)}) async-start(), calls=%async_computation.1 | async-start | bytes 4456448 | tf_op jit(solution)/shard_map/all_gather | solution.py:258
  20.5 6.2 %collective-permute-start.5 = (bf16[128,512]{1,0:T(8,128)(2,1)S(1)}, bf16[128,512]{1,0:T(8,128)(2,1)S(1)}, u32[]{:S(2)}, u32[]{:S(2)}) collective-permute-start(bf16[128,512]{1,0:T(8,128)(2,1)S(1)} %get-tuple-element.23), channel_id=1, source_target_pairs={{0,192},{64,0},{128,64},{192,128},{1,193},{65,1},{129,65},{193,129... | collective-permute-start | bytes 393224 | tf_op jit(solution)/shard_map/ppermute | solution.py:22
  21.2 7.7 %collective-permute-start.4 = (bf16[128,512]{1,0:T(8,128)(2,1)S(1)}, bf16[128,512]{1,0:T(8,128)(2,1)S(1)}, u32[]{:S(2)}, u32[]{:S(2)}) collective-permute-start(bf16[128,512]{1,0:T(8,128)(2,1)S(1)} %get-tuple-element.23), channel_id=1, source_target_pairs={{0,128},{64,192},{128,0},{192,64},{1,129},{65,193},{129,1},{193,65... | collective-permute-start | bytes 393224 | tf_op jit(solution)/shard_map/ppermute | solution.py:22
  21.8 7.9 %collective-permute-start.3 = (bf16[128,512]{1,0:T(8,128)(2,1)S(1)}, bf16[128,512]{1,0:T(8,128)(2,1)S(1)}, u32[]{:S(2)}, u32[]{:S(2)}) collective-permute-start(bf16[128,512]{1,0:T(8,128)(2,1)S(1)} %get-tuple-element.23), channel_id=1, source_target_pairs={{0,64},{64,128},{128,192},{192,0},{1,65},{65,129},{129,193},{193,1... | collective-permute-start | bytes 393224 | tf_op jit(solution)/shard_map/ppermute | solution.py:22
  29.8 39.1 %collective-permute-start.6 = (bf16[512,512]{1,0:T(8,128)(2,1)S(1)}, bf16[512,512]{1,0:T(8,128)(2,1)S(1)}, u32[]{:S(2)}, u32[]{:S(2)}) collective-permute-start(bf16[512,512]{1,0:T(8,128)(2,1)S(1)} %pad_maximum_fusion.a0), channel_id=1, source_target_pairs={{0,1},{1,2},{2,3},{3,0},{4,5},{5,6},{6,7},{7,4},{8,9},{9,10},{10,1... | collective-permute-start | bytes 1572872 | tf_op jit(solution)/shard_map/ppermute | solution.py:22
  31.3 5.6 %collective-permute-start.11 = (bf16[128,512]{1,0:T(8,128)(2,1)S(1)}, bf16[128,512]{1,0:T(8,128)(2,1)S(1)}, u32[]{:S(2)}, u32[]{:S(2)}) collective-permute-start(bf16[128,512]{1,0:T(8,128)(2,1)S(1)} %get-tuple-element.22), channel_id=1, source_target_pairs={{0,3},{1,0},{2,1},{3,2},{4,7},{5,4},{6,5},{7,6},{8,11},{9,8},{10,9... | collective-permute-start | bytes 393224 | tf_op jit(solution)/shard_map/ppermute | solution.py:22
  33.1 15.7 %collective-permute-start.10 = (bf16[128,512]{1,0:T(8,128)(2,1)S(1)}, bf16[128,512]{1,0:T(8,128)(2,1)S(1)}, u32[]{:S(2)}, u32[]{:S(2)}) collective-permute-start(bf16[128,512]{1,0:T(8,128)(2,1)S(1)} %get-tuple-element.22), channel_id=1, source_target_pairs={{0,2},{1,3},{2,0},{3,1},{4,6},{5,7},{6,4},{7,5},{8,10},{9,11},{10,... | collective-permute-start | bytes 393224 | tf_op jit(solution)/shard_map/ppermute | solution.py:22
  34.9 14.2 %collective-permute-start.9 = (bf16[128,512]{1,0:T(8,128)(2,1)S(1)}, bf16[128,512]{1,0:T(8,128)(2,1)S(1)}, u32[]{:S(2)}, u32[]{:S(2)}) collective-permute-start(bf16[128,512]{1,0:T(8,128)(2,1)S(1)} %get-tuple-element.22), channel_id=1, source_target_pairs={{0,1},{1,2},{2,3},{3,0},{4,5},{5,6},{6,7},{7,4},{8,9},{9,10},{10,1... | collective-permute-start | bytes 393224 | tf_op jit(solution)/shard_map/ppermute | solution.py:22
  50.7 12.7 %collective-permute-start.32 = (bf16[64,512]{1,0:T(8,128)(2,1)S(1)}, bf16[64,512]{1,0:T(8,128)(2,1)S(1)}, u32[]{:S(2)}, u32[]{:S(2)}) collective-permute-start(bf16[64,512]{1,0:T(8,128)(2,1)S(1)} %collective-permute-done.29), channel_id=1, source_target_pairs={{0,192},{64,0},{128,64},{192,128},{1,193},{65,1},{129,65},{193,129... | collective-permute-start | bytes 196616 | tf_op jit(solution)/shard_map/ppermute | solution.py:22
  60.3 6.5 %collective-permute-start.31 = (bf16[64,512]{1,0:T(8,128)(2,1)S(1)}, bf16[64,512]{1,0:T(8,128)(2,1)S(1)}, u32[]{:S(2)}, u32[]{:S(2)}) collective-permute-start(bf16[64,512]{1,0:T(8,128)(2,1)S(1)} %collective-permute-done.29), channel_id=1, source_target_pairs={{0,128},{64,192},{128,0},{192,64},{1,129},{65,193},{129,1},{193,65... | collective-permute-start | bytes 196616 | tf_op jit(solution)/shard_map/ppermute | solution.py:22
  60.3 6.9 %collective-permute-start.30 = (bf16[64,512]{1,0:T(8,128)(2,1)S(1)}, bf16[64,512]{1,0:T(8,128)(2,1)S(1)}, u32[]{:S(2)}, u32[]{:S(2)}) collective-permute-start(bf16[64,512]{1,0:T(8,128)(2,1)S(1)} %collective-permute-done.29), channel_id=1, source_target_pairs={{0,64},{64,128},{128,192},{192,0},{1,65},{65,129},{129,193},{193,1... | collective-permute-start | bytes 196616 | tf_op jit(solution)/shard_map/ppermute | solution.py:22
  61.2 10.7 %collective-permute-start.7 = (bf16[512,512]{1,0:T(8,128)(2,1)S(1)}, bf16[512,512]{1,0:T(8,128)(2,1)S(1)}, u32[]{:S(2)}, u32[]{:S(2)}) collective-permute-start(bf16[512,512]{1,0:T(8,128)(2,1)S(1)} %pad_maximum_fusion.a0), channel_id=1, source_target_pairs={{0,2},{1,3},{2,0},{3,1},{4,6},{5,7},{6,4},{7,5},{8,10},{9,11},{10,... | collective-permute-start | bytes 1572872 | tf_op jit(solution)/shard_map/ppermute | solution.py:22
  63.4 19.1 %collective-permute-start.8 = (bf16[512,512]{1,0:T(8,128)(2,1)S(1)}, bf16[512,512]{1,0:T(8,128)(2,1)S(1)}, u32[]{:S(2)}, u32[]{:S(2)}) collective-permute-start(bf16[512,512]{1,0:T(8,128)(2,1)S(1)} %pad_maximum_fusion.a0), channel_id=1, source_target_pairs={{0,3},{1,0},{2,1},{3,2},{4,7},{5,4},{6,5},{7,6},{8,11},{9,8},{10,9... | collective-permute-start | bytes 1572872 | tf_op jit(solution)/shard_map/ppermute | solution.py:22
  66.8 21.6 %collective-permute-start.12 = (bf16[512,512]{1,0:T(8,128)(2,1)S(1)}, bf16[512,512]{1,0:T(8,128)(2,1)S(1)}, u32[]{:S(2)}, u32[]{:S(2)}) collective-permute-start(bf16[512,512]{1,0:T(8,128)(2,1)S(1)} %pad_maximum_fusion.1.b0), channel_id=1, source_target_pairs={{0,64},{64,128},{128,192},{192,0},{1,65},{65,129},{129,193},{193,1... | collective-permute-start | bytes 1572872 | tf_op jit(solution)/shard_map/ppermute | solution.py:22
  67.2 21.3 %collective-permute-start.13 = (bf16[512,512]{1,0:T(8,128)(2,1)S(1)}, bf16[512,512]{1,0:T(8,128)(2,1)}, u32[]{:S(2)}, u32[]{:S(2)}) collective-permute-start(bf16[512,512]{1,0:T(8,128)(2,1)S(1)} %pad_maximum_fusion.1.b0), channel_id=1, source_target_pairs={{0,128},{64,192},{128,0},{192,64},{1,129},{65,193},{129,1},{193,65... | collective-permute-start | bytes 1572872 | tf_op jit(solution)/shard_map/ppermute | solution.py:22
  68.9 19.6 %collective-permute-start.14 = (bf16[512,512]{1,0:T(8,128)(2,1)S(1)}, bf16[512,512]{1,0:T(8,128)(2,1)}, u32[]{:S(2)}, u32[]{:S(2)}) collective-permute-start(bf16[512,512]{1,0:T(8,128)(2,1)S(1)} %pad_maximum_fusion.1.b0), channel_id=1, source_target_pairs={{0,192},{64,0},{128,64},{192,128},{1,193},{65,1},{129,65},{193,129... | collective-permute-start | bytes 1572872 | tf_op jit(solution)/shard_map/ppermute | solution.py:22
  96.7 31.8 %collective-permute-start.15 = (bf16[4,128,128]{2,1,0:T(8,128)(2,1)}, bf16[4,128,128]{2,1,0:T(8,128)(2,1)S(1)}, u32[]{:S(2)}, u32[]{:S(2)}) collective-permute-start(bf16[4,128,128]{2,1,0:T(8,128)(2,1)} %copy-done.4), channel_id=1, source_target_pairs={{0,4},{4,8},{8,12},{12,0},{1,5},{5,9},{9,13},{13,1},{2,6},{6,10},{... | collective-permute-start | bytes 393224 | tf_op jit(solution)/shard_map/ppermute | solution.py:22
  100.0 28.6 %collective-permute-start.16 = (bf16[4,128,128]{2,1,0:T(8,128)(2,1)}, bf16[4,128,128]{2,1,0:T(8,128)(2,1)S(1)}, u32[]{:S(2)}, u32[]{:S(2)}) collective-permute-start(bf16[4,128,128]{2,1,0:T(8,128)(2,1)} %copy-done.4), channel_id=1, source_target_pairs={{0,8},{4,12},{8,0},{12,4},{1,9},{5,13},{9,1},{13,5},{2,10},{6,14},... | collective-permute-start | bytes 393224 | tf_op jit(solution)/shard_map/ppermute | solution.py:22
  104.5 24.1 %collective-permute-start.17 = (bf16[4,128,128]{2,1,0:T(8,128)(2,1)}, bf16[4,128,128]{2,1,0:T(8,128)(2,1)S(1)}, u32[]{:S(2)}, u32[]{:S(2)}) collective-permute-start(bf16[4,128,128]{2,1,0:T(8,128)(2,1)} %copy-done.4), channel_id=1, source_target_pairs={{0,12},{4,0},{8,4},{12,8},{1,13},{5,1},{9,5},{13,9},{2,14},{6,2},{... | collective-permute-start | bytes 393224 | tf_op jit(solution)/shard_map/ppermute | solution.py:22
  107.2 20.4 %collective-permute-start.18 = (bf16[4,128,256]{2,1,0:T(8,128)(2,1)S(1)}, bf16[4,128,256]{2,1,0:T(8,128)(2,1)S(1)}, u32[]{:S(2)}, u32[]{:S(2)}) collective-permute-start(bf16[4,128,256]{2,1,0:T(8,128)(2,1)S(1)} %get-tuple-element.13), channel_id=1, source_target_pairs={{0,32},{32,0},{1,33},{33,1},{2,34},{34,2},{3,35},{35,3},{4,36},{36... | collective-permute-start | bytes 786440 | tf_op jit(solution)/shard_map/ppermute | solution.py:28
  143.4 7.8 %collective-permute-start.20 = (bf16[4,128,128]{2,1,0:T(8,128)(2,1)S(1)}, bf16[4,128,128]{2,1,0:T(8,128)(2,1)S(1)}, u32[]{:S(2)}, u32[]{:S(2)}) collective-permute-start(bf16[4,128,128]{2,1,0:T(8,128)(2,1)S(1)} %get-tuple-element.21), channel_id=1, source_target_pairs={{0,4},{4,8},{8,12},{12,0},{1,5},{5,9},{9,13},{13,1},{2,6},{6,10},{... | collective-permute-start | bytes 393224 | tf_op jit(solution)/shard_map/ppermute | solution.py:289
  143.5 12.2 %collective-permute-start.21 = (bf16[4,128,128]{2,1,0:T(8,128)(2,1)S(1)}, bf16[4,128,128]{2,1,0:T(8,128)(2,1)S(1)}, u32[]{:S(2)}, u32[]{:S(2)}) collective-permute-start(bf16[4,128,128]{2,1,0:T(8,128)(2,1)S(1)} %get-tuple-element.20), channel_id=1, source_target_pairs={{0,8},{4,12},{8,0},{12,4},{1,9},{5,13},{9,1},{13,5},{2,10},{6,14},... | collective-permute-start | bytes 393224 | tf_op jit(solution)/shard_map/ppermute | solution.py:289
  148.2 9.1 %collective-permute-start.22 = (bf16[4,128,128]{2,1,0:T(8,128)(2,1)S(1)}, bf16[4,128,128]{2,1,0:T(8,128)(2,1)S(1)}, u32[]{:S(2)}, u32[]{:S(2)}) collective-permute-start(bf16[4,128,128]{2,1,0:T(8,128)(2,1)S(1)} %get-tuple-element.19), channel_id=1, source_target_pairs={{0,12},{4,0},{8,4},{12,8},{1,13},{5,1},{9,5},{13,9},{2,14},{6,2},{... | collective-permute-start | bytes 393224 | tf_op jit(solution)/shard_map/ppermute | solution.py:289
  157.5 6.5 %collective-permute-start.25 = (bf16[128,128]{1,0:T(8,128)(2,1)S(1)}, bf16[128,128]{1,0:T(8,128)(2,1)S(1)}, u32[]{:S(2)}, u32[]{:S(2)}) collective-permute-start(bf16[128,128]{1,0:T(8,128)(2,1)S(1)} %get-tuple-element.31), channel_id=1, source_target_pairs={{0,64},{64,128},{128,192},{192,0},{1,65},{65,129},{129,193},{193,1... | collective-permute-start | bytes 98312 | tf_op jit(solution)/shard_map/ppermute | solution.py:303
  160.6 5.4 %collective-permute-start.24 = (bf16[128,128]{1,0:T(8,128)(2,1)S(1)}, bf16[128,128]{1,0:T(8,128)(2,1)S(1)}, u32[]{:S(2)}, u32[]{:S(2)}) collective-permute-start(bf16[128,128]{1,0:T(8,128)(2,1)S(1)} %get-tuple-element.32), channel_id=1, source_target_pairs={{0,128},{64,192},{128,0},{192,64},{1,129},{65,193},{129,1},{193,65... | collective-permute-start | bytes 98312 | tf_op jit(solution)/shard_map/ppermute | solution.py:303
  167.5 5.0 %collective-permute-start.28 = (bf16[128,512]{1,0:T(8,128)(2,1)S(1)}, bf16[128,512]{1,0:T(8,128)(2,1)S(1)}, u32[]{:S(2)}, u32[]{:S(2)}) collective-permute-start(bf16[128,512]{1,0:T(8,128)(2,1)S(1)} %get-tuple-element.29), channel_id=1, source_target_pairs={{0,3},{1,0},{2,1},{3,2},{4,7},{5,4},{6,5},{7,6},{8,11},{9,8},{10,9... | collective-permute-start | bytes 393224 | tf_op jit(solution)/shard_map/ppermute | solution.py:22
  169.3 6.6 %collective-permute-start.27 = (bf16[128,512]{1,0:T(8,128)(2,1)S(1)}, bf16[128,512]{1,0:T(8,128)(2,1)S(1)}, u32[]{:S(2)}, u32[]{:S(2)}) collective-permute-start(bf16[128,512]{1,0:T(8,128)(2,1)S(1)} %get-tuple-element.29), channel_id=1, source_target_pairs={{0,2},{1,3},{2,0},{3,1},{4,6},{5,7},{6,4},{7,5},{8,10},{9,11},{10,... | collective-permute-start | bytes 393224 | tf_op jit(solution)/shard_map/ppermute | solution.py:22
  170.0 7.2 %collective-permute-start.26 = (bf16[128,512]{1,0:T(8,128)(2,1)S(1)}, bf16[128,512]{1,0:T(8,128)(2,1)S(1)}, u32[]{:S(2)}, u32[]{:S(2)}) collective-permute-start(bf16[128,512]{1,0:T(8,128)(2,1)S(1)} %get-tuple-element.29), channel_id=1, source_target_pairs={{0,1},{1,2},{2,3},{3,0},{4,5},{5,6},{6,7},{7,4},{8,9},{9,10},{10,1... | collective-permute-start | bytes 393224 | tf_op jit(solution)/shard_map/ppermute | solution.py:22
  (10 other events, 275.9 us)
Sparse Core Ops, SparseCore 0:
  19.6 43.4 all-gather.4
  95.4 47.0 all-gather.6

commit v3 on v2

--- a/solution.py
+++ b/solution.py
@@ -36,7 +36,7 @@
         second = jnp.concatenate([b[kx * RUN : (kx + 1) * RUN, :] for b in seconds], axis=0)
         for m in range(4):
             left = first[...] if m < 2 else second
-            right = jnp.concatenate([weights[j * 4 + m, ky, :64, :] for j in range(4)], axis=0)
+            right = jnp.concatenate([weights[j * 4 + m, ky] for j in range(4)], axis=0)
             part = jnp.dot(
                 left[:, (m & 1) * 256 : (m & 1) * 256 + 256], right, preferred_element_type=jnp.float32
             )
@@ -69,7 +69,6 @@
     q_ids,
     k_ids,
     table,
-    own_ref,
     send_ref,
     queries,
     acc,
@@ -107,8 +106,8 @@
             values = jnp.concatenate([near[:, :DH], far[:, :DH]], axis=0)
             k_first = t * 1024 + zh * RUN
             k_last = k_first + BLOCK + RUN - 1
-            gap_low = jnp.clip(q_low - k_edges[ky, zl_from * 2 + 1], 0, NB - 1)
-            gap_high = jnp.clip(q_high - k_edges[ky, zl_from * 2], 0, NB - 1)
+            gap_low = jnp.clip(q_low - k_edges[ky, zx * 2 + 1], 0, NB - 1)
+            gap_high = jnp.clip(q_high - k_edges[ky, zx * 2], 0, NB - 1)
             plain = (k_last <= first) & (k_first >= start_high) & (gap_low == gap_high)
 
             def scores(part):
@@ -131,7 +130,7 @@
 
             @pl.when(jnp.logical_not(plain))
             def _():
-                k_row = k_ids[ky, pl.ds(zl_from, 1), :]
+                k_row = k_ids[ky, pl.ds(zx, 1), :]
                 column = lax.broadcasted_iota(jnp.int32, (1, PAIR), 1)
                 k_pos = k_first + ((column >> 7) ^ core) * BLOCK + (column & (RUN - 1))
                 for part in range(2):
@@ -160,43 +159,45 @@
 
         lowest = jnp.maximum((start_low - (BLOCK + RUN - 1) - zh * RUN + 1023) >> 10, 0)
         lax.fori_loop(lowest, group * 2 + zl + 1, tile, 0)
-        own_ref[r] = acc[pl.ds(pl.multiple_of(zh * RUN, RUN), RUN), :]
-        for k in range(1, 4):
-            rows = pl.ds(pl.multiple_of(((zh + k) & 3) * RUN, RUN), RUN)
-            send_ref[k - 1, r] = acc[rows, :].astype(jnp.bfloat16)
-
-
-def gate_kernel(own, p1, p2, p3, u, gain, out_ref):
-    attended = own[...]
-    for part in (p1, p2, p3):
-        attended += part[...].astype(jnp.float32)
-    mean = jnp.mean(attended, axis=-1, keepdims=True)
-    centered = attended - mean
-    var = jnp.mean(centered * centered, axis=-1, keepdims=True)
-    normed = centered * lax.rsqrt(var + NORM_EPS) * gain[...]
-    out_ref[...] = (normed * u[...].astype(jnp.float32)).astype(jnp.bfloat16)
-
-
-def output_kernel(place, tokens, gated, weights, out_ref, rows):
-    y, x = place[0], place[4]
-    for kx in range(4):
-        for k in range(4):
-            head = ((x - kx) & 3) * 4 + ((y + k) & 3)
-            rows[:, pl.ds(pl.multiple_of(head * DH, DH), DH)] = gated[kx, :, k * DH : (k + 1) * DH]
-    for m in range(4):
-        columns = slice(m * 256, (m + 1) * 256)
-        total = tokens[:, columns].astype(jnp.float32)
-        for ky in range(4):
-            source = (y - ky) & 3
-            left = rows[:, pl.ds(pl.multiple_of(source * 512, 512), 512)]
-            right = jnp.concatenate([weights[j * 4 + m, ky] for j in range(4)], axis=0)
-            total += lax.dot_general(
-                left, right, (((1,), (1,)), ((), ())), preferred_element_type=jnp.float32
-            )
-        out_ref[:, columns] = total.astype(jnp.bfloat16)
-
-
-def call(kernel, shapes, n_smem, n_vmem, scratch, flops, moved, name):
+        attended = acc[...]
+        centered = attended - jnp.mean(attended, axis=-1, keepdims=True)
+        for zh_to in range(4):
+            rows = slice(zh_to * RUN, (zh_to + 1) * RUN)
+            send_ref[group * 4 + zh_to] = centered[rows, :].astype(jnp.bfloat16)
+
+
+def gate_kernel(place, parts, u0, u1, u2, u3, gain, out_ref):
+    y = place[0]
+    for k, u in enumerate((u0, u1, u2, u3)):
+        head = (y + k) & 3
+        attended = parts[head * 4].astype(jnp.float32)
+        for part in range(1, 4):
+            attended += parts[head * 4 + part].astype(jnp.float32)
+        mean = jnp.mean(attended, axis=-1, keepdims=True)
+        centered = attended - mean
+        var = jnp.mean(centered * centered, axis=-1, keepdims=True)
+        normed = centered * lax.rsqrt(var + NORM_EPS) * gain[pl.ds(head, 1), :]
+        columns = pl.ds(pl.multiple_of(head * DH, DH), DH)
+        out_ref[:, columns] = (normed * u[...].astype(jnp.float32)).astype(jnp.bfloat16)
+
+
+def output_kernel(place, tokens, gated, near, far, out_ref):
+    y, core, x = place[0], place[2], place[4]
+    for zl in range(2):
+        for c, source in enumerate((near, far)):
+            block = zl * 2 + (core ^ c)
+            columns = pl.ds(pl.multiple_of(block * 256, 256), 256)
+            total = tokens[:, columns].astype(jnp.float32)
+            for ky in range(4):
+                left = gated[(x - (y - ky)) & 3]
+                right = jnp.concatenate([source[ky, j * 2 + zl] for j in range(4)], axis=0)
+                total += lax.dot_general(
+                    left, right, (((1,), (1,)), ((), ())), preferred_element_type=jnp.float32
+                )
+            out_ref[:, columns] = total.astype(jnp.bfloat16)
+
+
+def call(kernel, shapes, n_smem, n_vmem, scratch, flops, moved, vmem, name):
     return pl.pallas_call(
         kernel,
         out_shape=shapes,
@@ -204,7 +205,7 @@
         + [pl.BlockSpec(memory_space=pltpu.VMEM)] * n_vmem,
         out_specs=jax.tree.map(lambda _: pl.BlockSpec(memory_space=pltpu.VMEM), shapes),
         scratch_shapes=scratch,
-        compiler_params=pltpu.CompilerParams(vmem_limit_bytes=40 * 2**20),
+        compiler_params=pltpu.CompilerParams(vmem_limit_bytes=vmem * 2**20),
         cost_estimate=pl.CostEstimate(flops=flops, bytes_accessed=moved, transcendentals=0),
         name=name,
     )
@@ -216,12 +217,8 @@
     place = jnp.stack([y, zl, core, zh, x]).astype(jnp.int32)
     plane = ("zh", "zl", "core")
 
-    ids = jnp.stack([bucket_ids // 128, bucket_ids % 128]).astype(bf16)
-    ids = jnp.concatenate([ids, jnp.zeros((14, BLOCK), bf16)], axis=0)
-
     def columns(owner):
-        part = lax.dynamic_slice_in_dim(w_uvqk, owner * 512, 512, 1)
-        return jnp.concatenate([part, ids], axis=0)
+        return lax.dynamic_slice_in_dim(w_uvqk, owner * 512, 512, 1)
 
     pieces = [columns(y)] + [
         lax.ppermute(columns((y + k) & 3), "y", [(i, (i + k) % 4) for i in range(4)])
@@ -230,15 +227,21 @@
     piece = jnp.stack(pieces)
     weights = lax.all_gather(piece, plane)
 
-    first = jnp.concatenate(rotations(tokens[:, :512], "y", 4), axis=0)
-    second = jnp.concatenate(rotations(tokens[:, 512:], "x", 4), axis=0)
-    firsts = rotations(first, "x", 4)
-    seconds = rotations(second, "y", 4)
-
-    late, _ = lax.optimization_barrier((w_out.T, (first, second)))
+    first = rotations(tokens[:, :512], "y", 4)
+    second = rotations(tokens[:, 512:], "x", 4)
+    first, second = lax.optimization_barrier((first, second))
+    firsts = rotations(jnp.concatenate(first, axis=0), "x", 4)
+    seconds = rotations(jnp.concatenate(second, axis=0), "y", 4)
+
+    ids, late, _ = lax.optimization_barrier((bucket_ids, w_out.T, (first, second)))
+    ids_y = jnp.stack(rotations(ids, "y", 4))
+    ids_near = jnp.stack([ids_y, swap(ids_y, "zl")])
+    ids_far = swap(ids_near, "core")
     swapped = lax.ppermute(late, ("y", "x"), [(b * 4 + a, a * 4 + b) for a in range(4) for b in range(4)])
-    wo = jnp.stack(rotations(swapped, "y", 4))
-
+
+    firsts, seconds, ids_y, ids_near, ids_far, swapped = lax.optimization_barrier(
+        (firsts, seconds, ids_y, ids_near, ids_far, swapped)
+    )
     kv, q, u = call(
         project_kernel,
         [
@@ -251,69 +254,74 @@
         [pltpu.VMEM((512, 512), f32)],
         2 * 512 * 512 * 4096,
         9 * 2**20,
+        24,
         "project",
     )(place, *firsts, *seconds, weights)
 
-    wo, _ = lax.optimization_barrier((wo, kv))
-    wo_all = lax.all_gather(wo, plane)
+    wo_block = lax.all_gather(swapped, plane)
 
     kv_near = jnp.stack([kv, swap(kv, "zl")])
     kv_far = swap(kv_near, "core")
+    q, _ = lax.optimization_barrier((q, kv_near))
     q_all = rotations(q, "zh", 4)
 
-    coded = weights[:4, :, 64:66].astype(jnp.int32)
-    all_ids = (coded[:, :, 0] * 128 + coded[:, :, 1]).transpose(1, 0, 2)
-    q_ids = lax.dynamic_slice(all_ids, (0, zl * 2 + core, 0), (4, 1, BLOCK)).reshape(4, BLOCK, 1)
-    k_ids = lax.dynamic_slice(all_ids, (0, 0, zh * RUN), (4, 4, RUN))
-    q_edges = jnp.concatenate([q_ids[:, 0], q_ids[:, -1]], axis=1)
-    k_edges = jnp.stack([k_ids[:, ::2, 0], k_ids[:, 1::2, -1]], axis=-1).reshape(4, 4)
-    k_pairs = k_ids.reshape(4, 2, 2, RUN)
-    k_pairs = jnp.where(core == 0, k_pairs, k_pairs[:, :, ::-1]).reshape(4, 2, PAIR)
-    head = x * 4 + y
-    biases = lax.dynamic_slice(rab_table, (head, 0), (1, NB))
-    gain = lax.dynamic_slice(norm_gain, (head, 0), (1, DH))
+    q_ids = ids_y.reshape(4, BLOCK, 1)
+    k_ids = lax.dynamic_slice(jnp.stack([ids_near, ids_far]), (0, 0, 0, zh * RUN), (2, 2, 4, RUN))
+    k_edges = jnp.stack([jnp.min(k_ids[..., 0], axis=0), jnp.max(k_ids[..., -1], axis=0)], axis=-1)
+    k_edges = k_edges.transpose(1, 0, 2).reshape(4, 4)
+    k_ids = k_ids.transpose(2, 1, 0, 3).reshape(4, 2, PAIR)
+    q_edges = jnp.stack([ids_y[:, 0], ids_y[:, -1]], axis=1)
+    biases = lax.dynamic_slice(rab_table, (x * 4 + y, 0), (1, NB))
+    gains = lax.dynamic_slice(norm_gain, (x * 4, 0), (4, DH))
     table = jnp.pad(biases, ((0, 0), (0, DH - NB)))
 
-    own, parts = call(
+    parts = call(
         attend_kernel,
-        [jax.ShapeDtypeStruct((4, RUN, DH), f32), jax.ShapeDtypeStruct((3, 4, RUN, DH), bf16)],
+        jax.ShapeDtypeStruct((16, RUN, DH), bf16),
         5,
         9,
         [pltpu.VMEM((4, BLOCK, DH), bf16), pltpu.VMEM((BLOCK, DH), f32)],
         4 * 512 * 4096 * DH,
         5 * 2**20,
+        14,
         "attend",
-    )(place, user_lengths, q_edges, k_edges, biases[0], *q_all, kv_near, kv_far, q_ids, k_pairs, table)
-
-    arrived = [
-        lax.ppermute(parts[k - 1], "zh", [(i, (i + k) % 4) for i in range(4)]) for k in range(1, 4)
+    )(place, user_lengths, q_edges, k_edges, biases[0], *q_all, kv_near, kv_far, q_ids, k_ids, table)
+
+    half = lax.dynamic_index_in_dim(wo_block.reshape(8, 2, 64, 512), core, 1, keepdims=False)
+    half, u, _ = lax.optimization_barrier((half, u, (kv_far, q_all)))
+    u_own = [u[0]] + [
+        lax.ppermute(u[k], "y", [(i, (i - k) % 4) for i in range(4)]) for k in range(1, 4)
     ]
+    wo_parts = rotations(half, "y", 4)
+
+    arrived = lax.all_to_all(parts, ("y", "zh"), 0, 0, tiled=True)
     gated = call(
         gate_kernel,
-        jax.ShapeDtypeStruct((4, RUN, DH), bf16),
-        0,
+        jax.ShapeDtypeStruct((RUN, 4 * DH), bf16),
+        1,
         6,
         [],
         20 * 512 * DH,
         2**20,
+        4,
         "gate",
-    )(own, *arrived, u, gain)
-
-    owned = [gated[0]] + [
-        lax.ppermute(gated[k], "y", [(i, (i - k) % 4) for i in range(4)]) for k in range(1, 4)
-    ]
-    heads = jnp.stack(rotations(jnp.concatenate(owned, axis=1), "x", 4))
+    )(place, arrived, *u_own, gains)
+    wo_parts, gated = lax.optimization_barrier((wo_parts, gated))
+    heads = jnp.stack(rotations(gated, "x", 4))
+    wo_near = jnp.stack(wo_parts)
+    wo_far = swap(wo_near, "core")
 
     return call(
         output_kernel,
         jax.ShapeDtypeStruct((RUN, 1024), bf16),
         1,
-        3,
-        [pltpu.VMEM((RUN, 2048), bf16)],
+        4,
+        [],
         2 * RUN * 2048 * 1024,
         5 * 2**20,
+        14,
         "project_out",
-    )(place, tokens, heads, wo_all)
+    )(place, tokens, heads, wo_near, wo_far)
 
 
 def solution(mesh):

time: 190 us -> 202 us (1.063); the launches traced: 189 us -> 199 us
  starting transfers between devices: 57.6 us -> 68.6 us
  waiting for transfers between devices: 84.1 us -> 80.3 us
  local copies, waits for them, and re-layouts: 10.6 us -> 13.7 us
    ppermute x6 -> x3, waiting for transfers between devices: 12.9 us -> 27 us  [on_device(): lax.ppermute(u[k], 'y', [(i, (i - k) % 4) for i in range(4)])]
    ppermute x21 -> x24, starting transfers between devices: 39.4 us -> 49.3 us  [rotations(): lax.ppermute(value, axis, [(i, (i + step * k) % size) for i in range(size)])]
    ppermute x2 -> x5, waiting for transfers between devices: 19.3 us -> 11 us  [swap(): return lax.ppermute(value, axis, [(0, 1), (1, 0)])]
    all_to_all x0 -> x1, starting transfers between devices: none -> 8.22 us  [on_device(): arrived = lax.all_to_all(parts, ('y', 'zh'), 0, 0, tiled=True)]
    ppermute x21 -> x24, waiting for transfers between devices: 46.2 us -> 39.3 us  [rotations(): lax.ppermute(value, axis, [(i, (i + step * k) % size) for i in range(size)])]
    ppermute x6 -> x3, starting transfers between devices: 10.8 us -> 3.96 us  [on_device(): lax.ppermute(u[k], 'y', [(i, (i - k) % 4) for i in range(4)])]
    ppermute x3, waiting for transfers between devices: 5.56 us -> 2.92 us  [on_device(): lax.ppermute(columns(y + k & 3), 'y', [(i, (i + k) % 4) for i in range(4)])]
    unnamed x15 -> x36, local copies, waits for them, and re-layouts: 6.23 us -> 7.13 us
  transfers between devices with their start and end apart: 35 -> 39, of which waited for: 25 -> 19; matrix products, arithmetic and copies ran while one was open for 3% -> 4% of each run, Pallas kernels for 7% -> 9%
where the time goes in v3:
time: 202 us; the launch traced here: 199 us
  waiting for transfers between devices  80.3 us (40%)
  starting transfers between devices  68.6 us (34%)
  Pallas kernels  19.9 us (10%)
  local copies, waits for them, and re-layouts  13.7 us (7%)
  between operations  13.7 us (7%)
  other arithmetic  2.78 us (1%)
    ppermute x24, starting transfers between devices, rotations(): lax.ppermute(value, axis, [(i, (i + step * k) % size) for i in range(size)])  49.3 us
    ppermute x24, waiting for transfers between devices, rotations(): lax.ppermute(value, axis, [(i, (i + step * k) % size) for i in range(size)])  39.3 us
    ppermute x3, waiting for transfers between devices, on_device(): lax.ppermute(u[k], 'y', [(i, (i - k) % 4) for i in range(4)])  27 us
    pallas_call x1, Pallas kernels, on_device(): call(attend_kernel, jax.ShapeDtypeStruct((16, RUN, DH), bf16), 5, 9, [plt...  13.5 us
    ppermute x5, waiting for transfers between devices, swap(): return lax.ppermute(value, axis, [(0, 1), (1, 0)])  11 us
    all_to_all x1, starting transfers between devices, on_device(): arrived = lax.all_to_all(parts, ('y', 'zh'), 0, 0, tiled=True)  8.22 us
    unnamed x36, local copies, waits for them, and re-layouts  7.13 us
    ppermute x3, starting transfers between devices, on_device(): lax.ppermute(columns(y + k & 3), 'y', [(i, (i + k) % 4) for i in range(4)])  5.9 us
  transfers between devices with their start and end apart: 39, of which 19 were waited for; matrix products, arithmetic and copies ran while one was open for 4% of the time, Pallas kernels for 9%

profile of v3, /device:TPU:32, one launch (start us, length us, event | category | flops | bytes accessed | tf_op | source)
XLA Modules:
  0.0 199.0 jit_solution(6687339159149542072)
XLA Ops:
  9.2 2.9 %collective-permute-start.19 = (bf16[64,512]{1,0:T(8,128)(2,1)S(1)}, bf16[64,512]{1,0:T(8,128)(2,1)S(1)}, u32[]{:S(2)}, u32[]{:S(2)}) collective-permute-start(bf16[64,512]{1,0:T(8,128)(2,1)S(1)} %get-tuple-element.76), channel_id=1, source_target_pairs={{0,128},{64,192},{128,0},{192,64},{1,129},{65,193},{129,1},{193,65... | collective-permute-start | bytes 196616 | tf_op jit(solution)/shard_map/ppermute | solution.py:224
  18.6 3.7 %collective-permute-start.1 = (bf16[128,512]{1,0:T(8,128)(2,1)S(1)}, bf16[128,512]{1,0:T(8,128)(2,1)S(1)}, u32[]{:S(2)}, u32[]{:S(2)}) collective-permute-start(bf16[128,512]{1,0:T(8,128)(2,1)S(1)} %get-tuple-element.38), channel_id=1, source_target_pairs={{0,128},{64,192},{128,0},{192,64},{1,129},{65,193},{129,1},{193,65... | collective-permute-start | bytes 393224 | tf_op jit(solution)/shard_map/ppermute | solution.py:22
  23.9 2.7 %collective-permute-start.4 = (bf16[128,512]{1,0:T(8,128)(2,1)S(1)}, bf16[128,512]{1,0:T(8,128)(2,1)S(1)}, u32[]{:S(2)}, u32[]{:S(2)}) collective-permute-start(bf16[128,512]{1,0:T(8,128)(2,1)S(1)} %get-tuple-element.42), channel_id=1, source_target_pairs={{0,2},{1,3},{2,0},{3,1},{4,6},{5,7},{6,4},{7,5},{8,10},{9,11},{10,... | collective-permute-start | bytes 393224 | tf_op jit(solution)/shard_map/ppermute | solution.py:22
  29.0 2.0 %collective-permute-done.4 = bf16[128,512]{1,0:T(8,128)(2,1)S(1)} collective-permute-done((bf16[128,512]{1,0:T(8,128)(2,1)S(1)}, bf16[128,512]{1,0:T(8,128)(2,1)S(1)}, u32[]{:S(2)}, u32[]{:S(2)}) %collective-permute-start.4) | collective-permute-done | bytes 131104 | tf_op jit(solution)/shard_map/ppermute | solution.py:22
  31.6 1.9 collective-permute-start.12
  33.6 2.6 %collective-permute-start.14 = (s32[512]{0:T(512)}, s32[512]{0:T(512)S(1)}, u32[]{:S(2)}, u32[]{:S(2)}) collective-permute-start(s32[512]{0:T(512)} %param.13), channel_id=1, source_target_pairs={{0,192},{64,0},{128,64},{192,128},{1,193},{65,1},{129,65},{193,129... | collective-permute-start | bytes 6152 | tf_op jit(solution)/shard_map/ppermute | solution.py:22
  41.0 3.6 %collective-permute-done.15 = s32[4,512]{1,0:T(4,128)S(1)} collective-permute-done((s32[4,512]{1,0:T(4,128)S(1)}, s32[4,512]{1,0:T(4,128)S(1)}, u32[]{:S(2)}, u32[]{:S(2)}) %collective-permute-start.15) | collective-permute-done | bytes 8224 | tf_op jit(solution)/shard_map/ppermute | solution.py:28
  46.0 3.4 %collective-permute-start.6 = (bf16[512,512]{1,0:T(8,128)(2,1)S(1)}, bf16[512,512]{1,0:T(8,128)(2,1)S(1)}, u32[]{:S(2)}, u32[]{:S(2)}) collective-permute-start(bf16[512,512]{1,0:T(8,128)(2,1)S(1)} %constant_dynamic-update-slice_fusion.a0), channel_id=1, source_target_pairs={{0,1},{1,2},{2,3},{3,0},{4,5},{5,6},{6,7},{7,4},{8,9},{9,10},{10,1... | collective-permute-start | bytes 1572872 | tf_op jit(solution)/shard_map/ppermute | solution.py:22
  49.3 3.8 %collective-permute-start.7 = (bf16[512,512]{1,0:T(8,128)(2,1)S(1)}, bf16[512,512]{1,0:T(8,128)(2,1)S(1)}, u32[]{:S(2)}, u32[]{:S(2)}) collective-permute-start(bf16[512,512]{1,0:T(8,128)(2,1)S(1)} %constant_dynamic-update-slice_fusion.a0), channel_id=1, source_target_pairs={{0,2},{1,3},{2,0},{3,1},{4,6},{5,7},{6,4},{7,5},{8,10},{9,11},{10,... | collective-permute-start | bytes 1572872 | tf_op jit(solution)/shard_map/ppermute | solution.py:22
  53.2 2.0 collective-permute-start.8
  55.1 2.1 %collective-permute-done.11.b3 = bf16[512,512]{1,0:T(8,128)(2,1)S(1)} collective-permute-done((bf16[512,512]{1,0:T(8,128)(2,1)S(1)}, bf16[512,512]{1,0:T(8,128)(2,1)S(1)}, u32[]{:S(2)}, u32[]{:S(2)}) %collective-permute-start.11) | collective-permute-done | bytes 524320 | tf_op jit(solution)/shard_map/ppermute | solution.py:22
  58.7 5.2 %collective-permute-done.6.a1 = bf16[512,512]{1,0:T(8,128)(2,1)S(1)} collective-permute-done((bf16[512,512]{1,0:T(8,128)(2,1)S(1)}, bf16[512,512]{1,0:T(8,128)(2,1)S(1)}, u32[]{:S(2)}, u32[]{:S(2)}) %collective-permute-start.6) | collective-permute-done | bytes 524320 | tf_op jit(solution)/shard_map/ppermute | solution.py:22
  64.0 12.4 %collective-permute-done.7.a2 = bf16[512,512]{1,0:T(8,128)(2,1)S(1)} collective-permute-done((bf16[512,512]{1,0:T(8,128)(2,1)S(1)}, bf16[512,512]{1,0:T(8,128)(2,1)S(1)}, u32[]{:S(2)}, u32[]{:S(2)}) %collective-permute-start.7) | collective-permute-done | bytes 524320 | tf_op jit(solution)/shard_map/ppermute | solution.py:22
  78.8 2.2 %copy-done.1 = bf16[64,64,512]{2,1,0:T(8,128)(2,1)S(1)} copy-done((bf16[64,64,512]{2,1,0:T(8,128)(2,1)S(1)}, bf16[64,64,512]{2,1,0:T(8,128)(2,1)}, u32[]{:S(2)}) %copy-start.1) | copy-done | bytes 4194328
  83.1 2.9 %project.1 = (bf16[4,128,256]{2,1,0:T(8,128)(2,1)S(1)}, bf16[4,128,128]{2,1,0:T(8,128)(2,1)S(1)}, bf16[4,128,128]{2,1,0:T(8,128)(2,1)S(1)}) custom-call(s32[5]{0:T(128)S(1)} %stack.122.place, bf16[512,512]{1,0:T(8,128)(2,1)S(1)} %constant_dynamic-update-slice_fusion.a0, bf16[512,512]{1,0:T(8,128)(2,1)S(1)} %collective-permute-done.6.a1, ...), custom_call_target="tpu_custom_call" | custom-call | flops 2147483648 | bytes 9437184 | tf_op jit(solution)/shard_map/project/pallas_call | solution.py:245
  88.4 6.6 %collective-permute-done.21 = bf16[4,128,256]{2,1,0:T(8,128)(2,1)S(1)} collective-permute-done((bf16[4,128,256]{2,1,0:T(8,128)(2,1)S(1)}, bf16[4,128,256]{2,1,0:T(8,128)(2,1)S(1)}, u32[]{:S(2)}, u32[]{:S(2)}) %collective-permute-start.21) | collective-permute-done | bytes 262176 | tf_op jit(solution)/shard_map/ppermute | solution.py:28
  96.6 4.0 %collective-permute-start.23 = (bf16[4,128,128]{2,1,0:T(8,128)(2,1)}, bf16[4,128,128]{2,1,0:T(8,128)(2,1)S(1)}, u32[]{:S(2)}, u32[]{:S(2)}) collective-permute-start(bf16[4,128,128]{2,1,0:T(8,128)(2,1)} %copy-done.7), channel_id=1, source_target_pairs={{0,4},{4,8},{8,12},{12,0},{1,5},{5,9},{9,13},{13,1},{2,6},{6,10},{... | collective-permute-start | bytes 393224 | tf_op jit(solution)/shard_map/ppermute | solution.py:22
  100.6 4.4 %collective-permute-start.24 = (bf16[4,128,128]{2,1,0:T(8,128)(2,1)}, bf16[4,128,128]{2,1,0:T(8,128)(2,1)S(1)}, u32[]{:S(2)}, u32[]{:S(2)}) collective-permute-start(bf16[4,128,128]{2,1,0:T(8,128)(2,1)} %copy-done.7), channel_id=1, source_target_pairs={{0,8},{4,12},{8,0},{12,4},{1,9},{5,13},{9,1},{13,5},{2,10},{6,14},... | collective-permute-start | bytes 393224 | tf_op jit(solution)/shard_map/ppermute | solution.py:22
  105.0 2.8 %collective-permute-start.25 = (bf16[4,128,128]{2,1,0:T(8,128)(2,1)}, bf16[4,128,128]{2,1,0:T(8,128)(2,1)S(1)}, u32[]{:S(2)}, u32[]{:S(2)}) collective-permute-start(bf16[4,128,128]{2,1,0:T(8,128)(2,1)} %copy-done.7), channel_id=1, source_target_pairs={{0,12},{4,0},{8,4},{12,8},{1,13},{5,1},{9,5},{13,9},{2,14},{6,2},{... | collective-permute-start | bytes 393224 | tf_op jit(solution)/shard_map/ppermute | solution.py:22
  109.0 6.1 %collective-permute-done.23.q1 = bf16[4,128,128]{2,1,0:T(8,128)(2,1)S(1)} collective-permute-done((bf16[4,128,128]{2,1,0:T(8,128)(2,1)}, bf16[4,128,128]{2,1,0:T(8,128)(2,1)S(1)}, u32[]{:S(2)}, u32[]{:S(2)}) %collective-permute-start.23) | collective-permute-done | bytes 131104 | tf_op jit(solution)/shard_map/ppermute | solution.py:22
  115.1 2.5 %collective-permute-done.25.q3 = bf16[4,128,128]{2,1,0:T(8,128)(2,1)S(1)} collective-permute-done((bf16[4,128,128]{2,1,0:T(8,128)(2,1)}, bf16[4,128,128]{2,1,0:T(8,128)(2,1)S(1)}, u32[]{:S(2)}, u32[]{:S(2)}) %collective-permute-start.25) | collective-permute-done | bytes 131104 | tf_op jit(solution)/shard_map/ppermute | solution.py:22
  117.6 13.5 %attend.1 = bf16[16,128,128]{2,1,0:T(8,128)(2,1)} custom-call(s32[5]{0:T(128)S(1)} %stack.122.place, s32[4]{0:T(128)S(1)} %copy-done.9, s32[4,2]{1,0:T(4,128)S(1)} %pad_add_fusion.2.q_edges, s32[4,4]{1,0:T(4,128)S(1)} %copy.20.k_edges, f32[32]{0:T(128)S(1)} %fusion.5.biases, bf16[4,128,128]{2,1,0:T(8,128)(2,1)S(1)} %copy-done.8, ...), custom_call_target="tpu_custom_call" | custom-call | flops 1073741824 | bytes 5242880 | tf_op jit(solution)/shard_map/attend/pallas_call | solution.py:278
  131.1 8.2 %all-to-all-start = ((bf16[16,128,128]{2,1,0:T(8,128)(2,1)}), bf16[16,128,128]{2,1,0:T(8,128)(2,1)S(1)}, u32[]{:S(2)}, u32[]{:S(2)}) async-start(bf16[16,128,128]{2,1,0:T(8,128)(2,1)} %attend.1), calls=%async_computation | async-start | bytes 1048576 | tf_op jit(solution)/shard_map/all_to_all | solution.py:297
  140.4 2.0 %collective-permute-start.26 = (bf16[8,64,512]{2,1,0:T(8,128)(2,1)S(1)}, bf16[8,64,512]{2,1,0:T(8,128)(2,1)S(1)}, u32[]{:S(2)}, u32[]{:S(2)}) collective-permute-start(bf16[8,64,512]{2,1,0:T(8,128)(2,1)S(1)} %dynamic-slice_bitcast_fusion), channel_id=1, source_target_pairs={{0,64},{64,128},{128,192},{192,0},{1,65},{65,129},{129,193},{193,1... | collective-permute-start | bytes 1572872 | tf_op jit(solution)/shard_map/ppermute | solution.py:22
  142.4 2.7 %collective-permute-start.27 = (bf16[8,64,512]{2,1,0:T(8,128)(2,1)S(1)}, bf16[8,64,512]{2,1,0:T(8,128)(2,1)S(1)}, u32[]{:S(2)}, u32[]{:S(2)}) collective-permute-start(bf16[8,64,512]{2,1,0:T(8,128)(2,1)S(1)} %dynamic-slice_bitcast_fusion), channel_id=1, source_target_pairs={{0,128},{64,192},{128,0},{192,64},{1,129},{65,193},{129,1},{193,65... | collective-permute-start | bytes 1572872 | tf_op jit(solution)/shard_map/ppermute | solution.py:22
  146.7 2.6 %collective-permute-start.30 = (bf16[128,128]{1,0:T(8,128)(2,1)S(1)}, bf16[128,128]{1,0:T(8,128)(2,1)S(1)}, u32[]{:S(2)}, u32[]{:S(2)}) collective-permute-start(bf16[128,128]{1,0:T(8,128)(2,1)S(1)} %get-tuple-element.80), channel_id=1, source_target_pairs={{0,128},{64,192},{128,0},{192,64},{1,129},{65,193},{129,1},{193,65... | collective-permute-start | bytes 98312 | tf_op jit(solution)/shard_map/ppermute | solution.py:293
  149.3 23.2 %collective-permute-done.29.u1 = bf16[128,128]{1,0:T(8,128)(2,1)S(1)} collective-permute-done((bf16[128,128]{1,0:T(8,128)(2,1)S(1)}, bf16[128,128]{1,0:T(8,128)(2,1)S(1)}, u32[]{:S(2)}, u32[]{:S(2)}) %collective-permute-start.29) | collective-permute-done | bytes 32800 | tf_op jit(solution)/shard_map/ppermute | solution.py:293
  173.7 3.9 %collective-permute-done.31.u3 = bf16[128,128]{1,0:T(8,128)(2,1)S(1)} collective-permute-done((bf16[128,128]{1,0:T(8,128)(2,1)S(1)}, bf16[128,128]{1,0:T(8,128)(2,1)S(1)}, u32[]{:S(2)}, u32[]{:S(2)}) %collective-permute-start.31) | collective-permute-done | bytes 32800 | tf_op jit(solution)/shard_map/ppermute | solution.py:293
  180.6 1.9 collective-permute-start.33
  183.4 2.6 %collective-permute-done.32 = bf16[128,512]{1,0:T(8,128)(2,1)S(1)} collective-permute-done((bf16[128,512]{1,0:T(8,128)(2,1)S(1)}, bf16[128,512]{1,0:T(8,128)(2,1)S(1)}, u32[]{:S(2)}, u32[]{:S(2)}) %collective-permute-start.32) | collective-permute-done | bytes 131104 | tf_op jit(solution)/shard_map/ppermute | solution.py:22
  186.0 3.1 %collective-permute-done.33 = bf16[128,512]{1,0:T(8,128)(2,1)S(1)} collective-permute-done((bf16[128,512]{1,0:T(8,128)(2,1)S(1)}, bf16[128,512]{1,0:T(8,128)(2,1)S(1)}, u32[]{:S(2)}, u32[]{:S(2)}) %collective-permute-start.33) | collective-permute-done | bytes 131104 | tf_op jit(solution)/shard_map/ppermute | solution.py:22
  189.4 2.7 %project_out.1 = bf16[128,1024]{1,0:T(8,128)(2,1)} custom-call(s32[5]{0:T(128)S(1)} %stack.122.place, bf16[128,1024]{1,0:T(8,128)(2,1)S(1)} %copy-done.2, bf16[4,128,512]{2,1,0:T(8,128)(2,1)S(1)} %pad_maximum_fusion.2.gated, bf16[4,8,64,512]{3,2,1,0:T(8,128)(2,1)S(1)} %pad_maximum_fusion.near, bf16[4,8,64,512]{3,2,1,0:T(8,128)(2,1)S(1)} %collective-permute-done.35.far), custom_call_target="tpu_custom_call" | custom-call | flops 536870912 | bytes 5242880 | tf_op jit(solution)/shard_map/project_out/pallas_call | solution.py:314
  (116 shorter events, 39.0 us)
Async XLA Ops:
  6.5 72.3 %all-gather.7.cloned.1.call-start = ((), (), s32[]{:S(2)}) async-start(), calls=%async_computation.2 | async-start | bytes 4456448 | tf_op jit(solution)/shard_map/all_gather | solution.py:228
  9.2 6.1 %collective-permute-start.19 = (bf16[64,512]{1,0:T(8,128)(2,1)S(1)}, bf16[64,512]{1,0:T(8,128)(2,1)S(1)}, u32[]{:S(2)}, u32[]{:S(2)}) collective-permute-start(bf16[64,512]{1,0:T(8,128)(2,1)S(1)} %get-tuple-element.76), channel_id=1, source_target_pairs={{0,128},{64,192},{128,0},{192,64},{1,129},{65,193},{129,1},{193,65... | collective-permute-start | bytes 196616 | tf_op jit(solution)/shard_map/ppermute | solution.py:224
  17.1 122.2 %all-gather.5.cloned.1.call-start = ((), (), s32[]{:S(2)}) async-start(), calls=%async_computation.1 | async-start | bytes 1114112 | tf_op jit(solution)/shard_map/all_gather | solution.py:261
  18.2 8.4 %collective-permute-start = (bf16[128,512]{1,0:T(8,128)(2,1)S(1)}, bf16[128,512]{1,0:T(8,128)(2,1)S(1)}, u32[]{:S(2)}, u32[]{:S(2)}) collective-permute-start(bf16[128,512]{1,0:T(8,128)(2,1)S(1)} %get-tuple-element.38), channel_id=1, source_target_pairs={{0,64},{64,128},{128,192},{192,0},{1,65},{65,129},{129,193},{193,1... | collective-permute-start | bytes 393224 | tf_op jit(solution)/shard_map/ppermute | solution.py:22
  18.6 9.5 %collective-permute-start.1 = (bf16[128,512]{1,0:T(8,128)(2,1)S(1)}, bf16[128,512]{1,0:T(8,128)(2,1)S(1)}, u32[]{:S(2)}, u32[]{:S(2)}) collective-permute-start(bf16[128,512]{1,0:T(8,128)(2,1)S(1)} %get-tuple-element.38), channel_id=1, source_target_pairs={{0,128},{64,192},{128,0},{192,64},{1,129},{65,193},{129,1},{193,65... | collective-permute-start | bytes 393224 | tf_op jit(solution)/shard_map/ppermute | solution.py:22
  22.4 6.6 %collective-permute-start.3 = (bf16[128,512]{1,0:T(8,128)(2,1)S(1)}, bf16[128,512]{1,0:T(8,128)(2,1)S(1)}, u32[]{:S(2)}, u32[]{:S(2)}) collective-permute-start(bf16[128,512]{1,0:T(8,128)(2,1)S(1)} %get-tuple-element.42), channel_id=1, source_target_pairs={{0,1},{1,2},{2,3},{3,0},{4,5},{5,6},{6,7},{7,4},{8,9},{9,10},{10,1... | collective-permute-start | bytes 393224 | tf_op jit(solution)/shard_map/ppermute | solution.py:22
  23.9 7.1 %collective-permute-start.4 = (bf16[128,512]{1,0:T(8,128)(2,1)S(1)}, bf16[128,512]{1,0:T(8,128)(2,1)S(1)}, u32[]{:S(2)}, u32[]{:S(2)}) collective-permute-start(bf16[128,512]{1,0:T(8,128)(2,1)S(1)} %get-tuple-element.42), channel_id=1, source_target_pairs={{0,2},{1,3},{2,0},{3,1},{4,6},{5,7},{6,4},{7,5},{8,10},{9,11},{10,... | collective-permute-start | bytes 393224 | tf_op jit(solution)/shard_map/ppermute | solution.py:22
  31.6 7.0 %collective-permute-start.12 = (s32[512]{0:T(512)}, s32[512]{0:T(512)S(1)}, u32[]{:S(2)}, u32[]{:S(2)}) collective-permute-start(s32[512]{0:T(512)} %param.13), channel_id=1, source_target_pairs={{0,64},{64,128},{128,192},{192,0},{1,65},{65,129},{129,193},{193,1... | collective-permute-start | bytes 6152 | tf_op jit(solution)/shard_map/ppermute | solution.py:22
  33.5 6.6 %collective-permute-start.13 = (s32[512]{0:T(512)}, s32[512]{0:T(512)S(1)}, u32[]{:S(2)}, u32[]{:S(2)}) collective-permute-start(s32[512]{0:T(512)} %param.13), channel_id=1, source_target_pairs={{0,128},{64,192},{128,0},{192,64},{1,129},{65,193},{129,1},{193,65... | collective-permute-start | bytes 6152 | tf_op jit(solution)/shard_map/ppermute | solution.py:22
  33.6 7.1 %collective-permute-start.14 = (s32[512]{0:T(512)}, s32[512]{0:T(512)S(1)}, u32[]{:S(2)}, u32[]{:S(2)}) collective-permute-start(s32[512]{0:T(512)} %param.13), channel_id=1, source_target_pairs={{0,192},{64,0},{128,64},{192,128},{1,193},{65,1},{129,65},{193,129... | collective-permute-start | bytes 6152 | tf_op jit(solution)/shard_map/ppermute | solution.py:22
  36.3 16.9 %collective-permute-start.10 = (bf16[512,512]{1,0:T(8,128)(2,1)S(1)}, bf16[512,512]{1,0:T(8,128)(2,1)S(1)}, u32[]{:S(2)}, u32[]{:S(2)}) collective-permute-start(bf16[512,512]{1,0:T(8,128)(2,1)S(1)} %constant_dynamic-update-slice_fusion.4.b0), channel_id=1, source_target_pairs={{0,128},{64,192},{128,0},{192,64},{1,129},{65,193},{129,1},{193,65... | collective-permute-start | bytes 1572872 | tf_op jit(solution)/shard_map/ppermute | solution.py:22
  37.9 19.3 %collective-permute-start.11 = (bf16[512,512]{1,0:T(8,128)(2,1)S(1)}, bf16[512,512]{1,0:T(8,128)(2,1)S(1)}, u32[]{:S(2)}, u32[]{:S(2)}) collective-permute-start(bf16[512,512]{1,0:T(8,128)(2,1)S(1)} %constant_dynamic-update-slice_fusion.4.b0), channel_id=1, source_target_pairs={{0,192},{64,0},{128,64},{192,128},{1,193},{65,1},{129,65},{193,129... | collective-permute-start | bytes 1572872 | tf_op jit(solution)/shard_map/ppermute | solution.py:22
  38.6 20.2 %collective-permute-start.9 = (bf16[512,512]{1,0:T(8,128)(2,1)S(1)}, bf16[512,512]{1,0:T(8,128)(2,1)S(1)}, u32[]{:S(2)}, u32[]{:S(2)}) collective-permute-start(bf16[512,512]{1,0:T(8,128)(2,1)S(1)} %constant_dynamic-update-slice_fusion.4.b0), channel_id=1, source_target_pairs={{0,64},{64,128},{128,192},{192,0},{1,65},{65,129},{129,193},{193,1... | collective-permute-start | bytes 1572872 | tf_op jit(solution)/shard_map/ppermute | solution.py:22
  40.1 9.3 %collective-permute-start.17 = (bf16[64,512]{1,0:T(8,128)(2,1)S(1)}, bf16[64,512]{1,0:T(8,128)(2,1)S(1)}, u32[]{:S(2)}, u32[]{:S(2)}) collective-permute-start(bf16[64,512]{1,0:T(8,128)(2,1)S(1)} %bitcast.80), channel_id=1, source_target_pairs={{0,0},{64,1},{128,2},{192,3},{1,64},{65,65},{129,66},{193,67},{2,1... | collective-permute-start | bytes 196616 | tf_op jit(solution)/shard_map/ppermute | solution.py:240
  46.0 18.0 %collective-permute-start.6 = (bf16[512,512]{1,0:T(8,128)(2,1)S(1)}, bf16[512,512]{1,0:T(8,128)(2,1)S(1)}, u32[]{:S(2)}, u32[]{:S(2)}) collective-permute-start(bf16[512,512]{1,0:T(8,128)(2,1)S(1)} %constant_dynamic-update-slice_fusion.a0), channel_id=1, source_target_pairs={{0,1},{1,2},{2,3},{3,0},{4,5},{5,6},{6,7},{7,4},{8,9},{9,10},{10,1... | collective-permute-start | bytes 1572872 | tf_op jit(solution)/shard_map/ppermute | solution.py:22
  49.3 27.0 %collective-permute-start.7 = (bf16[512,512]{1,0:T(8,128)(2,1)S(1)}, bf16[512,512]{1,0:T(8,128)(2,1)S(1)}, u32[]{:S(2)}, u32[]{:S(2)}) collective-permute-start(bf16[512,512]{1,0:T(8,128)(2,1)S(1)} %constant_dynamic-update-slice_fusion.a0), channel_id=1, source_target_pairs={{0,2},{1,3},{2,0},{3,1},{4,6},{5,7},{6,4},{7,5},{8,10},{9,11},{10,... | collective-permute-start | bytes 1572872 | tf_op jit(solution)/shard_map/ppermute | solution.py:22
  53.2 24.0 %collective-permute-start.8 = (bf16[512,512]{1,0:T(8,128)(2,1)S(1)}, bf16[512,512]{1,0:T(8,128)(2,1)S(1)}, u32[]{:S(2)}, u32[]{:S(2)}) collective-permute-start(bf16[512,512]{1,0:T(8,128)(2,1)S(1)} %constant_dynamic-update-slice_fusion.a0), channel_id=1, source_target_pairs={{0,3},{1,0},{2,1},{3,2},{4,7},{5,4},{6,5},{7,6},{8,11},{9,8},{10,9... | collective-permute-start | bytes 1572872 | tf_op jit(solution)/shard_map/ppermute | solution.py:22
  86.7 8.2 %collective-permute-start.21 = (bf16[4,128,256]{2,1,0:T(8,128)(2,1)S(1)}, bf16[4,128,256]{2,1,0:T(8,128)(2,1)S(1)}, u32[]{:S(2)}, u32[]{:S(2)}) collective-permute-start(bf16[4,128,256]{2,1,0:T(8,128)(2,1)S(1)} %get-tuple-element.58), channel_id=1, source_target_pairs={{0,32},{32,0},{1,33},{33,1},{2,34},{34,2},{3,35},{35,3},{4,36},{36... | collective-permute-start | bytes 786440 | tf_op jit(solution)/shard_map/ppermute | solution.py:28
  95.0 22.6 %collective-permute-start.22 = (bf16[2,4,128,256]{3,2,1,0:T(8,128)(2,1)S(1)}, bf16[2,4,128,256]{3,2,1,0:T(8,128)(2,1)S(1)}, u32[]{:S(2)}, u32[]{:S(2)}) collective-permute-start(bf16[2,4,128,256]{3,2,1,0:T(8,128)(2,1)S(1)} %pad_maximum_fusion.1.kv_near), channel_id=1, source_target_pairs={{0,16},{16,0},{1,17},{17,1},{2,18},{18,2},{3,19},{19,3},{4,20},{20... | collective-permute-start | bytes 1572872 | tf_op jit(solution)/shard_map/ppermute | solution.py:28
  96.6 18.6 %collective-permute-start.23 = (bf16[4,128,128]{2,1,0:T(8,128)(2,1)}, bf16[4,128,128]{2,1,0:T(8,128)(2,1)S(1)}, u32[]{:S(2)}, u32[]{:S(2)}) collective-permute-start(bf16[4,128,128]{2,1,0:T(8,128)(2,1)} %copy-done.7), channel_id=1, source_target_pairs={{0,4},{4,8},{8,12},{12,0},{1,5},{5,9},{9,13},{13,1},{2,6},{6,10},{... | collective-permute-start | bytes 393224 | tf_op jit(solution)/shard_map/ppermute | solution.py:22
  100.6 14.5 %collective-permute-start.24 = (bf16[4,128,128]{2,1,0:T(8,128)(2,1)}, bf16[4,128,128]{2,1,0:T(8,128)(2,1)S(1)}, u32[]{:S(2)}, u32[]{:S(2)}) collective-permute-start(bf16[4,128,128]{2,1,0:T(8,128)(2,1)} %copy-done.7), channel_id=1, source_target_pairs={{0,8},{4,12},{8,0},{12,4},{1,9},{5,13},{9,1},{13,5},{2,10},{6,14},... | collective-permute-start | bytes 393224 | tf_op jit(solution)/shard_map/ppermute | solution.py:22
  105.0 12.6 %collective-permute-start.25 = (bf16[4,128,128]{2,1,0:T(8,128)(2,1)}, bf16[4,128,128]{2,1,0:T(8,128)(2,1)S(1)}, u32[]{:S(2)}, u32[]{:S(2)}) collective-permute-start(bf16[4,128,128]{2,1,0:T(8,128)(2,1)} %copy-done.7), channel_id=1, source_target_pairs={{0,12},{4,0},{8,4},{12,8},{1,13},{5,1},{9,5},{13,9},{2,14},{6,2},{... | collective-permute-start | bytes 393224 | tf_op jit(solution)/shard_map/ppermute | solution.py:22
  131.1 46.5 %all-to-all-start = ((bf16[16,128,128]{2,1,0:T(8,128)(2,1)}), bf16[16,128,128]{2,1,0:T(8,128)(2,1)S(1)}, u32[]{:S(2)}, u32[]{:S(2)}) async-start(bf16[16,128,128]{2,1,0:T(8,128)(2,1)} %attend.1), calls=%async_computation | async-start | bytes 1048576 | tf_op jit(solution)/shard_map/all_to_all | solution.py:297
  140.4 38.0 %collective-permute-start.26 = (bf16[8,64,512]{2,1,0:T(8,128)(2,1)S(1)}, bf16[8,64,512]{2,1,0:T(8,128)(2,1)S(1)}, u32[]{:S(2)}, u32[]{:S(2)}) collective-permute-start(bf16[8,64,512]{2,1,0:T(8,128)(2,1)S(1)} %dynamic-slice_bitcast_fusion), channel_id=1, source_target_pairs={{0,64},{64,128},{128,192},{192,0},{1,65},{65,129},{129,193},{193,1... | collective-permute-start | bytes 1572872 | tf_op jit(solution)/shard_map/ppermute | solution.py:22
  142.4 36.0 %collective-permute-start.27 = (bf16[8,64,512]{2,1,0:T(8,128)(2,1)S(1)}, bf16[8,64,512]{2,1,0:T(8,128)(2,1)S(1)}, u32[]{:S(2)}, u32[]{:S(2)}) collective-permute-start(bf16[8,64,512]{2,1,0:T(8,128)(2,1)S(1)} %dynamic-slice_bitcast_fusion), channel_id=1, source_target_pairs={{0,128},{64,192},{128,0},{192,64},{1,129},{65,193},{129,1},{193,65... | collective-permute-start | bytes 1572872 | tf_op jit(solution)/shard_map/ppermute | solution.py:22
  145.1 33.3 %collective-permute-start.28 = (bf16[8,64,512]{2,1,0:T(8,128)(2,1)S(1)}, bf16[8,64,512]{2,1,0:T(8,128)(2,1)S(1)}, u32[]{:S(2)}, u32[]{:S(2)}) collective-permute-start(bf16[8,64,512]{2,1,0:T(8,128)(2,1)S(1)} %dynamic-slice_bitcast_fusion), channel_id=1, source_target_pairs={{0,192},{64,0},{128,64},{192,128},{1,193},{65,1},{129,65},{193,129... | collective-permute-start | bytes 1572872 | tf_op jit(solution)/shard_map/ppermute | solution.py:22
  146.6 25.9 %collective-permute-start.29 = (bf16[128,128]{1,0:T(8,128)(2,1)S(1)}, bf16[128,128]{1,0:T(8,128)(2,1)S(1)}, u32[]{:S(2)}, u32[]{:S(2)}) collective-permute-start(bf16[128,128]{1,0:T(8,128)(2,1)S(1)} %get-tuple-element.81), channel_id=1, source_target_pairs={{0,192},{64,0},{128,64},{192,128},{1,193},{65,1},{129,65},{193,129... | collective-permute-start | bytes 98312 | tf_op jit(solution)/shard_map/ppermute | solution.py:293
  146.7 27.1 %collective-permute-start.30 = (bf16[128,128]{1,0:T(8,128)(2,1)S(1)}, bf16[128,128]{1,0:T(8,128)(2,1)S(1)}, u32[]{:S(2)}, u32[]{:S(2)}) collective-permute-start(bf16[128,128]{1,0:T(8,128)(2,1)S(1)} %get-tuple-element.80), channel_id=1, source_target_pairs={{0,128},{64,192},{128,0},{192,64},{1,129},{65,193},{129,1},{193,65... | collective-permute-start | bytes 98312 | tf_op jit(solution)/shard_map/ppermute | solution.py:293
  178.7 10.7 %collective-permute-start.35 = (bf16[4,8,64,512]{3,2,1,0:T(8,128)(2,1)S(1)}, bf16[4,8,64,512]{3,2,1,0:T(8,128)(2,1)S(1)}, u32[]{:S(2)}, u32[]{:S(2)}) collective-permute-start(bf16[4,8,64,512]{3,2,1,0:T(8,128)(2,1)S(1)} %pad_maximum_fusion.near), channel_id=1, source_target_pairs={{0,16},{16,0},{1,17},{17,1},{2,18},{18,2},{3,19},{19,3},{4,20},{20... | collective-permute-start | bytes 6291464 | tf_op jit(solution)/shard_map/ppermute | solution.py:28
  178.8 7.2 %collective-permute-start.32 = (bf16[128,512]{1,0:T(8,128)(2,1)S(1)}, bf16[128,512]{1,0:T(8,128)(2,1)S(1)}, u32[]{:S(2)}, u32[]{:S(2)}) collective-permute-start(bf16[128,512]{1,0:T(8,128)(2,1)S(1)} %gate.1), channel_id=1, source_target_pairs={{0,1},{1,2},{2,3},{3,0},{4,5},{5,6},{6,7},{7,4},{8,9},{9,10},{10,1... | collective-permute-start | bytes 393224 | tf_op jit(solution)/shard_map/ppermute | solution.py:22
  180.6 8.5 %collective-permute-start.33 = (bf16[128,512]{1,0:T(8,128)(2,1)S(1)}, bf16[128,512]{1,0:T(8,128)(2,1)S(1)}, u32[]{:S(2)}, u32[]{:S(2)}) collective-permute-start(bf16[128,512]{1,0:T(8,128)(2,1)S(1)} %gate.1), channel_id=1, source_target_pairs={{0,2},{1,3},{2,0},{3,1},{4,6},{5,7},{6,4},{7,5},{8,10},{9,11},{10,... | collective-permute-start | bytes 393224 | tf_op jit(solution)/shard_map/ppermute | solution.py:22
  182.5 6.8 %collective-permute-start.34 = (bf16[128,512]{1,0:T(8,128)(2,1)S(1)}, bf16[128,512]{1,0:T(8,128)(2,1)S(1)}, u32[]{:S(2)}, u32[]{:S(2)}) collective-permute-start(bf16[128,512]{1,0:T(8,128)(2,1)S(1)} %gate.1), channel_id=1, source_target_pairs={{0,3},{1,0},{2,1},{3,2},{4,7},{5,4},{6,5},{7,6},{8,11},{9,8},{10,9... | collective-permute-start | bytes 393224 | tf_op jit(solution)/shard_map/ppermute | solution.py:22
  (22 other events, 378.5 us)
Sparse Core Ops, SparseCore 0:
  17.3 43.7 all-gather.6
  78.2 42.3 all-gather.4

commit v4 on v3

--- a/solution.py
+++ b/solution.py
@@ -181,20 +181,18 @@
         out_ref[:, columns] = (normed * u[...].astype(jnp.float32)).astype(jnp.bfloat16)
 
 
-def output_kernel(place, tokens, gated, near, far, out_ref):
-    y, core, x = place[0], place[2], place[4]
-    for zl in range(2):
-        for c, source in enumerate((near, far)):
-            block = zl * 2 + (core ^ c)
-            columns = pl.ds(pl.multiple_of(block * 256, 256), 256)
-            total = tokens[:, columns].astype(jnp.float32)
-            for ky in range(4):
-                left = gated[(x - (y - ky)) & 3]
-                right = jnp.concatenate([source[ky, j * 2 + zl] for j in range(4)], axis=0)
-                total += lax.dot_general(
-                    left, right, (((1,), (1,)), ((), ())), preferred_element_type=jnp.float32
-                )
-            out_ref[:, columns] = total.astype(jnp.bfloat16)
+def output_kernel(place, tokens, gated, weights, out_ref):
+    y, x = place[0], place[4]
+    for m in range(4):
+        columns = slice(m * 256, (m + 1) * 256)
+        total = tokens[:, columns].astype(jnp.float32)
+        for ky in range(4):
+            left = gated[(x - (y - ky)) & 3]
+            right = jnp.concatenate([weights[j * 4 + m, ky] for j in range(4)], axis=0)
+            total += lax.dot_general(
+                left, right, (((1,), (1,)), ((), ())), preferred_element_type=jnp.float32
+            )
+        out_ref[:, columns] = total.astype(jnp.bfloat16)
 
 
 def call(kernel, shapes, n_smem, n_vmem, scratch, flops, moved, vmem, name):
@@ -233,14 +231,15 @@
     firsts = rotations(jnp.concatenate(first, axis=0), "x", 4)
     seconds = rotations(jnp.concatenate(second, axis=0), "y", 4)
 
-    ids, late, _ = lax.optimization_barrier((bucket_ids, w_out.T, (first, second)))
+    ids, late, _ = lax.optimization_barrier((bucket_ids, w_out.T, (firsts[1:3], seconds[1:3])))
     ids_y = jnp.stack(rotations(ids, "y", 4))
     ids_near = jnp.stack([ids_y, swap(ids_y, "zl")])
     ids_far = swap(ids_near, "core")
     swapped = lax.ppermute(late, ("y", "x"), [(b * 4 + a, a * 4 + b) for a in range(4) for b in range(4)])
-
-    firsts, seconds, ids_y, ids_near, ids_far, swapped = lax.optimization_barrier(
-        (firsts, seconds, ids_y, ids_near, ids_far, swapped)
+    wo_rows = jnp.stack(rotations(swapped, "y", 4))
+
+    firsts, seconds, ids_y, ids_near, ids_far, wo_rows = lax.optimization_barrier(
+        (firsts, seconds, ids_y, ids_near, ids_far, wo_rows)
     )
     kv, q, u = call(
         project_kernel,
@@ -258,11 +257,11 @@
         "project",
     )(place, *firsts, *seconds, weights)
 
-    wo_block = lax.all_gather(swapped, plane)
+    wo_rows, _ = lax.optimization_barrier((wo_rows, kv))
+    wo_all = lax.all_gather(wo_rows, plane)
 
     kv_near = jnp.stack([kv, swap(kv, "zl")])
     kv_far = swap(kv_near, "core")
-    q, _ = lax.optimization_barrier((q, kv_near))
     q_all = rotations(q, "zh", 4)
 
     q_ids = ids_y.reshape(4, BLOCK, 1)
@@ -287,13 +286,10 @@
         "attend",
     )(place, user_lengths, q_edges, k_edges, biases[0], *q_all, kv_near, kv_far, q_ids, k_ids, table)
 
-    half = lax.dynamic_index_in_dim(wo_block.reshape(8, 2, 64, 512), core, 1, keepdims=False)
-    half, u, _ = lax.optimization_barrier((half, u, (kv_far, q_all)))
+    u, _ = lax.optimization_barrier((u, (kv_far, q_all)))
     u_own = [u[0]] + [
         lax.ppermute(u[k], "y", [(i, (i - k) % 4) for i in range(4)]) for k in range(1, 4)
     ]
-    wo_parts = rotations(half, "y", 4)
-
     arrived = lax.all_to_all(parts, ("y", "zh"), 0, 0, tiled=True)
     gated = call(
         gate_kernel,
@@ -306,22 +302,19 @@
         4,
         "gate",
     )(place, arrived, *u_own, gains)
-    wo_parts, gated = lax.optimization_barrier((wo_parts, gated))
     heads = jnp.stack(rotations(gated, "x", 4))
-    wo_near = jnp.stack(wo_parts)
-    wo_far = swap(wo_near, "core")
 
     return call(
         output_kernel,
         jax.ShapeDtypeStruct((RUN, 1024), bf16),
         1,
-        4,
+        3,
         [],
         2 * RUN * 2048 * 1024,
         5 * 2**20,
         14,
         "project_out",
-    )(place, tokens, heads, wo_near, wo_far)
+    )(place, tokens, heads, wo_all)
 
 
 def solution(mesh):

time: 202 us -> 180 us (0.89)
  waiting for transfers between devices: 80.3 us -> 55.8 us
  starting transfers between devices: 68.6 us -> 75.6 us
    ppermute x3, waiting for transfers between devices: 27 us -> 5.04 us  [on_device(): lax.ppermute(u[k], 'y', [(i, (i - k) % 4) for i in range(4)])]
    all_to_all x1, waiting for transfers between devices: 0.01 us -> 6.01 us  [on_device(): arrived = lax.all_to_all(parts, ('y', 'zh'), 0, 0, tiled=True)]
    ppermute x5 -> x4, waiting for transfers between devices: 11 us -> 4.99 us  [swap(): return lax.ppermute(value, axis, [(0, 1), (1, 0)])]
    ppermute x24, starting transfers between devices: 49.3 us -> 53.9 us  [rotations(): lax.ppermute(value, axis, [(i, (i + step * k) % size) for i in range(size)])]
    pallas_call x1, Pallas kernels: 13.5 us -> 10.8 us  [on_device(): call(attend_kernel, jax.ShapeDtypeStruct((16, RUN, DH), bf16), 5, 9, [plt...]
    ppermute x24, waiting for transfers between devices: 39.3 us -> 36.8 us  [rotations(): lax.ppermute(value, axis, [(i, (i + step * k) % size) for i in range(size)])]
    unnamed x36 -> x26, local copies, waits for them, and re-layouts: 7.13 us -> 6.56 us
  transfers between devices with their start and end apart: 39 -> 38, of which waited for: 19 -> 21; matrix products, arithmetic and copies ran while one was open for 4% -> 4% of each run, Pallas kernels for 9% -> 6%
where the time goes in v4:
time: 180 us; the launch traced here: 179 us
  starting transfers between devices  75.6 us (42%)
  waiting for transfers between devices  55.8 us (31%)
  Pallas kernels  17.9 us (10%)
  between operations  13.7 us (8%)
  local copies, waits for them, and re-layouts  12 us (7%)
  other arithmetic  3.91 us (2%)
    ppermute x24, starting transfers between devices, rotations(): lax.ppermute(value, axis, [(i, (i + step * k) % size) for i in range(size)])  53.9 us
    ppermute x24, waiting for transfers between devices, rotations(): lax.ppermute(value, axis, [(i, (i + step * k) % size) for i in range(size)])  36.8 us
    pallas_call x1, Pallas kernels, on_device(): call(attend_kernel, jax.ShapeDtypeStruct((16, RUN, DH), bf16), 5, 9, [plt...  10.8 us
    all_to_all x1, starting transfers between devices, on_device(): arrived = lax.all_to_all(parts, ('y', 'zh'), 0, 0, tiled=True)  8.94 us
    unnamed x26, local copies, waits for them, and re-layouts  6.56 us
    all_to_all x1, waiting for transfers between devices, on_device(): arrived = lax.all_to_all(parts, ('y', 'zh'), 0, 0, tiled=True)  6.01 us
    ppermute x3, starting transfers between devices, on_device(): lax.ppermute(columns(y + k & 3), 'y', [(i, (i + k) % 4) for i in range(4)])  5.9 us
    ppermute x3, waiting for transfers between devices, on_device(): lax.ppermute(u[k], 'y', [(i, (i - k) % 4) for i in range(4)])  5.04 us
  transfers between devices with their start and end apart: 38, of which 21 were waited for; matrix products, arithmetic and copies ran while one was open for 4% of the time, Pallas kernels for 6%

profile of v4, /device:TPU:32, one launch (start us, length us, event | category | flops | bytes accessed | tf_op | source)
XLA Modules:
  0.0 178.9 jit_solution(16035669325597832577)
XLA Ops:
  9.2 2.9 %collective-permute-start.22 = (bf16[64,512]{1,0:T(8,128)(2,1)S(1)}, bf16[64,512]{1,0:T(8,128)(2,1)S(1)}, u32[]{:S(2)}, u32[]{:S(2)}) collective-permute-start(bf16[64,512]{1,0:T(8,128)(2,1)S(1)} %get-tuple-element.64), channel_id=1, source_target_pairs={{0,128},{64,192},{128,0},{192,64},{1,129},{65,193},{129,1},{193,65... | collective-permute-start | bytes 196616 | tf_op jit(solution)/shard_map/ppermute | solution.py:222
  18.5 3.7 %collective-permute-start.1 = (bf16[128,512]{1,0:T(8,128)(2,1)S(1)}, bf16[128,512]{1,0:T(8,128)(2,1)S(1)}, u32[]{:S(2)}, u32[]{:S(2)}) collective-permute-start(bf16[128,512]{1,0:T(8,128)(2,1)S(1)} %get-tuple-element.32), channel_id=1, source_target_pairs={{0,128},{64,192},{128,0},{192,64},{1,129},{65,193},{129,1},{193,65... | collective-permute-start | bytes 393224 | tf_op jit(solution)/shard_map/ppermute | solution.py:22
  23.8 2.7 %collective-permute-start.4 = (bf16[128,512]{1,0:T(8,128)(2,1)S(1)}, bf16[128,512]{1,0:T(8,128)(2,1)S(1)}, u32[]{:S(2)}, u32[]{:S(2)}) collective-permute-start(bf16[128,512]{1,0:T(8,128)(2,1)S(1)} %get-tuple-element.36), channel_id=1, source_target_pairs={{0,2},{1,3},{2,0},{3,1},{4,6},{5,7},{6,4},{7,5},{8,10},{9,11},{10,... | collective-permute-start | bytes 393224 | tf_op jit(solution)/shard_map/ppermute | solution.py:22
  28.9 2.0 %collective-permute-done.4 = bf16[128,512]{1,0:T(8,128)(2,1)S(1)} collective-permute-done((bf16[128,512]{1,0:T(8,128)(2,1)S(1)}, bf16[128,512]{1,0:T(8,128)(2,1)S(1)}, u32[]{:S(2)}, u32[]{:S(2)}) %collective-permute-start.4) | collective-permute-done | bytes 131104 | tf_op jit(solution)/shard_map/ppermute | solution.py:22
  31.6 2.1 %collective-permute-start.10 = (bf16[512,512]{1,0:T(8,128)(2,1)S(1)}, bf16[512,512]{1,0:T(8,128)(2,1)S(1)}, u32[]{:S(2)}, u32[]{:S(2)}) collective-permute-start(bf16[512,512]{1,0:T(8,128)(2,1)S(1)} %constant_dynamic-update-slice_fusion.4.b0), channel_id=1, source_target_pairs={{0,128},{64,192},{128,0},{192,64},{1,129},{65,193},{129,1},{193,65... | collective-permute-start | bytes 1572872 | tf_op jit(solution)/shard_map/ppermute | solution.py:22
  35.2 2.8 %collective-permute-start.7 = (bf16[512,512]{1,0:T(8,128)(2,1)S(1)}, bf16[512,512]{1,0:T(8,128)(2,1)S(1)}, u32[]{:S(2)}, u32[]{:S(2)}) collective-permute-start(bf16[512,512]{1,0:T(8,128)(2,1)S(1)} %constant_dynamic-update-slice_fusion.a0), channel_id=1, source_target_pairs={{0,2},{1,3},{2,0},{3,1},{4,6},{5,7},{6,4},{7,5},{8,10},{9,11},{10,... | collective-permute-start | bytes 1572872 | tf_op jit(solution)/shard_map/ppermute | solution.py:22
  38.0 3.2 %collective-permute-start.11 = (bf16[512,512]{1,0:T(8,128)(2,1)S(1)}, bf16[512,512]{1,0:T(8,128)(2,1)}, u32[]{:S(2)}, u32[]{:S(2)}) collective-permute-start(bf16[512,512]{1,0:T(8,128)(2,1)S(1)} %constant_dynamic-update-slice_fusion.4.b0), channel_id=1, source_target_pairs={{0,192},{64,0},{128,64},{192,128},{1,193},{65,1},{129,65},{193,129... | collective-permute-start | bytes 1572872 | tf_op jit(solution)/shard_map/ppermute | solution.py:22
  41.2 6.9 %collective-permute-done.10.b2 = bf16[512,512]{1,0:T(8,128)(2,1)S(1)} collective-permute-done((bf16[512,512]{1,0:T(8,128)(2,1)S(1)}, bf16[512,512]{1,0:T(8,128)(2,1)S(1)}, u32[]{:S(2)}, u32[]{:S(2)}) %collective-permute-start.10) | collective-permute-done | bytes 524320 | tf_op jit(solution)/shard_map/ppermute | solution.py:22
  48.1 2.6 %collective-permute-start.8 = (bf16[512,512]{1,0:T(8,128)(2,1)S(1)}, bf16[512,512]{1,0:T(8,128)(2,1)}, u32[]{:S(2)}, u32[]{:S(2)}) collective-permute-start(bf16[512,512]{1,0:T(8,128)(2,1)S(1)} %constant_dynamic-update-slice_fusion.a0), channel_id=1, source_target_pairs={{0,3},{1,0},{2,1},{3,2},{4,7},{5,4},{6,5},{7,6},{8,11},{9,8},{10,9... | collective-permute-start | bytes 1572872 | tf_op jit(solution)/shard_map/ppermute | solution.py:22
  50.7 3.7 %collective-permute-done.9.b1 = bf16[512,512]{1,0:T(8,128)(2,1)S(1)} collective-permute-done((bf16[512,512]{1,0:T(8,128)(2,1)S(1)}, bf16[512,512]{1,0:T(8,128)(2,1)S(1)}, u32[]{:S(2)}, u32[]{:S(2)}) %collective-permute-start.9) | collective-permute-done | bytes 524320 | tf_op jit(solution)/shard_map/ppermute | solution.py:22
  54.4 2.2 %collective-permute-done.7.a2 = bf16[512,512]{1,0:T(8,128)(2,1)S(1)} collective-permute-done((bf16[512,512]{1,0:T(8,128)(2,1)S(1)}, bf16[512,512]{1,0:T(8,128)(2,1)S(1)}, u32[]{:S(2)}, u32[]{:S(2)}) %collective-permute-start.7) | collective-permute-done | bytes 524320 | tf_op jit(solution)/shard_map/ppermute | solution.py:22
  57.8 3.2 %collective-permute-start.13 = (s32[512]{0:T(512)}, s32[512]{0:T(512)S(1)}, u32[]{:S(2)}, u32[]{:S(2)}) collective-permute-start(s32[512]{0:T(512)} %param.13), channel_id=1, source_target_pairs={{0,128},{64,192},{128,0},{192,64},{1,129},{65,193},{129,1},{193,65... | collective-permute-start | bytes 6152 | tf_op jit(solution)/shard_map/ppermute | solution.py:22
  65.8 4.5 %collective-permute-start.18 = (bf16[64,512]{1,0:T(8,128)(2,1)S(1)}, bf16[64,512]{1,0:T(8,128)(2,1)S(1)}, u32[]{:S(2)}, u32[]{:S(2)}) collective-permute-start(bf16[64,512]{1,0:T(8,128)(2,1)S(1)} %collective-permute-done.17), channel_id=1, source_target_pairs={{0,64},{64,128},{128,192},{192,0},{1,65},{65,129},{129,193},{193,1... | collective-permute-start | bytes 196616 | tf_op jit(solution)/shard_map/ppermute | solution.py:22
  70.3 4.7 %collective-permute-start.19 = (bf16[64,512]{1,0:T(8,128)(2,1)S(1)}, bf16[64,512]{1,0:T(8,128)(2,1)S(1)}, u32[]{:S(2)}, u32[]{:S(2)}) collective-permute-start(bf16[64,512]{1,0:T(8,128)(2,1)S(1)} %collective-permute-done.17), channel_id=1, source_target_pairs={{0,128},{64,192},{128,0},{192,64},{1,129},{65,193},{129,1},{193,65... | collective-permute-start | bytes 196616 | tf_op jit(solution)/shard_map/ppermute | solution.py:22
  80.6 2.2 %copy-done.1 = bf16[64,64,512]{2,1,0:T(8,128)(2,1)S(1)} copy-done((bf16[64,64,512]{2,1,0:T(8,128)(2,1)S(1)}, bf16[64,64,512]{2,1,0:T(8,128)(2,1)}, u32[]{:S(2)}) %copy-start.1) | copy-done | bytes 4194328
  82.8 3.6 %project.1 = (bf16[4,128,256]{2,1,0:T(8,128)(2,1)S(1)}, bf16[4,128,128]{2,1,0:T(8,128)(2,1)S(1)}, bf16[4,128,128]{2,1,0:T(8,128)(2,1)S(1)}) custom-call(s32[5]{0:T(128)S(1)} %stack.122.place, bf16[512,512]{1,0:T(8,128)(2,1)S(1)} %constant_dynamic-update-slice_fusion.a0, bf16[512,512]{1,0:T(8,128)(2,1)S(1)} %collective-permute-done.6.a1, ...), custom_call_target="tpu_custom_call" | custom-call | flops 2147483648 | bytes 9437184 | tf_op jit(solution)/shard_map/project/pallas_call | solution.py:244
  89.4 5.0 %collective-permute-done.27 = bf16[4,128,256]{2,1,0:T(8,128)(2,1)S(1)} collective-permute-done((bf16[4,128,256]{2,1,0:T(8,128)(2,1)S(1)}, bf16[4,128,256]{2,1,0:T(8,128)(2,1)S(1)}, u32[]{:S(2)}, u32[]{:S(2)}) %collective-permute-start.27) | collective-permute-done | bytes 262176 | tf_op jit(solution)/shard_map/ppermute | solution.py:28
  96.0 3.3 %collective-permute-start.24 = (bf16[4,128,128]{2,1,0:T(8,128)(2,1)}, bf16[4,128,128]{2,1,0:T(8,128)(2,1)S(1)}, u32[]{:S(2)}, u32[]{:S(2)}) collective-permute-start(bf16[4,128,128]{2,1,0:T(8,128)(2,1)} %copy-done.4), channel_id=1, source_target_pairs={{0,4},{4,8},{8,12},{12,0},{1,5},{5,9},{9,13},{13,1},{2,6},{6,10},{... | collective-permute-start | bytes 393224 | tf_op jit(solution)/shard_map/ppermute | solution.py:22
  99.3 4.5 %collective-permute-start.25 = (bf16[4,128,128]{2,1,0:T(8,128)(2,1)}, bf16[4,128,128]{2,1,0:T(8,128)(2,1)S(1)}, u32[]{:S(2)}, u32[]{:S(2)}) collective-permute-start(bf16[4,128,128]{2,1,0:T(8,128)(2,1)} %copy-done.4), channel_id=1, source_target_pairs={{0,8},{4,12},{8,0},{12,4},{1,9},{5,13},{9,1},{13,5},{2,10},{6,14},... | collective-permute-start | bytes 393224 | tf_op jit(solution)/shard_map/ppermute | solution.py:22
  103.8 2.7 %collective-permute-start.26 = (bf16[4,128,128]{2,1,0:T(8,128)(2,1)}, bf16[4,128,128]{2,1,0:T(8,128)(2,1)S(1)}, u32[]{:S(2)}, u32[]{:S(2)}) collective-permute-start(bf16[4,128,128]{2,1,0:T(8,128)(2,1)} %copy-done.4), channel_id=1, source_target_pairs={{0,12},{4,0},{8,4},{12,8},{1,13},{5,1},{9,5},{13,9},{2,14},{6,2},{... | collective-permute-start | bytes 393224 | tf_op jit(solution)/shard_map/ppermute | solution.py:22
  107.7 3.6 %collective-permute-done.24.q1 = bf16[4,128,128]{2,1,0:T(8,128)(2,1)S(1)} collective-permute-done((bf16[4,128,128]{2,1,0:T(8,128)(2,1)}, bf16[4,128,128]{2,1,0:T(8,128)(2,1)S(1)}, u32[]{:S(2)}, u32[]{:S(2)}) %collective-permute-start.24) | collective-permute-done | bytes 131104 | tf_op jit(solution)/shard_map/ppermute | solution.py:22
  111.3 4.6 %collective-permute-done.25.q2 = bf16[4,128,128]{2,1,0:T(8,128)(2,1)S(1)} collective-permute-done((bf16[4,128,128]{2,1,0:T(8,128)(2,1)}, bf16[4,128,128]{2,1,0:T(8,128)(2,1)S(1)}, u32[]{:S(2)}, u32[]{:S(2)}) %collective-permute-start.25) | collective-permute-done | bytes 131104 | tf_op jit(solution)/shard_map/ppermute | solution.py:22
  115.9 5.1 %collective-permute-done.26.q3 = bf16[4,128,128]{2,1,0:T(8,128)(2,1)S(1)} collective-permute-done((bf16[4,128,128]{2,1,0:T(8,128)(2,1)}, bf16[4,128,128]{2,1,0:T(8,128)(2,1)S(1)}, u32[]{:S(2)}, u32[]{:S(2)}) %collective-permute-start.26) | collective-permute-done | bytes 131104 | tf_op jit(solution)/shard_map/ppermute | solution.py:22
  122.0 10.8 %attend.1 = bf16[16,128,128]{2,1,0:T(8,128)(2,1)} custom-call(s32[5]{0:T(128)S(1)} %stack.122.place, s32[4]{0:T(128)S(1)} %copy-done.6, s32[4,2]{1,0:T(4,128)S(1)} %pad_add_fusion.2.q_edges, s32[4,4]{1,0:T(4,128)S(1)} %copy.17.k_edges, f32[32]{0:T(128)S(1)} %fusion.5.biases, bf16[4,128,128]{2,1,0:T(8,128)(2,1)S(1)} %copy-done.5, ...), custom_call_target="tpu_custom_call" | custom-call | flops 1073741824 | bytes 5242880 | tf_op jit(solution)/shard_map/attend/pallas_call | solution.py:277
  132.8 8.9 %all-to-all-start = ((bf16[16,128,128]{2,1,0:T(8,128)(2,1)}), bf16[16,128,128]{2,1,0:T(8,128)(2,1)S(1)}, u32[]{:S(2)}, u32[]{:S(2)}) async-start(bf16[16,128,128]{2,1,0:T(8,128)(2,1)} %attend.1), calls=%async_computation | async-start | bytes 1048576 | tf_op jit(solution)/shard_map/all_to_all | solution.py:293
  141.7 3.2 %collective-permute-start.29 = (bf16[128,128]{1,0:T(8,128)(2,1)S(1)}, bf16[128,128]{1,0:T(8,128)(2,1)S(1)}, u32[]{:S(2)}, u32[]{:S(2)}) collective-permute-start(bf16[128,128]{1,0:T(8,128)(2,1)S(1)} %get-tuple-element.69), channel_id=1, source_target_pairs={{0,192},{64,0},{128,64},{192,128},{1,193},{65,1},{129,65},{193,129... | collective-permute-start | bytes 98312 | tf_op jit(solution)/shard_map/ppermute | solution.py:291
  146.8 4.3 %collective-permute-done.30.u2 = bf16[128,128]{1,0:T(8,128)(2,1)S(1)} collective-permute-done((bf16[128,128]{1,0:T(8,128)(2,1)S(1)}, bf16[128,128]{1,0:T(8,128)(2,1)S(1)}, u32[]{:S(2)}, u32[]{:S(2)}) %collective-permute-start.30) | collective-permute-done | bytes 32800 | tf_op jit(solution)/shard_map/ppermute | solution.py:291
  151.7 6.0 %all-to-all-done.parts = bf16[16,128,128]{2,1,0:T(8,128)(2,1)S(1)} async-done(((bf16[16,128,128]{2,1,0:T(8,128)(2,1)}), bf16[16,128,128]{2,1,0:T(8,128)(2,1)S(1)}, u32[]{:S(2)}, u32[]{:S(2)}) %all-to-all-start) | async-done | bytes 524320 | tf_op jit(solution)/shard_map/all_to_all | solution.py:293
  160.1 2.5 %collective-permute-start.34 = (bf16[128,512]{1,0:T(8,128)(2,1)S(1)}, bf16[128,512]{1,0:T(8,128)(2,1)S(1)}, u32[]{:S(2)}, u32[]{:S(2)}) collective-permute-start(bf16[128,512]{1,0:T(8,128)(2,1)S(1)} %gate.1), channel_id=1, source_target_pairs={{0,3},{1,0},{2,1},{3,2},{4,7},{5,4},{6,5},{7,6},{8,11},{9,8},{10,9... | collective-permute-start | bytes 393224 | tf_op jit(solution)/shard_map/ppermute | solution.py:22
  162.6 3.7 %collective-permute-done.32 = bf16[128,512]{1,0:T(8,128)(2,1)S(1)} collective-permute-done((bf16[128,512]{1,0:T(8,128)(2,1)S(1)}, bf16[128,512]{1,0:T(8,128)(2,1)S(1)}, u32[]{:S(2)}, u32[]{:S(2)}) %collective-permute-start.32) | collective-permute-done | bytes 131104 | tf_op jit(solution)/shard_map/ppermute | solution.py:22
  167.1 2.2 %copy-done.2 = bf16[64,64,512]{2,1,0:T(8,128)(2,1)S(1)} copy-done((bf16[64,64,512]{2,1,0:T(8,128)(2,1)S(1)}, bf16[64,64,512]{2,1,0:T(8,128)(2,1)}, u32[]{:S(2)}) %copy-start.2) | copy-done | bytes 4194328
  169.3 2.7 %project_out.1 = bf16[128,1024]{1,0:T(8,128)(2,1)} custom-call(s32[5]{0:T(128)S(1)} %stack.122.place, bf16[128,1024]{1,0:T(8,128)(2,1)S(1)} %copy-done.3, bf16[4,128,512]{2,1,0:T(8,128)(2,1)S(1)} %pad_maximum_fusion.1.gated, bf16[16,4,64,512]{3,2,1,0:T(8,128)(2,1)S(1)} %bitcast.51), custom_call_target="tpu_custom_call" | custom-call | flops 536870912 | bytes 5242880 | tf_op jit(solution)/shard_map/project_out/pallas_call | solution.py:307
  (103 shorter events, 39.0 us)
Async XLA Ops:
  6.5 73.5 %all-gather.5.cloned.1.call-start = ((), (), s32[]{:S(2)}) async-start(), calls=%async_computation.1 | async-start | bytes 4456448 | tf_op jit(solution)/shard_map/all_gather | solution.py:226
  7.5 5.9 %collective-permute-start.21 = (bf16[64,512]{1,0:T(8,128)(2,1)S(1)}, bf16[64,512]{1,0:T(8,128)(2,1)S(1)}, u32[]{:S(2)}, u32[]{:S(2)}) collective-permute-start(bf16[64,512]{1,0:T(8,128)(2,1)S(1)} %get-tuple-element.62), channel_id=1, source_target_pairs={{0,64},{64,128},{128,192},{192,0},{1,65},{65,129},{129,193},{193,1... | collective-permute-start | bytes 196616 | tf_op jit(solution)/shard_map/ppermute | solution.py:222
  9.2 6.1 %collective-permute-start.22 = (bf16[64,512]{1,0:T(8,128)(2,1)S(1)}, bf16[64,512]{1,0:T(8,128)(2,1)S(1)}, u32[]{:S(2)}, u32[]{:S(2)}) collective-permute-start(bf16[64,512]{1,0:T(8,128)(2,1)S(1)} %get-tuple-element.64), channel_id=1, source_target_pairs={{0,128},{64,192},{128,0},{192,64},{1,129},{65,193},{129,1},{193,65... | collective-permute-start | bytes 196616 | tf_op jit(solution)/shard_map/ppermute | solution.py:222
  17.1 150.0 %all-gather.7.cloned.1.call-start = ((), (), s32[]{:S(2)}) async-start(), calls=%async_computation.2 | async-start | bytes 4456448 | tf_op jit(solution)/shard_map/all_gather | solution.py:261
  18.1 8.4 %collective-permute-start = (bf16[128,512]{1,0:T(8,128)(2,1)S(1)}, bf16[128,512]{1,0:T(8,128)(2,1)S(1)}, u32[]{:S(2)}, u32[]{:S(2)}) collective-permute-start(bf16[128,512]{1,0:T(8,128)(2,1)S(1)} %get-tuple-element.32), channel_id=1, source_target_pairs={{0,64},{64,128},{128,192},{192,0},{1,65},{65,129},{129,193},{193,1... | collective-permute-start | bytes 393224 | tf_op jit(solution)/shard_map/ppermute | solution.py:22
  18.5 9.5 %collective-permute-start.1 = (bf16[128,512]{1,0:T(8,128)(2,1)S(1)}, bf16[128,512]{1,0:T(8,128)(2,1)S(1)}, u32[]{:S(2)}, u32[]{:S(2)}) collective-permute-start(bf16[128,512]{1,0:T(8,128)(2,1)S(1)} %get-tuple-element.32), channel_id=1, source_target_pairs={{0,128},{64,192},{128,0},{192,64},{1,129},{65,193},{129,1},{193,65... | collective-permute-start | bytes 393224 | tf_op jit(solution)/shard_map/ppermute | solution.py:22
  22.2 5.8 %collective-permute-start.2 = (bf16[128,512]{1,0:T(8,128)(2,1)S(1)}, bf16[128,512]{1,0:T(8,128)(2,1)S(1)}, u32[]{:S(2)}, u32[]{:S(2)}) collective-permute-start(bf16[128,512]{1,0:T(8,128)(2,1)S(1)} %get-tuple-element.32), channel_id=1, source_target_pairs={{0,192},{64,0},{128,64},{192,128},{1,193},{65,1},{129,65},{193,129... | collective-permute-start | bytes 393224 | tf_op jit(solution)/shard_map/ppermute | solution.py:22
  22.3 6.6 %collective-permute-start.3 = (bf16[128,512]{1,0:T(8,128)(2,1)S(1)}, bf16[128,512]{1,0:T(8,128)(2,1)S(1)}, u32[]{:S(2)}, u32[]{:S(2)}) collective-permute-start(bf16[128,512]{1,0:T(8,128)(2,1)S(1)} %get-tuple-element.36), channel_id=1, source_target_pairs={{0,1},{1,2},{2,3},{3,0},{4,5},{5,6},{6,7},{7,4},{8,9},{9,10},{10,1... | collective-permute-start | bytes 393224 | tf_op jit(solution)/shard_map/ppermute | solution.py:22
  23.8 7.1 %collective-permute-start.4 = (bf16[128,512]{1,0:T(8,128)(2,1)S(1)}, bf16[128,512]{1,0:T(8,128)(2,1)S(1)}, u32[]{:S(2)}, u32[]{:S(2)}) collective-permute-start(bf16[128,512]{1,0:T(8,128)(2,1)S(1)} %get-tuple-element.36), channel_id=1, source_target_pairs={{0,2},{1,3},{2,0},{3,1},{4,6},{5,7},{6,4},{7,5},{8,10},{9,11},{10,... | collective-permute-start | bytes 393224 | tf_op jit(solution)/shard_map/ppermute | solution.py:22
  31.6 16.5 %collective-permute-start.10 = (bf16[512,512]{1,0:T(8,128)(2,1)S(1)}, bf16[512,512]{1,0:T(8,128)(2,1)S(1)}, u32[]{:S(2)}, u32[]{:S(2)}) collective-permute-start(bf16[512,512]{1,0:T(8,128)(2,1)S(1)} %constant_dynamic-update-slice_fusion.4.b0), channel_id=1, source_target_pairs={{0,128},{64,192},{128,0},{192,64},{1,129},{65,193},{129,1},{193,65... | collective-permute-start | bytes 1572872 | tf_op jit(solution)/shard_map/ppermute | solution.py:22
  33.7 20.7 %collective-permute-start.9 = (bf16[512,512]{1,0:T(8,128)(2,1)S(1)}, bf16[512,512]{1,0:T(8,128)(2,1)S(1)}, u32[]{:S(2)}, u32[]{:S(2)}) collective-permute-start(bf16[512,512]{1,0:T(8,128)(2,1)S(1)} %constant_dynamic-update-slice_fusion.4.b0), channel_id=1, source_target_pairs={{0,64},{64,128},{128,192},{192,0},{1,65},{65,129},{129,193},{193,1... | collective-permute-start | bytes 1572872 | tf_op jit(solution)/shard_map/ppermute | solution.py:22
  33.8 20.6 %collective-permute-start.6 = (bf16[512,512]{1,0:T(8,128)(2,1)S(1)}, bf16[512,512]{1,0:T(8,128)(2,1)S(1)}, u32[]{:S(2)}, u32[]{:S(2)}) collective-permute-start(bf16[512,512]{1,0:T(8,128)(2,1)S(1)} %constant_dynamic-update-slice_fusion.a0), channel_id=1, source_target_pairs={{0,1},{1,2},{2,3},{3,0},{4,5},{5,6},{6,7},{7,4},{8,9},{9,10},{10,1... | collective-permute-start | bytes 1572872 | tf_op jit(solution)/shard_map/ppermute | solution.py:22
  35.2 21.5 %collective-permute-start.7 = (bf16[512,512]{1,0:T(8,128)(2,1)S(1)}, bf16[512,512]{1,0:T(8,128)(2,1)S(1)}, u32[]{:S(2)}, u32[]{:S(2)}) collective-permute-start(bf16[512,512]{1,0:T(8,128)(2,1)S(1)} %constant_dynamic-update-slice_fusion.a0), channel_id=1, source_target_pairs={{0,2},{1,3},{2,0},{3,1},{4,6},{5,7},{6,4},{7,5},{8,10},{9,11},{10,... | collective-permute-start | bytes 1572872 | tf_op jit(solution)/shard_map/ppermute | solution.py:22
  38.0 42.0 %collective-permute-start.11 = (bf16[512,512]{1,0:T(8,128)(2,1)S(1)}, bf16[512,512]{1,0:T(8,128)(2,1)}, u32[]{:S(2)}, u32[]{:S(2)}) collective-permute-start(bf16[512,512]{1,0:T(8,128)(2,1)S(1)} %constant_dynamic-update-slice_fusion.4.b0), channel_id=1, source_target_pairs={{0,192},{64,0},{128,64},{192,128},{1,193},{65,1},{129,65},{193,129... | collective-permute-start | bytes 1572872 | tf_op jit(solution)/shard_map/ppermute | solution.py:22
  48.1 31.9 %collective-permute-start.8 = (bf16[512,512]{1,0:T(8,128)(2,1)S(1)}, bf16[512,512]{1,0:T(8,128)(2,1)}, u32[]{:S(2)}, u32[]{:S(2)}) collective-permute-start(bf16[512,512]{1,0:T(8,128)(2,1)S(1)} %constant_dynamic-update-slice_fusion.a0), channel_id=1, source_target_pairs={{0,3},{1,0},{2,1},{3,2},{4,7},{5,4},{6,5},{7,6},{8,11},{9,8},{10,9... | collective-permute-start | bytes 1572872 | tf_op jit(solution)/shard_map/ppermute | solution.py:22
  56.6 6.2 %collective-permute-start.12 = (s32[512]{0:T(512)}, s32[512]{0:T(512)S(1)}, u32[]{:S(2)}, u32[]{:S(2)}) collective-permute-start(s32[512]{0:T(512)} %param.13), channel_id=1, source_target_pairs={{0,64},{64,128},{128,192},{192,0},{1,65},{65,129},{129,193},{193,1... | collective-permute-start | bytes 6152 | tf_op jit(solution)/shard_map/ppermute | solution.py:22
  57.8 6.5 %collective-permute-start.13 = (s32[512]{0:T(512)}, s32[512]{0:T(512)S(1)}, u32[]{:S(2)}, u32[]{:S(2)}) collective-permute-start(s32[512]{0:T(512)} %param.13), channel_id=1, source_target_pairs={{0,128},{64,192},{128,0},{192,64},{1,129},{65,193},{129,1},{193,65... | collective-permute-start | bytes 6152 | tf_op jit(solution)/shard_map/ppermute | solution.py:22
  65.5 9.5 %collective-permute-start.15 = (s32[4,512]{1,0:T(4,128)S(1)}, s32[4,512]{1,0:T(4,128)S(1)}, u32[]{:S(2)}, u32[]{:S(2)}) collective-permute-start(s32[4,512]{1,0:T(4,128)S(1)} %get-tuple-element.42), channel_id=1, source_target_pairs={{0,32},{32,0},{1,33},{33,1},{2,34},{34,2},{3,35},{35,3},{4,36},{36... | collective-permute-start | bytes 24584 | tf_op jit(solution)/shard_map/ppermute | solution.py:28
  65.8 11.2 %collective-permute-start.18 = (bf16[64,512]{1,0:T(8,128)(2,1)S(1)}, bf16[64,512]{1,0:T(8,128)(2,1)S(1)}, u32[]{:S(2)}, u32[]{:S(2)}) collective-permute-start(bf16[64,512]{1,0:T(8,128)(2,1)S(1)} %collective-permute-done.17), channel_id=1, source_target_pairs={{0,64},{64,128},{128,192},{192,0},{1,65},{65,129},{129,193},{193,1... | collective-permute-start | bytes 196616 | tf_op jit(solution)/shard_map/ppermute | solution.py:22
  70.3 7.6 %collective-permute-start.19 = (bf16[64,512]{1,0:T(8,128)(2,1)S(1)}, bf16[64,512]{1,0:T(8,128)(2,1)S(1)}, u32[]{:S(2)}, u32[]{:S(2)}) collective-permute-start(bf16[64,512]{1,0:T(8,128)(2,1)S(1)} %collective-permute-done.17), channel_id=1, source_target_pairs={{0,128},{64,192},{128,0},{192,64},{1,129},{65,193},{129,1},{193,65... | collective-permute-start | bytes 196616 | tf_op jit(solution)/shard_map/ppermute | solution.py:22
  87.8 6.6 %collective-permute-start.27 = (bf16[4,128,256]{2,1,0:T(8,128)(2,1)S(1)}, bf16[4,128,256]{2,1,0:T(8,128)(2,1)S(1)}, u32[]{:S(2)}, u32[]{:S(2)}) collective-permute-start(bf16[4,128,256]{2,1,0:T(8,128)(2,1)S(1)} %get-tuple-element.54), channel_id=1, source_target_pairs={{0,32},{32,0},{1,33},{33,1},{2,34},{34,2},{3,35},{35,3},{4,36},{36... | collective-permute-start | bytes 786440 | tf_op jit(solution)/shard_map/ppermute | solution.py:28
  94.5 26.6 %collective-permute-start.28 = (bf16[2,4,128,256]{3,2,1,0:T(8,128)(2,1)S(1)}, bf16[2,4,128,256]{3,2,1,0:T(8,128)(2,1)S(1)}, u32[]{:S(2)}, u32[]{:S(2)}) collective-permute-start(bf16[2,4,128,256]{3,2,1,0:T(8,128)(2,1)S(1)} %pad_maximum_fusion.kv_near), channel_id=1, source_target_pairs={{0,16},{16,0},{1,17},{17,1},{2,18},{18,2},{3,19},{19,3},{4,20},{20... | collective-permute-start | bytes 1572872 | tf_op jit(solution)/shard_map/ppermute | solution.py:28
  96.0 15.3 %collective-permute-start.24 = (bf16[4,128,128]{2,1,0:T(8,128)(2,1)}, bf16[4,128,128]{2,1,0:T(8,128)(2,1)S(1)}, u32[]{:S(2)}, u32[]{:S(2)}) collective-permute-start(bf16[4,128,128]{2,1,0:T(8,128)(2,1)} %copy-done.4), channel_id=1, source_target_pairs={{0,4},{4,8},{8,12},{12,0},{1,5},{5,9},{9,13},{13,1},{2,6},{6,10},{... | collective-permute-start | bytes 393224 | tf_op jit(solution)/shard_map/ppermute | solution.py:22
  99.3 16.6 %collective-permute-start.25 = (bf16[4,128,128]{2,1,0:T(8,128)(2,1)}, bf16[4,128,128]{2,1,0:T(8,128)(2,1)S(1)}, u32[]{:S(2)}, u32[]{:S(2)}) collective-permute-start(bf16[4,128,128]{2,1,0:T(8,128)(2,1)} %copy-done.4), channel_id=1, source_target_pairs={{0,8},{4,12},{8,0},{12,4},{1,9},{5,13},{9,1},{13,5},{2,10},{6,14},... | collective-permute-start | bytes 393224 | tf_op jit(solution)/shard_map/ppermute | solution.py:22
  103.8 17.2 %collective-permute-start.26 = (bf16[4,128,128]{2,1,0:T(8,128)(2,1)}, bf16[4,128,128]{2,1,0:T(8,128)(2,1)S(1)}, u32[]{:S(2)}, u32[]{:S(2)}) collective-permute-start(bf16[4,128,128]{2,1,0:T(8,128)(2,1)} %copy-done.4), channel_id=1, source_target_pairs={{0,12},{4,0},{8,4},{12,8},{1,13},{5,1},{9,5},{13,9},{2,14},{6,2},{... | collective-permute-start | bytes 393224 | tf_op jit(solution)/shard_map/ppermute | solution.py:22
  132.8 25.0 %all-to-all-start = ((bf16[16,128,128]{2,1,0:T(8,128)(2,1)}), bf16[16,128,128]{2,1,0:T(8,128)(2,1)S(1)}, u32[]{:S(2)}, u32[]{:S(2)}) async-start(bf16[16,128,128]{2,1,0:T(8,128)(2,1)} %attend.1), calls=%async_computation | async-start | bytes 1048576 | tf_op jit(solution)/shard_map/all_to_all | solution.py:293
  141.7 5.1 %collective-permute-start.29 = (bf16[128,128]{1,0:T(8,128)(2,1)S(1)}, bf16[128,128]{1,0:T(8,128)(2,1)S(1)}, u32[]{:S(2)}, u32[]{:S(2)}) collective-permute-start(bf16[128,128]{1,0:T(8,128)(2,1)S(1)} %get-tuple-element.69), channel_id=1, source_target_pairs={{0,192},{64,0},{128,64},{192,128},{1,193},{65,1},{129,65},{193,129... | collective-permute-start | bytes 98312 | tf_op jit(solution)/shard_map/ppermute | solution.py:291
  144.9 6.1 %collective-permute-start.30 = (bf16[128,128]{1,0:T(8,128)(2,1)S(1)}, bf16[128,128]{1,0:T(8,128)(2,1)S(1)}, u32[]{:S(2)}, u32[]{:S(2)}) collective-permute-start(bf16[128,128]{1,0:T(8,128)(2,1)S(1)} %get-tuple-element.68), channel_id=1, source_target_pairs={{0,128},{64,192},{128,0},{192,64},{1,129},{65,193},{129,1},{193,65... | collective-permute-start | bytes 98312 | tf_op jit(solution)/shard_map/ppermute | solution.py:291
  145.8 5.9 %collective-permute-start.31 = (bf16[128,128]{1,0:T(8,128)(2,1)S(1)}, bf16[128,128]{1,0:T(8,128)(2,1)S(1)}, u32[]{:S(2)}, u32[]{:S(2)}) collective-permute-start(bf16[128,128]{1,0:T(8,128)(2,1)S(1)} %get-tuple-element.67), channel_id=1, source_target_pairs={{0,64},{64,128},{128,192},{192,0},{1,65},{65,129},{129,193},{193,1... | collective-permute-start | bytes 98312 | tf_op jit(solution)/shard_map/ppermute | solution.py:291
  158.5 7.8 %collective-permute-start.32 = (bf16[128,512]{1,0:T(8,128)(2,1)S(1)}, bf16[128,512]{1,0:T(8,128)(2,1)S(1)}, u32[]{:S(2)}, u32[]{:S(2)}) collective-permute-start(bf16[128,512]{1,0:T(8,128)(2,1)S(1)} %gate.1), channel_id=1, source_target_pairs={{0,1},{1,2},{2,3},{3,0},{4,5},{5,6},{6,7},{7,4},{8,9},{9,10},{10,1... | collective-permute-start | bytes 393224 | tf_op jit(solution)/shard_map/ppermute | solution.py:22
  158.6 7.7 %collective-permute-start.33 = (bf16[128,512]{1,0:T(8,128)(2,1)S(1)}, bf16[128,512]{1,0:T(8,128)(2,1)S(1)}, u32[]{:S(2)}, u32[]{:S(2)}) collective-permute-start(bf16[128,512]{1,0:T(8,128)(2,1)S(1)} %gate.1), channel_id=1, source_target_pairs={{0,2},{1,3},{2,0},{3,1},{4,6},{5,7},{6,4},{7,5},{8,10},{9,11},{10,... | collective-permute-start | bytes 393224 | tf_op jit(solution)/shard_map/ppermute | solution.py:22
  160.1 6.9 %collective-permute-start.34 = (bf16[128,512]{1,0:T(8,128)(2,1)S(1)}, bf16[128,512]{1,0:T(8,128)(2,1)S(1)}, u32[]{:S(2)}, u32[]{:S(2)}) collective-permute-start(bf16[128,512]{1,0:T(8,128)(2,1)S(1)} %gate.1), channel_id=1, source_target_pairs={{0,3},{1,0},{2,1},{3,2},{4,7},{5,4},{6,5},{7,6},{8,11},{9,8},{10,9... | collective-permute-start | bytes 393224 | tf_op jit(solution)/shard_map/ppermute | solution.py:22
  (16 other events, 295.5 us)
Sparse Core Ops, SparseCore 0:
  17.2 43.7 all-gather.4
  87.2 52.5 all-gather.6

commit v5 on v3

--- a/solution.py
+++ b/solution.py
@@ -28,7 +28,7 @@
     return lax.ppermute(value, axis, [(0, 1), (1, 0)])
 
 
-def project_kernel(place, a0, a1, a2, a3, b0, b1, b2, b3, weights, kv_ref, q_ref, u_ref, total):
+def project_kernel(place, a0, a1, a2, a3, b0, b1, b2, b3, weights, k_rows, kv_ref, q_ref, u_ref, total):
     y, x = place[0], place[4]
     seconds = (b0, b1, b2, b3)
     for kx, first in enumerate((a0, a1, a2, a3)):
@@ -49,9 +49,10 @@
     for r in range(4):
         rows = slice(r * RUN, (r + 1) * RUN)
         u_ref[r] = act[rows, :DH]
-        kv_ref[r, :, :DH] = act[rows, DH : 2 * DH]
+        kv_ref[r, :RUN, :DH] = act[rows, DH : 2 * DH]
         q_ref[r] = act[rows, 2 * DH : 3 * DH]
-        kv_ref[r, :, DH:] = act[rows, 3 * DH :]
+        kv_ref[r, :RUN, DH:] = act[rows, 3 * DH :]
+        kv_ref[r, RUN:, :] = k_rows[r]
 
 
 def attend_kernel(
@@ -101,7 +102,7 @@
         def tile(t, carry):
             ky, zl_from = (y - (t >> 1)) & 3, t & 1
             zx = zl ^ zl_from
-            near, far = kv_near[zx, ky], kv_far[zx, ky]
+            near, far = kv_near[zx, ky, :RUN, :], kv_far[zx, ky, :RUN, :]
             keys = jnp.concatenate([near[:, DH:], far[:, DH:]], axis=0)
             values = jnp.concatenate([near[:, :DH], far[:, :DH]], axis=0)
             k_first = t * 1024 + zh * RUN
@@ -182,15 +183,15 @@
 
 
 def output_kernel(place, tokens, gated, near, far, out_ref):
-    y, core, x = place[0], place[2], place[4]
-    for zl in range(2):
+    y, zl, core, zh, x = (place[i] for i in range(5))
+    for zx in range(2):
         for c, source in enumerate((near, far)):
-            block = zl * 2 + (core ^ c)
+            block = (zl ^ zx) * 2 + (core ^ c)
             columns = pl.ds(pl.multiple_of(block * 256, 256), 256)
             total = tokens[:, columns].astype(jnp.float32)
             for ky in range(4):
                 left = gated[(x - (y - ky)) & 3]
-                right = jnp.concatenate([source[ky, j * 2 + zl] for j in range(4)], axis=0)
+                right = jnp.concatenate([source[ky, zx, (zh - t) & 3] for t in range(4)], axis=0)
                 total += lax.dot_general(
                     left, right, (((1,), (1,)), ((), ())), preferred_element_type=jnp.float32
                 )
@@ -227,53 +228,60 @@
     piece = jnp.stack(pieces)
     weights = lax.all_gather(piece, plane)
 
-    first = rotations(tokens[:, :512], "y", 4)
+    ids = jnp.stack([bucket_ids // 128, bucket_ids % 128]).astype(bf16)
+    ids = jnp.concatenate([ids, jnp.zeros((14, BLOCK), bf16)], axis=0)
+    first = rotations(jnp.concatenate([tokens[:, :512], ids], axis=0), "y", 4)
     second = rotations(tokens[:, 512:], "x", 4)
     first, second = lax.optimization_barrier((first, second))
-    firsts = rotations(jnp.concatenate(first, axis=0), "x", 4)
+    firsts = rotations(jnp.concatenate([f[:RUN] for f in first], axis=0), "x", 4)
     seconds = rotations(jnp.concatenate(second, axis=0), "y", 4)
-
-    ids, late, _ = lax.optimization_barrier((bucket_ids, w_out.T, (first, second)))
-    ids_y = jnp.stack(rotations(ids, "y", 4))
-    ids_near = jnp.stack([ids_y, swap(ids_y, "zl")])
-    ids_far = swap(ids_near, "core")
+    id_rows = jnp.stack([f[RUN : RUN + 2] for f in first])
+    q_ids = (id_rows[:, 0].astype(f32) * 128 + id_rows[:, 1].astype(f32)).astype(jnp.int32)
+    q_edges = jnp.stack([q_ids[:, 0], q_ids[:, -1]], axis=1)
+    q_ids = q_ids.reshape(4, BLOCK, 1)
+    k_rows = lax.dynamic_slice(id_rows, (0, 0, zh * RUN), (4, 2, RUN)).reshape(4, 1, PAIR)
+    k_rows = jnp.pad(k_rows, ((0, 0), (0, 15), (0, 0)))
+
+    late, _ = lax.optimization_barrier((w_out.T, piece))
     swapped = lax.ppermute(late, ("y", "x"), [(b * 4 + a, a * 4 + b) for a in range(4) for b in range(4)])
-
-    firsts, seconds, ids_y, ids_near, ids_far, swapped = lax.optimization_barrier(
-        (firsts, seconds, ids_y, ids_near, ids_far, swapped)
+    over_zh = rotations(swapped, "zh", 4)
+    wo_zh = jnp.stack(over_zh)
+    wo_zh, _ = lax.optimization_barrier((wo_zh, (firsts[1:3], seconds[1:3])))
+    wo_half = jnp.stack([wo_zh, swap(wo_zh, "zl")])
+    wo_parts = rotations(wo_half, "y", 4)
+
+    firsts, seconds, k_rows, q_ids, q_edges = lax.optimization_barrier(
+        (firsts, seconds, k_rows, q_ids, q_edges)
     )
     kv, q, u = call(
         project_kernel,
         [
-            jax.ShapeDtypeStruct((4, RUN, 2 * DH), bf16),
+            jax.ShapeDtypeStruct((4, RUN + 16, 2 * DH), bf16),
             jax.ShapeDtypeStruct((4, RUN, DH), bf16),
             jax.ShapeDtypeStruct((4, RUN, DH), bf16),
         ],
         1,
-        9,
+        10,
         [pltpu.VMEM((512, 512), f32)],
         2 * 512 * 512 * 4096,
         9 * 2**20,
-        24,
+        20,
         "project",
-    )(place, *firsts, *seconds, weights)
-
-    wo_block = lax.all_gather(swapped, plane)
+    )(place, *firsts, *seconds, weights, k_rows)
 
     kv_near = jnp.stack([kv, swap(kv, "zl")])
     kv_far = swap(kv_near, "core")
-    q, _ = lax.optimization_barrier((q, kv_near))
     q_all = rotations(q, "zh", 4)
 
-    q_ids = ids_y.reshape(4, BLOCK, 1)
-    k_ids = lax.dynamic_slice(jnp.stack([ids_near, ids_far]), (0, 0, 0, zh * RUN), (2, 2, 4, RUN))
+    k_ids = jnp.stack([kv_near[:, :, RUN], kv_far[:, :, RUN]]).astype(f32)
+    k_ids = (k_ids[..., :DH] * 128 + k_ids[..., DH:]).astype(jnp.int32)
     k_edges = jnp.stack([jnp.min(k_ids[..., 0], axis=0), jnp.max(k_ids[..., -1], axis=0)], axis=-1)
     k_edges = k_edges.transpose(1, 0, 2).reshape(4, 4)
     k_ids = k_ids.transpose(2, 1, 0, 3).reshape(4, 2, PAIR)
-    q_edges = jnp.stack([ids_y[:, 0], ids_y[:, -1]], axis=1)
     biases = lax.dynamic_slice(rab_table, (x * 4 + y, 0), (1, NB))
     gains = lax.dynamic_slice(norm_gain, (x * 4, 0), (4, DH))
     table = jnp.pad(biases, ((0, 0), (0, DH - NB)))
+    wo_parts, q_all = lax.optimization_barrier((wo_parts, q_all))
 
     parts = call(
         attend_kernel,
@@ -287,14 +295,14 @@
         "attend",
     )(place, user_lengths, q_edges, k_edges, biases[0], *q_all, kv_near, kv_far, q_ids, k_ids, table)
 
-    half = lax.dynamic_index_in_dim(wo_block.reshape(8, 2, 64, 512), core, 1, keepdims=False)
-    half, u, _ = lax.optimization_barrier((half, u, (kv_far, q_all)))
+    wo_near = jnp.stack(wo_parts)
+    wo_far = swap(wo_near, "core")
+    u, _ = lax.optimization_barrier((u, (kv_far, q_all)))
     u_own = [u[0]] + [
         lax.ppermute(u[k], "y", [(i, (i - k) % 4) for i in range(4)]) for k in range(1, 4)
     ]
-    wo_parts = rotations(half, "y", 4)
-
     arrived = lax.all_to_all(parts, ("y", "zh"), 0, 0, tiled=True)
+    arrived, wo_near, wo_far = lax.optimization_barrier((arrived, wo_near, wo_far))
     gated = call(
         gate_kernel,
         jax.ShapeDtypeStruct((RUN, 4 * DH), bf16),
@@ -306,10 +314,7 @@
         4,
         "gate",
     )(place, arrived, *u_own, gains)
-    wo_parts, gated = lax.optimization_barrier((wo_parts, gated))
     heads = jnp.stack(rotations(gated, "x", 4))
-    wo_near = jnp.stack(wo_parts)
-    wo_far = swap(wo_near, "core")
 
     return call(
         output_kernel,

time: 202 us -> 183 us (0.906)
  waiting for transfers between devices: 80.3 us -> 53.1 us
  local copies, waits for them, and re-layouts: 13.7 us -> 19.1 us
  other arithmetic: 2.78 us -> 6.9 us
    ppermute x3, waiting for transfers between devices: 27 us -> 0.01 us  [on_device(): lax.ppermute(u[k], 'y', [(i, (i - k) % 4) for i in range(4)])]
    all_to_all x1, waiting for transfers between devices: 0.01 us -> 13.3 us  [on_device(): arrived = lax.all_to_all(parts, ('y', 'zh'), 0, 0, tiled=True)]
    ppermute x24, waiting for transfers between devices: 39.3 us -> 26.9 us  [rotations(): lax.ppermute(value, axis, [(i, (i + step * k) % size) for i in range(size)])]
    ppermute x5 -> x4, starting transfers between devices: 0.53 us -> 8.98 us  [swap(): return lax.ppermute(value, axis, [(0, 1), (1, 0)])]
    unnamed x36 -> x51, local copies, waits for them, and re-layouts: 7.13 us -> 12.7 us
    ppermute x24, starting transfers between devices: 49.3 us -> 45.3 us  [rotations(): lax.ppermute(value, axis, [(i, (i + step * k) % size) for i in range(size)])]
    all_to_all x1, starting transfers between devices: 8.22 us -> 4.79 us  [on_device(): arrived = lax.all_to_all(parts, ('y', 'zh'), 0, 0, tiled=True)]
    ppermute x5 -> x4, waiting for transfers between devices: 11 us -> 7.93 us  [swap(): return lax.ppermute(value, axis, [(0, 1), (1, 0)])]
  transfers between devices with their start and end apart: 39 -> 37, of which waited for: 19 -> 14; matrix products, arithmetic and copies ran while one was open for 4% -> 6% of each run, Pallas kernels for 9% -> 8%
where the time goes in v5:
time: 183 us; the launch traced here: 181 us
  starting transfers between devices  69.3 us (38%)
  waiting for transfers between devices  53.1 us (29%)
  Pallas kernels  19.3 us (11%)
  local copies, waits for them, and re-layouts  19.1 us (10%)
  between operations  13.8 us (8%)
  other arithmetic  6.9 us (4%)
    ppermute x24, starting transfers between devices, rotations(): lax.ppermute(value, axis, [(i, (i + step * k) % size) for i in range(size)])  45.3 us
    ppermute x24, waiting for transfers between devices, rotations(): lax.ppermute(value, axis, [(i, (i + step * k) % size) for i in range(size)])  26.9 us
    all_to_all x1, waiting for transfers between devices, on_device(): arrived = lax.all_to_all(parts, ('y', 'zh'), 0, 0, tiled=True)  13.3 us
    unnamed x51, local copies, waits for them, and re-layouts  12.7 us
    pallas_call x1, Pallas kernels, on_device(): call(attend_kernel, jax.ShapeDtypeStruct((16, RUN, DH), bf16), 5, 9, [plt...  11.1 us
    ppermute x4, starting transfers between devices, swap(): return lax.ppermute(value, axis, [(0, 1), (1, 0)])  8.98 us
    ppermute x4, waiting for transfers between devices, swap(): return lax.ppermute(value, axis, [(0, 1), (1, 0)])  7.93 us
    ppermute x3, starting transfers between devices, on_device(): lax.ppermute(u[k], 'y', [(i, (i - k) % 4) for i in range(4)])  4.93 us
  transfers between devices with their start and end apart: 37, of which 14 were waited for; matrix products, arithmetic and copies ran while one was open for 6% of the time, Pallas kernels for 8%

profile of v5, /device:TPU:32, one launch (start us, length us, event | category | flops | bytes accessed | tf_op | source)
XLA Modules:
  0.0 181.5 jit_solution(5728684783564759948)
XLA Ops:
  7.5 3.1 %collective-permute-start.14 = (bf16[64,512]{1,0:T(8,128)(2,1)S(1)}, bf16[64,512]{1,0:T(8,128)(2,1)S(1)}, u32[]{:S(2)}, u32[]{:S(2)}) collective-permute-start(bf16[64,512]{1,0:T(8,128)(2,1)S(1)} %get-tuple-element.81), channel_id=1, source_target_pairs={{0,192},{64,0},{128,64},{192,128},{1,193},{65,1},{129,65},{193,129... | collective-permute-start | bytes 196616 | tf_op jit(solution)/shard_map/ppermute | solution.py:225
  12.8 3.7 %collective-permute-done.13 = bf16[64,512]{1,0:T(8,128)(2,1)S(1)} collective-permute-done((bf16[64,512]{1,0:T(8,128)(2,1)S(1)}, bf16[64,512]{1,0:T(8,128)(2,1)S(1)}, u32[]{:S(2)}, u32[]{:S(2)}) %collective-permute-start.13) | collective-permute-done | bytes 65568 | tf_op jit(solution)/shard_map/ppermute | solution.py:225
  18.9 1.6 collective-permute-start.3
  20.4 2.7 %collective-permute-start.4 = (bf16[128,512]{1,0:T(8,128)(2,1)S(1)}, bf16[128,512]{1,0:T(8,128)(2,1)S(1)}, u32[]{:S(2)}, u32[]{:S(2)}) collective-permute-start(bf16[128,512]{1,0:T(8,128)(2,1)S(1)} %get-tuple-element.45), channel_id=1, source_target_pairs={{0,2},{1,3},{2,0},{3,1},{4,6},{5,7},{6,4},{7,5},{8,10},{9,11},{10,... | collective-permute-start | bytes 393224 | tf_op jit(solution)/shard_map/ppermute | solution.py:22
  24.1 2.0 %collective-permute-start.1 = (bf16[144,512]{1,0:T(8,128)(2,1)S(1)}, bf16[144,512]{1,0:T(8,128)(2,1)S(1)}, u32[]{:S(2)}, u32[]{:S(2)}) collective-permute-start(bf16[144,512]{1,0:T(8,128)(2,1)S(1)} %maximum_maximum_fusion), channel_id=1, source_target_pairs={{0,128},{64,192},{128,0},{192,64},{1,129},{65,193},{129,1},{193,65... | collective-permute-start | bytes 442376 | tf_op jit(solution)/shard_map/ppermute | solution.py:22
  26.1 1.9 %collective-permute-start.2 = (bf16[144,512]{1,0:T(8,128)(2,1)S(1)}, bf16[144,512]{1,0:T(8,128)(2,1)S(1)}, u32[]{:S(2)}, u32[]{:S(2)}) collective-permute-start(bf16[144,512]{1,0:T(8,128)(2,1)S(1)} %maximum_maximum_fusion), channel_id=1, source_target_pairs={{0,192},{64,0},{128,64},{192,128},{1,193},{65,1},{129,65},{193,129... | collective-permute-start | bytes 442376 | tf_op jit(solution)/shard_map/ppermute | solution.py:22
  30.3 5.4 %collective-permute-start.20 = (bf16[64,512]{1,0:T(8,128)(2,1)S(1)}, bf16[64,512]{1,0:T(8,128)(2,1)S(1)}, u32[]{:S(2)}, u32[]{:S(2)}) collective-permute-start(bf16[64,512]{1,0:T(8,128)(2,1)S(1)} %collective-permute-done.17), channel_id=1, source_target_pairs={{0,12},{4,0},{8,4},{12,8},{1,13},{5,1},{9,5},{13,9},{2,14},{6,2},{... | collective-permute-start | bytes 196616 | tf_op jit(solution)/shard_map/ppermute | solution.py:22
  36.5 7.3 %collective-permute-start.6 = (bf16[512,512]{1,0:T(8,128)(2,1)S(1)}, bf16[512,512]{1,0:T(8,128)(2,1)S(1)}, u32[]{:S(2)}, u32[]{:S(2)}) collective-permute-start(bf16[512,512]{1,0:T(8,128)(2,1)S(1)} %pad_maximum_fusion.2.a0), channel_id=1, source_target_pairs={{0,1},{1,2},{2,3},{3,0},{4,5},{5,6},{6,7},{7,4},{8,9},{9,10},{10,1... | collective-permute-start | bytes 1572872 | tf_op jit(solution)/shard_map/ppermute | solution.py:22
  43.8 3.5 %collective-permute-start.7 = (bf16[512,512]{1,0:T(8,128)(2,1)S(1)}, bf16[512,512]{1,0:T(8,128)(2,1)S(1)}, u32[]{:S(2)}, u32[]{:S(2)}) collective-permute-start(bf16[512,512]{1,0:T(8,128)(2,1)S(1)} %pad_maximum_fusion.2.a0), channel_id=1, source_target_pairs={{0,2},{1,3},{2,0},{3,1},{4,6},{5,7},{6,4},{7,5},{8,10},{9,11},{10,... | collective-permute-start | bytes 1572872 | tf_op jit(solution)/shard_map/ppermute | solution.py:22
  50.0 1.7 collective-permute-start.19
  51.8 7.8 %collective-permute-done.19 = bf16[64,512]{1,0:T(8,128)(2,1)S(1)} collective-permute-done((bf16[64,512]{1,0:T(8,128)(2,1)S(1)}, bf16[64,512]{1,0:T(8,128)(2,1)S(1)}, u32[]{:S(2)}, u32[]{:S(2)}) %collective-permute-start.19) | collective-permute-done | bytes 65568 | tf_op jit(solution)/shard_map/ppermute | solution.py:22
  60.2 5.8 %collective-permute-done.18 = bf16[64,512]{1,0:T(8,128)(2,1)S(1)} collective-permute-done((bf16[64,512]{1,0:T(8,128)(2,1)S(1)}, bf16[64,512]{1,0:T(8,128)(2,1)S(1)}, u32[]{:S(2)}, u32[]{:S(2)}) %collective-permute-start.18) | collective-permute-done | bytes 65568 | tf_op jit(solution)/shard_map/ppermute | solution.py:22
  65.9 3.1 %collective-permute-start.8 = (bf16[512,512]{1,0:T(8,128)(2,1)S(1)}, bf16[512,512]{1,0:T(8,128)(2,1)S(1)}, u32[]{:S(2)}, u32[]{:S(2)}) collective-permute-start(bf16[512,512]{1,0:T(8,128)(2,1)S(1)} %pad_maximum_fusion.2.a0), channel_id=1, source_target_pairs={{0,3},{1,0},{2,1},{3,2},{4,7},{5,4},{6,5},{7,6},{8,11},{9,8},{10,9... | collective-permute-start | bytes 1572872 | tf_op jit(solution)/shard_map/ppermute | solution.py:22
  69.1 1.6 collective-permute-start.11
  70.7 4.0 %collective-permute-start.21 = (bf16[4,64,512]{2,1,0:T(8,128)(2,1)S(1)}, bf16[4,64,512]{2,1,0:T(8,128)(2,1)S(1)}, u32[]{:S(2)}, u32[]{:S(2)}) collective-permute-start(bf16[4,64,512]{2,1,0:T(8,128)(2,1)S(1)} %pad_maximum_fusion.6), channel_id=1, source_target_pairs={{0,32},{32,0},{1,33},{33,1},{2,34},{34,2},{3,35},{35,3},{4,36},{36... | collective-permute-start | bytes 786440 | tf_op jit(solution)/shard_map/ppermute | solution.py:28
  74.8 4.3 %collective-permute-done.21 = bf16[4,64,512]{2,1,0:T(8,128)(2,1)S(1)} collective-permute-done((bf16[4,64,512]{2,1,0:T(8,128)(2,1)S(1)}, bf16[4,64,512]{2,1,0:T(8,128)(2,1)S(1)}, u32[]{:S(2)}, u32[]{:S(2)}) %collective-permute-start.21) | collective-permute-done | bytes 262176 | tf_op jit(solution)/shard_map/ppermute | solution.py:28
  80.8 2.6 %collective-permute-done.11.b3 = bf16[512,512]{1,0:T(8,128)(2,1)S(1)} collective-permute-done((bf16[512,512]{1,0:T(8,128)(2,1)S(1)}, bf16[512,512]{1,0:T(8,128)(2,1)S(1)}, u32[]{:S(2)}, u32[]{:S(2)}) %collective-permute-start.11) | collective-permute-done | bytes 524320 | tf_op jit(solution)/shard_map/ppermute | solution.py:22
  84.2 3.2 %collective-permute-start.23 = (bf16[2,4,64,512]{3,2,1,0:T(8,128)(2,1)}, bf16[2,4,64,512]{3,2,1,0:T(8,128)(2,1)}, u32[]{:S(2)}, u32[]{:S(2)}) collective-permute-start(bf16[2,4,64,512]{3,2,1,0:T(8,128)(2,1)} %pad_maximum_fusion.3), channel_id=1, source_target_pairs={{0,128},{64,192},{128,0},{192,64},{1,129},{65,193},{129,1},{193,65... | collective-permute-start | bytes 1572872 | tf_op jit(solution)/shard_map/ppermute | solution.py:22
  87.4 3.1 %collective-permute-start.24 = (bf16[2,4,64,512]{3,2,1,0:T(8,128)(2,1)}, bf16[2,4,64,512]{3,2,1,0:T(8,128)(2,1)}, u32[]{:S(2)}, u32[]{:S(2)}) collective-permute-start(bf16[2,4,64,512]{3,2,1,0:T(8,128)(2,1)} %pad_maximum_fusion.3), channel_id=1, source_target_pairs={{0,192},{64,0},{128,64},{192,128},{1,193},{65,1},{129,65},{193,129... | collective-permute-start | bytes 1572872 | tf_op jit(solution)/shard_map/ppermute | solution.py:22
  90.5 2.2 %copy-done.1 = bf16[64,64,512]{2,1,0:T(8,128)(2,1)S(1)} copy-done((bf16[64,64,512]{2,1,0:T(8,128)(2,1)S(1)}, bf16[64,64,512]{2,1,0:T(8,128)(2,1)}, u32[]{:S(2)}) %copy-start.1) | copy-done | bytes 4194328
  94.8 3.6 %project.1 = (bf16[4,144,256]{2,1,0:T(8,128)(2,1)S(1)}, bf16[4,128,128]{2,1,0:T(8,128)(2,1)}, bf16[4,128,128]{2,1,0:T(8,128)(2,1)S(1)}) custom-call(s32[5]{0:T(128)S(1)} %stack.141.place, bf16[512,512]{1,0:T(8,128)(2,1)S(1)} %pad_maximum_fusion.2.a0, bf16[512,512]{1,0:T(8,128)(2,1)S(1)} %collective-permute-done.6.a1, ...), custom_call_target="tpu_custom_call" | custom-call | flops 2147483648 | bytes 9437184 | tf_op jit(solution)/shard_map/project/pallas_call | solution.py:256
  99.0 4.9 %collective-permute-start.15 = (bf16[4,144,256]{2,1,0:T(8,128)(2,1)S(1)}, bf16[4,144,256]{2,1,0:T(8,128)(2,1)S(1)}, u32[]{:S(2)}, u32[]{:S(2)}) collective-permute-start(bf16[4,144,256]{2,1,0:T(8,128)(2,1)S(1)} %get-tuple-element.59), channel_id=1, source_target_pairs={{0,32},{32,0},{1,33},{33,1},{2,34},{34,2},{3,35},{35,3},{4,36},{36... | collective-permute-start | bytes 884744 | tf_op jit(solution)/shard_map/ppermute | solution.py:28
  104.9 3.7 %collective-permute-done.15 = bf16[4,144,256]{2,1,0:T(8,128)(2,1)S(1)} collective-permute-done((bf16[4,144,256]{2,1,0:T(8,128)(2,1)S(1)}, bf16[4,144,256]{2,1,0:T(8,128)(2,1)S(1)}, u32[]{:S(2)}, u32[]{:S(2)}) %collective-permute-start.15) | collective-permute-done | bytes 294944 | tf_op jit(solution)/shard_map/ppermute | solution.py:28
  109.5 5.4 %collective-permute-done.25.q1 = bf16[4,128,128]{2,1,0:T(8,128)(2,1)S(1)} collective-permute-done((bf16[4,128,128]{2,1,0:T(8,128)(2,1)}, bf16[4,128,128]{2,1,0:T(8,128)(2,1)S(1)}, u32[]{:S(2)}, u32[]{:S(2)}) %collective-permute-start.25) | collective-permute-done | bytes 131104 | tf_op jit(solution)/shard_map/ppermute | solution.py:22
  117.2 1.8 pad_maximum_fusion.near
  125.5 11.1 %attend.1 = bf16[16,128,128]{2,1,0:T(8,128)(2,1)S(1)} custom-call(s32[5]{0:T(128)S(1)} %stack.141.place, s32[4]{0:T(128)S(1)} %copy-done.16, s32[4,2]{1,0:T(4,128)S(1)} %pad_add_fusion.q_edges, s32[4,4]{1,0:T(4,128)S(1)} %copy.58.k_edges, f32[32]{0:T(128)S(1)} %fusion.8.biases, bf16[4,128,128]{2,1,0:T(8,128)(2,1)} %get-tuple-element.63.q0, ...), custom_call_target="tpu_custom_call" | custom-call | flops 1073741824 | bytes 5242880 | tf_op jit(solution)/shard_map/attend/pallas_call | solution.py:286
  137.4 4.8 %all-to-all-start = ((bf16[16,128,128]{2,1,0:T(8,128)(2,1)}), bf16[16,128,128]{2,1,0:T(8,128)(2,1)S(1)}, u32[]{:S(2)}, u32[]{:S(2)}) async-start(bf16[16,128,128]{2,1,0:T(8,128)(2,1)} %copy-done.7), calls=%async_computation | async-start | bytes 1048576 | tf_op jit(solution)/shard_map/all_to_all | solution.py:304
  142.3 3.2 %collective-permute-start.29 = (bf16[128,128]{1,0:T(8,128)(2,1)S(1)}, bf16[128,128]{1,0:T(8,128)(2,1)S(1)}, u32[]{:S(2)}, u32[]{:S(2)}) collective-permute-start(bf16[128,128]{1,0:T(8,128)(2,1)S(1)} %get-tuple-element.87), channel_id=1, source_target_pairs={{0,192},{64,0},{128,64},{192,128},{1,193},{65,1},{129,65},{193,129... | collective-permute-start | bytes 98312 | tf_op jit(solution)/shard_map/ppermute | solution.py:302
  147.2 13.3 %all-to-all-done.parts = bf16[16,128,128]{2,1,0:T(8,128)(2,1)S(1)} async-done(((bf16[16,128,128]{2,1,0:T(8,128)(2,1)}), bf16[16,128,128]{2,1,0:T(8,128)(2,1)S(1)}, u32[]{:S(2)}, u32[]{:S(2)}) %all-to-all-start) | async-done | bytes 524320 | tf_op jit(solution)/shard_map/all_to_all | solution.py:304
  162.9 1.6 collective-permute-start.33
  166.7 2.6 %collective-permute-done.33 = bf16[128,512]{1,0:T(8,128)(2,1)S(1)} collective-permute-done((bf16[128,512]{1,0:T(8,128)(2,1)S(1)}, bf16[128,512]{1,0:T(8,128)(2,1)S(1)}, u32[]{:S(2)}, u32[]{:S(2)}) %collective-permute-start.33) | collective-permute-done | bytes 131104 | tf_op jit(solution)/shard_map/ppermute | solution.py:22
  170.8 3.8 %project_out.1 = bf16[128,1024]{1,0:T(8,128)(2,1)} custom-call(s32[5]{0:T(128)S(1)} %stack.141.place, bf16[128,1024]{1,0:T(8,128)(2,1)S(1)} %copy-done.2, bf16[4,128,512]{2,1,0:T(8,128)(2,1)S(1)} %pad_maximum_fusion.4.gated, bf16[4,2,4,64,512]{4,3,2,1,0:T(8,128)(2,1)S(1)} %pad_maximum_fusion.near, bf16[4,2,4,64,512]{4,3,2,1,0:T(8,128)(2,1)} %collective-permute-done.28.far), custom_call_target="tpu_custom_call" | custom-call | flops 536870912 | bytes 5242880 | tf_op jit(solution)/shard_map/project_out/pallas_call | solution.py:319
  (149 shorter events, 37.4 us)
Async XLA Ops:
  6.5 84.0 %all-gather.3.cloned.1.call-start = ((), (), s32[]{:S(2)}) async-start(), calls=%async_computation.1 | async-start | bytes 4456448 | tf_op jit(solution)/shard_map/all_gather | solution.py:229
  18.9 9.2 %collective-permute-start.3 = (bf16[128,512]{1,0:T(8,128)(2,1)S(1)}, bf16[128,512]{1,0:T(8,128)(2,1)S(1)}, u32[]{:S(2)}, u32[]{:S(2)}) collective-permute-start(bf16[128,512]{1,0:T(8,128)(2,1)S(1)} %get-tuple-element.45), channel_id=1, source_target_pairs={{0,1},{1,2},{2,3},{3,0},{4,5},{5,6},{6,7},{7,4},{8,9},{9,10},{10,1... | collective-permute-start | bytes 393224 | tf_op jit(solution)/shard_map/ppermute | solution.py:22
  20.4 9.1 %collective-permute-start.4 = (bf16[128,512]{1,0:T(8,128)(2,1)S(1)}, bf16[128,512]{1,0:T(8,128)(2,1)S(1)}, u32[]{:S(2)}, u32[]{:S(2)}) collective-permute-start(bf16[128,512]{1,0:T(8,128)(2,1)S(1)} %get-tuple-element.45), channel_id=1, source_target_pairs={{0,2},{1,3},{2,0},{3,1},{4,6},{5,7},{6,4},{7,5},{8,10},{9,11},{10,... | collective-permute-start | bytes 393224 | tf_op jit(solution)/shard_map/ppermute | solution.py:22
  24.0 11.7 %collective-permute-start = (bf16[144,512]{1,0:T(8,128)(2,1)S(1)}, bf16[144,512]{1,0:T(8,128)(2,1)S(1)}, u32[]{:S(2)}, u32[]{:S(2)}) collective-permute-start(bf16[144,512]{1,0:T(8,128)(2,1)S(1)} %maximum_maximum_fusion), channel_id=1, source_target_pairs={{0,64},{64,128},{128,192},{192,0},{1,65},{65,129},{129,193},{193,1... | collective-permute-start | bytes 442376 | tf_op jit(solution)/shard_map/ppermute | solution.py:22
  24.1 11.6 %collective-permute-start.1 = (bf16[144,512]{1,0:T(8,128)(2,1)S(1)}, bf16[144,512]{1,0:T(8,128)(2,1)S(1)}, u32[]{:S(2)}, u32[]{:S(2)}) collective-permute-start(bf16[144,512]{1,0:T(8,128)(2,1)S(1)} %maximum_maximum_fusion), channel_id=1, source_target_pairs={{0,128},{64,192},{128,0},{192,64},{1,129},{65,193},{129,1},{193,65... | collective-permute-start | bytes 442376 | tf_op jit(solution)/shard_map/ppermute | solution.py:22
  26.1 9.6 %collective-permute-start.2 = (bf16[144,512]{1,0:T(8,128)(2,1)S(1)}, bf16[144,512]{1,0:T(8,128)(2,1)S(1)}, u32[]{:S(2)}, u32[]{:S(2)}) collective-permute-start(bf16[144,512]{1,0:T(8,128)(2,1)S(1)} %maximum_maximum_fusion), channel_id=1, source_target_pairs={{0,192},{64,0},{128,64},{192,128},{1,193},{65,1},{129,65},{193,129... | collective-permute-start | bytes 442376 | tf_op jit(solution)/shard_map/ppermute | solution.py:22
  28.1 7.6 %collective-permute-start.5 = (bf16[128,512]{1,0:T(8,128)(2,1)S(1)}, bf16[128,512]{1,0:T(8,128)(2,1)S(1)}, u32[]{:S(2)}, u32[]{:S(2)}) collective-permute-start(bf16[128,512]{1,0:T(8,128)(2,1)S(1)} %get-tuple-element.45), channel_id=1, source_target_pairs={{0,3},{1,0},{2,1},{3,2},{4,7},{5,4},{6,5},{7,6},{8,11},{9,8},{10,9... | collective-permute-start | bytes 393224 | tf_op jit(solution)/shard_map/ppermute | solution.py:22
  30.3 19.8 %collective-permute-start.20 = (bf16[64,512]{1,0:T(8,128)(2,1)S(1)}, bf16[64,512]{1,0:T(8,128)(2,1)S(1)}, u32[]{:S(2)}, u32[]{:S(2)}) collective-permute-start(bf16[64,512]{1,0:T(8,128)(2,1)S(1)} %collective-permute-done.17), channel_id=1, source_target_pairs={{0,12},{4,0},{8,4},{12,8},{1,13},{5,1},{9,5},{13,9},{2,14},{6,2},{... | collective-permute-start | bytes 196616 | tf_op jit(solution)/shard_map/ppermute | solution.py:22
  36.5 32.5 %collective-permute-start.6 = (bf16[512,512]{1,0:T(8,128)(2,1)S(1)}, bf16[512,512]{1,0:T(8,128)(2,1)S(1)}, u32[]{:S(2)}, u32[]{:S(2)}) collective-permute-start(bf16[512,512]{1,0:T(8,128)(2,1)S(1)} %pad_maximum_fusion.2.a0), channel_id=1, source_target_pairs={{0,1},{1,2},{2,3},{3,0},{4,5},{5,6},{6,7},{7,4},{8,9},{9,10},{10,1... | collective-permute-start | bytes 1572872 | tf_op jit(solution)/shard_map/ppermute | solution.py:22
  43.8 26.8 %collective-permute-start.7 = (bf16[512,512]{1,0:T(8,128)(2,1)S(1)}, bf16[512,512]{1,0:T(8,128)(2,1)S(1)}, u32[]{:S(2)}, u32[]{:S(2)}) collective-permute-start(bf16[512,512]{1,0:T(8,128)(2,1)S(1)} %pad_maximum_fusion.2.a0), channel_id=1, source_target_pairs={{0,2},{1,3},{2,0},{3,1},{4,6},{5,7},{6,4},{7,5},{8,10},{9,11},{10,... | collective-permute-start | bytes 1572872 | tf_op jit(solution)/shard_map/ppermute | solution.py:22
  47.5 23.2 %collective-permute-start.9 = (bf16[512,512]{1,0:T(8,128)(2,1)S(1)}, bf16[512,512]{1,0:T(8,128)(2,1)S(1)}, u32[]{:S(2)}, u32[]{:S(2)}) collective-permute-start(bf16[512,512]{1,0:T(8,128)(2,1)S(1)} %constant_dynamic-update-slice_fusion.b0), channel_id=1, source_target_pairs={{0,64},{64,128},{128,192},{192,0},{1,65},{65,129},{129,193},{193,1... | collective-permute-start | bytes 1572872 | tf_op jit(solution)/shard_map/ppermute | solution.py:22
  47.7 22.9 %collective-permute-start.10 = (bf16[512,512]{1,0:T(8,128)(2,1)S(1)}, bf16[512,512]{1,0:T(8,128)(2,1)S(1)}, u32[]{:S(2)}, u32[]{:S(2)}) collective-permute-start(bf16[512,512]{1,0:T(8,128)(2,1)S(1)} %constant_dynamic-update-slice_fusion.b0), channel_id=1, source_target_pairs={{0,128},{64,192},{128,0},{192,64},{1,129},{65,193},{129,1},{193,65... | collective-permute-start | bytes 1572872 | tf_op jit(solution)/shard_map/ppermute | solution.py:22
  50.0 9.5 %collective-permute-start.19 = (bf16[64,512]{1,0:T(8,128)(2,1)S(1)}, bf16[64,512]{1,0:T(8,128)(2,1)S(1)}, u32[]{:S(2)}, u32[]{:S(2)}) collective-permute-start(bf16[64,512]{1,0:T(8,128)(2,1)S(1)} %collective-permute-done.17), channel_id=1, source_target_pairs={{0,8},{4,12},{8,0},{12,4},{1,9},{5,13},{9,1},{13,5},{2,10},{6,14},... | collective-permute-start | bytes 196616 | tf_op jit(solution)/shard_map/ppermute | solution.py:22
  59.6 6.4 %collective-permute-start.18 = (bf16[64,512]{1,0:T(8,128)(2,1)S(1)}, bf16[64,512]{1,0:T(8,128)(2,1)S(1)}, u32[]{:S(2)}, u32[]{:S(2)}) collective-permute-start(bf16[64,512]{1,0:T(8,128)(2,1)S(1)} %collective-permute-done.17), channel_id=1, source_target_pairs={{0,4},{4,8},{8,12},{12,0},{1,5},{5,9},{9,13},{13,1},{2,6},{6,10},{... | collective-permute-start | bytes 196616 | tf_op jit(solution)/shard_map/ppermute | solution.py:22
  65.9 14.1 %collective-permute-start.8 = (bf16[512,512]{1,0:T(8,128)(2,1)S(1)}, bf16[512,512]{1,0:T(8,128)(2,1)S(1)}, u32[]{:S(2)}, u32[]{:S(2)}) collective-permute-start(bf16[512,512]{1,0:T(8,128)(2,1)S(1)} %pad_maximum_fusion.2.a0), channel_id=1, source_target_pairs={{0,3},{1,0},{2,1},{3,2},{4,7},{5,4},{6,5},{7,6},{8,11},{9,8},{10,9... | collective-permute-start | bytes 1572872 | tf_op jit(solution)/shard_map/ppermute | solution.py:22
  69.1 14.3 %collective-permute-start.11 = (bf16[512,512]{1,0:T(8,128)(2,1)S(1)}, bf16[512,512]{1,0:T(8,128)(2,1)S(1)}, u32[]{:S(2)}, u32[]{:S(2)}) collective-permute-start(bf16[512,512]{1,0:T(8,128)(2,1)S(1)} %constant_dynamic-update-slice_fusion.b0), channel_id=1, source_target_pairs={{0,192},{64,0},{128,64},{192,128},{1,193},{65,1},{129,65},{193,129... | collective-permute-start | bytes 1572872 | tf_op jit(solution)/shard_map/ppermute | solution.py:22
  70.7 8.4 %collective-permute-start.21 = (bf16[4,64,512]{2,1,0:T(8,128)(2,1)S(1)}, bf16[4,64,512]{2,1,0:T(8,128)(2,1)S(1)}, u32[]{:S(2)}, u32[]{:S(2)}) collective-permute-start(bf16[4,64,512]{2,1,0:T(8,128)(2,1)S(1)} %pad_maximum_fusion.6), channel_id=1, source_target_pairs={{0,32},{32,0},{1,33},{33,1},{2,34},{34,2},{3,35},{35,3},{4,36},{36... | collective-permute-start | bytes 786440 | tf_op jit(solution)/shard_map/ppermute | solution.py:28
  79.9 24.0 %collective-permute-start.22 = (bf16[2,4,64,512]{3,2,1,0:T(8,128)(2,1)}, bf16[2,4,64,512]{3,2,1,0:T(8,128)(2,1)}, u32[]{:S(2)}, u32[]{:S(2)}) collective-permute-start(bf16[2,4,64,512]{3,2,1,0:T(8,128)(2,1)} %pad_maximum_fusion.3), channel_id=1, source_target_pairs={{0,64},{64,128},{128,192},{192,0},{1,65},{65,129},{129,193},{193,1... | collective-permute-start | bytes 1572872 | tf_op jit(solution)/shard_map/ppermute | solution.py:22
  84.2 25.3 %collective-permute-start.23 = (bf16[2,4,64,512]{3,2,1,0:T(8,128)(2,1)}, bf16[2,4,64,512]{3,2,1,0:T(8,128)(2,1)}, u32[]{:S(2)}, u32[]{:S(2)}) collective-permute-start(bf16[2,4,64,512]{3,2,1,0:T(8,128)(2,1)} %pad_maximum_fusion.3), channel_id=1, source_target_pairs={{0,128},{64,192},{128,0},{192,64},{1,129},{65,193},{129,1},{193,65... | collective-permute-start | bytes 1572872 | tf_op jit(solution)/shard_map/ppermute | solution.py:22
  87.4 22.1 %collective-permute-start.24 = (bf16[2,4,64,512]{3,2,1,0:T(8,128)(2,1)}, bf16[2,4,64,512]{3,2,1,0:T(8,128)(2,1)}, u32[]{:S(2)}, u32[]{:S(2)}) collective-permute-start(bf16[2,4,64,512]{3,2,1,0:T(8,128)(2,1)} %pad_maximum_fusion.3), channel_id=1, source_target_pairs={{0,192},{64,0},{128,64},{192,128},{1,193},{65,1},{129,65},{193,129... | collective-permute-start | bytes 1572872 | tf_op jit(solution)/shard_map/ppermute | solution.py:22
  99.0 9.6 %collective-permute-start.15 = (bf16[4,144,256]{2,1,0:T(8,128)(2,1)S(1)}, bf16[4,144,256]{2,1,0:T(8,128)(2,1)S(1)}, u32[]{:S(2)}, u32[]{:S(2)}) collective-permute-start(bf16[4,144,256]{2,1,0:T(8,128)(2,1)S(1)} %get-tuple-element.59), channel_id=1, source_target_pairs={{0,32},{32,0},{1,33},{33,1},{2,34},{34,2},{3,35},{35,3},{4,36},{36... | collective-permute-start | bytes 884744 | tf_op jit(solution)/shard_map/ppermute | solution.py:28
  103.9 11.1 %collective-permute-start.25 = (bf16[4,128,128]{2,1,0:T(8,128)(2,1)}, bf16[4,128,128]{2,1,0:T(8,128)(2,1)S(1)}, u32[]{:S(2)}, u32[]{:S(2)}) collective-permute-start(bf16[4,128,128]{2,1,0:T(8,128)(2,1)} %get-tuple-element.63.q0), channel_id=1, source_target_pairs={{0,4},{4,8},{8,12},{12,0},{1,5},{5,9},{9,13},{13,1},{2,6},{6,10},{... | collective-permute-start | bytes 393224 | tf_op jit(solution)/shard_map/ppermute | solution.py:22
  103.9 11.7 %collective-permute-start.26 = (bf16[4,128,128]{2,1,0:T(8,128)(2,1)}, bf16[4,128,128]{2,1,0:T(8,128)(2,1)S(1)}, u32[]{:S(2)}, u32[]{:S(2)}) collective-permute-start(bf16[4,128,128]{2,1,0:T(8,128)(2,1)} %get-tuple-element.63.q0), channel_id=1, source_target_pairs={{0,8},{4,12},{8,0},{12,4},{1,9},{5,13},{9,1},{13,5},{2,10},{6,14},... | collective-permute-start | bytes 393224 | tf_op jit(solution)/shard_map/ppermute | solution.py:22
  108.6 8.0 %collective-permute-start.27 = (bf16[4,128,128]{2,1,0:T(8,128)(2,1)}, bf16[4,128,128]{2,1,0:T(8,128)(2,1)S(1)}, u32[]{:S(2)}, u32[]{:S(2)}) collective-permute-start(bf16[4,128,128]{2,1,0:T(8,128)(2,1)} %get-tuple-element.63.q0), channel_id=1, source_target_pairs={{0,12},{4,0},{8,4},{12,8},{1,13},{5,1},{9,5},{13,9},{2,14},{6,2},{... | collective-permute-start | bytes 393224 | tf_op jit(solution)/shard_map/ppermute | solution.py:22
  109.5 12.1 %collective-permute-start.16 = (bf16[2,4,144,256]{3,2,1,0:T(8,128)(2,1)}, bf16[2,4,144,256]{3,2,1,0:T(8,128)(2,1)}, u32[]{:S(2)}, u32[]{:S(2)}) collective-permute-start(bf16[2,4,144,256]{3,2,1,0:T(8,128)(2,1)} %pad_maximum_fusion.1.kv_near), channel_id=1, source_target_pairs={{0,16},{16,0},{1,17},{17,1},{2,18},{18,2},{3,19},{19,3},{4,20},{20... | collective-permute-start | bytes 1769480 | tf_op jit(solution)/shard_map/ppermute | solution.py:28
  119.0 41.5 %collective-permute-start.28 = (bf16[4,2,4,64,512]{4,3,2,1,0:T(8,128)(2,1)S(1)}, bf16[4,2,4,64,512]{4,3,2,1,0:T(8,128)(2,1)}, u32[]{:S(2)}, u32[]{:S(2)}) collective-permute-start(bf16[4,2,4,64,512]{4,3,2,1,0:T(8,128)(2,1)S(1)} %pad_maximum_fusion.near), channel_id=1, source_target_pairs={{0,16},{16,0},{1,17},{17,1},{2,18},{18,2},{3,19},{19,3},{4,20},{20... | collective-permute-start | bytes 6291464 | tf_op jit(solution)/shard_map/ppermute | solution.py:28
  137.4 23.1 %all-to-all-start = ((bf16[16,128,128]{2,1,0:T(8,128)(2,1)}), bf16[16,128,128]{2,1,0:T(8,128)(2,1)S(1)}, u32[]{:S(2)}, u32[]{:S(2)}) async-start(bf16[16,128,128]{2,1,0:T(8,128)(2,1)} %copy-done.7), calls=%async_computation | async-start | bytes 1048576 | tf_op jit(solution)/shard_map/all_to_all | solution.py:304
  142.3 18.3 %collective-permute-start.29 = (bf16[128,128]{1,0:T(8,128)(2,1)S(1)}, bf16[128,128]{1,0:T(8,128)(2,1)S(1)}, u32[]{:S(2)}, u32[]{:S(2)}) collective-permute-start(bf16[128,128]{1,0:T(8,128)(2,1)S(1)} %get-tuple-element.87), channel_id=1, source_target_pairs={{0,192},{64,0},{128,64},{192,128},{1,193},{65,1},{129,65},{193,129... | collective-permute-start | bytes 98312 | tf_op jit(solution)/shard_map/ppermute | solution.py:302
  145.5 15.1 %collective-permute-start.30 = (bf16[128,128]{1,0:T(8,128)(2,1)S(1)}, bf16[128,128]{1,0:T(8,128)(2,1)S(1)}, u32[]{:S(2)}, u32[]{:S(2)}) collective-permute-start(bf16[128,128]{1,0:T(8,128)(2,1)S(1)} %get-tuple-element.86), channel_id=1, source_target_pairs={{0,128},{64,192},{128,0},{192,64},{1,129},{65,193},{129,1},{193,65... | collective-permute-start | bytes 98312 | tf_op jit(solution)/shard_map/ppermute | solution.py:302
  146.3 14.2 %collective-permute-start.31 = (bf16[128,128]{1,0:T(8,128)(2,1)S(1)}, bf16[128,128]{1,0:T(8,128)(2,1)S(1)}, u32[]{:S(2)}, u32[]{:S(2)}) collective-permute-start(bf16[128,128]{1,0:T(8,128)(2,1)S(1)} %get-tuple-element.85), channel_id=1, source_target_pairs={{0,64},{64,128},{128,192},{192,0},{1,65},{65,129},{129,193},{193,1... | collective-permute-start | bytes 98312 | tf_op jit(solution)/shard_map/ppermute | solution.py:302
  162.9 6.5 %collective-permute-start.33 = (bf16[128,512]{1,0:T(8,128)(2,1)S(1)}, bf16[128,512]{1,0:T(8,128)(2,1)S(1)}, u32[]{:S(2)}, u32[]{:S(2)}) collective-permute-start(bf16[128,512]{1,0:T(8,128)(2,1)S(1)} %gate.1), channel_id=1, source_target_pairs={{0,2},{1,3},{2,0},{3,1},{4,6},{5,7},{6,4},{7,5},{8,10},{9,11},{10,... | collective-permute-start | bytes 393224 | tf_op jit(solution)/shard_map/ppermute | solution.py:22
  164.4 6.3 %collective-permute-start.32 = (bf16[128,512]{1,0:T(8,128)(2,1)S(1)}, bf16[128,512]{1,0:T(8,128)(2,1)S(1)}, u32[]{:S(2)}, u32[]{:S(2)}) collective-permute-start(bf16[128,512]{1,0:T(8,128)(2,1)S(1)} %gate.1), channel_id=1, source_target_pairs={{0,1},{1,2},{2,3},{3,0},{4,5},{5,6},{6,7},{7,4},{8,9},{9,10},{10,1... | collective-permute-start | bytes 393224 | tf_op jit(solution)/shard_map/ppermute | solution.py:22
  (28 other events, 268.4 us)
Sparse Core Ops, SparseCore 0:
  18.0 45.5 all-gather.2

commit v6 on v4

--- a/solution.py
+++ b/solution.py
@@ -29,29 +29,34 @@
 
 
 def project_kernel(place, a0, a1, a2, a3, b0, b1, b2, b3, weights, kv_ref, q_ref, u_ref, total):
-    y, x = place[0], place[4]
+    step = pl.program_id(0)
     seconds = (b0, b1, b2, b3)
     for kx, first in enumerate((a0, a1, a2, a3)):
-        ky = (y - (x - kx)) & 3
-        second = jnp.concatenate([b[kx * RUN : (kx + 1) * RUN, :] for b in seconds], axis=0)
-        for m in range(4):
-            left = first[...] if m < 2 else second
-            right = jnp.concatenate([weights[j * 4 + m, ky] for j in range(4)], axis=0)
-            part = jnp.dot(
-                left[:, (m & 1) * 256 : (m & 1) * 256 + 256], right, preferred_element_type=jnp.float32
-            )
-            if kx == 0 and m == 0:
-                total[...] = part
-            else:
-                total[...] += part
-    half = 0.5 * total[...]
-    act = (half + half * jnp.tanh(half)).astype(jnp.bfloat16)
-    for r in range(4):
-        rows = slice(r * RUN, (r + 1) * RUN)
-        u_ref[r] = act[rows, :DH]
-        kv_ref[r, :, :DH] = act[rows, DH : 2 * DH]
-        q_ref[r] = act[rows, 2 * DH : 3 * DH]
-        kv_ref[r, :, DH:] = act[rows, 3 * DH :]
+
+        @pl.when(step == kx)
+        def _():
+            second = jnp.concatenate([b[kx * RUN : (kx + 1) * RUN, :] for b in seconds], axis=0)
+            for m in range(4):
+                left = first[...] if m < 2 else second
+                right = jnp.concatenate([weights[j * 4 + m, 0, :64, :] for j in range(4)], axis=0)
+                part = jnp.dot(
+                    left[:, (m & 1) * 256 : (m & 1) * 256 + 256], right, preferred_element_type=jnp.float32
+                )
+                if kx == 0 and m == 0:
+                    total[...] = part
+                else:
+                    total[...] += part
+
+    @pl.when(step == 3)
+    def _():
+        half = 0.5 * total[...]
+        act = (half + half * jnp.tanh(half)).astype(jnp.bfloat16)
+        for r in range(4):
+            rows = slice(r * RUN, (r + 1) * RUN)
+            u_ref[r] = act[rows, :DH]
+            kv_ref[r, :, :DH] = act[rows, DH : 2 * DH]
+            q_ref[r] = act[rows, 2 * DH : 3 * DH]
+            kv_ref[r, :, DH:] = act[rows, 3 * DH :]
 
 
 def attend_kernel(
@@ -106,8 +111,8 @@
             values = jnp.concatenate([near[:, :DH], far[:, :DH]], axis=0)
             k_first = t * 1024 + zh * RUN
             k_last = k_first + BLOCK + RUN - 1
-            gap_low = jnp.clip(q_low - k_edges[ky, zx * 2 + 1], 0, NB - 1)
-            gap_high = jnp.clip(q_high - k_edges[ky, zx * 2], 0, NB - 1)
+            gap_low = jnp.clip(q_low - k_edges[ky, zl_from * 2 + 1], 0, NB - 1)
+            gap_high = jnp.clip(q_high - k_edges[ky, zl_from * 2], 0, NB - 1)
             plain = (k_last <= first) & (k_first >= start_high) & (gap_low == gap_high)
 
             def scores(part):
@@ -130,7 +135,7 @@
 
             @pl.when(jnp.logical_not(plain))
             def _():
-                k_row = k_ids[ky, pl.ds(zx, 1), :]
+                k_row = k_ids[ky, pl.ds(zl_from, 1), :]
                 column = lax.broadcasted_iota(jnp.int32, (1, PAIR), 1)
                 k_pos = k_first + ((column >> 7) ^ core) * BLOCK + (column & (RUN - 1))
                 for part in range(2):
@@ -183,16 +188,14 @@
 
 def output_kernel(place, tokens, gated, weights, out_ref):
     y, x = place[0], place[4]
-    for m in range(4):
-        columns = slice(m * 256, (m + 1) * 256)
-        total = tokens[:, columns].astype(jnp.float32)
-        for ky in range(4):
-            left = gated[(x - (y - ky)) & 3]
-            right = jnp.concatenate([weights[j * 4 + m, ky] for j in range(4)], axis=0)
-            total += lax.dot_general(
-                left, right, (((1,), (1,)), ((), ())), preferred_element_type=jnp.float32
-            )
-        out_ref[:, columns] = total.astype(jnp.bfloat16)
+    total = tokens[...].astype(jnp.float32)
+    for ky in range(4):
+        left = gated[(x - (y - ky)) & 3]
+        right = jnp.concatenate([weights[j, 0, ky] for j in range(4)], axis=0)
+        total += lax.dot_general(
+            left, right, (((1,), (1,)), ((), ())), preferred_element_type=jnp.float32
+        )
+    out_ref[...] = total.astype(jnp.bfloat16)
 
 
 def call(kernel, shapes, n_smem, n_vmem, scratch, flops, moved, vmem, name):
@@ -215,8 +218,12 @@
     place = jnp.stack([y, zl, core, zh, x]).astype(jnp.int32)
     plane = ("zh", "zl", "core")
 
+    ids = jnp.stack([bucket_ids // 128, bucket_ids % 128]).astype(bf16)
+    ids = jnp.concatenate([ids, jnp.zeros((14, BLOCK), bf16)], axis=0)
+
     def columns(owner):
-        return lax.dynamic_slice_in_dim(w_uvqk, owner * 512, 512, 1)
+        part = lax.dynamic_slice_in_dim(w_uvqk, owner * 512, 512, 1)
+        return jnp.concatenate([part, ids], axis=0)
 
     pieces = [columns(y)] + [
         lax.ppermute(columns((y + k) & 3), "y", [(i, (i + k) % 4) for i in range(4)])
@@ -231,45 +238,47 @@
     firsts = rotations(jnp.concatenate(first, axis=0), "x", 4)
     seconds = rotations(jnp.concatenate(second, axis=0), "y", 4)
 
-    ids, late, _ = lax.optimization_barrier((bucket_ids, w_out.T, (firsts[1:3], seconds[1:3])))
-    ids_y = jnp.stack(rotations(ids, "y", 4))
-    ids_near = jnp.stack([ids_y, swap(ids_y, "zl")])
-    ids_far = swap(ids_near, "core")
+    late, _ = lax.optimization_barrier((w_out.T, piece))
     swapped = lax.ppermute(late, ("y", "x"), [(b * 4 + a, a * 4 + b) for a in range(4) for b in range(4)])
-    wo_rows = jnp.stack(rotations(swapped, "y", 4))
-
-    firsts, seconds, ids_y, ids_near, ids_far, wo_rows = lax.optimization_barrier(
-        (firsts, seconds, ids_y, ids_near, ids_far, wo_rows)
-    )
-    kv, q, u = call(
+    swapped, firsts, seconds = lax.optimization_barrier((swapped, firsts, seconds))
+    wo_rows = rotations(swapped, "y", 4)
+
+    whole = pl.BlockSpec(memory_space=pltpu.VMEM)
+    small = jax.ShapeDtypeStruct((4, RUN, DH), bf16)
+    kv, q, u = pl.pallas_call(
         project_kernel,
-        [
-            jax.ShapeDtypeStruct((4, RUN, 2 * DH), bf16),
-            jax.ShapeDtypeStruct((4, RUN, DH), bf16),
-            jax.ShapeDtypeStruct((4, RUN, DH), bf16),
-        ],
-        1,
-        9,
-        [pltpu.VMEM((512, 512), f32)],
-        2 * 512 * 512 * 4096,
-        9 * 2**20,
-        24,
-        "project",
+        out_shape=[jax.ShapeDtypeStruct((4, RUN, 2 * DH), bf16), small, small],
+        grid_spec=pltpu.PrefetchScalarGridSpec(
+            num_scalar_prefetch=1,
+            grid=(4,),
+            in_specs=[whole] * 8
+            + [pl.BlockSpec((16, 1, 80, 512), lambda i, p: (0, (p[0] - (p[4] - i)) & 3, 0, 0))],
+            out_specs=[whole] * 3,
+            scratch_shapes=[pltpu.VMEM((512, 512), f32)],
+        ),
+        compiler_params=pltpu.CompilerParams(vmem_limit_bytes=20 * 2**20),
+        cost_estimate=pl.CostEstimate(
+            flops=2 * 512 * 512 * 4096, bytes_accessed=9 * 2**20, transcendentals=0
+        ),
+        name="project",
     )(place, *firsts, *seconds, weights)
 
     wo_rows, _ = lax.optimization_barrier((wo_rows, kv))
-    wo_all = lax.all_gather(wo_rows, plane)
-
-    kv_near = jnp.stack([kv, swap(kv, "zl")])
+    wo_all = lax.all_gather(jnp.stack(wo_rows), plane)
+
+    q_all = rotations(q, "zh", 4)
+    from_zl, q_all[1] = lax.optimization_barrier((swap(kv, "zl"), q_all[1]))
+    kv_near = jnp.stack([kv, from_zl])
     kv_far = swap(kv_near, "core")
-    q_all = rotations(q, "zh", 4)
-
-    q_ids = ids_y.reshape(4, BLOCK, 1)
-    k_ids = lax.dynamic_slice(jnp.stack([ids_near, ids_far]), (0, 0, 0, zh * RUN), (2, 2, 4, RUN))
-    k_edges = jnp.stack([jnp.min(k_ids[..., 0], axis=0), jnp.max(k_ids[..., -1], axis=0)], axis=-1)
-    k_edges = k_edges.transpose(1, 0, 2).reshape(4, 4)
-    k_ids = k_ids.transpose(2, 1, 0, 3).reshape(4, 2, PAIR)
-    q_edges = jnp.stack([ids_y[:, 0], ids_y[:, -1]], axis=1)
+
+    coded = weights[:4, :, 64:66].astype(f32)
+    all_ids = (coded[:, :, 0] * 128 + coded[:, :, 1]).astype(jnp.int32).transpose(1, 0, 2)
+    q_ids = lax.dynamic_slice(all_ids, (0, zl * 2 + core, 0), (4, 1, BLOCK)).reshape(4, BLOCK, 1)
+    q_edges = jnp.concatenate([q_ids[:, 0], q_ids[:, -1]], axis=1)
+    k_ids = lax.dynamic_slice(all_ids, (0, 0, zh * RUN), (4, 4, RUN))
+    k_edges = jnp.stack([k_ids[:, ::2, 0], k_ids[:, 1::2, -1]], axis=-1).reshape(4, 4)
+    k_ids = k_ids.reshape(4, 2, 2, RUN)
+    k_ids = jnp.where(core == 0, k_ids, k_ids[:, :, ::-1]).reshape(4, 2, PAIR)
     biases = lax.dynamic_slice(rab_table, (x * 4 + y, 0), (1, NB))
     gains = lax.dynamic_slice(norm_gain, (x * 4, 0), (4, DH))
     table = jnp.pad(biases, ((0, 0), (0, DH - NB)))
@@ -291,6 +300,7 @@
         lax.ppermute(u[k], "y", [(i, (i - k) % 4) for i in range(4)]) for k in range(1, 4)
     ]
     arrived = lax.all_to_all(parts, ("y", "zh"), 0, 0, tiled=True)
+    arrived, wo_all = lax.optimization_barrier((arrived, wo_all))
     gated = call(
         gate_kernel,
         jax.ShapeDtypeStruct((RUN, 4 * DH), bf16),
@@ -304,17 +314,25 @@
     )(place, arrived, *u_own, gains)
     heads = jnp.stack(rotations(gated, "x", 4))
 
-    return call(
+    return pl.pallas_call(
         output_kernel,
-        jax.ShapeDtypeStruct((RUN, 1024), bf16),
-        1,
-        3,
-        [],
-        2 * RUN * 2048 * 1024,
-        5 * 2**20,
-        14,
-        "project_out",
-    )(place, tokens, heads, wo_all)
+        out_shape=jax.ShapeDtypeStruct((RUN, 1024), bf16),
+        grid_spec=pltpu.PrefetchScalarGridSpec(
+            num_scalar_prefetch=1,
+            grid=(4,),
+            in_specs=[
+                pl.BlockSpec((RUN, 256), lambda i, p: (0, i)),
+                whole,
+                pl.BlockSpec((4, 1, 4, 64, 512), lambda i, p: (0, i, 0, 0, 0)),
+            ],
+            out_specs=pl.BlockSpec((RUN, 256), lambda i, p: (0, i)),
+        ),
+        compiler_params=pltpu.CompilerParams(vmem_limit_bytes=14 * 2**20),
+        cost_estimate=pl.CostEstimate(
+            flops=2 * RUN * 2048 * 1024, bytes_accessed=5 * 2**20, transcendentals=0
+        ),
+        name="project_out",
+    )(place, tokens, heads, wo_all.reshape(4, 4, 4, 64, 512))
 
 
 def solution(mesh):

time: 180 us -> 173 us (0.961)
  waiting for transfers between devices: 55.8 us -> 46.5 us
  starting transfers between devices: 75.6 us -> 80.1 us
    ppermute x24 -> x21, waiting for transfers between devices: 36.8 us -> 31.3 us  [rotations(): lax.ppermute(value, axis, [(i, (i + step * k) % size) for i in range(size)])]
    ppermute x3, waiting for transfers between devices: 5.04 us -> 0.01 us  [on_device(): lax.ppermute(u[k], 'y', [(i, (i - k) % 4) for i in range(4)])]
    ppermute x4 -> x2, waiting for transfers between devices: 4.99 us -> 0.01 us  [swap(): return lax.ppermute(value, axis, [(0, 1), (1, 0)])]
    all_to_all x1, waiting for transfers between devices: 6.01 us -> 9.65 us  [on_device(): arrived = lax.all_to_all(parts, ('y', 'zh'), 0, 0, tiled=True)]
    all_to_all x1, starting transfers between devices: 8.94 us -> 12.1 us  [on_device(): arrived = lax.all_to_all(parts, ('y', 'zh'), 0, 0, tiled=True)]
    ppermute x3, waiting for transfers between devices: 2.92 us -> 5.56 us  [on_device(): lax.ppermute(columns(y + k & 3), 'y', [(i, (i + k) % 4) for i in range(4)])]
    pallas_call x2, Pallas kernels: 6.32 us -> 8.6 us  [the longest x1 5.09 us: on_device(): pl.pallas_call(project_kernel, out_shape=[jax.ShapeDtypeStruct((4, RUN, 2...]
    pallas_call x1, Pallas kernels: 10.8 us -> 8.54 us  [on_device(): call(attend_kernel, jax.ShapeDtypeStruct((16, RUN, DH), bf16), 5, 9, [plt...]
  transfers between devices with their start and end apart: 38 -> 33, of which waited for: 21 -> 14; matrix products, arithmetic and copies ran while one was open for 4% -> 3% of each run, Pallas kernels for 6% -> 8%
where the time goes in v6:
time: 173 us
  starting transfers between devices  80.1 us (46%)
  waiting for transfers between devices  46.5 us (27%)
  Pallas kernels  17.9 us (10%)
  between operations  13.7 us (8%)
  local copies, waits for them, and re-layouts  10.6 us (6%)
  other arithmetic  4.58 us (3%)
    ppermute x21, starting transfers between devices, rotations(): lax.ppermute(value, axis, [(i, (i + step * k) % size) for i in range(size)])  56 us
    ppermute x21, waiting for transfers between devices, rotations(): lax.ppermute(value, axis, [(i, (i + step * k) % size) for i in range(size)])  31.3 us
    all_to_all x1, starting transfers between devices, on_device(): arrived = lax.all_to_all(parts, ('y', 'zh'), 0, 0, tiled=True)  12.1 us
    all_to_all x1, waiting for transfers between devices, on_device(): arrived = lax.all_to_all(parts, ('y', 'zh'), 0, 0, tiled=True)  9.65 us
    pallas_call x1, Pallas kernels, on_device(): call(attend_kernel, jax.ShapeDtypeStruct((16, RUN, DH), bf16), 5, 9, [plt...  8.54 us
    unnamed x21, local copies, waits for them, and re-layouts  6.3 us
    ppermute x3, waiting for transfers between devices, on_device(): lax.ppermute(columns(y + k & 3), 'y', [(i, (i + k) % 4) for i in range(4)])  5.56 us
    pallas_call x1, Pallas kernels, on_device(): pl.pallas_call(project_kernel, out_shape=[jax.ShapeDtypeStruct((4, RUN, 2...  5.09 us
  transfers between devices with their start and end apart: 33, of which 14 were waited for; matrix products, arithmetic and copies ran while one was open for 3% of the time, Pallas kernels for 8%

profile of v6, /device:TPU:32, one launch (start us, length us, event | category | flops | bytes accessed | tf_op | source)
XLA Modules:
  0.0 173.5 jit_solution(2461577358500881605)
XLA Ops:
  8.4 3.1 %collective-permute-start.2 = (bf16[80,512]{1,0:T(8,128)(2,1)S(1)}, bf16[80,512]{1,0:T(8,128)(2,1)S(1)}, u32[]{:S(2)}, u32[]{:S(2)}) collective-permute-start(bf16[80,512]{1,0:T(8,128)(2,1)S(1)} %get-tuple-element.82), channel_id=1, source_target_pairs={{0,192},{64,0},{128,64},{192,128},{1,193},{65,1},{129,65},{193,129... | collective-permute-start | bytes 245768 | tf_op jit(solution)/shard_map/ppermute | solution.py:229
  13.1 1.9 %collective-permute-done.2 = bf16[80,512]{1,0:T(8,128)(2,1)S(1)} collective-permute-done((bf16[80,512]{1,0:T(8,128)(2,1)S(1)}, bf16[80,512]{1,0:T(8,128)(2,1)S(1)}, u32[]{:S(2)}, u32[]{:S(2)}) %collective-permute-start.2) | collective-permute-done | bytes 81952 | tf_op jit(solution)/shard_map/ppermute | solution.py:229
  15.0 2.9 %collective-permute-done.1 = bf16[80,512]{1,0:T(8,128)(2,1)S(1)} collective-permute-done((bf16[80,512]{1,0:T(8,128)(2,1)S(1)}, bf16[80,512]{1,0:T(8,128)(2,1)S(1)}, u32[]{:S(2)}, u32[]{:S(2)}) %collective-permute-start.1) | collective-permute-done | bytes 81952 | tf_op jit(solution)/shard_map/ppermute | solution.py:229
  20.6 2.0 %collective-permute-start.5 = (bf16[128,512]{1,0:T(8,128)(2,1)S(1)}, bf16[128,512]{1,0:T(8,128)(2,1)S(1)}, u32[]{:S(2)}, u32[]{:S(2)}) collective-permute-start(bf16[128,512]{1,0:T(8,128)(2,1)S(1)} %get-tuple-element.36), channel_id=1, source_target_pairs={{0,128},{64,192},{128,0},{192,64},{1,129},{65,193},{129,1},{193,65... | collective-permute-start | bytes 393224 | tf_op jit(solution)/shard_map/ppermute | solution.py:22
  25.6 2.7 %collective-permute-start.8 = (bf16[128,512]{1,0:T(8,128)(2,1)S(1)}, bf16[128,512]{1,0:T(8,128)(2,1)S(1)}, u32[]{:S(2)}, u32[]{:S(2)}) collective-permute-start(bf16[128,512]{1,0:T(8,128)(2,1)S(1)} %get-tuple-element.40), channel_id=1, source_target_pairs={{0,2},{1,3},{2,0},{3,1},{4,6},{5,7},{6,4},{7,5},{8,10},{9,11},{10,... | collective-permute-start | bytes 393224 | tf_op jit(solution)/shard_map/ppermute | solution.py:22
  29.4 2.8 %collective-permute-start.9 = (bf16[128,512]{1,0:T(8,128)(2,1)S(1)}, bf16[128,512]{1,0:T(8,128)(2,1)S(1)}, u32[]{:S(2)}, u32[]{:S(2)}) collective-permute-start(bf16[128,512]{1,0:T(8,128)(2,1)S(1)} %get-tuple-element.40), channel_id=1, source_target_pairs={{0,3},{1,0},{2,1},{3,2},{4,7},{5,4},{6,5},{7,6},{8,11},{9,8},{10,9... | collective-permute-start | bytes 393224 | tf_op jit(solution)/shard_map/ppermute | solution.py:22
  33.0 1.6 collective-permute-done.9
  34.7 1.5 collective-permute-start.10
  36.2 2.1 %collective-permute-start.3 = (bf16[64,512]{1,0:T(8,128)(2,1)}, bf16[64,512]{1,0:T(8,128)(2,1)}, u32[]{:S(2)}, u32[]{:S(2)}) collective-permute-start(bf16[64,512]{1,0:T(8,128)(2,1)} %bitcast.65), channel_id=1, source_target_pairs={{0,0},{64,1},{128,2},{192,3},{1,64},{65,65},{129,66},{193,67},{2,1... | collective-permute-start | bytes 196616 | tf_op jit(solution)/shard_map/ppermute | solution.py:242
  38.4 4.0 %collective-permute-start.11 = (bf16[512,512]{1,0:T(8,128)(2,1)S(1)}, bf16[512,512]{1,0:T(8,128)(2,1)S(1)}, u32[]{:S(2)}, u32[]{:S(2)}) collective-permute-start(bf16[512,512]{1,0:T(8,128)(2,1)S(1)} %constant_dynamic-update-slice_fusion.a0), channel_id=1, source_target_pairs={{0,2},{1,3},{2,0},{3,1},{4,6},{5,7},{6,4},{7,5},{8,10},{9,11},{10,... | collective-permute-start | bytes 1572872 | tf_op jit(solution)/shard_map/ppermute | solution.py:22
  42.5 14.8 %collective-permute-start.14 = (bf16[512,512]{1,0:T(8,128)(2,1)S(1)}, bf16[512,512]{1,0:T(8,128)(2,1)}, u32[]{:S(2)}, u32[]{:S(2)}) collective-permute-start(bf16[512,512]{1,0:T(8,128)(2,1)S(1)} %constant_dynamic-update-slice_fusion.4.b0), channel_id=1, source_target_pairs={{0,128},{64,192},{128,0},{192,64},{1,129},{65,193},{129,1},{193,65... | collective-permute-start | bytes 1572872 | tf_op jit(solution)/shard_map/ppermute | solution.py:22
  57.3 7.5 %collective-permute-start.15 = (bf16[512,512]{1,0:T(8,128)(2,1)S(1)}, bf16[512,512]{1,0:T(8,128)(2,1)}, u32[]{:S(2)}, u32[]{:S(2)}) collective-permute-start(bf16[512,512]{1,0:T(8,128)(2,1)S(1)} %constant_dynamic-update-slice_fusion.4.b0), channel_id=1, source_target_pairs={{0,192},{64,0},{128,64},{192,128},{1,193},{65,1},{129,65},{193,129... | collective-permute-start | bytes 1572872 | tf_op jit(solution)/shard_map/ppermute | solution.py:22
  64.9 1.8 %collective-permute-done.14.b2 = bf16[512,512]{1,0:T(8,128)(2,1)} collective-permute-done((bf16[512,512]{1,0:T(8,128)(2,1)S(1)}, bf16[512,512]{1,0:T(8,128)(2,1)}, u32[]{:S(2)}, u32[]{:S(2)}) %collective-permute-start.14) | collective-permute-done | bytes 524320 | tf_op jit(solution)/shard_map/ppermute | solution.py:22
  66.7 13.2 %collective-permute-done.15.b3 = bf16[512,512]{1,0:T(8,128)(2,1)} collective-permute-done((bf16[512,512]{1,0:T(8,128)(2,1)S(1)}, bf16[512,512]{1,0:T(8,128)(2,1)}, u32[]{:S(2)}, u32[]{:S(2)}) %collective-permute-start.15) | collective-permute-done | bytes 524320 | tf_op jit(solution)/shard_map/ppermute | solution.py:22
  80.0 3.8 %collective-permute-start.22 = (bf16[64,512]{1,0:T(8,128)(2,1)}, bf16[64,512]{1,0:T(8,128)(2,1)}, u32[]{:S(2)}, u32[]{:S(2)}) collective-permute-start(bf16[64,512]{1,0:T(8,128)(2,1)} %collective-permute-done.3), channel_id=1, source_target_pairs={{0,128},{64,192},{128,0},{192,64},{1,129},{65,193},{129,1},{193,65... | collective-permute-start | bytes 196616 | tf_op jit(solution)/shard_map/ppermute | solution.py:22
  83.8 2.5 %copy-done.1 = bf16[64,80,512]{2,1,0:T(8,128)(2,1)S(1)} copy-done((bf16[64,80,512]{2,1,0:T(8,128)(2,1)S(1)}, bf16[64,80,512]{2,1,0:T(8,128)(2,1)}, u32[]{:S(2)}) %copy-start.1) | copy-done | bytes 5242904
  86.3 5.1 %project.1 = (bf16[4,128,256]{2,1,0:T(8,128)(2,1)S(1)}, bf16[4,128,128]{2,1,0:T(8,128)(2,1)S(1)}, bf16[4,128,128]{2,1,0:T(8,128)(2,1)S(1)}) custom-call(s32[5]{0:T(128)S(1)} %stack.90.place, bf16[512,512]{1,0:T(8,128)(2,1)S(1)} %constant_dynamic-update-slice_fusion.a0, bf16[512,512]{1,0:T(8,128)(2,1)S(1)} %collective-permute-done.10.a1, ...), custom_call_target="tpu_custom_call" | custom-call | flops 2147483648 | bytes 9437184 | tf_op jit(solution)/shard_map/project/pallas_call | solution.py:248
  92.1 1.7 pad_maximum_fusion.3
  95.3 3.3 %collective-permute-start.17 = (bf16[4,128,128]{2,1,0:T(8,128)(2,1)}, bf16[4,128,128]{2,1,0:T(8,128)(2,1)S(1)}, u32[]{:S(2)}, u32[]{:S(2)}) collective-permute-start(bf16[4,128,128]{2,1,0:T(8,128)(2,1)} %copy-done.4), channel_id=1, source_target_pairs={{0,4},{4,8},{8,12},{12,0},{1,5},{5,9},{9,13},{13,1},{2,6},{6,10},{... | collective-permute-start | bytes 393224 | tf_op jit(solution)/shard_map/ppermute | solution.py:22
  98.6 5.4 %collective-permute-start.18 = (bf16[4,128,128]{2,1,0:T(8,128)(2,1)}, bf16[4,128,128]{2,1,0:T(8,128)(2,1)S(1)}, u32[]{:S(2)}, u32[]{:S(2)}) collective-permute-start(bf16[4,128,128]{2,1,0:T(8,128)(2,1)} %copy-done.4), channel_id=1, source_target_pairs={{0,8},{4,12},{8,0},{12,4},{1,9},{5,13},{9,1},{13,5},{2,10},{6,14},... | collective-permute-start | bytes 393224 | tf_op jit(solution)/shard_map/ppermute | solution.py:22
  104.0 3.1 %collective-permute-start.19 = (bf16[4,128,128]{2,1,0:T(8,128)(2,1)}, bf16[4,128,128]{2,1,0:T(8,128)(2,1)S(1)}, u32[]{:S(2)}, u32[]{:S(2)}) collective-permute-start(bf16[4,128,128]{2,1,0:T(8,128)(2,1)} %copy-done.4), channel_id=1, source_target_pairs={{0,12},{4,0},{8,4},{12,8},{1,13},{5,1},{9,5},{13,9},{2,14},{6,2},{... | collective-permute-start | bytes 393224 | tf_op jit(solution)/shard_map/ppermute | solution.py:22
  109.2 2.1 %collective-permute-done.18.q2 = bf16[4,128,128]{2,1,0:T(8,128)(2,1)S(1)} collective-permute-done((bf16[4,128,128]{2,1,0:T(8,128)(2,1)}, bf16[4,128,128]{2,1,0:T(8,128)(2,1)S(1)}, u32[]{:S(2)}, u32[]{:S(2)}) %collective-permute-start.18) | collective-permute-done | bytes 131104 | tf_op jit(solution)/shard_map/ppermute | solution.py:22
  111.3 4.5 %collective-permute-done.19.q3 = bf16[4,128,128]{2,1,0:T(8,128)(2,1)S(1)} collective-permute-done((bf16[4,128,128]{2,1,0:T(8,128)(2,1)}, bf16[4,128,128]{2,1,0:T(8,128)(2,1)S(1)}, u32[]{:S(2)}, u32[]{:S(2)}) %collective-permute-start.19) | collective-permute-done | bytes 131104 | tf_op jit(solution)/shard_map/ppermute | solution.py:22
  116.8 8.5 %attend.1 = bf16[16,128,128]{2,1,0:T(8,128)(2,1)} custom-call(s32[5]{0:T(128)S(1)} %stack.90.place, s32[4]{0:T(128)S(1)} %copy-done.6, s32[4,2]{1,0:T(4,128)S(1)} %pad_add_fusion.1.q_edges, s32[4,4]{1,0:T(4,128)S(1)} %copy.25.k_edges, f32[32]{0:T(128)S(1)} %fusion.11.biases, bf16[4,128,128]{2,1,0:T(8,128)(2,1)S(1)} %copy-done.5, ...), custom_call_target="tpu_custom_call" | custom-call | flops 1073741824 | bytes 5242880 | tf_op jit(solution)/shard_map/attend/pallas_call | solution.py:286
  125.3 12.1 %all-to-all-start = ((bf16[16,128,128]{2,1,0:T(8,128)(2,1)}), bf16[16,128,128]{2,1,0:T(8,128)(2,1)S(1)}, u32[]{:S(2)}, u32[]{:S(2)}) async-start(bf16[16,128,128]{2,1,0:T(8,128)(2,1)} %attend.1), calls=%async_computation | async-start | bytes 1048576 | tf_op jit(solution)/shard_map/all_to_all | solution.py:302
  137.4 3.2 %collective-permute-start.24 = (bf16[128,128]{1,0:T(8,128)(2,1)S(1)}, bf16[128,128]{1,0:T(8,128)(2,1)S(1)}, u32[]{:S(2)}, u32[]{:S(2)}) collective-permute-start(bf16[128,128]{1,0:T(8,128)(2,1)S(1)} %get-tuple-element.73), channel_id=1, source_target_pairs={{0,192},{64,0},{128,64},{192,128},{1,193},{65,1},{129,65},{193,129... | collective-permute-start | bytes 98312 | tf_op jit(solution)/shard_map/ppermute | solution.py:300
  142.3 9.7 %all-to-all-done.parts = bf16[16,128,128]{2,1,0:T(8,128)(2,1)S(1)} async-done(((bf16[16,128,128]{2,1,0:T(8,128)(2,1)}), bf16[16,128,128]{2,1,0:T(8,128)(2,1)S(1)}, u32[]{:S(2)}, u32[]{:S(2)}) %all-to-all-start) | async-done | bytes 524320 | tf_op jit(solution)/shard_map/all_to_all | solution.py:302
  153.0 1.9 %collective-permute-start.27 = (bf16[128,512]{1,0:T(8,128)(2,1)S(1)}, bf16[128,512]{1,0:T(8,128)(2,1)S(1)}, u32[]{:S(2)}, u32[]{:S(2)}) collective-permute-start(bf16[128,512]{1,0:T(8,128)(2,1)S(1)} %gate.1), channel_id=1, source_target_pairs={{0,1},{1,2},{2,3},{3,0},{4,5},{5,6},{6,7},{7,4},{8,9},{9,10},{10,1... | collective-permute-start | bytes 393224 | tf_op jit(solution)/shard_map/ppermute | solution.py:22
  154.9 2.9 %collective-permute-done.29 = bf16[128,512]{1,0:T(8,128)(2,1)S(1)} collective-permute-done((bf16[128,512]{1,0:T(8,128)(2,1)S(1)}, bf16[128,512]{1,0:T(8,128)(2,1)S(1)}, u32[]{:S(2)}, u32[]{:S(2)}) %collective-permute-start.29) | collective-permute-done | bytes 131104 | tf_op jit(solution)/shard_map/ppermute | solution.py:22
  157.9 1.6 collective-permute-done.28
  161.0 2.2 %copy-done.2 = bf16[64,64,512]{2,1,0:T(8,128)(2,1)S(1)} copy-done((bf16[64,64,512]{2,1,0:T(8,128)(2,1)S(1)}, bf16[64,64,512]{2,1,0:T(8,128)(2,1)}, u32[]{:S(2)}) %copy-start.2) | copy-done | bytes 4194328
  163.1 3.5 %project_out.1 = bf16[128,1024]{1,0:T(8,128)(2,1)} custom-call(s32[5]{0:T(128)S(1)} %stack.90.place, bf16[128,1024]{1,0:T(8,128)(2,1)S(1)} %copy-done.3, bf16[4,128,512]{2,1,0:T(8,128)(2,1)S(1)} %pad_maximum_fusion.1.gated, bf16[4,4,4,64,512]{4,3,2,1,0:T(8,128)(2,1)S(1)} %bitcast.49), custom_call_target="tpu_custom_call" | custom-call | flops 536870912 | bytes 5242880 | tf_op jit(solution)/shard_map/project_out/pallas_call | solution.py:317
  (96 shorter events, 20.7 us)
Async XLA Ops:
  6.5 77.2 %all-gather.5.cloned.1.call-start = ((), (), s32[]{:S(2)}) async-start(), calls=%async_computation.1 | async-start | bytes 5570560 | tf_op jit(solution)/shard_map/all_gather | solution.py:233
  8.4 6.6 %collective-permute-start.2 = (bf16[80,512]{1,0:T(8,128)(2,1)S(1)}, bf16[80,512]{1,0:T(8,128)(2,1)S(1)}, u32[]{:S(2)}, u32[]{:S(2)}) collective-permute-start(bf16[80,512]{1,0:T(8,128)(2,1)S(1)} %get-tuple-element.82), channel_id=1, source_target_pairs={{0,192},{64,0},{128,64},{192,128},{1,193},{65,1},{129,65},{193,129... | collective-permute-start | bytes 245768 | tf_op jit(solution)/shard_map/ppermute | solution.py:229
  11.5 6.3 %collective-permute-start.1 = (bf16[80,512]{1,0:T(8,128)(2,1)S(1)}, bf16[80,512]{1,0:T(8,128)(2,1)S(1)}, u32[]{:S(2)}, u32[]{:S(2)}) collective-permute-start(bf16[80,512]{1,0:T(8,128)(2,1)S(1)} %get-tuple-element.81), channel_id=1, source_target_pairs={{0,128},{64,192},{128,0},{192,64},{1,129},{65,193},{129,1},{193,65... | collective-permute-start | bytes 245768 | tf_op jit(solution)/shard_map/ppermute | solution.py:229
  12.1 6.5 %collective-permute-start = (bf16[80,512]{1,0:T(8,128)(2,1)S(1)}, bf16[80,512]{1,0:T(8,128)(2,1)S(1)}, u32[]{:S(2)}, u32[]{:S(2)}) collective-permute-start(bf16[80,512]{1,0:T(8,128)(2,1)S(1)} %get-tuple-element.80), channel_id=1, source_target_pairs={{0,64},{64,128},{128,192},{192,0},{1,65},{65,129},{129,193},{193,1... | collective-permute-start | bytes 245768 | tf_op jit(solution)/shard_map/ppermute | solution.py:229
  19.5 132.5 %all-gather.7.cloned.1.call-start = ((), (), s32[]{:S(2)}) async-start(), calls=%async_computation.2 | async-start | bytes 4456448 | tf_op jit(solution)/shard_map/all_gather | solution.py:267
  20.5 8.8 %collective-permute-start.4 = (bf16[128,512]{1,0:T(8,128)(2,1)S(1)}, bf16[128,512]{1,0:T(8,128)(2,1)S(1)}, u32[]{:S(2)}, u32[]{:S(2)}) collective-permute-start(bf16[128,512]{1,0:T(8,128)(2,1)S(1)} %get-tuple-element.36), channel_id=1, source_target_pairs={{0,64},{64,128},{128,192},{192,0},{1,65},{65,129},{129,193},{193,1... | collective-permute-start | bytes 393224 | tf_op jit(solution)/shard_map/ppermute | solution.py:22
  20.6 11.5 %collective-permute-start.5 = (bf16[128,512]{1,0:T(8,128)(2,1)S(1)}, bf16[128,512]{1,0:T(8,128)(2,1)S(1)}, u32[]{:S(2)}, u32[]{:S(2)}) collective-permute-start(bf16[128,512]{1,0:T(8,128)(2,1)S(1)} %get-tuple-element.36), channel_id=1, source_target_pairs={{0,128},{64,192},{128,0},{192,64},{1,129},{65,193},{129,1},{193,65... | collective-permute-start | bytes 393224 | tf_op jit(solution)/shard_map/ppermute | solution.py:22
  22.6 9.5 %collective-permute-start.6 = (bf16[128,512]{1,0:T(8,128)(2,1)S(1)}, bf16[128,512]{1,0:T(8,128)(2,1)S(1)}, u32[]{:S(2)}, u32[]{:S(2)}) collective-permute-start(bf16[128,512]{1,0:T(8,128)(2,1)S(1)} %get-tuple-element.36), channel_id=1, source_target_pairs={{0,192},{64,0},{128,64},{192,128},{1,193},{65,1},{129,65},{193,129... | collective-permute-start | bytes 393224 | tf_op jit(solution)/shard_map/ppermute | solution.py:22
  24.1 8.0 %collective-permute-start.7 = (bf16[128,512]{1,0:T(8,128)(2,1)S(1)}, bf16[128,512]{1,0:T(8,128)(2,1)S(1)}, u32[]{:S(2)}, u32[]{:S(2)}) collective-permute-start(bf16[128,512]{1,0:T(8,128)(2,1)S(1)} %get-tuple-element.40), channel_id=1, source_target_pairs={{0,1},{1,2},{2,3},{3,0},{4,5},{5,6},{6,7},{7,4},{8,9},{9,10},{10,1... | collective-permute-start | bytes 393224 | tf_op jit(solution)/shard_map/ppermute | solution.py:22
  25.6 7.4 %collective-permute-start.8 = (bf16[128,512]{1,0:T(8,128)(2,1)S(1)}, bf16[128,512]{1,0:T(8,128)(2,1)S(1)}, u32[]{:S(2)}, u32[]{:S(2)}) collective-permute-start(bf16[128,512]{1,0:T(8,128)(2,1)S(1)} %get-tuple-element.40), channel_id=1, source_target_pairs={{0,2},{1,3},{2,0},{3,1},{4,6},{5,7},{6,4},{7,5},{8,10},{9,11},{10,... | collective-permute-start | bytes 393224 | tf_op jit(solution)/shard_map/ppermute | solution.py:22
  29.4 5.3 %collective-permute-start.9 = (bf16[128,512]{1,0:T(8,128)(2,1)S(1)}, bf16[128,512]{1,0:T(8,128)(2,1)S(1)}, u32[]{:S(2)}, u32[]{:S(2)}) collective-permute-start(bf16[128,512]{1,0:T(8,128)(2,1)S(1)} %get-tuple-element.40), channel_id=1, source_target_pairs={{0,3},{1,0},{2,1},{3,2},{4,7},{5,4},{6,5},{7,6},{8,11},{9,8},{10,9... | collective-permute-start | bytes 393224 | tf_op jit(solution)/shard_map/ppermute | solution.py:22
  34.7 22.6 %collective-permute-start.10 = (bf16[512,512]{1,0:T(8,128)(2,1)S(1)}, bf16[512,512]{1,0:T(8,128)(2,1)S(1)}, u32[]{:S(2)}, u32[]{:S(2)}) collective-permute-start(bf16[512,512]{1,0:T(8,128)(2,1)S(1)} %constant_dynamic-update-slice_fusion.a0), channel_id=1, source_target_pairs={{0,1},{1,2},{2,3},{3,0},{4,5},{5,6},{6,7},{7,4},{8,9},{9,10},{10,1... | collective-permute-start | bytes 1572872 | tf_op jit(solution)/shard_map/ppermute | solution.py:22
  36.2 6.3 %collective-permute-start.3 = (bf16[64,512]{1,0:T(8,128)(2,1)}, bf16[64,512]{1,0:T(8,128)(2,1)}, u32[]{:S(2)}, u32[]{:S(2)}) collective-permute-start(bf16[64,512]{1,0:T(8,128)(2,1)} %bitcast.65), channel_id=1, source_target_pairs={{0,0},{64,1},{128,2},{192,3},{1,64},{65,65},{129,66},{193,67},{2,1... | collective-permute-start | bytes 196616 | tf_op jit(solution)/shard_map/ppermute | solution.py:242
  38.4 26.5 %collective-permute-start.11 = (bf16[512,512]{1,0:T(8,128)(2,1)S(1)}, bf16[512,512]{1,0:T(8,128)(2,1)S(1)}, u32[]{:S(2)}, u32[]{:S(2)}) collective-permute-start(bf16[512,512]{1,0:T(8,128)(2,1)S(1)} %constant_dynamic-update-slice_fusion.a0), channel_id=1, source_target_pairs={{0,2},{1,3},{2,0},{3,1},{4,6},{5,7},{6,4},{7,5},{8,10},{9,11},{10,... | collective-permute-start | bytes 1572872 | tf_op jit(solution)/shard_map/ppermute | solution.py:22
  42.4 22.5 %collective-permute-start.12 = (bf16[512,512]{1,0:T(8,128)(2,1)S(1)}, bf16[512,512]{1,0:T(8,128)(2,1)S(1)}, u32[]{:S(2)}, u32[]{:S(2)}) collective-permute-start(bf16[512,512]{1,0:T(8,128)(2,1)S(1)} %constant_dynamic-update-slice_fusion.a0), channel_id=1, source_target_pairs={{0,3},{1,0},{2,1},{3,2},{4,7},{5,4},{6,5},{7,6},{8,11},{9,8},{10,9... | collective-permute-start | bytes 1572872 | tf_op jit(solution)/shard_map/ppermute | solution.py:22
  42.4 22.5 %collective-permute-start.13 = (bf16[512,512]{1,0:T(8,128)(2,1)S(1)}, bf16[512,512]{1,0:T(8,128)(2,1)S(1)}, u32[]{:S(2)}, u32[]{:S(2)}) collective-permute-start(bf16[512,512]{1,0:T(8,128)(2,1)S(1)} %constant_dynamic-update-slice_fusion.4.b0), channel_id=1, source_target_pairs={{0,64},{64,128},{128,192},{192,0},{1,65},{65,129},{129,193},{193,1... | collective-permute-start | bytes 1572872 | tf_op jit(solution)/shard_map/ppermute | solution.py:22
  42.5 24.2 %collective-permute-start.14 = (bf16[512,512]{1,0:T(8,128)(2,1)S(1)}, bf16[512,512]{1,0:T(8,128)(2,1)}, u32[]{:S(2)}, u32[]{:S(2)}) collective-permute-start(bf16[512,512]{1,0:T(8,128)(2,1)S(1)} %constant_dynamic-update-slice_fusion.4.b0), channel_id=1, source_target_pairs={{0,128},{64,192},{128,0},{192,64},{1,129},{65,193},{129,1},{193,65... | collective-permute-start | bytes 1572872 | tf_op jit(solution)/shard_map/ppermute | solution.py:22
  57.3 22.7 %collective-permute-start.15 = (bf16[512,512]{1,0:T(8,128)(2,1)S(1)}, bf16[512,512]{1,0:T(8,128)(2,1)}, u32[]{:S(2)}, u32[]{:S(2)}) collective-permute-start(bf16[512,512]{1,0:T(8,128)(2,1)S(1)} %constant_dynamic-update-slice_fusion.4.b0), channel_id=1, source_target_pairs={{0,192},{64,0},{128,64},{192,128},{1,193},{65,1},{129,65},{193,129... | collective-permute-start | bytes 1572872 | tf_op jit(solution)/shard_map/ppermute | solution.py:22
  80.0 12.1 %collective-permute-start.21 = (bf16[64,512]{1,0:T(8,128)(2,1)}, bf16[64,512]{1,0:T(8,128)(2,1)}, u32[]{:S(2)}, u32[]{:S(2)}) collective-permute-start(bf16[64,512]{1,0:T(8,128)(2,1)} %collective-permute-done.3), channel_id=1, source_target_pairs={{0,64},{64,128},{128,192},{192,0},{1,65},{65,129},{129,193},{193,1... | collective-permute-start | bytes 196616 | tf_op jit(solution)/shard_map/ppermute | solution.py:22
  80.0 12.1 %collective-permute-start.22 = (bf16[64,512]{1,0:T(8,128)(2,1)}, bf16[64,512]{1,0:T(8,128)(2,1)}, u32[]{:S(2)}, u32[]{:S(2)}) collective-permute-start(bf16[64,512]{1,0:T(8,128)(2,1)} %collective-permute-done.3), channel_id=1, source_target_pairs={{0,128},{64,192},{128,0},{192,64},{1,129},{65,193},{129,1},{193,65... | collective-permute-start | bytes 196616 | tf_op jit(solution)/shard_map/ppermute | solution.py:22
  83.8 8.3 %collective-permute-start.23 = (bf16[64,512]{1,0:T(8,128)(2,1)}, bf16[64,512]{1,0:T(8,128)(2,1)}, u32[]{:S(2)}, u32[]{:S(2)}) collective-permute-start(bf16[64,512]{1,0:T(8,128)(2,1)} %collective-permute-done.3), channel_id=1, source_target_pairs={{0,192},{64,0},{128,64},{192,128},{1,193},{65,1},{129,65},{193,129... | collective-permute-start | bytes 196616 | tf_op jit(solution)/shard_map/ppermute | solution.py:22
  95.2 13.0 %collective-permute-start.16 = (bf16[4,128,256]{2,1,0:T(8,128)(2,1)S(1)}, bf16[4,128,256]{2,1,0:T(8,128)(2,1)S(1)}, u32[]{:S(2)}, u32[]{:S(2)}) collective-permute-start(bf16[4,128,256]{2,1,0:T(8,128)(2,1)S(1)} %get-tuple-element.53), channel_id=1, source_target_pairs={{0,32},{32,0},{1,33},{33,1},{2,34},{34,2},{3,35},{35,3},{4,36},{36... | collective-permute-start | bytes 786440 | tf_op jit(solution)/shard_map/ppermute | solution.py:28
  95.3 12.8 %collective-permute-start.17 = (bf16[4,128,128]{2,1,0:T(8,128)(2,1)}, bf16[4,128,128]{2,1,0:T(8,128)(2,1)S(1)}, u32[]{:S(2)}, u32[]{:S(2)}) collective-permute-start(bf16[4,128,128]{2,1,0:T(8,128)(2,1)} %copy-done.4), channel_id=1, source_target_pairs={{0,4},{4,8},{8,12},{12,0},{1,5},{5,9},{9,13},{13,1},{2,6},{6,10},{... | collective-permute-start | bytes 393224 | tf_op jit(solution)/shard_map/ppermute | solution.py:22
  98.6 12.7 %collective-permute-start.18 = (bf16[4,128,128]{2,1,0:T(8,128)(2,1)}, bf16[4,128,128]{2,1,0:T(8,128)(2,1)S(1)}, u32[]{:S(2)}, u32[]{:S(2)}) collective-permute-start(bf16[4,128,128]{2,1,0:T(8,128)(2,1)} %copy-done.4), channel_id=1, source_target_pairs={{0,8},{4,12},{8,0},{12,4},{1,9},{5,13},{9,1},{13,5},{2,10},{6,14},... | collective-permute-start | bytes 393224 | tf_op jit(solution)/shard_map/ppermute | solution.py:22
  104.0 11.9 %collective-permute-start.19 = (bf16[4,128,128]{2,1,0:T(8,128)(2,1)}, bf16[4,128,128]{2,1,0:T(8,128)(2,1)S(1)}, u32[]{:S(2)}, u32[]{:S(2)}) collective-permute-start(bf16[4,128,128]{2,1,0:T(8,128)(2,1)} %copy-done.4), channel_id=1, source_target_pairs={{0,12},{4,0},{8,4},{12,8},{1,13},{5,1},{9,5},{13,9},{2,14},{6,2},{... | collective-permute-start | bytes 393224 | tf_op jit(solution)/shard_map/ppermute | solution.py:22
  108.2 7.6 %collective-permute-start.20 = (bf16[2,4,128,256]{3,2,1,0:T(8,128)(2,1)S(1)}, bf16[2,4,128,256]{3,2,1,0:T(8,128)(2,1)S(1)}, u32[]{:S(2)}, u32[]{:S(2)}) collective-permute-start(bf16[2,4,128,256]{3,2,1,0:T(8,128)(2,1)S(1)} %pad_maximum_fusion.kv_near), channel_id=1, source_target_pairs={{0,16},{16,0},{1,17},{17,1},{2,18},{18,2},{3,19},{19,3},{4,20},{20... | collective-permute-start | bytes 1572872 | tf_op jit(solution)/shard_map/ppermute | solution.py:28
  125.3 26.7 %all-to-all-start = ((bf16[16,128,128]{2,1,0:T(8,128)(2,1)}), bf16[16,128,128]{2,1,0:T(8,128)(2,1)S(1)}, u32[]{:S(2)}, u32[]{:S(2)}) async-start(bf16[16,128,128]{2,1,0:T(8,128)(2,1)} %attend.1), calls=%async_computation | async-start | bytes 1048576 | tf_op jit(solution)/shard_map/all_to_all | solution.py:302
  137.4 14.6 %collective-permute-start.24 = (bf16[128,128]{1,0:T(8,128)(2,1)S(1)}, bf16[128,128]{1,0:T(8,128)(2,1)S(1)}, u32[]{:S(2)}, u32[]{:S(2)}) collective-permute-start(bf16[128,128]{1,0:T(8,128)(2,1)S(1)} %get-tuple-element.73), channel_id=1, source_target_pairs={{0,192},{64,0},{128,64},{192,128},{1,193},{65,1},{129,65},{193,129... | collective-permute-start | bytes 98312 | tf_op jit(solution)/shard_map/ppermute | solution.py:300
  140.6 11.4 %collective-permute-start.25 = (bf16[128,128]{1,0:T(8,128)(2,1)S(1)}, bf16[128,128]{1,0:T(8,128)(2,1)S(1)}, u32[]{:S(2)}, u32[]{:S(2)}) collective-permute-start(bf16[128,128]{1,0:T(8,128)(2,1)S(1)} %get-tuple-element.72), channel_id=1, source_target_pairs={{0,128},{64,192},{128,0},{192,64},{1,129},{65,193},{129,1},{193,65... | collective-permute-start | bytes 98312 | tf_op jit(solution)/shard_map/ppermute | solution.py:300
  141.5 10.5 %collective-permute-start.26 = (bf16[128,128]{1,0:T(8,128)(2,1)S(1)}, bf16[128,128]{1,0:T(8,128)(2,1)S(1)}, u32[]{:S(2)}, u32[]{:S(2)}) collective-permute-start(bf16[128,128]{1,0:T(8,128)(2,1)S(1)} %get-tuple-element.71), channel_id=1, source_target_pairs={{0,64},{64,128},{128,192},{192,0},{1,65},{65,129},{129,193},{193,1... | collective-permute-start | bytes 98312 | tf_op jit(solution)/shard_map/ppermute | solution.py:300
  152.9 6.6 %collective-permute-start.28 = (bf16[128,512]{1,0:T(8,128)(2,1)S(1)}, bf16[128,512]{1,0:T(8,128)(2,1)S(1)}, u32[]{:S(2)}, u32[]{:S(2)}) collective-permute-start(bf16[128,512]{1,0:T(8,128)(2,1)S(1)} %gate.1), channel_id=1, source_target_pairs={{0,2},{1,3},{2,0},{3,1},{4,6},{5,7},{6,4},{7,5},{8,10},{9,11},{10,... | collective-permute-start | bytes 393224 | tf_op jit(solution)/shard_map/ppermute | solution.py:22
  153.0 7.9 %collective-permute-start.27 = (bf16[128,512]{1,0:T(8,128)(2,1)S(1)}, bf16[128,512]{1,0:T(8,128)(2,1)S(1)}, u32[]{:S(2)}, u32[]{:S(2)}) collective-permute-start(bf16[128,512]{1,0:T(8,128)(2,1)S(1)} %gate.1), channel_id=1, source_target_pairs={{0,1},{1,2},{2,3},{3,0},{4,5},{5,6},{6,7},{7,4},{8,9},{9,10},{10,1... | collective-permute-start | bytes 393224 | tf_op jit(solution)/shard_map/ppermute | solution.py:22
  (8 other events, 245.6 us)
Sparse Core Ops, SparseCore 0:
  19.6 43.4 all-gather.4
  93.9 45.2 all-gather.6

commit v7 on v6

--- a/solution.py
+++ b/solution.py
@@ -232,14 +232,18 @@
     piece = jnp.stack(pieces)
     weights = lax.all_gather(piece, plane)
 
-    first = rotations(tokens[:, :512], "y", 4)
-    second = rotations(tokens[:, 512:], "x", 4)
-    first, second = lax.optimization_barrier((first, second))
+    late, _ = lax.optimization_barrier((w_out.T, piece))
+    swapped = lax.ppermute(
+        late, ("y", "x"), [(b * 4 + a, a * 4 + b) for a in range(4) for b in range(4)]
+    )
+    travelling, _ = lax.optimization_barrier((tokens, piece))
+
+    first = rotations(travelling[:, :512], "y", 4)
+    second = rotations(travelling[:, 512:], "x", 4)
+    first, second, swapped = lax.optimization_barrier((first, second, swapped))
     firsts = rotations(jnp.concatenate(first, axis=0), "x", 4)
     seconds = rotations(jnp.concatenate(second, axis=0), "y", 4)
 
-    late, _ = lax.optimization_barrier((w_out.T, piece))
-    swapped = lax.ppermute(late, ("y", "x"), [(b * 4 + a, a * 4 + b) for a in range(4) for b in range(4)])
     swapped, firsts, seconds = lax.optimization_barrier((swapped, firsts, seconds))
     wo_rows = rotations(swapped, "y", 4)
 
@@ -256,7 +260,7 @@
             out_specs=[whole] * 3,
             scratch_shapes=[pltpu.VMEM((512, 512), f32)],
         ),
-        compiler_params=pltpu.CompilerParams(vmem_limit_bytes=20 * 2**20),
+        compiler_params=pltpu.CompilerParams(vmem_limit_bytes=56 * 2**20),
         cost_estimate=pl.CostEstimate(
             flops=2 * 512 * 512 * 4096, bytes_accessed=9 * 2**20, transcendentals=0
         ),
@@ -327,7 +331,7 @@
             ],
             out_specs=pl.BlockSpec((RUN, 256), lambda i, p: (0, i)),
         ),
-        compiler_params=pltpu.CompilerParams(vmem_limit_bytes=14 * 2**20),
+        compiler_params=pltpu.CompilerParams(vmem_limit_bytes=60 * 2**20),
         cost_estimate=pl.CostEstimate(
             flops=2 * RUN * 2048 * 1024, bytes_accessed=5 * 2**20, transcendentals=0
         ),

time: 173 us -> 165 us (0.954)
  starting transfers between devices: 80.1 us -> 67.7 us
  Pallas kernels: 17.9 us -> 22.8 us
  local copies, waits for them, and re-layouts: 10.6 us -> 5.95 us
  waiting for transfers between devices: 46.5 us -> 49.3 us
    ppermute x21, starting transfers between devices: 56 us -> 42.9 us  [rotations(): lax.ppermute(value, axis, [(i, (i + step * k) % size) for i in range(size)])]
    unnamed x21 -> x29, local copies, waits for them, and re-layouts: 6.3 us -> 1.01 us
    pallas_call x1, Pallas kernels: 5.09 us -> 7.82 us  [on_device(): pl.pallas_call(project_kernel, out_shape=[jax.ShapeDtypeStruct((4, RUN, 2...]
    ppermute x21, waiting for transfers between devices: 31.3 us -> 33.5 us  [rotations(): lax.ppermute(value, axis, [(i, (i + step * k) % size) for i in range(size)])]
    pallas_call x1, Pallas kernels: 3.51 us -> 5.62 us  [on_device(): pl.pallas_call(output_kernel, out_shape=jax.ShapeDtypeStruct((RUN, 1024),...]
  transfers between devices with their start and end apart: 33 -> 33, of which waited for: 14 -> 15; matrix products, arithmetic and copies ran while one was open for 3% -> 4% of each run, Pallas kernels for 8% -> 10%
where the time goes in v7:
time: 165 us
  starting transfers between devices  67.7 us (41%)
  waiting for transfers between devices  49.3 us (30%)
  Pallas kernels  22.8 us (14%)
  between operations  13.7 us (8%)
  local copies, waits for them, and re-layouts  5.95 us (4%)
  other arithmetic  5.38 us (3%)
    ppermute x21, starting transfers between devices, rotations(): lax.ppermute(value, axis, [(i, (i + step * k) % size) for i in range(size)])  42.9 us
    ppermute x21, waiting for transfers between devices, rotations(): lax.ppermute(value, axis, [(i, (i + step * k) % size) for i in range(size)])  33.5 us
    all_to_all x1, starting transfers between devices, on_device(): arrived = lax.all_to_all(parts, ('y', 'zh'), 0, 0, tiled=True)  13 us
    all_to_all x1, waiting for transfers between devices, on_device(): arrived = lax.all_to_all(parts, ('y', 'zh'), 0, 0, tiled=True)  10.2 us
    pallas_call x1, Pallas kernels, on_device(): call(attend_kernel, jax.ShapeDtypeStruct((16, RUN, DH), bf16), 5, 9, [plt...  8.56 us
    pallas_call x1, Pallas kernels, on_device(): pl.pallas_call(project_kernel, out_shape=[jax.ShapeDtypeStruct((4, RUN, 2...  7.82 us
    pallas_call x1, Pallas kernels, on_device(): pl.pallas_call(output_kernel, out_shape=jax.ShapeDtypeStruct((RUN, 1024),...  5.62 us
    ppermute x3, waiting for transfers between devices, on_device(): lax.ppermute(columns(y + k & 3), 'y', [(i, (i + k) % 4) for i in range(4)])  5.56 us
  transfers between devices with their start and end apart: 33, of which 15 were waited for; matrix products, arithmetic and copies ran while one was open for 4% of the time, Pallas kernels for 10%

profile of v7, /device:TPU:32, one launch (start us, length us, event | category | flops | bytes accessed | tf_op | source)
XLA Modules:
  0.0 164.9 jit_solution(1051876808987299903)
XLA Ops:
  8.4 3.1 %collective-permute-start.2 = (bf16[80,512]{1,0:T(8,128)(2,1)S(1)}, bf16[80,512]{1,0:T(8,128)(2,1)S(1)}, u32[]{:S(2)}, u32[]{:S(2)}) collective-permute-start(bf16[80,512]{1,0:T(8,128)(2,1)S(1)} %get-tuple-element.86), channel_id=1, source_target_pairs={{0,192},{64,0},{128,64},{192,128},{1,193},{65,1},{129,65},{193,129... | collective-permute-start | bytes 245768 | tf_op jit(solution)/shard_map/ppermute | solution.py:229
  12.1 1.0 collective-permute-start
  13.1 1.9 %collective-permute-done.2 = bf16[80,512]{1,0:T(8,128)(2,1)S(1)} collective-permute-done((bf16[80,512]{1,0:T(8,128)(2,1)S(1)}, bf16[80,512]{1,0:T(8,128)(2,1)S(1)}, u32[]{:S(2)}, u32[]{:S(2)}) %collective-permute-start.2) | collective-permute-done | bytes 81952 | tf_op jit(solution)/shard_map/ppermute | solution.py:229
  15.0 2.9 %collective-permute-done.1 = bf16[80,512]{1,0:T(8,128)(2,1)S(1)} collective-permute-done((bf16[80,512]{1,0:T(8,128)(2,1)S(1)}, bf16[80,512]{1,0:T(8,128)(2,1)S(1)}, u32[]{:S(2)}, u32[]{:S(2)}) %collective-permute-start.1) | collective-permute-done | bytes 81952 | tf_op jit(solution)/shard_map/ppermute | solution.py:229
  19.5 1.0 fusion.9
  20.6 1.5 collective-permute-start.9
  22.1 6.5 %collective-permute-start.4 = (bf16[128,512]{1,0:T(8,128)(2,1)S(1)}, bf16[128,512]{1,0:T(8,128)(2,1)S(1)}, u32[]{:S(2)}, u32[]{:S(2)}) collective-permute-start(bf16[128,512]{1,0:T(8,128)(2,1)S(1)} %get-tuple-element.40), channel_id=1, source_target_pairs={{0,128},{64,192},{128,0},{192,64},{1,129},{65,193},{129,1},{193,65... | collective-permute-start | bytes 393224 | tf_op jit(solution)/shard_map/ppermute | solution.py:22
  29.3 5.2 %collective-permute-start.7 = (bf16[128,512]{1,0:T(8,128)(2,1)S(1)}, bf16[128,512]{1,0:T(8,128)(2,1)S(1)}, u32[]{:S(2)}, u32[]{:S(2)}) collective-permute-start(bf16[128,512]{1,0:T(8,128)(2,1)S(1)} %get-tuple-element.44), channel_id=1, source_target_pairs={{0,2},{1,3},{2,0},{3,1},{4,6},{5,7},{6,4},{7,5},{8,10},{9,11},{10,... | collective-permute-start | bytes 393224 | tf_op jit(solution)/shard_map/ppermute | solution.py:22
  34.6 2.8 %collective-permute-done.6 = bf16[128,512]{1,0:T(8,128)(2,1)S(1)} collective-permute-done((bf16[128,512]{1,0:T(8,128)(2,1)S(1)}, bf16[128,512]{1,0:T(8,128)(2,1)S(1)}, u32[]{:S(2)}, u32[]{:S(2)}) %collective-permute-start.6) | collective-permute-done | bytes 131104 | tf_op jit(solution)/shard_map/ppermute | solution.py:22
  37.3 1.5 collective-permute-done.7
  40.3 3.4 %collective-permute-start.11 = (bf16[512,512]{1,0:T(8,128)(2,1)S(1)}, bf16[512,512]{1,0:T(8,128)(2,1)S(1)}, u32[]{:S(2)}, u32[]{:S(2)}) collective-permute-start(bf16[512,512]{1,0:T(8,128)(2,1)S(1)} %constant_dynamic-update-slice_fusion.a0), channel_id=1, source_target_pairs={{0,2},{1,3},{2,0},{3,1},{4,6},{5,7},{6,4},{7,5},{8,10},{9,11},{10,... | collective-permute-start | bytes 1572872 | tf_op jit(solution)/shard_map/ppermute | solution.py:22
  44.0 4.7 %collective-permute-start.14 = (bf16[512,512]{1,0:T(8,128)(2,1)S(1)}, bf16[512,512]{1,0:T(8,128)(2,1)}, u32[]{:S(2)}, u32[]{:S(2)}) collective-permute-start(bf16[512,512]{1,0:T(8,128)(2,1)S(1)} %constant_dynamic-update-slice_fusion.4.b0), channel_id=1, source_target_pairs={{0,128},{64,192},{128,0},{192,64},{1,129},{65,193},{129,1},{193,65... | collective-permute-start | bytes 1572872 | tf_op jit(solution)/shard_map/ppermute | solution.py:22
  48.7 7.4 %collective-permute-done.10.a1 = bf16[512,512]{1,0:T(8,128)(2,1)S(1)} collective-permute-done((bf16[512,512]{1,0:T(8,128)(2,1)S(1)}, bf16[512,512]{1,0:T(8,128)(2,1)S(1)}, u32[]{:S(2)}, u32[]{:S(2)}) %collective-permute-start.10) | collective-permute-done | bytes 524320 | tf_op jit(solution)/shard_map/ppermute | solution.py:22
  57.4 6.2 %collective-permute-done.11.a2 = bf16[512,512]{1,0:T(8,128)(2,1)S(1)} collective-permute-done((bf16[512,512]{1,0:T(8,128)(2,1)S(1)}, bf16[512,512]{1,0:T(8,128)(2,1)S(1)}, u32[]{:S(2)}, u32[]{:S(2)}) %collective-permute-start.11) | collective-permute-done | bytes 524320 | tf_op jit(solution)/shard_map/ppermute | solution.py:22
  64.0 4.3 %collective-permute-done.14.b2 = bf16[512,512]{1,0:T(8,128)(2,1)} collective-permute-done((bf16[512,512]{1,0:T(8,128)(2,1)S(1)}, bf16[512,512]{1,0:T(8,128)(2,1)}, u32[]{:S(2)}, u32[]{:S(2)}) %collective-permute-start.14) | collective-permute-done | bytes 524320 | tf_op jit(solution)/shard_map/ppermute | solution.py:22
  68.4 4.2 %collective-permute-start.22 = (bf16[64,512]{1,0:T(8,128)(2,1)S(1)}, bf16[64,512]{1,0:T(8,128)(2,1)S(1)}, u32[]{:S(2)}, u32[]{:S(2)}) collective-permute-start(bf16[64,512]{1,0:T(8,128)(2,1)S(1)} %collective-permute-done.9), channel_id=1, source_target_pairs={{0,128},{64,192},{128,0},{192,64},{1,129},{65,193},{129,1},{193,65... | collective-permute-start | bytes 196616 | tf_op jit(solution)/shard_map/ppermute | solution.py:22
  72.6 7.8 %project.1 = (bf16[4,128,256]{2,1,0:T(8,128)(2,1)}, bf16[4,128,128]{2,1,0:T(8,128)(2,1)}, bf16[4,128,128]{2,1,0:T(8,128)(2,1)}) custom-call(s32[5]{0:T(128)} %stack.90.place, bf16[512,512]{1,0:T(8,128)(2,1)} %copy-done.4, bf16[512,512]{1,0:T(8,128)(2,1)} %copy-done.6, bf16[512,512]{1,0:T(8,128)(2,1)} %copy-done.7, bf16[512,512]{1,0:T(8,128)(2,1)} %copy-done.8, ...), custom_call_target="tpu_custom_call" | custom-call | flops 2147483648 | bytes 9437184 | tf_op jit(solution)/shard_map/project/pallas_call | solution.py:252
  83.2 3.2 %collective-permute-start.17 = (bf16[4,128,128]{2,1,0:T(8,128)(2,1)}, bf16[4,128,128]{2,1,0:T(8,128)(2,1)S(1)}, u32[]{:S(2)}, u32[]{:S(2)}) collective-permute-start(bf16[4,128,128]{2,1,0:T(8,128)(2,1)} %get-tuple-element.56.q0), channel_id=1, source_target_pairs={{0,4},{4,8},{8,12},{12,0},{1,5},{5,9},{9,13},{13,1},{2,6},{6,10},{... | collective-permute-start | bytes 393224 | tf_op jit(solution)/shard_map/ppermute | solution.py:22
  86.4 5.0 %collective-permute-start.18 = (bf16[4,128,128]{2,1,0:T(8,128)(2,1)}, bf16[4,128,128]{2,1,0:T(8,128)(2,1)S(1)}, u32[]{:S(2)}, u32[]{:S(2)}) collective-permute-start(bf16[4,128,128]{2,1,0:T(8,128)(2,1)} %get-tuple-element.56.q0), channel_id=1, source_target_pairs={{0,8},{4,12},{8,0},{12,4},{1,9},{5,13},{9,1},{13,5},{2,10},{6,14},... | collective-permute-start | bytes 393224 | tf_op jit(solution)/shard_map/ppermute | solution.py:22
  91.4 3.1 %collective-permute-start.19 = (bf16[4,128,128]{2,1,0:T(8,128)(2,1)}, bf16[4,128,128]{2,1,0:T(8,128)(2,1)S(1)}, u32[]{:S(2)}, u32[]{:S(2)}) collective-permute-start(bf16[4,128,128]{2,1,0:T(8,128)(2,1)} %get-tuple-element.56.q0), channel_id=1, source_target_pairs={{0,12},{4,0},{8,4},{12,8},{1,13},{5,1},{9,5},{13,9},{2,14},{6,2},{... | collective-permute-start | bytes 393224 | tf_op jit(solution)/shard_map/ppermute | solution.py:22
  95.7 1.0 pad_maximum_fusion.kv_near
  97.7 5.1 %collective-permute-done.18.q2 = bf16[4,128,128]{2,1,0:T(8,128)(2,1)S(1)} collective-permute-done((bf16[4,128,128]{2,1,0:T(8,128)(2,1)}, bf16[4,128,128]{2,1,0:T(8,128)(2,1)S(1)}, u32[]{:S(2)}, u32[]{:S(2)}) %collective-permute-start.18) | collective-permute-done | bytes 131104 | tf_op jit(solution)/shard_map/ppermute | solution.py:22
  103.7 8.6 %attend.1 = bf16[16,128,128]{2,1,0:T(8,128)(2,1)} custom-call(s32[5]{0:T(128)S(1)} %copy-done.1, s32[4]{0:T(128)S(1)} %copy-done.3, s32[4,2]{1,0:T(4,128)S(1)} %pad_add_fusion.1.q_edges, s32[4,4]{1,0:T(4,128)S(1)} %copy.25.k_edges, f32[32]{0:T(128)S(1)} %fusion.11.biases, bf16[4,128,128]{2,1,0:T(8,128)(2,1)S(1)} %copy-done.2, ...), custom_call_target="tpu_custom_call" | custom-call | flops 1073741824 | bytes 5242880 | tf_op jit(solution)/shard_map/attend/pallas_call | solution.py:290
  112.2 13.0 %all-to-all-start = ((bf16[16,128,128]{2,1,0:T(8,128)(2,1)}), bf16[16,128,128]{2,1,0:T(8,128)(2,1)S(1)}, u32[]{:S(2)}, u32[]{:S(2)}) async-start(bf16[16,128,128]{2,1,0:T(8,128)(2,1)} %attend.1), calls=%async_computation | async-start | bytes 1048576 | tf_op jit(solution)/shard_map/all_to_all | solution.py:306
  125.2 3.2 %collective-permute-start.24 = (bf16[128,128]{1,0:T(8,128)(2,1)S(1)}, bf16[128,128]{1,0:T(8,128)(2,1)S(1)}, u32[]{:S(2)}, u32[]{:S(2)}) collective-permute-start(bf16[128,128]{1,0:T(8,128)(2,1)S(1)} %get-tuple-element.77), channel_id=1, source_target_pairs={{0,192},{64,0},{128,64},{192,128},{1,193},{65,1},{129,65},{193,129... | collective-permute-start | bytes 98312 | tf_op jit(solution)/shard_map/ppermute | solution.py:304
  130.2 10.2 %all-to-all-done.parts = bf16[16,128,128]{2,1,0:T(8,128)(2,1)S(1)} async-done(((bf16[16,128,128]{2,1,0:T(8,128)(2,1)}), bf16[16,128,128]{2,1,0:T(8,128)(2,1)S(1)}, u32[]{:S(2)}, u32[]{:S(2)}) %all-to-all-start) | async-done | bytes 524320 | tf_op jit(solution)/shard_map/all_to_all | solution.py:306
  141.2 2.0 %collective-permute-start.29 = (bf16[128,512]{1,0:T(8,128)(2,1)S(1)}, bf16[128,512]{1,0:T(8,128)(2,1)S(1)}, u32[]{:S(2)}, u32[]{:S(2)}) collective-permute-start(bf16[128,512]{1,0:T(8,128)(2,1)S(1)} %gate.1), channel_id=1, source_target_pairs={{0,3},{1,0},{2,1},{3,2},{4,7},{5,4},{6,5},{7,6},{8,11},{9,8},{10,9... | collective-permute-start | bytes 393224 | tf_op jit(solution)/shard_map/ppermute | solution.py:22
  143.2 2.2 %collective-permute-start.28 = (bf16[128,512]{1,0:T(8,128)(2,1)S(1)}, bf16[128,512]{1,0:T(8,128)(2,1)S(1)}, u32[]{:S(2)}, u32[]{:S(2)}) collective-permute-start(bf16[128,512]{1,0:T(8,128)(2,1)S(1)} %gate.1), channel_id=1, source_target_pairs={{0,2},{1,3},{2,0},{3,1},{4,6},{5,7},{6,4},{7,5},{8,10},{9,11},{10,... | collective-permute-start | bytes 393224 | tf_op jit(solution)/shard_map/ppermute | solution.py:22
  145.4 1.3 collective-permute-start.27
  146.6 3.0 %collective-permute-done.28 = bf16[128,512]{1,0:T(8,128)(2,1)S(1)} collective-permute-done((bf16[128,512]{1,0:T(8,128)(2,1)S(1)}, bf16[128,512]{1,0:T(8,128)(2,1)S(1)}, u32[]{:S(2)}, u32[]{:S(2)}) %collective-permute-start.28) | collective-permute-done | bytes 131104 | tf_op jit(solution)/shard_map/ppermute | solution.py:22
  149.6 1.9 %collective-permute-done.27 = bf16[128,512]{1,0:T(8,128)(2,1)S(1)} collective-permute-done((bf16[128,512]{1,0:T(8,128)(2,1)S(1)}, bf16[128,512]{1,0:T(8,128)(2,1)S(1)}, u32[]{:S(2)}, u32[]{:S(2)}) %collective-permute-start.27) | collective-permute-done | bytes 131104 | tf_op jit(solution)/shard_map/ppermute | solution.py:22
  152.4 5.6 %project_out.1 = bf16[128,1024]{1,0:T(8,128)(2,1)} custom-call(s32[5]{0:T(128)} %stack.90.place, bf16[128,1024]{1,0:T(8,128)(2,1)} %tokens.1, bf16[4,128,512]{2,1,0:T(8,128)(2,1)} %pad_maximum_fusion.1.gated, bf16[4,4,4,64,512]{4,3,2,1,0:T(8,128)(2,1)} %bitcast.50), custom_call_target="tpu_custom_call" | custom-call | flops 536870912 | bytes 5242880 | tf_op jit(solution)/shard_map/project_out/pallas_call | solution.py:321
  (104 shorter events, 17.6 us)
Async XLA Ops:
  6.5 66.0 %all-gather.5.cloned.1.call-start = ((), (), s32[]{:S(2)}) async-start(), calls=%async_computation.1 | async-start | bytes 5570560 | tf_op jit(solution)/shard_map/all_gather | solution.py:233
  8.4 6.6 %collective-permute-start.2 = (bf16[80,512]{1,0:T(8,128)(2,1)S(1)}, bf16[80,512]{1,0:T(8,128)(2,1)S(1)}, u32[]{:S(2)}, u32[]{:S(2)}) collective-permute-start(bf16[80,512]{1,0:T(8,128)(2,1)S(1)} %get-tuple-element.86), channel_id=1, source_target_pairs={{0,192},{64,0},{128,64},{192,128},{1,193},{65,1},{129,65},{193,129... | collective-permute-start | bytes 245768 | tf_op jit(solution)/shard_map/ppermute | solution.py:229
  11.5 6.3 %collective-permute-start.1 = (bf16[80,512]{1,0:T(8,128)(2,1)S(1)}, bf16[80,512]{1,0:T(8,128)(2,1)S(1)}, u32[]{:S(2)}, u32[]{:S(2)}) collective-permute-start(bf16[80,512]{1,0:T(8,128)(2,1)S(1)} %get-tuple-element.85), channel_id=1, source_target_pairs={{0,128},{64,192},{128,0},{192,64},{1,129},{65,193},{129,1},{193,65... | collective-permute-start | bytes 245768 | tf_op jit(solution)/shard_map/ppermute | solution.py:229
  12.1 6.5 %collective-permute-start = (bf16[80,512]{1,0:T(8,128)(2,1)S(1)}, bf16[80,512]{1,0:T(8,128)(2,1)S(1)}, u32[]{:S(2)}, u32[]{:S(2)}) collective-permute-start(bf16[80,512]{1,0:T(8,128)(2,1)S(1)} %get-tuple-element.84), channel_id=1, source_target_pairs={{0,64},{64,128},{128,192},{192,0},{1,65},{65,129},{129,193},{193,1... | collective-permute-start | bytes 245768 | tf_op jit(solution)/shard_map/ppermute | solution.py:229
  19.5 120.9 %all-gather.7.cloned.1.call-start = ((), (), s32[]{:S(2)}) async-start(), calls=%async_computation.2 | async-start | bytes 4456448 | tf_op jit(solution)/shard_map/all_gather | solution.py:271
  20.5 13.9 %collective-permute-start.3 = (bf16[128,512]{1,0:T(8,128)(2,1)S(1)}, bf16[128,512]{1,0:T(8,128)(2,1)S(1)}, u32[]{:S(2)}, u32[]{:S(2)}) collective-permute-start(bf16[128,512]{1,0:T(8,128)(2,1)S(1)} %get-tuple-element.40), channel_id=1, source_target_pairs={{0,64},{64,128},{128,192},{192,0},{1,65},{65,129},{129,193},{193,1... | collective-permute-start | bytes 393224 | tf_op jit(solution)/shard_map/ppermute | solution.py:22
  20.6 8.6 %collective-permute-start.9 = (bf16[64,512]{1,0:T(8,128)(2,1)}, bf16[64,512]{1,0:T(8,128)(2,1)S(1)}, u32[]{:S(2)}, u32[]{:S(2)}) collective-permute-start(bf16[64,512]{1,0:T(8,128)(2,1)} %bitcast.69), channel_id=1, source_target_pairs={{0,0},{64,1},{128,2},{192,3},{1,64},{65,65},{129,66},{193,67},{2,1... | collective-permute-start | bytes 196616 | tf_op jit(solution)/shard_map/ppermute | solution.py:236
  22.1 12.3 %collective-permute-start.4 = (bf16[128,512]{1,0:T(8,128)(2,1)S(1)}, bf16[128,512]{1,0:T(8,128)(2,1)S(1)}, u32[]{:S(2)}, u32[]{:S(2)}) collective-permute-start(bf16[128,512]{1,0:T(8,128)(2,1)S(1)} %get-tuple-element.40), channel_id=1, source_target_pairs={{0,128},{64,192},{128,0},{192,64},{1,129},{65,193},{129,1},{193,65... | collective-permute-start | bytes 393224 | tf_op jit(solution)/shard_map/ppermute | solution.py:22
  28.6 5.9 %collective-permute-start.5 = (bf16[128,512]{1,0:T(8,128)(2,1)S(1)}, bf16[128,512]{1,0:T(8,128)(2,1)S(1)}, u32[]{:S(2)}, u32[]{:S(2)}) collective-permute-start(bf16[128,512]{1,0:T(8,128)(2,1)S(1)} %get-tuple-element.40), channel_id=1, source_target_pairs={{0,192},{64,0},{128,64},{192,128},{1,193},{65,1},{129,65},{193,129... | collective-permute-start | bytes 393224 | tf_op jit(solution)/shard_map/ppermute | solution.py:22
  28.6 8.7 %collective-permute-start.6 = (bf16[128,512]{1,0:T(8,128)(2,1)S(1)}, bf16[128,512]{1,0:T(8,128)(2,1)S(1)}, u32[]{:S(2)}, u32[]{:S(2)}) collective-permute-start(bf16[128,512]{1,0:T(8,128)(2,1)S(1)} %get-tuple-element.44), channel_id=1, source_target_pairs={{0,1},{1,2},{2,3},{3,0},{4,5},{5,6},{6,7},{7,4},{8,9},{9,10},{10,1... | collective-permute-start | bytes 393224 | tf_op jit(solution)/shard_map/ppermute | solution.py:22
  29.3 9.6 %collective-permute-start.7 = (bf16[128,512]{1,0:T(8,128)(2,1)S(1)}, bf16[128,512]{1,0:T(8,128)(2,1)S(1)}, u32[]{:S(2)}, u32[]{:S(2)}) collective-permute-start(bf16[128,512]{1,0:T(8,128)(2,1)S(1)} %get-tuple-element.44), channel_id=1, source_target_pairs={{0,2},{1,3},{2,0},{3,1},{4,6},{5,7},{6,4},{7,5},{8,10},{9,11},{10,... | collective-permute-start | bytes 393224 | tf_op jit(solution)/shard_map/ppermute | solution.py:22
  39.7 16.3 %collective-permute-start.10 = (bf16[512,512]{1,0:T(8,128)(2,1)S(1)}, bf16[512,512]{1,0:T(8,128)(2,1)S(1)}, u32[]{:S(2)}, u32[]{:S(2)}) collective-permute-start(bf16[512,512]{1,0:T(8,128)(2,1)S(1)} %constant_dynamic-update-slice_fusion.a0), channel_id=1, source_target_pairs={{0,1},{1,2},{2,3},{3,0},{4,5},{5,6},{6,7},{7,4},{8,9},{9,10},{10,1... | collective-permute-start | bytes 1572872 | tf_op jit(solution)/shard_map/ppermute | solution.py:22
  40.3 23.3 %collective-permute-start.11 = (bf16[512,512]{1,0:T(8,128)(2,1)S(1)}, bf16[512,512]{1,0:T(8,128)(2,1)S(1)}, u32[]{:S(2)}, u32[]{:S(2)}) collective-permute-start(bf16[512,512]{1,0:T(8,128)(2,1)S(1)} %constant_dynamic-update-slice_fusion.a0), channel_id=1, source_target_pairs={{0,2},{1,3},{2,0},{3,1},{4,6},{5,7},{6,4},{7,5},{8,10},{9,11},{10,... | collective-permute-start | bytes 1572872 | tf_op jit(solution)/shard_map/ppermute | solution.py:22
  43.7 20.4 %collective-permute-start.12 = (bf16[512,512]{1,0:T(8,128)(2,1)S(1)}, bf16[512,512]{1,0:T(8,128)(2,1)S(1)}, u32[]{:S(2)}, u32[]{:S(2)}) collective-permute-start(bf16[512,512]{1,0:T(8,128)(2,1)S(1)} %constant_dynamic-update-slice_fusion.a0), channel_id=1, source_target_pairs={{0,3},{1,0},{2,1},{3,2},{4,7},{5,4},{6,5},{7,6},{8,11},{9,8},{10,9... | collective-permute-start | bytes 1572872 | tf_op jit(solution)/shard_map/ppermute | solution.py:22
  43.8 20.2 %collective-permute-start.13 = (bf16[512,512]{1,0:T(8,128)(2,1)S(1)}, bf16[512,512]{1,0:T(8,128)(2,1)S(1)}, u32[]{:S(2)}, u32[]{:S(2)}) collective-permute-start(bf16[512,512]{1,0:T(8,128)(2,1)S(1)} %constant_dynamic-update-slice_fusion.4.b0), channel_id=1, source_target_pairs={{0,64},{64,128},{128,192},{192,0},{1,65},{65,129},{129,193},{193,1... | collective-permute-start | bytes 1572872 | tf_op jit(solution)/shard_map/ppermute | solution.py:22
  44.0 24.4 %collective-permute-start.14 = (bf16[512,512]{1,0:T(8,128)(2,1)S(1)}, bf16[512,512]{1,0:T(8,128)(2,1)}, u32[]{:S(2)}, u32[]{:S(2)}) collective-permute-start(bf16[512,512]{1,0:T(8,128)(2,1)S(1)} %constant_dynamic-update-slice_fusion.4.b0), channel_id=1, source_target_pairs={{0,128},{64,192},{128,0},{192,64},{1,129},{65,193},{129,1},{193,65... | collective-permute-start | bytes 1572872 | tf_op jit(solution)/shard_map/ppermute | solution.py:22
  56.0 12.3 %collective-permute-start.15 = (bf16[512,512]{1,0:T(8,128)(2,1)S(1)}, bf16[512,512]{1,0:T(8,128)(2,1)}, u32[]{:S(2)}, u32[]{:S(2)}) collective-permute-start(bf16[512,512]{1,0:T(8,128)(2,1)S(1)} %constant_dynamic-update-slice_fusion.4.b0), channel_id=1, source_target_pairs={{0,192},{64,0},{128,64},{192,128},{1,193},{65,1},{129,65},{193,129... | collective-permute-start | bytes 1572872 | tf_op jit(solution)/shard_map/ppermute | solution.py:22
  68.4 12.1 %collective-permute-start.21 = (bf16[64,512]{1,0:T(8,128)(2,1)S(1)}, bf16[64,512]{1,0:T(8,128)(2,1)S(1)}, u32[]{:S(2)}, u32[]{:S(2)}) collective-permute-start(bf16[64,512]{1,0:T(8,128)(2,1)S(1)} %collective-permute-done.9), channel_id=1, source_target_pairs={{0,64},{64,128},{128,192},{192,0},{1,65},{65,129},{129,193},{193,1... | collective-permute-start | bytes 196616 | tf_op jit(solution)/shard_map/ppermute | solution.py:22
  68.4 12.1 %collective-permute-start.22 = (bf16[64,512]{1,0:T(8,128)(2,1)S(1)}, bf16[64,512]{1,0:T(8,128)(2,1)S(1)}, u32[]{:S(2)}, u32[]{:S(2)}) collective-permute-start(bf16[64,512]{1,0:T(8,128)(2,1)S(1)} %collective-permute-done.9), channel_id=1, source_target_pairs={{0,128},{64,192},{128,0},{192,64},{1,129},{65,193},{129,1},{193,65... | collective-permute-start | bytes 196616 | tf_op jit(solution)/shard_map/ppermute | solution.py:22
  72.6 7.9 %collective-permute-start.23 = (bf16[64,512]{1,0:T(8,128)(2,1)S(1)}, bf16[64,512]{1,0:T(8,128)(2,1)S(1)}, u32[]{:S(2)}, u32[]{:S(2)}) collective-permute-start(bf16[64,512]{1,0:T(8,128)(2,1)S(1)} %collective-permute-done.9), channel_id=1, source_target_pairs={{0,192},{64,0},{128,64},{192,128},{1,193},{65,1},{129,65},{193,129... | collective-permute-start | bytes 196616 | tf_op jit(solution)/shard_map/ppermute | solution.py:22
  82.7 13.0 %collective-permute-start.16 = (bf16[4,128,256]{2,1,0:T(8,128)(2,1)}, bf16[4,128,256]{2,1,0:T(8,128)(2,1)S(1)}, u32[]{:S(2)}, u32[]{:S(2)}) collective-permute-start(bf16[4,128,256]{2,1,0:T(8,128)(2,1)} %get-tuple-element.57), channel_id=1, source_target_pairs={{0,32},{32,0},{1,33},{33,1},{2,34},{34,2},{3,35},{35,3},{4,36},{36... | collective-permute-start | bytes 786440 | tf_op jit(solution)/shard_map/ppermute | solution.py:28
  83.2 12.4 %collective-permute-start.17 = (bf16[4,128,128]{2,1,0:T(8,128)(2,1)}, bf16[4,128,128]{2,1,0:T(8,128)(2,1)S(1)}, u32[]{:S(2)}, u32[]{:S(2)}) collective-permute-start(bf16[4,128,128]{2,1,0:T(8,128)(2,1)} %get-tuple-element.56.q0), channel_id=1, source_target_pairs={{0,4},{4,8},{8,12},{12,0},{1,5},{5,9},{9,13},{13,1},{2,6},{6,10},{... | collective-permute-start | bytes 393224 | tf_op jit(solution)/shard_map/ppermute | solution.py:22
  86.4 16.3 %collective-permute-start.18 = (bf16[4,128,128]{2,1,0:T(8,128)(2,1)}, bf16[4,128,128]{2,1,0:T(8,128)(2,1)S(1)}, u32[]{:S(2)}, u32[]{:S(2)}) collective-permute-start(bf16[4,128,128]{2,1,0:T(8,128)(2,1)} %get-tuple-element.56.q0), channel_id=1, source_target_pairs={{0,8},{4,12},{8,0},{12,4},{1,9},{5,13},{9,1},{13,5},{2,10},{6,14},... | collective-permute-start | bytes 393224 | tf_op jit(solution)/shard_map/ppermute | solution.py:22
  91.4 11.3 %collective-permute-start.19 = (bf16[4,128,128]{2,1,0:T(8,128)(2,1)}, bf16[4,128,128]{2,1,0:T(8,128)(2,1)S(1)}, u32[]{:S(2)}, u32[]{:S(2)}) collective-permute-start(bf16[4,128,128]{2,1,0:T(8,128)(2,1)} %get-tuple-element.56.q0), channel_id=1, source_target_pairs={{0,12},{4,0},{8,4},{12,8},{1,13},{5,1},{9,5},{13,9},{2,14},{6,2},{... | collective-permute-start | bytes 393224 | tf_op jit(solution)/shard_map/ppermute | solution.py:22
  96.7 6.0 %collective-permute-start.20 = (bf16[2,4,128,256]{3,2,1,0:T(8,128)(2,1)S(1)}, bf16[2,4,128,256]{3,2,1,0:T(8,128)(2,1)S(1)}, u32[]{:S(2)}, u32[]{:S(2)}) collective-permute-start(bf16[2,4,128,256]{3,2,1,0:T(8,128)(2,1)S(1)} %pad_maximum_fusion.kv_near), channel_id=1, source_target_pairs={{0,16},{16,0},{1,17},{17,1},{2,18},{18,2},{3,19},{19,3},{4,20},{20... | collective-permute-start | bytes 1572872 | tf_op jit(solution)/shard_map/ppermute | solution.py:28
  112.2 28.1 %all-to-all-start = ((bf16[16,128,128]{2,1,0:T(8,128)(2,1)}), bf16[16,128,128]{2,1,0:T(8,128)(2,1)S(1)}, u32[]{:S(2)}, u32[]{:S(2)}) async-start(bf16[16,128,128]{2,1,0:T(8,128)(2,1)} %attend.1), calls=%async_computation | async-start | bytes 1048576 | tf_op jit(solution)/shard_map/all_to_all | solution.py:306
  125.2 15.1 %collective-permute-start.24 = (bf16[128,128]{1,0:T(8,128)(2,1)S(1)}, bf16[128,128]{1,0:T(8,128)(2,1)S(1)}, u32[]{:S(2)}, u32[]{:S(2)}) collective-permute-start(bf16[128,128]{1,0:T(8,128)(2,1)S(1)} %get-tuple-element.77), channel_id=1, source_target_pairs={{0,192},{64,0},{128,64},{192,128},{1,193},{65,1},{129,65},{193,129... | collective-permute-start | bytes 98312 | tf_op jit(solution)/shard_map/ppermute | solution.py:304
  128.4 11.9 %collective-permute-start.25 = (bf16[128,128]{1,0:T(8,128)(2,1)S(1)}, bf16[128,128]{1,0:T(8,128)(2,1)S(1)}, u32[]{:S(2)}, u32[]{:S(2)}) collective-permute-start(bf16[128,128]{1,0:T(8,128)(2,1)S(1)} %get-tuple-element.76), channel_id=1, source_target_pairs={{0,128},{64,192},{128,0},{192,64},{1,129},{65,193},{129,1},{193,65... | collective-permute-start | bytes 98312 | tf_op jit(solution)/shard_map/ppermute | solution.py:304
  129.3 11.1 %collective-permute-start.26 = (bf16[128,128]{1,0:T(8,128)(2,1)S(1)}, bf16[128,128]{1,0:T(8,128)(2,1)S(1)}, u32[]{:S(2)}, u32[]{:S(2)}) collective-permute-start(bf16[128,128]{1,0:T(8,128)(2,1)S(1)} %get-tuple-element.75), channel_id=1, source_target_pairs={{0,64},{64,128},{128,192},{192,0},{1,65},{65,129},{129,193},{193,1... | collective-permute-start | bytes 98312 | tf_op jit(solution)/shard_map/ppermute | solution.py:304
  141.2 5.5 %collective-permute-start.29 = (bf16[128,512]{1,0:T(8,128)(2,1)S(1)}, bf16[128,512]{1,0:T(8,128)(2,1)S(1)}, u32[]{:S(2)}, u32[]{:S(2)}) collective-permute-start(bf16[128,512]{1,0:T(8,128)(2,1)S(1)} %gate.1), channel_id=1, source_target_pairs={{0,3},{1,0},{2,1},{3,2},{4,7},{5,4},{6,5},{7,6},{8,11},{9,8},{10,9... | collective-permute-start | bytes 393224 | tf_op jit(solution)/shard_map/ppermute | solution.py:22
  143.2 6.5 %collective-permute-start.28 = (bf16[128,512]{1,0:T(8,128)(2,1)S(1)}, bf16[128,512]{1,0:T(8,128)(2,1)S(1)}, u32[]{:S(2)}, u32[]{:S(2)}) collective-permute-start(bf16[128,512]{1,0:T(8,128)(2,1)S(1)} %gate.1), channel_id=1, source_target_pairs={{0,2},{1,3},{2,0},{3,1},{4,6},{5,7},{6,4},{7,5},{8,10},{9,11},{10,... | collective-permute-start | bytes 393224 | tf_op jit(solution)/shard_map/ppermute | solution.py:22
  145.4 6.2 %collective-permute-start.27 = (bf16[128,512]{1,0:T(8,128)(2,1)S(1)}, bf16[128,512]{1,0:T(8,128)(2,1)S(1)}, u32[]{:S(2)}, u32[]{:S(2)}) collective-permute-start(bf16[128,512]{1,0:T(8,128)(2,1)S(1)} %gate.1), channel_id=1, source_target_pairs={{0,1},{1,2},{2,3},{3,0},{4,5},{5,6},{6,7},{7,4},{8,9},{9,10},{10,1... | collective-permute-start | bytes 393224 | tf_op jit(solution)/shard_map/ppermute | solution.py:22
  (12 other events, 339.0 us)
Sparse Core Ops, SparseCore 0:
  19.6 43.4 all-gather.4
  81.4 54.1 all-gather.6

commit v8 on v4

--- a/solution.py
+++ b/solution.py
@@ -36,7 +36,7 @@
         second = jnp.concatenate([b[kx * RUN : (kx + 1) * RUN, :] for b in seconds], axis=0)
         for m in range(4):
             left = first[...] if m < 2 else second
-            right = jnp.concatenate([weights[j * 4 + m, ky] for j in range(4)], axis=0)
+            right = jnp.concatenate([weights[j * 4 + m, ky, :64, :] for j in range(4)], axis=0)
             part = jnp.dot(
                 left[:, (m & 1) * 256 : (m & 1) * 256 + 256], right, preferred_element_type=jnp.float32
             )
@@ -106,8 +106,8 @@
             values = jnp.concatenate([near[:, :DH], far[:, :DH]], axis=0)
             k_first = t * 1024 + zh * RUN
             k_last = k_first + BLOCK + RUN - 1
-            gap_low = jnp.clip(q_low - k_edges[ky, zx * 2 + 1], 0, NB - 1)
-            gap_high = jnp.clip(q_high - k_edges[ky, zx * 2], 0, NB - 1)
+            gap_low = jnp.clip(q_low - k_edges[ky, zl_from * 2 + 1], 0, NB - 1)
+            gap_high = jnp.clip(q_high - k_edges[ky, zl_from * 2], 0, NB - 1)
             plain = (k_last <= first) & (k_first >= start_high) & (gap_low == gap_high)
 
             def scores(part):
@@ -130,7 +130,7 @@
 
             @pl.when(jnp.logical_not(plain))
             def _():
-                k_row = k_ids[ky, pl.ds(zx, 1), :]
+                k_row = k_ids[ky, pl.ds(zl_from, 1), :]
                 column = lax.broadcasted_iota(jnp.int32, (1, PAIR), 1)
                 k_pos = k_first + ((column >> 7) ^ core) * BLOCK + (column & (RUN - 1))
                 for part in range(2):
@@ -215,8 +215,12 @@
     place = jnp.stack([y, zl, core, zh, x]).astype(jnp.int32)
     plane = ("zh", "zl", "core")
 
+    ids = jnp.stack([bucket_ids // 128, bucket_ids % 128]).astype(bf16)
+    ids = jnp.concatenate([ids, jnp.zeros((14, BLOCK), bf16)], axis=0)
+
     def columns(owner):
-        return lax.dynamic_slice_in_dim(w_uvqk, owner * 512, 512, 1)
+        part = lax.dynamic_slice_in_dim(w_uvqk, owner * 512, 512, 1)
+        return jnp.concatenate([part, ids], axis=0)
 
     pieces = [columns(y)] + [
         lax.ppermute(columns((y + k) & 3), "y", [(i, (i + k) % 4) for i in range(4)])
@@ -225,22 +229,22 @@
     piece = jnp.stack(pieces)
     weights = lax.all_gather(piece, plane)
 
-    first = rotations(tokens[:, :512], "y", 4)
-    second = rotations(tokens[:, 512:], "x", 4)
+    travelling, _ = lax.optimization_barrier((tokens, piece))
+
+    first = rotations(travelling[:, :512], "y", 4)
+    second = rotations(travelling[:, 512:], "x", 4)
     first, second = lax.optimization_barrier((first, second))
     firsts = rotations(jnp.concatenate(first, axis=0), "x", 4)
     seconds = rotations(jnp.concatenate(second, axis=0), "y", 4)
 
-    ids, late, _ = lax.optimization_barrier((bucket_ids, w_out.T, (firsts[1:3], seconds[1:3])))
-    ids_y = jnp.stack(rotations(ids, "y", 4))
-    ids_near = jnp.stack([ids_y, swap(ids_y, "zl")])
-    ids_far = swap(ids_near, "core")
-    swapped = lax.ppermute(late, ("y", "x"), [(b * 4 + a, a * 4 + b) for a in range(4) for b in range(4)])
-    wo_rows = jnp.stack(rotations(swapped, "y", 4))
-
-    firsts, seconds, ids_y, ids_near, ids_far, wo_rows = lax.optimization_barrier(
-        (firsts, seconds, ids_y, ids_near, ids_far, wo_rows)
-    )
+    late, firsts, seconds = lax.optimization_barrier((w_out.T, firsts, seconds))
+    wo_rows = [
+        lax.ppermute(
+            late, ("y", "x"), [(b * 4 + a, (a + k) % 4 * 4 + b) for a in range(4) for b in range(4)]
+        )
+        for k in range(4)
+    ]
+
     kv, q, u = call(
         project_kernel,
         [
@@ -258,18 +262,21 @@
     )(place, *firsts, *seconds, weights)
 
     wo_rows, _ = lax.optimization_barrier((wo_rows, kv))
-    wo_all = lax.all_gather(wo_rows, plane)
+    wo_all = lax.all_gather(jnp.stack(wo_rows), plane)
 
     kv_near = jnp.stack([kv, swap(kv, "zl")])
     kv_far = swap(kv_near, "core")
     q_all = rotations(q, "zh", 4)
-
-    q_ids = ids_y.reshape(4, BLOCK, 1)
-    k_ids = lax.dynamic_slice(jnp.stack([ids_near, ids_far]), (0, 0, 0, zh * RUN), (2, 2, 4, RUN))
-    k_edges = jnp.stack([jnp.min(k_ids[..., 0], axis=0), jnp.max(k_ids[..., -1], axis=0)], axis=-1)
-    k_edges = k_edges.transpose(1, 0, 2).reshape(4, 4)
-    k_ids = k_ids.transpose(2, 1, 0, 3).reshape(4, 2, PAIR)
-    q_edges = jnp.stack([ids_y[:, 0], ids_y[:, -1]], axis=1)
+    kv_far, q_all[1], q_all[2] = lax.optimization_barrier((kv_far, q_all[1], q_all[2]))
+
+    coded = weights[:4, :, 64:66].astype(f32)
+    all_ids = (coded[:, :, 0] * 128 + coded[:, :, 1]).astype(jnp.int32).transpose(1, 0, 2)
+    q_ids = lax.dynamic_slice(all_ids, (0, zl * 2 + core, 0), (4, 1, BLOCK)).reshape(4, BLOCK, 1)
+    q_edges = jnp.concatenate([q_ids[:, 0], q_ids[:, -1]], axis=1)
+    k_ids = lax.dynamic_slice(all_ids, (0, 0, zh * RUN), (4, 4, RUN))
+    k_edges = jnp.stack([k_ids[:, ::2, 0], k_ids[:, 1::2, -1]], axis=-1).reshape(4, 4)
+    k_ids = k_ids.reshape(4, 2, 2, RUN)
+    k_ids = jnp.where(core == 0, k_ids, k_ids[:, :, ::-1]).reshape(4, 2, PAIR)
     biases = lax.dynamic_slice(rab_table, (x * 4 + y, 0), (1, NB))
     gains = lax.dynamic_slice(norm_gain, (x * 4, 0), (4, DH))
     table = jnp.pad(biases, ((0, 0), (0, DH - NB)))
@@ -291,6 +298,7 @@
         lax.ppermute(u[k], "y", [(i, (i - k) % 4) for i in range(4)]) for k in range(1, 4)
     ]
     arrived = lax.all_to_all(parts, ("y", "zh"), 0, 0, tiled=True)
+    arrived, wo_all = lax.optimization_barrier((arrived, wo_all))
     gated = call(
         gate_kernel,
         jax.ShapeDtypeStruct((RUN, 4 * DH), bf16),

time: 180 us -> 169 us (0.939)
  starting transfers between devices: 75.6 us -> 62.9 us
  Pallas kernels: 17.9 us -> 20.5 us
    ppermute x24 -> x18, starting transfers between devices: 53.9 us -> 31 us  [rotations(): lax.ppermute(value, axis, [(i, (i + step * k) % size) for i in range(size)])]
    ppermute x1 -> x4, starting transfers between devices: 1.49 us -> 11.2 us  [on_device(): lax.ppermute(late, ('y', 'x'), [(b * 4 + a, (a + k) % 4 * 4 + b) for a in...]
    ppermute x3, waiting for transfers between devices: 5.04 us -> 0.01 us  [on_device(): lax.ppermute(u[k], 'y', [(i, (i - k) % 4) for i in range(4)])]
    ppermute x4 -> x2, waiting for transfers between devices: 4.99 us -> 0.01 us  [swap(): return lax.ppermute(value, axis, [(0, 1), (1, 0)])]
    ppermute x24 -> x18, waiting for transfers between devices: 36.8 us -> 41.5 us  [rotations(): lax.ppermute(value, axis, [(i, (i + step * k) % size) for i in range(size)])]
    all_to_all x1, waiting for transfers between devices: 6.01 us -> 9.12 us  [on_device(): arrived = lax.all_to_all(parts, ('y', 'zh'), 0, 0, tiled=True)]
    ppermute x3, waiting for transfers between devices: 2.92 us -> 5.56 us  [on_device(): lax.ppermute(columns(y + k & 3), 'y', [(i, (i + k) % 4) for i in range(4)])]
    pallas_call x1, Pallas kernels: 10.8 us -> 13.4 us  [on_device(): call(attend_kernel, jax.ShapeDtypeStruct((16, RUN, DH), bf16), 5, 9, [plt...]
  transfers between devices with their start and end apart: 38 -> 33, of which waited for: 21 -> 16; matrix products, arithmetic and copies ran while one was open for 4% -> 3% of each run, Pallas kernels for 6% -> 10%
where the time goes in v8:
time: 169 us
  starting transfers between devices  62.9 us (37%)
  waiting for transfers between devices  56.2 us (33%)
  Pallas kernels  20.5 us (12%)
  between operations  13.7 us (8%)
  local copies, waits for them, and re-layouts  10.6 us (6%)
  other arithmetic  4.58 us (3%)
    ppermute x18, waiting for transfers between devices, rotations(): lax.ppermute(value, axis, [(i, (i + step * k) % size) for i in range(size)])  41.5 us
    ppermute x18, starting transfers between devices, rotations(): lax.ppermute(value, axis, [(i, (i + step * k) % size) for i in range(size)])  31 us
    pallas_call x1, Pallas kernels, on_device(): call(attend_kernel, jax.ShapeDtypeStruct((16, RUN, DH), bf16), 5, 9, [plt...  13.4 us
    ppermute x4, starting transfers between devices, on_device(): lax.ppermute(late, ('y', 'x'), [(b * 4 + a, (a + k) % 4 * 4 + b) for a in...  11.2 us
    all_to_all x1, starting transfers between devices, on_device(): arrived = lax.all_to_all(parts, ('y', 'zh'), 0, 0, tiled=True)  10.9 us
    all_to_all x1, waiting for transfers between devices, on_device(): arrived = lax.all_to_all(parts, ('y', 'zh'), 0, 0, tiled=True)  9.12 us
    unnamed x21, local copies, waits for them, and re-layouts  6.3 us
    ppermute x3, waiting for transfers between devices, on_device(): lax.ppermute(columns(y + k & 3), 'y', [(i, (i + k) % 4) for i in range(4)])  5.56 us
  transfers between devices with their start and end apart: 33, of which 16 were waited for; matrix products, arithmetic and copies ran while one was open for 3% of the time, Pallas kernels for 10%

profile of v8, /device:TPU:32, one launch (start us, length us, event | category | flops | bytes accessed | tf_op | source)
XLA Modules:
  0.0 168.6 jit_solution(11872838456185689217)
XLA Ops:
  8.4 3.1 %collective-permute-start.2 = (bf16[80,512]{1,0:T(8,128)(2,1)S(1)}, bf16[80,512]{1,0:T(8,128)(2,1)S(1)}, u32[]{:S(2)}, u32[]{:S(2)}) collective-permute-start(bf16[80,512]{1,0:T(8,128)(2,1)S(1)} %get-tuple-element.84), channel_id=1, source_target_pairs={{0,192},{64,0},{128,64},{192,128},{1,193},{65,1},{129,65},{193,129... | collective-permute-start | bytes 245768 | tf_op jit(solution)/shard_map/ppermute | solution.py:226
  13.1 1.9 %collective-permute-done.2 = bf16[80,512]{1,0:T(8,128)(2,1)S(1)} collective-permute-done((bf16[80,512]{1,0:T(8,128)(2,1)S(1)}, bf16[80,512]{1,0:T(8,128)(2,1)S(1)}, u32[]{:S(2)}, u32[]{:S(2)}) %collective-permute-start.2) | collective-permute-done | bytes 81952 | tf_op jit(solution)/shard_map/ppermute | solution.py:226
  15.0 2.9 %collective-permute-done.1 = bf16[80,512]{1,0:T(8,128)(2,1)S(1)} collective-permute-done((bf16[80,512]{1,0:T(8,128)(2,1)S(1)}, bf16[80,512]{1,0:T(8,128)(2,1)S(1)}, u32[]{:S(2)}, u32[]{:S(2)}) %collective-permute-start.1) | collective-permute-done | bytes 81952 | tf_op jit(solution)/shard_map/ppermute | solution.py:226
  20.6 2.0 %collective-permute-start.4 = (bf16[128,512]{1,0:T(8,128)(2,1)S(1)}, bf16[128,512]{1,0:T(8,128)(2,1)S(1)}, u32[]{:S(2)}, u32[]{:S(2)}) collective-permute-start(bf16[128,512]{1,0:T(8,128)(2,1)S(1)} %get-tuple-element.37), channel_id=1, source_target_pairs={{0,128},{64,192},{128,0},{192,64},{1,129},{65,193},{129,1},{193,65... | collective-permute-start | bytes 393224 | tf_op jit(solution)/shard_map/ppermute | solution.py:22
  24.1 1.5 collective-permute-start.6
  25.6 2.7 %collective-permute-start.7 = (bf16[128,512]{1,0:T(8,128)(2,1)S(1)}, bf16[128,512]{1,0:T(8,128)(2,1)S(1)}, u32[]{:S(2)}, u32[]{:S(2)}) collective-permute-start(bf16[128,512]{1,0:T(8,128)(2,1)S(1)} %get-tuple-element.41), channel_id=1, source_target_pairs={{0,2},{1,3},{2,0},{3,1},{4,6},{5,7},{6,4},{7,5},{8,10},{9,11},{10,... | collective-permute-start | bytes 393224 | tf_op jit(solution)/shard_map/ppermute | solution.py:22
  29.4 2.8 %collective-permute-start.8 = (bf16[128,512]{1,0:T(8,128)(2,1)S(1)}, bf16[128,512]{1,0:T(8,128)(2,1)S(1)}, u32[]{:S(2)}, u32[]{:S(2)}) collective-permute-start(bf16[128,512]{1,0:T(8,128)(2,1)S(1)} %get-tuple-element.41), channel_id=1, source_target_pairs={{0,3},{1,0},{2,1},{3,2},{4,7},{5,4},{6,5},{7,6},{8,11},{9,8},{10,9... | collective-permute-start | bytes 393224 | tf_op jit(solution)/shard_map/ppermute | solution.py:22
  33.0 1.6 collective-permute-done.8
  34.7 1.5 collective-permute-start.9
  36.2 3.7 %collective-permute-start.10 = (bf16[512,512]{1,0:T(8,128)(2,1)S(1)}, bf16[512,512]{1,0:T(8,128)(2,1)S(1)}, u32[]{:S(2)}, u32[]{:S(2)}) collective-permute-start(bf16[512,512]{1,0:T(8,128)(2,1)S(1)} %constant_dynamic-update-slice_fusion.a0), channel_id=1, source_target_pairs={{0,2},{1,3},{2,0},{3,1},{4,6},{5,7},{6,4},{7,5},{8,10},{9,11},{10,... | collective-permute-start | bytes 1572872 | tf_op jit(solution)/shard_map/ppermute | solution.py:22
  41.4 9.0 %collective-permute-done.9.a1 = bf16[512,512]{1,0:T(8,128)(2,1)S(1)} collective-permute-done((bf16[512,512]{1,0:T(8,128)(2,1)S(1)}, bf16[512,512]{1,0:T(8,128)(2,1)S(1)}, u32[]{:S(2)}, u32[]{:S(2)}) %collective-permute-start.9) | collective-permute-done | bytes 524320 | tf_op jit(solution)/shard_map/ppermute | solution.py:22
  50.5 9.8 %collective-permute-done.10.a2 = bf16[512,512]{1,0:T(8,128)(2,1)S(1)} collective-permute-done((bf16[512,512]{1,0:T(8,128)(2,1)S(1)}, bf16[512,512]{1,0:T(8,128)(2,1)S(1)}, u32[]{:S(2)}, u32[]{:S(2)}) %collective-permute-start.10) | collective-permute-done | bytes 524320 | tf_op jit(solution)/shard_map/ppermute | solution.py:22
  60.3 3.2 %collective-permute-done.12.b1 = bf16[512,512]{1,0:T(8,128)(2,1)S(1)} collective-permute-done((bf16[512,512]{1,0:T(8,128)(2,1)S(1)}, bf16[512,512]{1,0:T(8,128)(2,1)S(1)}, u32[]{:S(2)}, u32[]{:S(2)}) %collective-permute-start.12) | collective-permute-done | bytes 524320 | tf_op jit(solution)/shard_map/ppermute | solution.py:22
  64.2 2.1 %collective-permute-start.20 = (bf16[64,512]{1,0:T(8,128)(2,1)}, bf16[64,512]{1,0:T(8,128)(2,1)}, u32[]{:S(2)}, u32[]{:S(2)}) collective-permute-start(bf16[64,512]{1,0:T(8,128)(2,1)} %bitcast.64), channel_id=1, source_target_pairs={{0,0},{64,1},{128,2},{192,3},{1,64},{65,65},{129,66},{193,67},{2,1... | collective-permute-start | bytes 196616 | tf_op jit(solution)/shard_map/ppermute | solution.py:242
  66.3 4.2 %collective-permute-start.21 = (bf16[64,512]{1,0:T(8,128)(2,1)}, bf16[64,512]{1,0:T(8,128)(2,1)}, u32[]{:S(2)}, u32[]{:S(2)}) collective-permute-start(bf16[64,512]{1,0:T(8,128)(2,1)} %bitcast.65), channel_id=1, source_target_pairs={{0,64},{64,65},{128,66},{192,67},{1,128},{65,129},{129,130},{193,1... | collective-permute-start | bytes 196616 | tf_op jit(solution)/shard_map/ppermute | solution.py:242
  70.5 4.3 %collective-permute-start.22 = (bf16[64,512]{1,0:T(8,128)(2,1)}, bf16[64,512]{1,0:T(8,128)(2,1)}, u32[]{:S(2)}, u32[]{:S(2)}) collective-permute-start(bf16[64,512]{1,0:T(8,128)(2,1)} %bitcast.66), channel_id=1, source_target_pairs={{0,128},{64,129},{128,130},{192,131},{1,192},{65,193},{129,194},{1... | collective-permute-start | bytes 196616 | tf_op jit(solution)/shard_map/ppermute | solution.py:242
  75.4 2.5 %copy-done.1 = bf16[64,80,512]{2,1,0:T(8,128)(2,1)S(1)} copy-done((bf16[64,80,512]{2,1,0:T(8,128)(2,1)S(1)}, bf16[64,80,512]{2,1,0:T(8,128)(2,1)}, u32[]{:S(2)}) %copy-start.1) | copy-done | bytes 5242904
  77.9 3.6 %project.1 = (bf16[4,128,256]{2,1,0:T(8,128)(2,1)S(1)}, bf16[4,128,128]{2,1,0:T(8,128)(2,1)S(1)}, bf16[4,128,128]{2,1,0:T(8,128)(2,1)S(1)}) custom-call(s32[5]{0:T(128)S(1)} %stack.90.place, bf16[512,512]{1,0:T(8,128)(2,1)S(1)} %constant_dynamic-update-slice_fusion.a0, bf16[512,512]{1,0:T(8,128)(2,1)S(1)} %collective-permute-done.9.a1, ...), custom_call_target="tpu_custom_call" | custom-call | flops 2147483648 | bytes 9437184 | tf_op jit(solution)/shard_map/project/pallas_call | solution.py:248
  82.2 1.7 %pad_maximum_fusion.3 = bf16[4,64,512]{2,1,0:T(8,128)(2,1)} fusion(bf16[1,64,512]{2,1,0:T(8,128)(2,1)} %bitcast.24, bf16[1,64,512]{2,1,0:T(8,128)(2,1)} %bitcast.23, bf16[1,64,512]{2,1,0:T(8,128)(2,1)} %bitcast.22, bf16[1,64,512]{2,1,0:T(8,128)(2,1)} %bitcast.21), kind=kLoop, calls=%fused_computation.3 | loop fusion | flops 393216 | bytes 524288 | tf_op jit(solution)/shard_map/stack | solution.py:265
  85.4 3.6 %collective-permute-start.17 = (bf16[4,128,128]{2,1,0:T(8,128)(2,1)}, bf16[4,128,128]{2,1,0:T(8,128)(2,1)S(1)}, u32[]{:S(2)}, u32[]{:S(2)}) collective-permute-start(bf16[4,128,128]{2,1,0:T(8,128)(2,1)} %copy-done.4), channel_id=1, source_target_pairs={{0,4},{4,8},{8,12},{12,0},{1,5},{5,9},{9,13},{13,1},{2,6},{6,10},{... | collective-permute-start | bytes 393224 | tf_op jit(solution)/shard_map/ppermute | solution.py:22
  89.1 5.4 %collective-permute-start.18 = (bf16[4,128,128]{2,1,0:T(8,128)(2,1)}, bf16[4,128,128]{2,1,0:T(8,128)(2,1)S(1)}, u32[]{:S(2)}, u32[]{:S(2)}) collective-permute-start(bf16[4,128,128]{2,1,0:T(8,128)(2,1)} %copy-done.4), channel_id=1, source_target_pairs={{0,8},{4,12},{8,0},{12,4},{1,9},{5,13},{9,1},{13,5},{2,10},{6,14},... | collective-permute-start | bytes 393224 | tf_op jit(solution)/shard_map/ppermute | solution.py:22
  94.5 2.7 %collective-permute-start.19 = (bf16[4,128,128]{2,1,0:T(8,128)(2,1)}, bf16[4,128,128]{2,1,0:T(8,128)(2,1)S(1)}, u32[]{:S(2)}, u32[]{:S(2)}) collective-permute-start(bf16[4,128,128]{2,1,0:T(8,128)(2,1)} %copy-done.4), channel_id=1, source_target_pairs={{0,12},{4,0},{8,4},{12,8},{1,13},{5,1},{9,5},{13,9},{2,14},{6,2},{... | collective-permute-start | bytes 393224 | tf_op jit(solution)/shard_map/ppermute | solution.py:22
  99.3 4.0 %collective-permute-done.18.q2 = bf16[4,128,128]{2,1,0:T(8,128)(2,1)S(1)} collective-permute-done((bf16[4,128,128]{2,1,0:T(8,128)(2,1)}, bf16[4,128,128]{2,1,0:T(8,128)(2,1)S(1)}, u32[]{:S(2)}, u32[]{:S(2)}) %collective-permute-start.18) | collective-permute-done | bytes 131104 | tf_op jit(solution)/shard_map/ppermute | solution.py:22
  103.3 5.3 %collective-permute-done.19.q3 = bf16[4,128,128]{2,1,0:T(8,128)(2,1)S(1)} collective-permute-done((bf16[4,128,128]{2,1,0:T(8,128)(2,1)}, bf16[4,128,128]{2,1,0:T(8,128)(2,1)S(1)}, u32[]{:S(2)}, u32[]{:S(2)}) %collective-permute-start.19) | collective-permute-done | bytes 131104 | tf_op jit(solution)/shard_map/ppermute | solution.py:22
  109.5 13.4 %attend.1 = bf16[16,128,128]{2,1,0:T(8,128)(2,1)} custom-call(s32[5]{0:T(128)S(1)} %stack.90.place, s32[4]{0:T(128)S(1)} %copy-done.6, s32[4,2]{1,0:T(4,128)S(1)} %pad_add_fusion.1.q_edges, s32[4,4]{1,0:T(4,128)S(1)} %copy.25.k_edges, f32[32]{0:T(128)S(1)} %fusion.11.biases, bf16[4,128,128]{2,1,0:T(8,128)(2,1)S(1)} %copy-done.5, ...), custom_call_target="tpu_custom_call" | custom-call | flops 1073741824 | bytes 5242880 | tf_op jit(solution)/shard_map/attend/pallas_call | solution.py:284
  123.0 10.9 %all-to-all-start = ((bf16[16,128,128]{2,1,0:T(8,128)(2,1)}), bf16[16,128,128]{2,1,0:T(8,128)(2,1)S(1)}, u32[]{:S(2)}, u32[]{:S(2)}) async-start(bf16[16,128,128]{2,1,0:T(8,128)(2,1)} %attend.1), calls=%async_computation | async-start | bytes 1048576 | tf_op jit(solution)/shard_map/all_to_all | solution.py:300
  133.8 3.2 %collective-permute-start.24 = (bf16[128,128]{1,0:T(8,128)(2,1)S(1)}, bf16[128,128]{1,0:T(8,128)(2,1)S(1)}, u32[]{:S(2)}, u32[]{:S(2)}) collective-permute-start(bf16[128,128]{1,0:T(8,128)(2,1)S(1)} %get-tuple-element.75), channel_id=1, source_target_pairs={{0,192},{64,0},{128,64},{192,128},{1,193},{65,1},{129,65},{193,129... | collective-permute-start | bytes 98312 | tf_op jit(solution)/shard_map/ppermute | solution.py:298
  138.8 9.1 %all-to-all-done.parts = bf16[16,128,128]{2,1,0:T(8,128)(2,1)S(1)} async-done(((bf16[16,128,128]{2,1,0:T(8,128)(2,1)}), bf16[16,128,128]{2,1,0:T(8,128)(2,1)S(1)}, u32[]{:S(2)}, u32[]{:S(2)}) %all-to-all-start) | async-done | bytes 524320 | tf_op jit(solution)/shard_map/all_to_all | solution.py:300
  150.8 2.9 %collective-permute-done.29 = bf16[128,512]{1,0:T(8,128)(2,1)S(1)} collective-permute-done((bf16[128,512]{1,0:T(8,128)(2,1)S(1)}, bf16[128,512]{1,0:T(8,128)(2,1)S(1)}, u32[]{:S(2)}, u32[]{:S(2)}) %collective-permute-start.29) | collective-permute-done | bytes 131104 | tf_op jit(solution)/shard_map/ppermute | solution.py:22
  153.8 1.6 collective-permute-done.28
  156.9 2.2 %copy-done.2 = bf16[64,64,512]{2,1,0:T(8,128)(2,1)S(1)} copy-done((bf16[64,64,512]{2,1,0:T(8,128)(2,1)S(1)}, bf16[64,64,512]{2,1,0:T(8,128)(2,1)}, u32[]{:S(2)}) %copy-start.2) | copy-done | bytes 4194328
  159.0 2.7 %project_out.1 = bf16[128,1024]{1,0:T(8,128)(2,1)} custom-call(s32[5]{0:T(128)S(1)} %stack.90.place, bf16[128,1024]{1,0:T(8,128)(2,1)S(1)} %copy-done.3, bf16[4,128,512]{2,1,0:T(8,128)(2,1)S(1)} %pad_maximum_fusion.1.gated, bf16[16,4,64,512]{3,2,1,0:T(8,128)(2,1)S(1)} %bitcast.48), custom_call_target="tpu_custom_call" | custom-call | flops 536870912 | bytes 5242880 | tf_op jit(solution)/shard_map/project_out/pallas_call | solution.py:315
  (96 shorter events, 23.7 us)
Async XLA Ops:
  6.5 68.8 %all-gather.5.cloned.1.call-start = ((), (), s32[]{:S(2)}) async-start(), calls=%async_computation.1 | async-start | bytes 5570560 | tf_op jit(solution)/shard_map/all_gather | solution.py:230
  8.4 6.6 %collective-permute-start.2 = (bf16[80,512]{1,0:T(8,128)(2,1)S(1)}, bf16[80,512]{1,0:T(8,128)(2,1)S(1)}, u32[]{:S(2)}, u32[]{:S(2)}) collective-permute-start(bf16[80,512]{1,0:T(8,128)(2,1)S(1)} %get-tuple-element.84), channel_id=1, source_target_pairs={{0,192},{64,0},{128,64},{192,128},{1,193},{65,1},{129,65},{193,129... | collective-permute-start | bytes 245768 | tf_op jit(solution)/shard_map/ppermute | solution.py:226
  11.5 6.3 %collective-permute-start.1 = (bf16[80,512]{1,0:T(8,128)(2,1)S(1)}, bf16[80,512]{1,0:T(8,128)(2,1)S(1)}, u32[]{:S(2)}, u32[]{:S(2)}) collective-permute-start(bf16[80,512]{1,0:T(8,128)(2,1)S(1)} %get-tuple-element.83), channel_id=1, source_target_pairs={{0,128},{64,192},{128,0},{192,64},{1,129},{65,193},{129,1},{193,65... | collective-permute-start | bytes 245768 | tf_op jit(solution)/shard_map/ppermute | solution.py:226
  12.1 6.5 %collective-permute-start = (bf16[80,512]{1,0:T(8,128)(2,1)S(1)}, bf16[80,512]{1,0:T(8,128)(2,1)S(1)}, u32[]{:S(2)}, u32[]{:S(2)}) collective-permute-start(bf16[80,512]{1,0:T(8,128)(2,1)S(1)} %get-tuple-element.82), channel_id=1, source_target_pairs={{0,64},{64,128},{128,192},{192,0},{1,65},{65,129},{129,193},{193,1... | collective-permute-start | bytes 245768 | tf_op jit(solution)/shard_map/ppermute | solution.py:226
  19.5 128.4 %all-gather.7.cloned.1.call-start = ((), (), s32[]{:S(2)}) async-start(), calls=%async_computation.2 | async-start | bytes 4456448 | tf_op jit(solution)/shard_map/all_gather | solution.py:265
  20.5 8.8 %collective-permute-start.3 = (bf16[128,512]{1,0:T(8,128)(2,1)S(1)}, bf16[128,512]{1,0:T(8,128)(2,1)S(1)}, u32[]{:S(2)}, u32[]{:S(2)}) collective-permute-start(bf16[128,512]{1,0:T(8,128)(2,1)S(1)} %get-tuple-element.37), channel_id=1, source_target_pairs={{0,64},{64,128},{128,192},{192,0},{1,65},{65,129},{129,193},{193,1... | collective-permute-start | bytes 393224 | tf_op jit(solution)/shard_map/ppermute | solution.py:22
  20.6 11.5 %collective-permute-start.4 = (bf16[128,512]{1,0:T(8,128)(2,1)S(1)}, bf16[128,512]{1,0:T(8,128)(2,1)S(1)}, u32[]{:S(2)}, u32[]{:S(2)}) collective-permute-start(bf16[128,512]{1,0:T(8,128)(2,1)S(1)} %get-tuple-element.37), channel_id=1, source_target_pairs={{0,128},{64,192},{128,0},{192,64},{1,129},{65,193},{129,1},{193,65... | collective-permute-start | bytes 393224 | tf_op jit(solution)/shard_map/ppermute | solution.py:22
  22.6 9.5 %collective-permute-start.5 = (bf16[128,512]{1,0:T(8,128)(2,1)S(1)}, bf16[128,512]{1,0:T(8,128)(2,1)S(1)}, u32[]{:S(2)}, u32[]{:S(2)}) collective-permute-start(bf16[128,512]{1,0:T(8,128)(2,1)S(1)} %get-tuple-element.37), channel_id=1, source_target_pairs={{0,192},{64,0},{128,64},{192,128},{1,193},{65,1},{129,65},{193,129... | collective-permute-start | bytes 393224 | tf_op jit(solution)/shard_map/ppermute | solution.py:22
  24.1 8.0 %collective-permute-start.6 = (bf16[128,512]{1,0:T(8,128)(2,1)S(1)}, bf16[128,512]{1,0:T(8,128)(2,1)S(1)}, u32[]{:S(2)}, u32[]{:S(2)}) collective-permute-start(bf16[128,512]{1,0:T(8,128)(2,1)S(1)} %get-tuple-element.41), channel_id=1, source_target_pairs={{0,1},{1,2},{2,3},{3,0},{4,5},{5,6},{6,7},{7,4},{8,9},{9,10},{10,1... | collective-permute-start | bytes 393224 | tf_op jit(solution)/shard_map/ppermute | solution.py:22
  25.6 7.4 %collective-permute-start.7 = (bf16[128,512]{1,0:T(8,128)(2,1)S(1)}, bf16[128,512]{1,0:T(8,128)(2,1)S(1)}, u32[]{:S(2)}, u32[]{:S(2)}) collective-permute-start(bf16[128,512]{1,0:T(8,128)(2,1)S(1)} %get-tuple-element.41), channel_id=1, source_target_pairs={{0,2},{1,3},{2,0},{3,1},{4,6},{5,7},{6,4},{7,5},{8,10},{9,11},{10,... | collective-permute-start | bytes 393224 | tf_op jit(solution)/shard_map/ppermute | solution.py:22
  29.4 5.3 %collective-permute-start.8 = (bf16[128,512]{1,0:T(8,128)(2,1)S(1)}, bf16[128,512]{1,0:T(8,128)(2,1)S(1)}, u32[]{:S(2)}, u32[]{:S(2)}) collective-permute-start(bf16[128,512]{1,0:T(8,128)(2,1)S(1)} %get-tuple-element.41), channel_id=1, source_target_pairs={{0,3},{1,0},{2,1},{3,2},{4,7},{5,4},{6,5},{7,6},{8,11},{9,8},{10,9... | collective-permute-start | bytes 393224 | tf_op jit(solution)/shard_map/ppermute | solution.py:22
  34.7 15.7 %collective-permute-start.9 = (bf16[512,512]{1,0:T(8,128)(2,1)S(1)}, bf16[512,512]{1,0:T(8,128)(2,1)S(1)}, u32[]{:S(2)}, u32[]{:S(2)}) collective-permute-start(bf16[512,512]{1,0:T(8,128)(2,1)S(1)} %constant_dynamic-update-slice_fusion.a0), channel_id=1, source_target_pairs={{0,1},{1,2},{2,3},{3,0},{4,5},{5,6},{6,7},{7,4},{8,9},{9,10},{10,1... | collective-permute-start | bytes 1572872 | tf_op jit(solution)/shard_map/ppermute | solution.py:22
  36.2 24.0 %collective-permute-start.10 = (bf16[512,512]{1,0:T(8,128)(2,1)S(1)}, bf16[512,512]{1,0:T(8,128)(2,1)S(1)}, u32[]{:S(2)}, u32[]{:S(2)}) collective-permute-start(bf16[512,512]{1,0:T(8,128)(2,1)S(1)} %constant_dynamic-update-slice_fusion.a0), channel_id=1, source_target_pairs={{0,2},{1,3},{2,0},{3,1},{4,6},{5,7},{6,4},{7,5},{8,10},{9,11},{10,... | collective-permute-start | bytes 1572872 | tf_op jit(solution)/shard_map/ppermute | solution.py:22
  39.9 20.4 %collective-permute-start.11 = (bf16[512,512]{1,0:T(8,128)(2,1)S(1)}, bf16[512,512]{1,0:T(8,128)(2,1)S(1)}, u32[]{:S(2)}, u32[]{:S(2)}) collective-permute-start(bf16[512,512]{1,0:T(8,128)(2,1)S(1)} %constant_dynamic-update-slice_fusion.a0), channel_id=1, source_target_pairs={{0,3},{1,0},{2,1},{3,2},{4,7},{5,4},{6,5},{7,6},{8,11},{9,8},{10,9... | collective-permute-start | bytes 1572872 | tf_op jit(solution)/shard_map/ppermute | solution.py:22
  40.2 23.2 %collective-permute-start.12 = (bf16[512,512]{1,0:T(8,128)(2,1)S(1)}, bf16[512,512]{1,0:T(8,128)(2,1)S(1)}, u32[]{:S(2)}, u32[]{:S(2)}) collective-permute-start(bf16[512,512]{1,0:T(8,128)(2,1)S(1)} %constant_dynamic-update-slice_fusion.4.b0), channel_id=1, source_target_pairs={{0,64},{64,128},{128,192},{192,0},{1,65},{65,129},{129,193},{193,1... | collective-permute-start | bytes 1572872 | tf_op jit(solution)/shard_map/ppermute | solution.py:22
  40.3 23.2 %collective-permute-start.13 = (bf16[512,512]{1,0:T(8,128)(2,1)S(1)}, bf16[512,512]{1,0:T(8,128)(2,1)}, u32[]{:S(2)}, u32[]{:S(2)}) collective-permute-start(bf16[512,512]{1,0:T(8,128)(2,1)S(1)} %constant_dynamic-update-slice_fusion.4.b0), channel_id=1, source_target_pairs={{0,128},{64,192},{128,0},{192,64},{1,129},{65,193},{129,1},{193,65... | collective-permute-start | bytes 1572872 | tf_op jit(solution)/shard_map/ppermute | solution.py:22
  50.4 13.8 %collective-permute-start.14 = (bf16[512,512]{1,0:T(8,128)(2,1)S(1)}, bf16[512,512]{1,0:T(8,128)(2,1)}, u32[]{:S(2)}, u32[]{:S(2)}) collective-permute-start(bf16[512,512]{1,0:T(8,128)(2,1)S(1)} %constant_dynamic-update-slice_fusion.4.b0), channel_id=1, source_target_pairs={{0,192},{64,0},{128,64},{192,128},{1,193},{65,1},{129,65},{193,129... | collective-permute-start | bytes 1572872 | tf_op jit(solution)/shard_map/ppermute | solution.py:22
  64.2 18.0 %collective-permute-start.20 = (bf16[64,512]{1,0:T(8,128)(2,1)}, bf16[64,512]{1,0:T(8,128)(2,1)}, u32[]{:S(2)}, u32[]{:S(2)}) collective-permute-start(bf16[64,512]{1,0:T(8,128)(2,1)} %bitcast.64), channel_id=1, source_target_pairs={{0,0},{64,1},{128,2},{192,3},{1,64},{65,65},{129,66},{193,67},{2,1... | collective-permute-start | bytes 196616 | tf_op jit(solution)/shard_map/ppermute | solution.py:242
  66.3 15.8 %collective-permute-start.21 = (bf16[64,512]{1,0:T(8,128)(2,1)}, bf16[64,512]{1,0:T(8,128)(2,1)}, u32[]{:S(2)}, u32[]{:S(2)}) collective-permute-start(bf16[64,512]{1,0:T(8,128)(2,1)} %bitcast.65), channel_id=1, source_target_pairs={{0,64},{64,65},{128,66},{192,67},{1,128},{65,129},{129,130},{193,1... | collective-permute-start | bytes 196616 | tf_op jit(solution)/shard_map/ppermute | solution.py:242
  70.5 11.6 %collective-permute-start.22 = (bf16[64,512]{1,0:T(8,128)(2,1)}, bf16[64,512]{1,0:T(8,128)(2,1)}, u32[]{:S(2)}, u32[]{:S(2)}) collective-permute-start(bf16[64,512]{1,0:T(8,128)(2,1)} %bitcast.66), channel_id=1, source_target_pairs={{0,128},{64,129},{128,130},{192,131},{1,192},{65,193},{129,194},{1... | collective-permute-start | bytes 196616 | tf_op jit(solution)/shard_map/ppermute | solution.py:242
  74.8 7.3 %collective-permute-start.23 = (bf16[64,512]{1,0:T(8,128)(2,1)}, bf16[64,512]{1,0:T(8,128)(2,1)}, u32[]{:S(2)}, u32[]{:S(2)}) collective-permute-start(bf16[64,512]{1,0:T(8,128)(2,1)} %bitcast.67), channel_id=1, source_target_pairs={{0,192},{64,193},{128,194},{192,195},{1,0},{65,1},{129,2},{193,3},... | collective-permute-start | bytes 196616 | tf_op jit(solution)/shard_map/ppermute | solution.py:242
  85.3 12.9 %collective-permute-start.15 = (bf16[4,128,256]{2,1,0:T(8,128)(2,1)S(1)}, bf16[4,128,256]{2,1,0:T(8,128)(2,1)S(1)}, u32[]{:S(2)}, u32[]{:S(2)}) collective-permute-start(bf16[4,128,256]{2,1,0:T(8,128)(2,1)S(1)} %get-tuple-element.54), channel_id=1, source_target_pairs={{0,32},{32,0},{1,33},{33,1},{2,34},{34,2},{3,35},{35,3},{4,36},{36... | collective-permute-start | bytes 786440 | tf_op jit(solution)/shard_map/ppermute | solution.py:28
  85.4 13.8 %collective-permute-start.17 = (bf16[4,128,128]{2,1,0:T(8,128)(2,1)}, bf16[4,128,128]{2,1,0:T(8,128)(2,1)S(1)}, u32[]{:S(2)}, u32[]{:S(2)}) collective-permute-start(bf16[4,128,128]{2,1,0:T(8,128)(2,1)} %copy-done.4), channel_id=1, source_target_pairs={{0,4},{4,8},{8,12},{12,0},{1,5},{5,9},{9,13},{13,1},{2,6},{6,10},{... | collective-permute-start | bytes 393224 | tf_op jit(solution)/shard_map/ppermute | solution.py:22
  89.1 14.2 %collective-permute-start.18 = (bf16[4,128,128]{2,1,0:T(8,128)(2,1)}, bf16[4,128,128]{2,1,0:T(8,128)(2,1)S(1)}, u32[]{:S(2)}, u32[]{:S(2)}) collective-permute-start(bf16[4,128,128]{2,1,0:T(8,128)(2,1)} %copy-done.4), channel_id=1, source_target_pairs={{0,8},{4,12},{8,0},{12,4},{1,9},{5,13},{9,1},{13,5},{2,10},{6,14},... | collective-permute-start | bytes 393224 | tf_op jit(solution)/shard_map/ppermute | solution.py:22
  94.5 14.1 %collective-permute-start.19 = (bf16[4,128,128]{2,1,0:T(8,128)(2,1)}, bf16[4,128,128]{2,1,0:T(8,128)(2,1)S(1)}, u32[]{:S(2)}, u32[]{:S(2)}) collective-permute-start(bf16[4,128,128]{2,1,0:T(8,128)(2,1)} %copy-done.4), channel_id=1, source_target_pairs={{0,12},{4,0},{8,4},{12,8},{1,13},{5,1},{9,5},{13,9},{2,14},{6,2},{... | collective-permute-start | bytes 393224 | tf_op jit(solution)/shard_map/ppermute | solution.py:22
  123.0 24.9 %all-to-all-start = ((bf16[16,128,128]{2,1,0:T(8,128)(2,1)}), bf16[16,128,128]{2,1,0:T(8,128)(2,1)S(1)}, u32[]{:S(2)}, u32[]{:S(2)}) async-start(bf16[16,128,128]{2,1,0:T(8,128)(2,1)} %attend.1), calls=%async_computation | async-start | bytes 1048576 | tf_op jit(solution)/shard_map/all_to_all | solution.py:300
  133.8 14.1 %collective-permute-start.24 = (bf16[128,128]{1,0:T(8,128)(2,1)S(1)}, bf16[128,128]{1,0:T(8,128)(2,1)S(1)}, u32[]{:S(2)}, u32[]{:S(2)}) collective-permute-start(bf16[128,128]{1,0:T(8,128)(2,1)S(1)} %get-tuple-element.75), channel_id=1, source_target_pairs={{0,192},{64,0},{128,64},{192,128},{1,193},{65,1},{129,65},{193,129... | collective-permute-start | bytes 98312 | tf_op jit(solution)/shard_map/ppermute | solution.py:298
  137.1 10.8 %collective-permute-start.25 = (bf16[128,128]{1,0:T(8,128)(2,1)S(1)}, bf16[128,128]{1,0:T(8,128)(2,1)S(1)}, u32[]{:S(2)}, u32[]{:S(2)}) collective-permute-start(bf16[128,128]{1,0:T(8,128)(2,1)S(1)} %get-tuple-element.74), channel_id=1, source_target_pairs={{0,128},{64,192},{128,0},{192,64},{1,129},{65,193},{129,1},{193,65... | collective-permute-start | bytes 98312 | tf_op jit(solution)/shard_map/ppermute | solution.py:298
  137.9 10.0 %collective-permute-start.26 = (bf16[128,128]{1,0:T(8,128)(2,1)S(1)}, bf16[128,128]{1,0:T(8,128)(2,1)S(1)}, u32[]{:S(2)}, u32[]{:S(2)}) collective-permute-start(bf16[128,128]{1,0:T(8,128)(2,1)S(1)} %get-tuple-element.73), channel_id=1, source_target_pairs={{0,64},{64,128},{128,192},{192,0},{1,65},{65,129},{129,193},{193,1... | collective-permute-start | bytes 98312 | tf_op jit(solution)/shard_map/ppermute | solution.py:298
  148.7 5.0 %collective-permute-start.29 = (bf16[128,512]{1,0:T(8,128)(2,1)S(1)}, bf16[128,512]{1,0:T(8,128)(2,1)S(1)}, u32[]{:S(2)}, u32[]{:S(2)}) collective-permute-start(bf16[128,512]{1,0:T(8,128)(2,1)S(1)} %gate.1), channel_id=1, source_target_pairs={{0,3},{1,0},{2,1},{3,2},{4,7},{5,4},{6,5},{7,6},{8,11},{9,8},{10,9... | collective-permute-start | bytes 393224 | tf_op jit(solution)/shard_map/ppermute | solution.py:22
  148.8 6.6 %collective-permute-start.28 = (bf16[128,512]{1,0:T(8,128)(2,1)S(1)}, bf16[128,512]{1,0:T(8,128)(2,1)S(1)}, u32[]{:S(2)}, u32[]{:S(2)}) collective-permute-start(bf16[128,512]{1,0:T(8,128)(2,1)S(1)} %gate.1), channel_id=1, source_target_pairs={{0,2},{1,3},{2,0},{3,1},{4,6},{5,7},{6,4},{7,5},{8,10},{9,11},{10,... | collective-permute-start | bytes 393224 | tf_op jit(solution)/shard_map/ppermute | solution.py:22
  149.4 7.3 %collective-permute-start.27 = (bf16[128,512]{1,0:T(8,128)(2,1)S(1)}, bf16[128,512]{1,0:T(8,128)(2,1)S(1)}, u32[]{:S(2)}, u32[]{:S(2)}) collective-permute-start(bf16[128,512]{1,0:T(8,128)(2,1)S(1)} %gate.1), channel_id=1, source_target_pairs={{0,1},{1,2},{2,3},{3,0},{4,5},{5,6},{6,7},{7,4},{8,9},{9,10},{10,1... | collective-permute-start | bytes 393224 | tf_op jit(solution)/shard_map/ppermute | solution.py:22
  (8 other events, 248.9 us)
Sparse Core Ops, SparseCore 0:
  19.6 43.7 all-gather.4
  84.0 47.5 all-gather.6

commit v9 on v8

--- a/solution.py
+++ b/solution.py
@@ -226,24 +226,22 @@
         lax.ppermute(columns((y + k) & 3), "y", [(i, (i + k) % 4) for i in range(4)])
         for k in range(1, 4)
     ]
+    swapped = lax.ppermute(
+        w_out.T, ("y", "x"), [(b * 4 + a, a * 4 + b) for a in range(4) for b in range(4)]
+    )
+    pieces, swapped = lax.optimization_barrier((pieces, swapped))
     piece = jnp.stack(pieces)
     weights = lax.all_gather(piece, plane)
 
     travelling, _ = lax.optimization_barrier((tokens, piece))
 
-    first = rotations(travelling[:, :512], "y", 4)
+    first = rotations(jnp.concatenate([travelling[:, :512], swapped], axis=0), "y", 4)
     second = rotations(travelling[:, 512:], "x", 4)
     first, second = lax.optimization_barrier((first, second))
-    firsts = rotations(jnp.concatenate(first, axis=0), "x", 4)
+    firsts = rotations(jnp.concatenate([f[:RUN] for f in first], axis=0), "x", 4)
     seconds = rotations(jnp.concatenate(second, axis=0), "y", 4)
-
-    late, firsts, seconds = lax.optimization_barrier((w_out.T, firsts, seconds))
-    wo_rows = [
-        lax.ppermute(
-            late, ("y", "x"), [(b * 4 + a, (a + k) % 4 * 4 + b) for a in range(4) for b in range(4)]
-        )
-        for k in range(4)
-    ]
+    wo_rows = jnp.stack([f[RUN:] for f in first])
+    firsts, seconds, wo_rows = lax.optimization_barrier((firsts, seconds, wo_rows))
 
     kv, q, u = call(
         project_kernel,
@@ -261,13 +259,17 @@
         "project",
     )(place, *firsts, *seconds, weights)
 
-    wo_rows, _ = lax.optimization_barrier((wo_rows, kv))
-    wo_all = lax.all_gather(jnp.stack(wo_rows), plane)
-
-    kv_near = jnp.stack([kv, swap(kv, "zl")])
+    wo_rows, _ = lax.optimization_barrier((wo_rows, weights))
+    wo_all = lax.all_gather(wo_rows, plane)
+
+    from_zl = swap(kv, "zl")
+    later, from_zl = lax.optimization_barrier((q, from_zl))
+    kv_near = jnp.stack([kv, from_zl])
     kv_far = swap(kv_near, "core")
-    q_all = rotations(q, "zh", 4)
-    kv_far, q_all[1], q_all[2] = lax.optimization_barrier((kv_far, q_all[1], q_all[2]))
+    q_all = [q] + [
+        lax.ppermute(q if k == 1 else later, "zh", [(i, (i + k) % 4) for i in range(4)])
+        for k in range(1, 4)
+    ]
 
     coded = weights[:4, :, 64:66].astype(f32)
     all_ids = (coded[:, :, 0] * 128 + coded[:, :, 1]).astype(jnp.int32).transpose(1, 0, 2)

time: 169 us -> 172 us (1.018)
  waiting for transfers between devices: 56.2 us -> 67.4 us
  starting transfers between devices: 62.9 us -> 59.9 us
  Pallas kernels: 20.5 us -> 18.3 us
  other arithmetic: 4.58 us -> 2.73 us
    ppermute x4, waiting for transfers between devices: 0.01 us -> 16.1 us  [the longest x3 16.1 us: on_device(): lax.ppermute(q if k == 1 else later, 'zh', [(i, (i + k) % 4) for i in ran...]
    ppermute x18 -> x15, waiting for transfers between devices: 41.5 us -> 27.6 us  [rotations(): lax.ppermute(value, axis, [(i, (i + step * k) % size) for i in range(size)])]
    ppermute x2, waiting for transfers between devices: 0.01 us -> 11.6 us  [swap(): return lax.ppermute(value, axis, [(0, 1), (1, 0)])]
    all_to_all x1, starting transfers between devices: 10.9 us -> 5.88 us  [on_device(): arrived = lax.all_to_all(parts, ('y', 'zh'), 0, 0, tiled=True)]
    ppermute x3, waiting for transfers between devices: 5.56 us -> 1.6 us  [on_device(): lax.ppermute(columns(y + k & 3), 'y', [(i, (i + k) % 4) for i in range(4)])]
    pallas_call x1, Pallas kernels: 13.4 us -> 11.2 us  [on_device(): call(attend_kernel, jax.ShapeDtypeStruct((16, RUN, DH), bf16), 5, 9, [plt...]
    ppermute x18 -> x15, starting transfers between devices: 31 us -> 32.8 us  [rotations(): lax.ppermute(value, axis, [(i, (i + step * k) % size) for i in range(size)])]
    unnamed x21 -> x14, local copies, waits for them, and re-layouts: 6.3 us -> 4.72 us
  transfers between devices with their start and end apart: 33 -> 30, of which waited for: 16 -> 14; matrix products, arithmetic and copies ran while one was open for 3% -> 3% of each run, Pallas kernels for 10% -> 9%
where the time goes in v9:
time: 172 us; the launch traced here: 171 us
  waiting for transfers between devices  67.4 us (39%)
  starting transfers between devices  59.9 us (35%)
  Pallas kernels  18.3 us (11%)
  between operations  13.7 us (8%)
  local copies, waits for them, and re-layouts  9.11 us (5%)
  other arithmetic  2.73 us (2%)
    ppermute x15, starting transfers between devices, rotations(): lax.ppermute(value, axis, [(i, (i + step * k) % size) for i in range(size)])  32.8 us
    ppermute x15, waiting for transfers between devices, rotations(): lax.ppermute(value, axis, [(i, (i + step * k) % size) for i in range(size)])  27.6 us
    ppermute x3, waiting for transfers between devices, on_device(): lax.ppermute(q if k == 1 else later, 'zh', [(i, (i + k) % 4) for i in ran...  16.1 us
    ppermute x2, waiting for transfers between devices, swap(): return lax.ppermute(value, axis, [(0, 1), (1, 0)])  11.6 us
    pallas_call x1, Pallas kernels, on_device(): call(attend_kernel, jax.ShapeDtypeStruct((16, RUN, DH), bf16), 5, 9, [plt...  11.2 us
    all_to_all x1, waiting for transfers between devices, on_device(): arrived = lax.all_to_all(parts, ('y', 'zh'), 0, 0, tiled=True)  10.5 us
    ppermute x3, starting transfers between devices, on_device(): lax.ppermute(q if k == 1 else later, 'zh', [(i, (i + k) % 4) for i in ran...  8.55 us
    ppermute x3, starting transfers between devices, on_device(): lax.ppermute(columns(y + k & 3), 'y', [(i, (i + k) % 4) for i in range(4)])  5.9 us
  transfers between devices with their start and end apart: 30, of which 14 were waited for; matrix products, arithmetic and copies ran while one was open for 3% of the time, Pallas kernels for 9%

profile of v9, /device:TPU:32, one launch (start us, length us, event | category | flops | bytes accessed | tf_op | source)
XLA Modules:
  0.0 171.1 jit_solution(3831345064100078713)
XLA Ops:
  8.4 1.7 collective-permute-start
  10.1 2.9 %collective-permute-start.1 = (bf16[80,512]{1,0:T(8,128)(2,1)S(1)}, bf16[80,512]{1,0:T(8,128)(2,1)S(1)}, u32[]{:S(2)}, u32[]{:S(2)}) collective-permute-start(bf16[80,512]{1,0:T(8,128)(2,1)S(1)} %get-tuple-element.85), channel_id=1, source_target_pairs={{0,128},{64,192},{128,0},{192,64},{1,129},{65,193},{129,1},{193,65... | collective-permute-start | bytes 245768 | tf_op jit(solution)/shard_map/ppermute | solution.py:226
  13.0 1.3 collective-permute-start.2
  14.3 1.5 collective-permute-start.3
  19.3 6.1 %collective-permute-start.7 = (bf16[128,512]{1,0:T(8,128)(2,1)S(1)}, bf16[128,512]{1,0:T(8,128)(2,1)S(1)}, u32[]{:S(2)}, u32[]{:S(2)}) collective-permute-start(bf16[128,512]{1,0:T(8,128)(2,1)S(1)} %get-tuple-element.47), channel_id=1, source_target_pairs={{0,1},{1,2},{2,3},{3,0},{4,5},{5,6},{6,7},{7,4},{8,9},{9,10},{10,1... | collective-permute-start | bytes 393224 | tf_op jit(solution)/shard_map/ppermute | solution.py:22
  25.5 4.5 %collective-permute-start.5 = (bf16[192,512]{1,0:T(8,128)(2,1)S(1)}, bf16[192,512]{1,0:T(8,128)(2,1)S(1)}, u32[]{:S(2)}, u32[]{:S(2)}) collective-permute-start(bf16[192,512]{1,0:T(8,128)(2,1)S(1)} %pad_maximum_fusion.5), channel_id=1, source_target_pairs={{0,128},{64,192},{128,0},{192,64},{1,129},{65,193},{129,1},{193,65... | collective-permute-start | bytes 589832 | tf_op jit(solution)/shard_map/ppermute | solution.py:22
  29.9 4.5 %collective-permute-start.8 = (bf16[128,512]{1,0:T(8,128)(2,1)S(1)}, bf16[128,512]{1,0:T(8,128)(2,1)S(1)}, u32[]{:S(2)}, u32[]{:S(2)}) collective-permute-start(bf16[128,512]{1,0:T(8,128)(2,1)S(1)} %get-tuple-element.47), channel_id=1, source_target_pairs={{0,2},{1,3},{2,0},{3,1},{4,6},{5,7},{6,4},{7,5},{8,10},{9,11},{10,... | collective-permute-start | bytes 393224 | tf_op jit(solution)/shard_map/ppermute | solution.py:22
  35.7 1.7 collective-permute-done.8
  37.3 2.0 %collective-permute-done.9 = bf16[128,512]{1,0:T(8,128)(2,1)S(1)} collective-permute-done((bf16[128,512]{1,0:T(8,128)(2,1)S(1)}, bf16[128,512]{1,0:T(8,128)(2,1)S(1)}, u32[]{:S(2)}, u32[]{:S(2)}) %collective-permute-start.9) | collective-permute-done | bytes 131104 | tf_op jit(solution)/shard_map/ppermute | solution.py:22
  40.2 2.2 %collective-permute-start.14 = (bf16[512,512]{1,0:T(8,128)(2,1)S(1)}, bf16[512,512]{1,0:T(8,128)(2,1)S(1)}, u32[]{:S(2)}, u32[]{:S(2)}) collective-permute-start(bf16[512,512]{1,0:T(8,128)(2,1)S(1)} %constant_dynamic-update-slice_fusion.b0), channel_id=1, source_target_pairs={{0,128},{64,192},{128,0},{192,64},{1,129},{65,193},{129,1},{193,65... | collective-permute-start | bytes 1572872 | tf_op jit(solution)/shard_map/ppermute | solution.py:22
  42.4 2.5 %collective-permute-start.15 = (bf16[512,512]{1,0:T(8,128)(2,1)S(1)}, bf16[512,512]{1,0:T(8,128)(2,1)S(1)}, u32[]{:S(2)}, u32[]{:S(2)}) collective-permute-start(bf16[512,512]{1,0:T(8,128)(2,1)S(1)} %constant_dynamic-update-slice_fusion.b0), channel_id=1, source_target_pairs={{0,192},{64,0},{128,64},{192,128},{1,193},{65,1},{129,65},{193,129... | collective-permute-start | bytes 1572872 | tf_op jit(solution)/shard_map/ppermute | solution.py:22
  45.9 3.3 %collective-permute-start.11 = (bf16[512,512]{1,0:T(8,128)(2,1)S(1)}, bf16[512,512]{1,0:T(8,128)(2,1)}, u32[]{:S(2)}, u32[]{:S(2)}) collective-permute-start(bf16[512,512]{1,0:T(8,128)(2,1)S(1)} %pad_maximum_fusion.a0), channel_id=1, source_target_pairs={{0,2},{1,3},{2,0},{3,1},{4,6},{5,7},{6,4},{7,5},{8,10},{9,11},{10,... | collective-permute-start | bytes 1572872 | tf_op jit(solution)/shard_map/ppermute | solution.py:22
  49.2 12.4 %collective-permute-done.13.b1 = bf16[512,512]{1,0:T(8,128)(2,1)S(1)} collective-permute-done((bf16[512,512]{1,0:T(8,128)(2,1)S(1)}, bf16[512,512]{1,0:T(8,128)(2,1)S(1)}, u32[]{:S(2)}, u32[]{:S(2)}) %collective-permute-start.13) | collective-permute-done | bytes 524320 | tf_op jit(solution)/shard_map/ppermute | solution.py:22
  62.5 4.9 %collective-permute-done.11.a2 = bf16[512,512]{1,0:T(8,128)(2,1)} collective-permute-done((bf16[512,512]{1,0:T(8,128)(2,1)S(1)}, bf16[512,512]{1,0:T(8,128)(2,1)}, u32[]{:S(2)}, u32[]{:S(2)}) %collective-permute-start.11) | collective-permute-done | bytes 524320 | tf_op jit(solution)/shard_map/ppermute | solution.py:22
  67.3 3.6 %collective-permute-done.12.a3 = bf16[512,512]{1,0:T(8,128)(2,1)} collective-permute-done((bf16[512,512]{1,0:T(8,128)(2,1)S(1)}, bf16[512,512]{1,0:T(8,128)(2,1)}, u32[]{:S(2)}, u32[]{:S(2)}) %collective-permute-start.12) | collective-permute-done | bytes 524320 | tf_op jit(solution)/shard_map/ppermute | solution.py:22
  72.5 2.5 %copy-done.1 = bf16[64,80,512]{2,1,0:T(8,128)(2,1)S(1)} copy-done((bf16[64,80,512]{2,1,0:T(8,128)(2,1)S(1)}, bf16[64,80,512]{2,1,0:T(8,128)(2,1)}, u32[]{:S(2)}) %copy-start.1) | copy-done | bytes 5242904
  75.0 3.6 %project.1 = (bf16[4,128,256]{2,1,0:T(8,128)(2,1)S(1)}, bf16[4,128,128]{2,1,0:T(8,128)(2,1)S(1)}, bf16[4,128,128]{2,1,0:T(8,128)(2,1)S(1)}) custom-call(s32[5]{0:T(128)S(1)} %stack.90.place, bf16[512,512]{1,0:T(8,128)(2,1)S(1)} %pad_maximum_fusion.a0, bf16[512,512]{1,0:T(8,128)(2,1)S(1)} %collective-permute-done.10.a1, ...), custom_call_target="tpu_custom_call" | custom-call | flops 2147483648 | bytes 9437184 | tf_op jit(solution)/shard_map/project/pallas_call | solution.py:246
  78.8 3.3 %collective-permute-start.16 = (bf16[4,128,128]{2,1,0:T(8,128)(2,1)S(1)}, bf16[4,128,128]{2,1,0:T(8,128)(2,1)S(1)}, u32[]{:S(2)}, u32[]{:S(2)}) collective-permute-start(bf16[4,128,128]{2,1,0:T(8,128)(2,1)S(1)} %get-tuple-element.61.q0), channel_id=1, source_target_pairs={{0,4},{4,8},{8,12},{12,0},{1,5},{5,9},{9,13},{13,1},{2,6},{6,10},{... | collective-permute-start | bytes 393224 | tf_op jit(solution)/shard_map/ppermute | solution.py:270
  82.3 11.6 %collective-permute-done.17 = bf16[4,128,256]{2,1,0:T(8,128)(2,1)S(1)} collective-permute-done((bf16[4,128,256]{2,1,0:T(8,128)(2,1)S(1)}, bf16[4,128,256]{2,1,0:T(8,128)(2,1)S(1)}, u32[]{:S(2)}, u32[]{:S(2)}) %collective-permute-start.17) | collective-permute-done | bytes 262176 | tf_op jit(solution)/shard_map/ppermute | solution.py:28
  94.7 4.7 %collective-permute-start.19 = (bf16[4,128,128]{2,1,0:T(8,128)(2,1)S(1)}, bf16[4,128,128]{2,1,0:T(8,128)(2,1)S(1)}, u32[]{:S(2)}, u32[]{:S(2)}) collective-permute-start(bf16[4,128,128]{2,1,0:T(8,128)(2,1)S(1)} %get-tuple-element.61.q0), channel_id=1, source_target_pairs={{0,12},{4,0},{8,4},{12,8},{1,13},{5,1},{9,5},{13,9},{2,14},{6,2},{... | collective-permute-start | bytes 393224 | tf_op jit(solution)/shard_map/ppermute | solution.py:270
  100.2 11.9 %collective-permute-done.18.q2 = bf16[4,128,128]{2,1,0:T(8,128)(2,1)S(1)} collective-permute-done((bf16[4,128,128]{2,1,0:T(8,128)(2,1)S(1)}, bf16[4,128,128]{2,1,0:T(8,128)(2,1)S(1)}, u32[]{:S(2)}, u32[]{:S(2)}) %collective-permute-start.18) | collective-permute-done | bytes 131104 | tf_op jit(solution)/shard_map/ppermute | solution.py:270
  112.0 4.2 %collective-permute-done.19.q3 = bf16[4,128,128]{2,1,0:T(8,128)(2,1)S(1)} collective-permute-done((bf16[4,128,128]{2,1,0:T(8,128)(2,1)S(1)}, bf16[4,128,128]{2,1,0:T(8,128)(2,1)S(1)}, u32[]{:S(2)}, u32[]{:S(2)}) %collective-permute-start.19) | collective-permute-done | bytes 131104 | tf_op jit(solution)/shard_map/ppermute | solution.py:270
  116.3 11.2 %attend.1 = bf16[16,128,128]{2,1,0:T(8,128)(2,1)} custom-call(s32[5]{0:T(128)S(1)} %stack.90.place, s32[4]{0:T(128)S(1)} %copy-done.4, s32[4,2]{1,0:T(4,128)S(1)} %pad_add_fusion.1.q_edges, s32[4,4]{1,0:T(4,128)S(1)} %copy.25.k_edges, f32[32]{0:T(128)S(1)} %fusion.10.biases, bf16[4,128,128]{2,1,0:T(8,128)(2,1)S(1)} %get-tuple-element.61.q0, ...), custom_call_target="tpu_custom_call" | custom-call | flops 1073741824 | bytes 5242880 | tf_op jit(solution)/shard_map/attend/pallas_call | solution.py:286
  127.5 5.9 %all-to-all-start = ((bf16[16,128,128]{2,1,0:T(8,128)(2,1)}), bf16[16,128,128]{2,1,0:T(8,128)(2,1)S(1)}, u32[]{:S(2)}, u32[]{:S(2)}) async-start(bf16[16,128,128]{2,1,0:T(8,128)(2,1)} %attend.1), calls=%async_computation | async-start | bytes 1048576 | tf_op jit(solution)/shard_map/all_to_all | solution.py:302
  133.4 3.2 %collective-permute-start.21 = (bf16[128,128]{1,0:T(8,128)(2,1)S(1)}, bf16[128,128]{1,0:T(8,128)(2,1)S(1)}, u32[]{:S(2)}, u32[]{:S(2)}) collective-permute-start(bf16[128,128]{1,0:T(8,128)(2,1)S(1)} %get-tuple-element.77), channel_id=1, source_target_pairs={{0,192},{64,0},{128,64},{192,128},{1,193},{65,1},{129,65},{193,129... | collective-permute-start | bytes 98312 | tf_op jit(solution)/shard_map/ppermute | solution.py:300
  138.3 10.5 %all-to-all-done.parts = bf16[16,128,128]{2,1,0:T(8,128)(2,1)S(1)} async-done(((bf16[16,128,128]{2,1,0:T(8,128)(2,1)}), bf16[16,128,128]{2,1,0:T(8,128)(2,1)S(1)}, u32[]{:S(2)}, u32[]{:S(2)}) %all-to-all-start) | async-done | bytes 524320 | tf_op jit(solution)/shard_map/all_to_all | solution.py:302
  149.6 1.9 %collective-permute-start.24 = (bf16[128,512]{1,0:T(8,128)(2,1)S(1)}, bf16[128,512]{1,0:T(8,128)(2,1)S(1)}, u32[]{:S(2)}, u32[]{:S(2)}) collective-permute-start(bf16[128,512]{1,0:T(8,128)(2,1)S(1)} %gate.1), channel_id=1, source_target_pairs={{0,1},{1,2},{2,3},{3,0},{4,5},{5,6},{6,7},{7,4},{8,9},{9,10},{10,1... | collective-permute-start | bytes 393224 | tf_op jit(solution)/shard_map/ppermute | solution.py:22
  151.5 2.8 %collective-permute-start.25 = (bf16[128,512]{1,0:T(8,128)(2,1)S(1)}, bf16[128,512]{1,0:T(8,128)(2,1)S(1)}, u32[]{:S(2)}, u32[]{:S(2)}) collective-permute-start(bf16[128,512]{1,0:T(8,128)(2,1)S(1)} %gate.1), channel_id=1, source_target_pairs={{0,2},{1,3},{2,0},{3,1},{4,6},{5,7},{6,4},{7,5},{8,10},{9,11},{10,... | collective-permute-start | bytes 393224 | tf_op jit(solution)/shard_map/ppermute | solution.py:22
  154.3 2.0 %collective-permute-start.26 = (bf16[128,512]{1,0:T(8,128)(2,1)S(1)}, bf16[128,512]{1,0:T(8,128)(2,1)S(1)}, u32[]{:S(2)}, u32[]{:S(2)}) collective-permute-start(bf16[128,512]{1,0:T(8,128)(2,1)S(1)} %gate.1), channel_id=1, source_target_pairs={{0,3},{1,0},{2,1},{3,2},{4,7},{5,4},{6,5},{7,6},{8,11},{9,8},{10,9... | collective-permute-start | bytes 393224 | tf_op jit(solution)/shard_map/ppermute | solution.py:22
  157.2 1.5 collective-permute-done.25
  159.3 2.2 %copy-done.2 = bf16[64,64,512]{2,1,0:T(8,128)(2,1)S(1)} copy-done((bf16[64,64,512]{2,1,0:T(8,128)(2,1)S(1)}, bf16[64,64,512]{2,1,0:T(8,128)(2,1)}, u32[]{:S(2)}) %copy-start.2) | copy-done | bytes 4194328
  161.5 2.7 %project_out.1 = bf16[128,1024]{1,0:T(8,128)(2,1)} custom-call(s32[5]{0:T(128)S(1)} %stack.90.place, bf16[128,1024]{1,0:T(8,128)(2,1)S(1)} %copy-done.3, bf16[4,128,512]{2,1,0:T(8,128)(2,1)S(1)} %pad_maximum_fusion.2.gated, bf16[16,4,64,512]{3,2,1,0:T(8,128)(2,1)S(1)} %bitcast.51), custom_call_target="tpu_custom_call" | custom-call | flops 536870912 | bytes 5242880 | tf_op jit(solution)/shard_map/project_out/pallas_call | solution.py:317
  (90 shorter events, 16.6 us)
Async XLA Ops:
  6.5 131.8 %copy-start = (f32[16,128]{1,0:T(8,128)S(1)}, f32[16,128]{1,0:T(8,128)}, u32[]{:S(2)}) copy-start(f32[16,128]{1,0:T(8,128)} %param.11) | copy-start | bytes 24580
  6.5 64.4 %all-gather.5.cloned.1.call-start = ((), (), s32[]{:S(2)}) async-start(), calls=%async_computation.1 | async-start | bytes 5570560 | tf_op jit(solution)/shard_map/all_gather | solution.py:234
  8.4 7.4 %collective-permute-start = (bf16[80,512]{1,0:T(8,128)(2,1)S(1)}, bf16[80,512]{1,0:T(8,128)(2,1)S(1)}, u32[]{:S(2)}, u32[]{:S(2)}) collective-permute-start(bf16[80,512]{1,0:T(8,128)(2,1)S(1)} %get-tuple-element.84), channel_id=1, source_target_pairs={{0,64},{64,128},{128,192},{192,0},{1,65},{65,129},{129,193},{193,1... | collective-permute-start | bytes 245768 | tf_op jit(solution)/shard_map/ppermute | solution.py:226
  10.1 6.8 %collective-permute-start.1 = (bf16[80,512]{1,0:T(8,128)(2,1)S(1)}, bf16[80,512]{1,0:T(8,128)(2,1)S(1)}, u32[]{:S(2)}, u32[]{:S(2)}) collective-permute-start(bf16[80,512]{1,0:T(8,128)(2,1)S(1)} %get-tuple-element.85), channel_id=1, source_target_pairs={{0,128},{64,192},{128,0},{192,64},{1,129},{65,193},{129,1},{193,65... | collective-permute-start | bytes 245768 | tf_op jit(solution)/shard_map/ppermute | solution.py:226
  13.0 4.4 %collective-permute-start.2 = (bf16[80,512]{1,0:T(8,128)(2,1)S(1)}, bf16[80,512]{1,0:T(8,128)(2,1)S(1)}, u32[]{:S(2)}, u32[]{:S(2)}) collective-permute-start(bf16[80,512]{1,0:T(8,128)(2,1)S(1)} %get-tuple-element.83), channel_id=1, source_target_pairs={{0,192},{64,0},{128,64},{192,128},{1,193},{65,1},{129,65},{193,129... | collective-permute-start | bytes 245768 | tf_op jit(solution)/shard_map/ppermute | solution.py:226
  14.3 1.5 collective-permute-start.3
  18.2 130.6 %all-gather.7.cloned.1.call-start = ((), (), s32[]{:S(2)}) async-start(), calls=%async_computation.2 | async-start | bytes 4456448 | tf_op jit(solution)/shard_map/all_gather | solution.py:263
  19.3 15.1 %collective-permute-start.7 = (bf16[128,512]{1,0:T(8,128)(2,1)S(1)}, bf16[128,512]{1,0:T(8,128)(2,1)S(1)}, u32[]{:S(2)}, u32[]{:S(2)}) collective-permute-start(bf16[128,512]{1,0:T(8,128)(2,1)S(1)} %get-tuple-element.47), channel_id=1, source_target_pairs={{0,1},{1,2},{2,3},{3,0},{4,5},{5,6},{6,7},{7,4},{8,9},{9,10},{10,1... | collective-permute-start | bytes 393224 | tf_op jit(solution)/shard_map/ppermute | solution.py:22
  25.4 14.0 %collective-permute-start.4 = (bf16[192,512]{1,0:T(8,128)(2,1)S(1)}, bf16[192,512]{1,0:T(8,128)(2,1)S(1)}, u32[]{:S(2)}, u32[]{:S(2)}) collective-permute-start(bf16[192,512]{1,0:T(8,128)(2,1)S(1)} %pad_maximum_fusion.5), channel_id=1, source_target_pairs={{0,64},{64,128},{128,192},{192,0},{1,65},{65,129},{129,193},{193,1... | collective-permute-start | bytes 589832 | tf_op jit(solution)/shard_map/ppermute | solution.py:22
  25.5 13.9 %collective-permute-start.5 = (bf16[192,512]{1,0:T(8,128)(2,1)S(1)}, bf16[192,512]{1,0:T(8,128)(2,1)S(1)}, u32[]{:S(2)}, u32[]{:S(2)}) collective-permute-start(bf16[192,512]{1,0:T(8,128)(2,1)S(1)} %pad_maximum_fusion.5), channel_id=1, source_target_pairs={{0,128},{64,192},{128,0},{192,64},{1,129},{65,193},{129,1},{193,65... | collective-permute-start | bytes 589832 | tf_op jit(solution)/shard_map/ppermute | solution.py:22
  29.9 9.4 %collective-permute-start.6 = (bf16[192,512]{1,0:T(8,128)(2,1)S(1)}, bf16[192,512]{1,0:T(8,128)(2,1)S(1)}, u32[]{:S(2)}, u32[]{:S(2)}) collective-permute-start(bf16[192,512]{1,0:T(8,128)(2,1)S(1)} %pad_maximum_fusion.5), channel_id=1, source_target_pairs={{0,192},{64,0},{128,64},{192,128},{1,193},{65,1},{129,65},{193,129... | collective-permute-start | bytes 589832 | tf_op jit(solution)/shard_map/ppermute | solution.py:22
  29.9 7.4 %collective-permute-start.8 = (bf16[128,512]{1,0:T(8,128)(2,1)S(1)}, bf16[128,512]{1,0:T(8,128)(2,1)S(1)}, u32[]{:S(2)}, u32[]{:S(2)}) collective-permute-start(bf16[128,512]{1,0:T(8,128)(2,1)S(1)} %get-tuple-element.47), channel_id=1, source_target_pairs={{0,2},{1,3},{2,0},{3,1},{4,6},{5,7},{6,4},{7,5},{8,10},{9,11},{10,... | collective-permute-start | bytes 393224 | tf_op jit(solution)/shard_map/ppermute | solution.py:22
  34.4 5.0 %collective-permute-start.9 = (bf16[128,512]{1,0:T(8,128)(2,1)S(1)}, bf16[128,512]{1,0:T(8,128)(2,1)S(1)}, u32[]{:S(2)}, u32[]{:S(2)}) collective-permute-start(bf16[128,512]{1,0:T(8,128)(2,1)S(1)} %get-tuple-element.47), channel_id=1, source_target_pairs={{0,3},{1,0},{2,1},{3,2},{4,7},{5,4},{6,5},{7,6},{8,11},{9,8},{10,9... | collective-permute-start | bytes 393224 | tf_op jit(solution)/shard_map/ppermute | solution.py:22
  39.5 22.2 %collective-permute-start.13 = (bf16[512,512]{1,0:T(8,128)(2,1)S(1)}, bf16[512,512]{1,0:T(8,128)(2,1)S(1)}, u32[]{:S(2)}, u32[]{:S(2)}) collective-permute-start(bf16[512,512]{1,0:T(8,128)(2,1)S(1)} %constant_dynamic-update-slice_fusion.b0), channel_id=1, source_target_pairs={{0,64},{64,128},{128,192},{192,0},{1,65},{65,129},{129,193},{193,1... | collective-permute-start | bytes 1572872 | tf_op jit(solution)/shard_map/ppermute | solution.py:22
  40.2 22.3 %collective-permute-start.14 = (bf16[512,512]{1,0:T(8,128)(2,1)S(1)}, bf16[512,512]{1,0:T(8,128)(2,1)S(1)}, u32[]{:S(2)}, u32[]{:S(2)}) collective-permute-start(bf16[512,512]{1,0:T(8,128)(2,1)S(1)} %constant_dynamic-update-slice_fusion.b0), channel_id=1, source_target_pairs={{0,128},{64,192},{128,0},{192,64},{1,129},{65,193},{129,1},{193,65... | collective-permute-start | bytes 1572872 | tf_op jit(solution)/shard_map/ppermute | solution.py:22
  42.4 20.1 %collective-permute-start.15 = (bf16[512,512]{1,0:T(8,128)(2,1)S(1)}, bf16[512,512]{1,0:T(8,128)(2,1)S(1)}, u32[]{:S(2)}, u32[]{:S(2)}) collective-permute-start(bf16[512,512]{1,0:T(8,128)(2,1)S(1)} %constant_dynamic-update-slice_fusion.b0), channel_id=1, source_target_pairs={{0,192},{64,0},{128,64},{192,128},{1,193},{65,1},{129,65},{193,129... | collective-permute-start | bytes 1572872 | tf_op jit(solution)/shard_map/ppermute | solution.py:22
  45.0 17.5 %collective-permute-start.10 = (bf16[512,512]{1,0:T(8,128)(2,1)S(1)}, bf16[512,512]{1,0:T(8,128)(2,1)S(1)}, u32[]{:S(2)}, u32[]{:S(2)}) collective-permute-start(bf16[512,512]{1,0:T(8,128)(2,1)S(1)} %pad_maximum_fusion.a0), channel_id=1, source_target_pairs={{0,1},{1,2},{2,3},{3,0},{4,5},{5,6},{6,7},{7,4},{8,9},{9,10},{10,1... | collective-permute-start | bytes 1572872 | tf_op jit(solution)/shard_map/ppermute | solution.py:22
  45.9 21.4 %collective-permute-start.11 = (bf16[512,512]{1,0:T(8,128)(2,1)S(1)}, bf16[512,512]{1,0:T(8,128)(2,1)}, u32[]{:S(2)}, u32[]{:S(2)}) collective-permute-start(bf16[512,512]{1,0:T(8,128)(2,1)S(1)} %pad_maximum_fusion.a0), channel_id=1, source_target_pairs={{0,2},{1,3},{2,0},{3,1},{4,6},{5,7},{6,4},{7,5},{8,10},{9,11},{10,... | collective-permute-start | bytes 1572872 | tf_op jit(solution)/shard_map/ppermute | solution.py:22
  61.7 9.3 %collective-permute-start.12 = (bf16[512,512]{1,0:T(8,128)(2,1)S(1)}, bf16[512,512]{1,0:T(8,128)(2,1)}, u32[]{:S(2)}, u32[]{:S(2)}) collective-permute-start(bf16[512,512]{1,0:T(8,128)(2,1)S(1)} %pad_maximum_fusion.a0), channel_id=1, source_target_pairs={{0,3},{1,0},{2,1},{3,2},{4,7},{5,4},{6,5},{7,6},{8,11},{9,8},{10,9... | collective-permute-start | bytes 1572872 | tf_op jit(solution)/shard_map/ppermute | solution.py:22
  78.6 80.7 %copy-start.3 = (bf16[128,1024]{1,0:T(8,128)(2,1)S(1)}, bf16[128,1024]{1,0:T(8,128)(2,1)}, u32[]{:S(2)}) copy-start(bf16[128,1024]{1,0:T(8,128)(2,1)} %tokens.1) | copy-start | bytes 786436
  78.6 15.2 %collective-permute-start.17 = (bf16[4,128,256]{2,1,0:T(8,128)(2,1)S(1)}, bf16[4,128,256]{2,1,0:T(8,128)(2,1)S(1)}, u32[]{:S(2)}, u32[]{:S(2)}) collective-permute-start(bf16[4,128,256]{2,1,0:T(8,128)(2,1)S(1)} %get-tuple-element.60), channel_id=1, source_target_pairs={{0,32},{32,0},{1,33},{33,1},{2,34},{34,2},{3,35},{35,3},{4,36},{36... | collective-permute-start | bytes 786440 | tf_op jit(solution)/shard_map/ppermute | solution.py:28
  78.8 21.3 %collective-permute-start.16 = (bf16[4,128,128]{2,1,0:T(8,128)(2,1)S(1)}, bf16[4,128,128]{2,1,0:T(8,128)(2,1)S(1)}, u32[]{:S(2)}, u32[]{:S(2)}) collective-permute-start(bf16[4,128,128]{2,1,0:T(8,128)(2,1)S(1)} %get-tuple-element.61.q0), channel_id=1, source_target_pairs={{0,4},{4,8},{8,12},{12,0},{1,5},{5,9},{9,13},{13,1},{2,6},{6,10},{... | collective-permute-start | bytes 393224 | tf_op jit(solution)/shard_map/ppermute | solution.py:270
  93.9 22.3 %collective-permute-start.20 = (bf16[2,4,128,256]{3,2,1,0:T(8,128)(2,1)S(1)}, bf16[2,4,128,256]{3,2,1,0:T(8,128)(2,1)S(1)}, u32[]{:S(2)}, u32[]{:S(2)}) collective-permute-start(bf16[2,4,128,256]{3,2,1,0:T(8,128)(2,1)S(1)} %pad_maximum_fusion.1.kv_near), channel_id=1, source_target_pairs={{0,16},{16,0},{1,17},{17,1},{2,18},{18,2},{3,19},{19,3},{4,20},{20... | collective-permute-start | bytes 1572872 | tf_op jit(solution)/shard_map/ppermute | solution.py:28
  94.1 17.9 %collective-permute-start.18 = (bf16[4,128,128]{2,1,0:T(8,128)(2,1)S(1)}, bf16[4,128,128]{2,1,0:T(8,128)(2,1)S(1)}, u32[]{:S(2)}, u32[]{:S(2)}) collective-permute-start(bf16[4,128,128]{2,1,0:T(8,128)(2,1)S(1)} %get-tuple-element.61.q0), channel_id=1, source_target_pairs={{0,8},{4,12},{8,0},{12,4},{1,9},{5,13},{9,1},{13,5},{2,10},{6,14},... | collective-permute-start | bytes 393224 | tf_op jit(solution)/shard_map/ppermute | solution.py:270
  94.7 21.6 %collective-permute-start.19 = (bf16[4,128,128]{2,1,0:T(8,128)(2,1)S(1)}, bf16[4,128,128]{2,1,0:T(8,128)(2,1)S(1)}, u32[]{:S(2)}, u32[]{:S(2)}) collective-permute-start(bf16[4,128,128]{2,1,0:T(8,128)(2,1)S(1)} %get-tuple-element.61.q0), channel_id=1, source_target_pairs={{0,12},{4,0},{8,4},{12,8},{1,13},{5,1},{9,5},{13,9},{2,14},{6,2},{... | collective-permute-start | bytes 393224 | tf_op jit(solution)/shard_map/ppermute | solution.py:270
  127.5 21.3 %all-to-all-start = ((bf16[16,128,128]{2,1,0:T(8,128)(2,1)}), bf16[16,128,128]{2,1,0:T(8,128)(2,1)S(1)}, u32[]{:S(2)}, u32[]{:S(2)}) async-start(bf16[16,128,128]{2,1,0:T(8,128)(2,1)} %attend.1), calls=%async_computation | async-start | bytes 1048576 | tf_op jit(solution)/shard_map/all_to_all | solution.py:302
  133.4 15.4 %collective-permute-start.21 = (bf16[128,128]{1,0:T(8,128)(2,1)S(1)}, bf16[128,128]{1,0:T(8,128)(2,1)S(1)}, u32[]{:S(2)}, u32[]{:S(2)}) collective-permute-start(bf16[128,128]{1,0:T(8,128)(2,1)S(1)} %get-tuple-element.77), channel_id=1, source_target_pairs={{0,192},{64,0},{128,64},{192,128},{1,193},{65,1},{129,65},{193,129... | collective-permute-start | bytes 98312 | tf_op jit(solution)/shard_map/ppermute | solution.py:300
  136.6 12.2 %collective-permute-start.22 = (bf16[128,128]{1,0:T(8,128)(2,1)S(1)}, bf16[128,128]{1,0:T(8,128)(2,1)S(1)}, u32[]{:S(2)}, u32[]{:S(2)}) collective-permute-start(bf16[128,128]{1,0:T(8,128)(2,1)S(1)} %get-tuple-element.76), channel_id=1, source_target_pairs={{0,128},{64,192},{128,0},{192,64},{1,129},{65,193},{129,1},{193,65... | collective-permute-start | bytes 98312 | tf_op jit(solution)/shard_map/ppermute | solution.py:300
  137.4 11.4 %collective-permute-start.23 = (bf16[128,128]{1,0:T(8,128)(2,1)S(1)}, bf16[128,128]{1,0:T(8,128)(2,1)S(1)}, u32[]{:S(2)}, u32[]{:S(2)}) collective-permute-start(bf16[128,128]{1,0:T(8,128)(2,1)S(1)} %get-tuple-element.75), channel_id=1, source_target_pairs={{0,64},{64,128},{128,192},{192,0},{1,65},{65,129},{129,193},{193,1... | collective-permute-start | bytes 98312 | tf_op jit(solution)/shard_map/ppermute | solution.py:300
  149.6 7.7 %collective-permute-start.24 = (bf16[128,512]{1,0:T(8,128)(2,1)S(1)}, bf16[128,512]{1,0:T(8,128)(2,1)S(1)}, u32[]{:S(2)}, u32[]{:S(2)}) collective-permute-start(bf16[128,512]{1,0:T(8,128)(2,1)S(1)} %gate.1), channel_id=1, source_target_pairs={{0,1},{1,2},{2,3},{3,0},{4,5},{5,6},{6,7},{7,4},{8,9},{9,10},{10,1... | collective-permute-start | bytes 393224 | tf_op jit(solution)/shard_map/ppermute | solution.py:22
  151.5 7.3 %collective-permute-start.25 = (bf16[128,512]{1,0:T(8,128)(2,1)S(1)}, bf16[128,512]{1,0:T(8,128)(2,1)S(1)}, u32[]{:S(2)}, u32[]{:S(2)}) collective-permute-start(bf16[128,512]{1,0:T(8,128)(2,1)S(1)} %gate.1), channel_id=1, source_target_pairs={{0,2},{1,3},{2,0},{3,1},{4,6},{5,7},{6,4},{7,5},{8,10},{9,11},{10,... | collective-permute-start | bytes 393224 | tf_op jit(solution)/shard_map/ppermute | solution.py:22
  154.3 5.0 %collective-permute-start.26 = (bf16[128,512]{1,0:T(8,128)(2,1)S(1)}, bf16[128,512]{1,0:T(8,128)(2,1)S(1)}, u32[]{:S(2)}, u32[]{:S(2)}) collective-permute-start(bf16[128,512]{1,0:T(8,128)(2,1)S(1)} %gate.1), channel_id=1, source_target_pairs={{0,3},{1,0},{2,1},{3,2},{4,7},{5,4},{6,5},{7,6},{8,11},{9,8},{10,9... | collective-permute-start | bytes 393224 | tf_op jit(solution)/shard_map/ppermute | solution.py:22
  (3 other events, 46.0 us)
Sparse Core Ops, SparseCore 0:
  18.3 50.5 all-gather.4
  71.1 54.3 all-gather.6

commit v10 on v8

--- a/solution.py
+++ b/solution.py
@@ -237,14 +237,6 @@
     firsts = rotations(jnp.concatenate(first, axis=0), "x", 4)
     seconds = rotations(jnp.concatenate(second, axis=0), "y", 4)
 
-    late, firsts, seconds = lax.optimization_barrier((w_out.T, firsts, seconds))
-    wo_rows = [
-        lax.ppermute(
-            late, ("y", "x"), [(b * 4 + a, (a + k) % 4 * 4 + b) for a in range(4) for b in range(4)]
-        )
-        for k in range(4)
-    ]
-
     kv, q, u = call(
         project_kernel,
         [
@@ -261,13 +253,21 @@
         "project",
     )(place, *firsts, *seconds, weights)
 
-    wo_rows, _ = lax.optimization_barrier((wo_rows, kv))
-    wo_all = lax.all_gather(jnp.stack(wo_rows), plane)
-
-    kv_near = jnp.stack([kv, swap(kv, "zl")])
+    from_zl = swap(kv, "zl")
+    kv_near = jnp.stack([kv, from_zl])
     kv_far = swap(kv_near, "core")
     q_all = rotations(q, "zh", 4)
     kv_far, q_all[1], q_all[2] = lax.optimization_barrier((kv_far, q_all[1], q_all[2]))
+
+    late, _ = lax.optimization_barrier((w_out.T, from_zl))
+    wo_rows = [
+        lax.ppermute(
+            late, ("y", "x"), [(b * 4 + a, (a + k) % 4 * 4 + b) for a in range(4) for b in range(4)]
+        )
+        for k in range(4)
+    ]
+    wo_rows, kv_far, q_all = lax.optimization_barrier((wo_rows, kv_far, q_all))
+    wo_all = lax.all_gather(jnp.stack(wo_rows), plane)
 
     coded = weights[:4, :, 64:66].astype(f32)
     all_ids = (coded[:, :, 0] * 128 + coded[:, :, 1]).astype(jnp.int32).transpose(1, 0, 2)
@@ -298,7 +298,6 @@
         lax.ppermute(u[k], "y", [(i, (i - k) % 4) for i in range(4)]) for k in range(1, 4)
     ]
     arrived = lax.all_to_all(parts, ("y", "zh"), 0, 0, tiled=True)
-    arrived, wo_all = lax.optimization_barrier((arrived, wo_all))
     gated = call(
         gate_kernel,
         jax.ShapeDtypeStruct((RUN, 4 * DH), bf16),

time: 169 us -> 176 us (1.041)
  waiting for transfers between devices: 56.2 us -> 69.7 us
  starting transfers between devices: 62.9 us -> 60.2 us
  Pallas kernels: 20.5 us -> 18.1 us
    ppermute x18, waiting for transfers between devices: 41.5 us -> 33.2 us  [rotations(): lax.ppermute(value, axis, [(i, (i + step * k) % size) for i in range(size)])]
    ppermute x2, waiting for transfers between devices: 0.01 us -> 7.58 us  [swap(): return lax.ppermute(value, axis, [(0, 1), (1, 0)])]
    ppermute x4, waiting for transfers between devices: 0.01 us -> 5.13 us  [on_device(): lax.ppermute(late, ('y', 'x'), [(b * 4 + a, (a + k) % 4 * 4 + b) for a in...]
    all_to_all x1, waiting for transfers between devices: 9.12 us -> 13.8 us  [on_device(): arrived = lax.all_to_all(parts, ('y', 'zh'), 0, 0, tiled=True)]
    ppermute x3, waiting for transfers between devices: 0.01 us -> 4.36 us  [on_device(): lax.ppermute(u[k], 'y', [(i, (i - k) % 4) for i in range(4)])]
    pallas_call x1, Pallas kernels: 13.4 us -> 11 us  [on_device(): call(attend_kernel, jax.ShapeDtypeStruct((16, RUN, DH), bf16), 5, 9, [plt...]
    all_to_all x1, starting transfers between devices: 10.9 us -> 9.06 us  [on_device(): arrived = lax.all_to_all(parts, ('y', 'zh'), 0, 0, tiled=True)]
    unnamed x21 -> x19, local copies, waits for them, and re-layouts: 6.3 us -> 4.75 us
  transfers between devices with their start and end apart: 33 -> 33, of which waited for: 16 -> 20; matrix products, arithmetic and copies ran while one was open for 3% -> 3% of each run, Pallas kernels for 10% -> 7%
where the time goes in v10:
time: 176 us; the launch traced here: 174 us
  waiting for transfers between devices  69.7 us (40%)
  starting transfers between devices  60.2 us (34%)
  Pallas kernels  18.1 us (10%)
  between operations  13.7 us (8%)
  local copies, waits for them, and re-layouts  9.09 us (5%)
  other arithmetic  3.59 us (2%)
    ppermute x18, waiting for transfers between devices, rotations(): lax.ppermute(value, axis, [(i, (i + step * k) % size) for i in range(size)])  33.2 us
    ppermute x18, starting transfers between devices, rotations(): lax.ppermute(value, axis, [(i, (i + step * k) % size) for i in range(size)])  31.4 us
    all_to_all x1, waiting for transfers between devices, on_device(): arrived = lax.all_to_all(parts, ('y', 'zh'), 0, 0, tiled=True)  13.8 us
    pallas_call x1, Pallas kernels, on_device(): call(attend_kernel, jax.ShapeDtypeStruct((16, RUN, DH), bf16), 5, 9, [plt...  11 us
    ppermute x4, starting transfers between devices, on_device(): lax.ppermute(late, ('y', 'x'), [(b * 4 + a, (a + k) % 4 * 4 + b) for a in...  9.68 us
    all_to_all x1, starting transfers between devices, on_device(): arrived = lax.all_to_all(parts, ('y', 'zh'), 0, 0, tiled=True)  9.06 us
    ppermute x2, waiting for transfers between devices, swap(): return lax.ppermute(value, axis, [(0, 1), (1, 0)])  7.58 us
    ppermute x3, waiting for transfers between devices, on_device(): lax.ppermute(columns(y + k & 3), 'y', [(i, (i + k) % 4) for i in range(4)])  5.56 us
  transfers between devices with their start and end apart: 33, of which 20 were waited for; matrix products, arithmetic and copies ran while one was open for 3% of the time, Pallas kernels for 7%

profile of v10, /device:TPU:32, one launch (start us, length us, event | category | flops | bytes accessed | tf_op | source)
XLA Modules:
  0.0 174.5 jit_solution(17790690163477843885)
XLA Ops:
  8.4 3.1 %collective-permute-start.2 = (bf16[80,512]{1,0:T(8,128)(2,1)S(1)}, bf16[80,512]{1,0:T(8,128)(2,1)S(1)}, u32[]{:S(2)}, u32[]{:S(2)}) collective-permute-start(bf16[80,512]{1,0:T(8,128)(2,1)S(1)} %get-tuple-element.74), channel_id=1, source_target_pairs={{0,192},{64,0},{128,64},{192,128},{1,193},{65,1},{129,65},{193,129... | collective-permute-start | bytes 245768 | tf_op jit(solution)/shard_map/ppermute | solution.py:226
  13.1 1.9 %collective-permute-done.2 = bf16[80,512]{1,0:T(8,128)(2,1)S(1)} collective-permute-done((bf16[80,512]{1,0:T(8,128)(2,1)S(1)}, bf16[80,512]{1,0:T(8,128)(2,1)S(1)}, u32[]{:S(2)}, u32[]{:S(2)}) %collective-permute-start.2) | collective-permute-done | bytes 81952 | tf_op jit(solution)/shard_map/ppermute | solution.py:226
  15.0 2.9 %collective-permute-done.1 = bf16[80,512]{1,0:T(8,128)(2,1)S(1)} collective-permute-done((bf16[80,512]{1,0:T(8,128)(2,1)S(1)}, bf16[80,512]{1,0:T(8,128)(2,1)S(1)}, u32[]{:S(2)}, u32[]{:S(2)}) %collective-permute-start.1) | collective-permute-done | bytes 81952 | tf_op jit(solution)/shard_map/ppermute | solution.py:226
  20.6 2.0 %collective-permute-start.4 = (bf16[128,512]{1,0:T(8,128)(2,1)S(1)}, bf16[128,512]{1,0:T(8,128)(2,1)S(1)}, u32[]{:S(2)}, u32[]{:S(2)}) collective-permute-start(bf16[128,512]{1,0:T(8,128)(2,1)S(1)} %get-tuple-element.32), channel_id=1, source_target_pairs={{0,128},{64,192},{128,0},{192,64},{1,129},{65,193},{129,1},{193,65... | collective-permute-start | bytes 393224 | tf_op jit(solution)/shard_map/ppermute | solution.py:22
  24.1 1.5 collective-permute-start.6
  25.6 2.7 %collective-permute-start.7 = (bf16[128,512]{1,0:T(8,128)(2,1)S(1)}, bf16[128,512]{1,0:T(8,128)(2,1)S(1)}, u32[]{:S(2)}, u32[]{:S(2)}) collective-permute-start(bf16[128,512]{1,0:T(8,128)(2,1)S(1)} %get-tuple-element.36), channel_id=1, source_target_pairs={{0,2},{1,3},{2,0},{3,1},{4,6},{5,7},{6,4},{7,5},{8,10},{9,11},{10,... | collective-permute-start | bytes 393224 | tf_op jit(solution)/shard_map/ppermute | solution.py:22
  29.3 2.8 %collective-permute-start.8 = (bf16[128,512]{1,0:T(8,128)(2,1)S(1)}, bf16[128,512]{1,0:T(8,128)(2,1)S(1)}, u32[]{:S(2)}, u32[]{:S(2)}) collective-permute-start(bf16[128,512]{1,0:T(8,128)(2,1)S(1)} %get-tuple-element.36), channel_id=1, source_target_pairs={{0,3},{1,0},{2,1},{3,2},{4,7},{5,4},{6,5},{7,6},{8,11},{9,8},{10,9... | collective-permute-start | bytes 393224 | tf_op jit(solution)/shard_map/ppermute | solution.py:22
  33.0 1.6 collective-permute-done.8
  34.7 1.5 collective-permute-start.9
  36.2 3.7 %collective-permute-start.10 = (bf16[512,512]{1,0:T(8,128)(2,1)S(1)}, bf16[512,512]{1,0:T(8,128)(2,1)S(1)}, u32[]{:S(2)}, u32[]{:S(2)}) collective-permute-start(bf16[512,512]{1,0:T(8,128)(2,1)S(1)} %constant_dynamic-update-slice_fusion.a0), channel_id=1, source_target_pairs={{0,2},{1,3},{2,0},{3,1},{4,6},{5,7},{6,4},{7,5},{8,10},{9,11},{10,... | collective-permute-start | bytes 1572872 | tf_op jit(solution)/shard_map/ppermute | solution.py:22
  41.4 9.0 %collective-permute-done.9.a1 = bf16[512,512]{1,0:T(8,128)(2,1)S(1)} collective-permute-done((bf16[512,512]{1,0:T(8,128)(2,1)S(1)}, bf16[512,512]{1,0:T(8,128)(2,1)S(1)}, u32[]{:S(2)}, u32[]{:S(2)}) %collective-permute-start.9) | collective-permute-done | bytes 524320 | tf_op jit(solution)/shard_map/ppermute | solution.py:22
  50.5 9.8 %collective-permute-done.10.a2 = bf16[512,512]{1,0:T(8,128)(2,1)S(1)} collective-permute-done((bf16[512,512]{1,0:T(8,128)(2,1)S(1)}, bf16[512,512]{1,0:T(8,128)(2,1)S(1)}, u32[]{:S(2)}, u32[]{:S(2)}) %collective-permute-start.10) | collective-permute-done | bytes 524320 | tf_op jit(solution)/shard_map/ppermute | solution.py:22
  60.3 3.2 %collective-permute-done.12.b1 = bf16[512,512]{1,0:T(8,128)(2,1)S(1)} collective-permute-done((bf16[512,512]{1,0:T(8,128)(2,1)S(1)}, bf16[512,512]{1,0:T(8,128)(2,1)S(1)}, u32[]{:S(2)}, u32[]{:S(2)}) %collective-permute-start.12) | collective-permute-done | bytes 524320 | tf_op jit(solution)/shard_map/ppermute | solution.py:22
  64.2 2.5 %copy-done.1 = bf16[64,80,512]{2,1,0:T(8,128)(2,1)S(1)} copy-done((bf16[64,80,512]{2,1,0:T(8,128)(2,1)S(1)}, bf16[64,80,512]{2,1,0:T(8,128)(2,1)}, u32[]{:S(2)}) %copy-start.1) | copy-done | bytes 5242904
  66.6 3.6 %project.1 = (bf16[4,128,256]{2,1,0:T(8,128)(2,1)S(1)}, bf16[4,128,128]{2,1,0:T(8,128)(2,1)S(1)}, bf16[4,128,128]{2,1,0:T(8,128)(2,1)S(1)}) custom-call(s32[5]{0:T(128)S(1)} %stack.90.place, bf16[512,512]{1,0:T(8,128)(2,1)S(1)} %constant_dynamic-update-slice_fusion.a0, bf16[512,512]{1,0:T(8,128)(2,1)S(1)} %collective-permute-done.9.a1, ...), custom_call_target="tpu_custom_call" | custom-call | flops 2147483648 | bytes 9437184 | tf_op jit(solution)/shard_map/project/pallas_call | solution.py:240
  70.7 7.6 %collective-permute-done.15 = bf16[4,128,256]{2,1,0:T(8,128)(2,1)S(1)} collective-permute-done((bf16[4,128,256]{2,1,0:T(8,128)(2,1)S(1)}, bf16[4,128,256]{2,1,0:T(8,128)(2,1)S(1)}, u32[]{:S(2)}, u32[]{:S(2)}) %collective-permute-start.15) | collective-permute-done | bytes 262176 | tf_op jit(solution)/shard_map/ppermute | solution.py:28
  78.4 2.4 %collective-permute-start.21 = (bf16[4,128,128]{2,1,0:T(8,128)(2,1)S(1)}, bf16[4,128,128]{2,1,0:T(8,128)(2,1)S(1)}, u32[]{:S(2)}, u32[]{:S(2)}) collective-permute-start(bf16[4,128,128]{2,1,0:T(8,128)(2,1)S(1)} %get-tuple-element.46.q0), channel_id=1, source_target_pairs={{0,4},{4,8},{8,12},{12,0},{1,5},{5,9},{9,13},{13,1},{2,6},{6,10},{... | collective-permute-start | bytes 393224 | tf_op jit(solution)/shard_map/ppermute | solution.py:22
  80.8 4.5 %collective-permute-start.22 = (bf16[4,128,128]{2,1,0:T(8,128)(2,1)S(1)}, bf16[4,128,128]{2,1,0:T(8,128)(2,1)S(1)}, u32[]{:S(2)}, u32[]{:S(2)}) collective-permute-start(bf16[4,128,128]{2,1,0:T(8,128)(2,1)S(1)} %get-tuple-element.46.q0), channel_id=1, source_target_pairs={{0,8},{4,12},{8,0},{12,4},{1,9},{5,13},{9,1},{13,5},{2,10},{6,14},... | collective-permute-start | bytes 393224 | tf_op jit(solution)/shard_map/ppermute | solution.py:22
  85.3 2.7 %collective-permute-start.23 = (bf16[4,128,128]{2,1,0:T(8,128)(2,1)S(1)}, bf16[4,128,128]{2,1,0:T(8,128)(2,1)S(1)}, u32[]{:S(2)}, u32[]{:S(2)}) collective-permute-start(bf16[4,128,128]{2,1,0:T(8,128)(2,1)S(1)} %get-tuple-element.46.q0), channel_id=1, source_target_pairs={{0,12},{4,0},{8,4},{12,8},{1,13},{5,1},{9,5},{13,9},{2,14},{6,2},{... | collective-permute-start | bytes 393224 | tf_op jit(solution)/shard_map/ppermute | solution.py:22
  88.6 1.9 %collective-permute-done.21.q1 = bf16[4,128,128]{2,1,0:T(8,128)(2,1)S(1)} collective-permute-done((bf16[4,128,128]{2,1,0:T(8,128)(2,1)S(1)}, bf16[4,128,128]{2,1,0:T(8,128)(2,1)S(1)}, u32[]{:S(2)}, u32[]{:S(2)}) %collective-permute-start.21) | collective-permute-done | bytes 131104 | tf_op jit(solution)/shard_map/ppermute | solution.py:22
  90.6 3.7 %collective-permute-start.17 = (bf16[64,512]{1,0:T(8,128)(2,1)S(1)}, bf16[64,512]{1,0:T(8,128)(2,1)S(1)}, u32[]{:S(2)}, u32[]{:S(2)}) collective-permute-start(bf16[64,512]{1,0:T(8,128)(2,1)S(1)} %bitcast.69), channel_id=1, source_target_pairs={{0,64},{64,65},{128,66},{192,67},{1,128},{65,129},{129,130},{193,1... | collective-permute-start | bytes 196616 | tf_op jit(solution)/shard_map/ppermute | solution.py:264
  94.3 4.1 %collective-permute-start.18 = (bf16[64,512]{1,0:T(8,128)(2,1)S(1)}, bf16[64,512]{1,0:T(8,128)(2,1)S(1)}, u32[]{:S(2)}, u32[]{:S(2)}) collective-permute-start(bf16[64,512]{1,0:T(8,128)(2,1)S(1)} %bitcast.70), channel_id=1, source_target_pairs={{0,128},{64,129},{128,130},{192,131},{1,192},{65,193},{129,194},{1... | collective-permute-start | bytes 196616 | tf_op jit(solution)/shard_map/ppermute | solution.py:264
  99.6 4.6 %collective-permute-done.17 = bf16[64,512]{1,0:T(8,128)(2,1)S(1)} collective-permute-done((bf16[64,512]{1,0:T(8,128)(2,1)S(1)}, bf16[64,512]{1,0:T(8,128)(2,1)S(1)}, u32[]{:S(2)}, u32[]{:S(2)}) %collective-permute-start.17) | collective-permute-done | bytes 65568 | tf_op jit(solution)/shard_map/ppermute | solution.py:264
  108.9 11.0 %attend.1 = bf16[16,128,128]{2,1,0:T(8,128)(2,1)} custom-call(s32[5]{0:T(128)S(1)} %stack.90.place, s32[4]{0:T(128)S(1)} %copy-done.4, s32[4,2]{1,0:T(4,128)S(1)} %pad_add_fusion.1.q_edges, s32[4,4]{1,0:T(4,128)S(1)} %copy.25.k_edges, f32[32]{0:T(128)S(1)} %fusion.11.biases, bf16[4,128,128]{2,1,0:T(8,128)(2,1)S(1)} %get-tuple-element.46.q0, ...), custom_call_target="tpu_custom_call" | custom-call | flops 1073741824 | bytes 5242880 | tf_op jit(solution)/shard_map/attend/pallas_call | solution.py:284
  119.9 9.1 %all-to-all-start = ((bf16[16,128,128]{2,1,0:T(8,128)(2,1)}), bf16[16,128,128]{2,1,0:T(8,128)(2,1)S(1)}, u32[]{:S(2)}, u32[]{:S(2)}) async-start(bf16[16,128,128]{2,1,0:T(8,128)(2,1)} %attend.1), calls=%async_computation | async-start | bytes 1048576 | tf_op jit(solution)/shard_map/all_to_all | solution.py:300
  129.0 3.2 %collective-permute-start.24 = (bf16[128,128]{1,0:T(8,128)(2,1)S(1)}, bf16[128,128]{1,0:T(8,128)(2,1)S(1)}, u32[]{:S(2)}, u32[]{:S(2)}) collective-permute-start(bf16[128,128]{1,0:T(8,128)(2,1)S(1)} %get-tuple-element.65), channel_id=1, source_target_pairs={{0,192},{64,0},{128,64},{192,128},{1,193},{65,1},{129,65},{193,129... | collective-permute-start | bytes 98312 | tf_op jit(solution)/shard_map/ppermute | solution.py:298
  134.0 3.8 %collective-permute-done.25.u2 = bf16[128,128]{1,0:T(8,128)(2,1)S(1)} collective-permute-done((bf16[128,128]{1,0:T(8,128)(2,1)S(1)}, bf16[128,128]{1,0:T(8,128)(2,1)S(1)}, u32[]{:S(2)}, u32[]{:S(2)}) %collective-permute-start.25) | collective-permute-done | bytes 32800 | tf_op jit(solution)/shard_map/ppermute | solution.py:298
  138.3 13.8 %all-to-all-done.parts = bf16[16,128,128]{2,1,0:T(8,128)(2,1)S(1)} async-done(((bf16[16,128,128]{2,1,0:T(8,128)(2,1)}), bf16[16,128,128]{2,1,0:T(8,128)(2,1)S(1)}, u32[]{:S(2)}, u32[]{:S(2)}) %all-to-all-start) | async-done | bytes 524320 | tf_op jit(solution)/shard_map/all_to_all | solution.py:300
  153.9 2.3 %collective-permute-start.28 = (bf16[128,512]{1,0:T(8,128)(2,1)S(1)}, bf16[128,512]{1,0:T(8,128)(2,1)S(1)}, u32[]{:S(2)}, u32[]{:S(2)}) collective-permute-start(bf16[128,512]{1,0:T(8,128)(2,1)S(1)} %gate.1), channel_id=1, source_target_pairs={{0,2},{1,3},{2,0},{3,1},{4,6},{5,7},{6,4},{7,5},{8,10},{9,11},{10,... | collective-permute-start | bytes 393224 | tf_op jit(solution)/shard_map/ppermute | solution.py:22
  158.7 2.5 %collective-permute-done.28 = bf16[128,512]{1,0:T(8,128)(2,1)S(1)} collective-permute-done((bf16[128,512]{1,0:T(8,128)(2,1)S(1)}, bf16[128,512]{1,0:T(8,128)(2,1)S(1)}, u32[]{:S(2)}, u32[]{:S(2)}) %collective-permute-start.28) | collective-permute-done | bytes 131104 | tf_op jit(solution)/shard_map/ppermute | solution.py:22
  162.7 2.2 %copy-done.2 = bf16[64,64,512]{2,1,0:T(8,128)(2,1)S(1)} copy-done((bf16[64,64,512]{2,1,0:T(8,128)(2,1)S(1)}, bf16[64,64,512]{2,1,0:T(8,128)(2,1)}, u32[]{:S(2)}) %copy-start.2) | copy-done | bytes 4194328
  164.9 2.7 %project_out.1 = bf16[128,1024]{1,0:T(8,128)(2,1)} custom-call(s32[5]{0:T(128)S(1)} %stack.90.place, bf16[128,1024]{1,0:T(8,128)(2,1)S(1)} %copy-done.3, bf16[4,128,512]{2,1,0:T(8,128)(2,1)S(1)} %pad_maximum_fusion.1.gated, bf16[16,4,64,512]{3,2,1,0:T(8,128)(2,1)S(1)} %bitcast.48), custom_call_target="tpu_custom_call" | custom-call | flops 536870912 | bytes 5242880 | tf_op jit(solution)/shard_map/project_out/pallas_call | solution.py:314
  (94 shorter events, 26.9 us)
Async XLA Ops:
  6.5 57.6 %all-gather.5.cloned.1.call-start = ((), (), s32[]{:S(2)}) async-start(), calls=%async_computation.1 | async-start | bytes 5570560 | tf_op jit(solution)/shard_map/all_gather | solution.py:230
  8.4 6.6 %collective-permute-start.2 = (bf16[80,512]{1,0:T(8,128)(2,1)S(1)}, bf16[80,512]{1,0:T(8,128)(2,1)S(1)}, u32[]{:S(2)}, u32[]{:S(2)}) collective-permute-start(bf16[80,512]{1,0:T(8,128)(2,1)S(1)} %get-tuple-element.74), channel_id=1, source_target_pairs={{0,192},{64,0},{128,64},{192,128},{1,193},{65,1},{129,65},{193,129... | collective-permute-start | bytes 245768 | tf_op jit(solution)/shard_map/ppermute | solution.py:226
  11.5 6.3 %collective-permute-start.1 = (bf16[80,512]{1,0:T(8,128)(2,1)S(1)}, bf16[80,512]{1,0:T(8,128)(2,1)S(1)}, u32[]{:S(2)}, u32[]{:S(2)}) collective-permute-start(bf16[80,512]{1,0:T(8,128)(2,1)S(1)} %get-tuple-element.73), channel_id=1, source_target_pairs={{0,128},{64,192},{128,0},{192,64},{1,129},{65,193},{129,1},{193,65... | collective-permute-start | bytes 245768 | tf_op jit(solution)/shard_map/ppermute | solution.py:226
  12.1 6.5 %collective-permute-start = (bf16[80,512]{1,0:T(8,128)(2,1)S(1)}, bf16[80,512]{1,0:T(8,128)(2,1)S(1)}, u32[]{:S(2)}, u32[]{:S(2)}) collective-permute-start(bf16[80,512]{1,0:T(8,128)(2,1)S(1)} %get-tuple-element.72), channel_id=1, source_target_pairs={{0,64},{64,128},{128,192},{192,0},{1,65},{65,129},{129,193},{193,1... | collective-permute-start | bytes 245768 | tf_op jit(solution)/shard_map/ppermute | solution.py:226
  19.5 143.2 %all-gather.7.cloned.1.call-start = ((), (), s32[]{:S(2)}) async-start(), calls=%async_computation.2 | async-start | bytes 4456448 | tf_op jit(solution)/shard_map/all_gather | solution.py:270
  20.5 8.8 %collective-permute-start.3 = (bf16[128,512]{1,0:T(8,128)(2,1)S(1)}, bf16[128,512]{1,0:T(8,128)(2,1)S(1)}, u32[]{:S(2)}, u32[]{:S(2)}) collective-permute-start(bf16[128,512]{1,0:T(8,128)(2,1)S(1)} %get-tuple-element.32), channel_id=1, source_target_pairs={{0,64},{64,128},{128,192},{192,0},{1,65},{65,129},{129,193},{193,1... | collective-permute-start | bytes 393224 | tf_op jit(solution)/shard_map/ppermute | solution.py:22
  20.6 11.5 %collective-permute-start.4 = (bf16[128,512]{1,0:T(8,128)(2,1)S(1)}, bf16[128,512]{1,0:T(8,128)(2,1)S(1)}, u32[]{:S(2)}, u32[]{:S(2)}) collective-permute-start(bf16[128,512]{1,0:T(8,128)(2,1)S(1)} %get-tuple-element.32), channel_id=1, source_target_pairs={{0,128},{64,192},{128,0},{192,64},{1,129},{65,193},{129,1},{193,65... | collective-permute-start | bytes 393224 | tf_op jit(solution)/shard_map/ppermute | solution.py:22
  22.6 9.5 %collective-permute-start.5 = (bf16[128,512]{1,0:T(8,128)(2,1)S(1)}, bf16[128,512]{1,0:T(8,128)(2,1)S(1)}, u32[]{:S(2)}, u32[]{:S(2)}) collective-permute-start(bf16[128,512]{1,0:T(8,128)(2,1)S(1)} %get-tuple-element.32), channel_id=1, source_target_pairs={{0,192},{64,0},{128,64},{192,128},{1,193},{65,1},{129,65},{193,129... | collective-permute-start | bytes 393224 | tf_op jit(solution)/shard_map/ppermute | solution.py:22
  24.1 8.0 %collective-permute-start.6 = (bf16[128,512]{1,0:T(8,128)(2,1)S(1)}, bf16[128,512]{1,0:T(8,128)(2,1)S(1)}, u32[]{:S(2)}, u32[]{:S(2)}) collective-permute-start(bf16[128,512]{1,0:T(8,128)(2,1)S(1)} %get-tuple-element.36), channel_id=1, source_target_pairs={{0,1},{1,2},{2,3},{3,0},{4,5},{5,6},{6,7},{7,4},{8,9},{9,10},{10,1... | collective-permute-start | bytes 393224 | tf_op jit(solution)/shard_map/ppermute | solution.py:22
  25.6 7.4 %collective-permute-start.7 = (bf16[128,512]{1,0:T(8,128)(2,1)S(1)}, bf16[128,512]{1,0:T(8,128)(2,1)S(1)}, u32[]{:S(2)}, u32[]{:S(2)}) collective-permute-start(bf16[128,512]{1,0:T(8,128)(2,1)S(1)} %get-tuple-element.36), channel_id=1, source_target_pairs={{0,2},{1,3},{2,0},{3,1},{4,6},{5,7},{6,4},{7,5},{8,10},{9,11},{10,... | collective-permute-start | bytes 393224 | tf_op jit(solution)/shard_map/ppermute | solution.py:22
  29.3 5.3 %collective-permute-start.8 = (bf16[128,512]{1,0:T(8,128)(2,1)S(1)}, bf16[128,512]{1,0:T(8,128)(2,1)S(1)}, u32[]{:S(2)}, u32[]{:S(2)}) collective-permute-start(bf16[128,512]{1,0:T(8,128)(2,1)S(1)} %get-tuple-element.36), channel_id=1, source_target_pairs={{0,3},{1,0},{2,1},{3,2},{4,7},{5,4},{6,5},{7,6},{8,11},{9,8},{10,9... | collective-permute-start | bytes 393224 | tf_op jit(solution)/shard_map/ppermute | solution.py:22
  34.7 15.7 %collective-permute-start.9 = (bf16[512,512]{1,0:T(8,128)(2,1)S(1)}, bf16[512,512]{1,0:T(8,128)(2,1)S(1)}, u32[]{:S(2)}, u32[]{:S(2)}) collective-permute-start(bf16[512,512]{1,0:T(8,128)(2,1)S(1)} %constant_dynamic-update-slice_fusion.a0), channel_id=1, source_target_pairs={{0,1},{1,2},{2,3},{3,0},{4,5},{5,6},{6,7},{7,4},{8,9},{9,10},{10,1... | collective-permute-start | bytes 1572872 | tf_op jit(solution)/shard_map/ppermute | solution.py:22
  36.2 24.0 %collective-permute-start.10 = (bf16[512,512]{1,0:T(8,128)(2,1)S(1)}, bf16[512,512]{1,0:T(8,128)(2,1)S(1)}, u32[]{:S(2)}, u32[]{:S(2)}) collective-permute-start(bf16[512,512]{1,0:T(8,128)(2,1)S(1)} %constant_dynamic-update-slice_fusion.a0), channel_id=1, source_target_pairs={{0,2},{1,3},{2,0},{3,1},{4,6},{5,7},{6,4},{7,5},{8,10},{9,11},{10,... | collective-permute-start | bytes 1572872 | tf_op jit(solution)/shard_map/ppermute | solution.py:22
  39.9 20.4 %collective-permute-start.11 = (bf16[512,512]{1,0:T(8,128)(2,1)S(1)}, bf16[512,512]{1,0:T(8,128)(2,1)S(1)}, u32[]{:S(2)}, u32[]{:S(2)}) collective-permute-start(bf16[512,512]{1,0:T(8,128)(2,1)S(1)} %constant_dynamic-update-slice_fusion.a0), channel_id=1, source_target_pairs={{0,3},{1,0},{2,1},{3,2},{4,7},{5,4},{6,5},{7,6},{8,11},{9,8},{10,9... | collective-permute-start | bytes 1572872 | tf_op jit(solution)/shard_map/ppermute | solution.py:22
  40.2 23.2 %collective-permute-start.12 = (bf16[512,512]{1,0:T(8,128)(2,1)S(1)}, bf16[512,512]{1,0:T(8,128)(2,1)S(1)}, u32[]{:S(2)}, u32[]{:S(2)}) collective-permute-start(bf16[512,512]{1,0:T(8,128)(2,1)S(1)} %constant_dynamic-update-slice_fusion.4.b0), channel_id=1, source_target_pairs={{0,64},{64,128},{128,192},{192,0},{1,65},{65,129},{129,193},{193,1... | collective-permute-start | bytes 1572872 | tf_op jit(solution)/shard_map/ppermute | solution.py:22
  40.3 23.2 %collective-permute-start.13 = (bf16[512,512]{1,0:T(8,128)(2,1)S(1)}, bf16[512,512]{1,0:T(8,128)(2,1)}, u32[]{:S(2)}, u32[]{:S(2)}) collective-permute-start(bf16[512,512]{1,0:T(8,128)(2,1)S(1)} %constant_dynamic-update-slice_fusion.4.b0), channel_id=1, source_target_pairs={{0,128},{64,192},{128,0},{192,64},{1,129},{65,193},{129,1},{193,65... | collective-permute-start | bytes 1572872 | tf_op jit(solution)/shard_map/ppermute | solution.py:22
  50.4 13.8 %collective-permute-start.14 = (bf16[512,512]{1,0:T(8,128)(2,1)S(1)}, bf16[512,512]{1,0:T(8,128)(2,1)}, u32[]{:S(2)}, u32[]{:S(2)}) collective-permute-start(bf16[512,512]{1,0:T(8,128)(2,1)S(1)} %constant_dynamic-update-slice_fusion.4.b0), channel_id=1, source_target_pairs={{0,192},{64,0},{128,64},{192,128},{1,193},{65,1},{129,65},{193,129... | collective-permute-start | bytes 1572872 | tf_op jit(solution)/shard_map/ppermute | solution.py:22
  70.3 8.0 %collective-permute-start.15 = (bf16[4,128,256]{2,1,0:T(8,128)(2,1)S(1)}, bf16[4,128,256]{2,1,0:T(8,128)(2,1)S(1)}, u32[]{:S(2)}, u32[]{:S(2)}) collective-permute-start(bf16[4,128,256]{2,1,0:T(8,128)(2,1)S(1)} %get-tuple-element.40), channel_id=1, source_target_pairs={{0,32},{32,0},{1,33},{33,1},{2,34},{34,2},{3,35},{35,3},{4,36},{36... | collective-permute-start | bytes 786440 | tf_op jit(solution)/shard_map/ppermute | solution.py:28
  78.3 20.2 %collective-permute-start.20 = (bf16[2,4,128,256]{3,2,1,0:T(8,128)(2,1)S(1)}, bf16[2,4,128,256]{3,2,1,0:T(8,128)(2,1)S(1)}, u32[]{:S(2)}, u32[]{:S(2)}) collective-permute-start(bf16[2,4,128,256]{3,2,1,0:T(8,128)(2,1)S(1)} %pad_maximum_fusion.kv_near), channel_id=1, source_target_pairs={{0,16},{16,0},{1,17},{17,1},{2,18},{18,2},{3,19},{19,3},{4,20},{20... | collective-permute-start | bytes 1572872 | tf_op jit(solution)/shard_map/ppermute | solution.py:28
  78.4 12.2 %collective-permute-start.21 = (bf16[4,128,128]{2,1,0:T(8,128)(2,1)S(1)}, bf16[4,128,128]{2,1,0:T(8,128)(2,1)S(1)}, u32[]{:S(2)}, u32[]{:S(2)}) collective-permute-start(bf16[4,128,128]{2,1,0:T(8,128)(2,1)S(1)} %get-tuple-element.46.q0), channel_id=1, source_target_pairs={{0,4},{4,8},{8,12},{12,0},{1,5},{5,9},{9,13},{13,1},{2,6},{6,10},{... | collective-permute-start | bytes 393224 | tf_op jit(solution)/shard_map/ppermute | solution.py:22
  80.8 13.5 %collective-permute-start.22 = (bf16[4,128,128]{2,1,0:T(8,128)(2,1)S(1)}, bf16[4,128,128]{2,1,0:T(8,128)(2,1)S(1)}, u32[]{:S(2)}, u32[]{:S(2)}) collective-permute-start(bf16[4,128,128]{2,1,0:T(8,128)(2,1)S(1)} %get-tuple-element.46.q0), channel_id=1, source_target_pairs={{0,8},{4,12},{8,0},{12,4},{1,9},{5,13},{9,1},{13,5},{2,10},{6,14},... | collective-permute-start | bytes 393224 | tf_op jit(solution)/shard_map/ppermute | solution.py:22
  85.3 14.3 %collective-permute-start.23 = (bf16[4,128,128]{2,1,0:T(8,128)(2,1)S(1)}, bf16[4,128,128]{2,1,0:T(8,128)(2,1)S(1)}, u32[]{:S(2)}, u32[]{:S(2)}) collective-permute-start(bf16[4,128,128]{2,1,0:T(8,128)(2,1)S(1)} %get-tuple-element.46.q0), channel_id=1, source_target_pairs={{0,12},{4,0},{8,4},{12,8},{1,13},{5,1},{9,5},{13,9},{2,14},{6,2},{... | collective-permute-start | bytes 393224 | tf_op jit(solution)/shard_map/ppermute | solution.py:22
  88.0 11.6 %collective-permute-start.16 = (bf16[64,512]{1,0:T(8,128)(2,1)S(1)}, bf16[64,512]{1,0:T(8,128)(2,1)S(1)}, u32[]{:S(2)}, u32[]{:S(2)}) collective-permute-start(bf16[64,512]{1,0:T(8,128)(2,1)S(1)} %bitcast.68), channel_id=1, source_target_pairs={{0,0},{64,1},{128,2},{192,3},{1,64},{65,65},{129,66},{193,67},{2,1... | collective-permute-start | bytes 196616 | tf_op jit(solution)/shard_map/ppermute | solution.py:264
  90.6 13.7 %collective-permute-start.17 = (bf16[64,512]{1,0:T(8,128)(2,1)S(1)}, bf16[64,512]{1,0:T(8,128)(2,1)S(1)}, u32[]{:S(2)}, u32[]{:S(2)}) collective-permute-start(bf16[64,512]{1,0:T(8,128)(2,1)S(1)} %bitcast.69), channel_id=1, source_target_pairs={{0,64},{64,65},{128,66},{192,67},{1,128},{65,129},{129,130},{193,1... | collective-permute-start | bytes 196616 | tf_op jit(solution)/shard_map/ppermute | solution.py:264
  94.3 9.9 %collective-permute-start.18 = (bf16[64,512]{1,0:T(8,128)(2,1)S(1)}, bf16[64,512]{1,0:T(8,128)(2,1)S(1)}, u32[]{:S(2)}, u32[]{:S(2)}) collective-permute-start(bf16[64,512]{1,0:T(8,128)(2,1)S(1)} %bitcast.70), channel_id=1, source_target_pairs={{0,128},{64,129},{128,130},{192,131},{1,192},{65,193},{129,194},{1... | collective-permute-start | bytes 196616 | tf_op jit(solution)/shard_map/ppermute | solution.py:264
  98.5 6.3 %collective-permute-start.19 = (bf16[64,512]{1,0:T(8,128)(2,1)S(1)}, bf16[64,512]{1,0:T(8,128)(2,1)S(1)}, u32[]{:S(2)}, u32[]{:S(2)}) collective-permute-start(bf16[64,512]{1,0:T(8,128)(2,1)S(1)} %bitcast.71), channel_id=1, source_target_pairs={{0,192},{64,193},{128,194},{192,195},{1,0},{65,1},{129,2},{193,3},... | collective-permute-start | bytes 196616 | tf_op jit(solution)/shard_map/ppermute | solution.py:264
  119.9 32.2 %all-to-all-start = ((bf16[16,128,128]{2,1,0:T(8,128)(2,1)}), bf16[16,128,128]{2,1,0:T(8,128)(2,1)S(1)}, u32[]{:S(2)}, u32[]{:S(2)}) async-start(bf16[16,128,128]{2,1,0:T(8,128)(2,1)} %attend.1), calls=%async_computation | async-start | bytes 1048576 | tf_op jit(solution)/shard_map/all_to_all | solution.py:300
  132.2 5.5 %collective-permute-start.25 = (bf16[128,128]{1,0:T(8,128)(2,1)S(1)}, bf16[128,128]{1,0:T(8,128)(2,1)S(1)}, u32[]{:S(2)}, u32[]{:S(2)}) collective-permute-start(bf16[128,128]{1,0:T(8,128)(2,1)S(1)} %get-tuple-element.64), channel_id=1, source_target_pairs={{0,128},{64,192},{128,0},{192,64},{1,129},{65,193},{129,1},{193,65... | collective-permute-start | bytes 98312 | tf_op jit(solution)/shard_map/ppermute | solution.py:298
  133.1 5.2 %collective-permute-start.26 = (bf16[128,128]{1,0:T(8,128)(2,1)S(1)}, bf16[128,128]{1,0:T(8,128)(2,1)S(1)}, u32[]{:S(2)}, u32[]{:S(2)}) collective-permute-start(bf16[128,128]{1,0:T(8,128)(2,1)S(1)} %get-tuple-element.63), channel_id=1, source_target_pairs={{0,64},{64,128},{128,192},{192,0},{1,65},{65,129},{129,193},{193,1... | collective-permute-start | bytes 98312 | tf_op jit(solution)/shard_map/ppermute | solution.py:298
  152.9 5.8 %collective-permute-start.29 = (bf16[128,512]{1,0:T(8,128)(2,1)S(1)}, bf16[128,512]{1,0:T(8,128)(2,1)S(1)}, u32[]{:S(2)}, u32[]{:S(2)}) collective-permute-start(bf16[128,512]{1,0:T(8,128)(2,1)S(1)} %gate.1), channel_id=1, source_target_pairs={{0,3},{1,0},{2,1},{3,2},{4,7},{5,4},{6,5},{7,6},{8,11},{9,8},{10,9... | collective-permute-start | bytes 393224 | tf_op jit(solution)/shard_map/ppermute | solution.py:22
  153.9 7.3 %collective-permute-start.28 = (bf16[128,512]{1,0:T(8,128)(2,1)S(1)}, bf16[128,512]{1,0:T(8,128)(2,1)S(1)}, u32[]{:S(2)}, u32[]{:S(2)}) collective-permute-start(bf16[128,512]{1,0:T(8,128)(2,1)S(1)} %gate.1), channel_id=1, source_target_pairs={{0,2},{1,3},{2,0},{3,1},{4,6},{5,7},{6,4},{7,5},{8,10},{9,11},{10,... | collective-permute-start | bytes 393224 | tf_op jit(solution)/shard_map/ppermute | solution.py:22
  156.2 6.4 %collective-permute-start.27 = (bf16[128,512]{1,0:T(8,128)(2,1)S(1)}, bf16[128,512]{1,0:T(8,128)(2,1)S(1)}, u32[]{:S(2)}, u32[]{:S(2)}) collective-permute-start(bf16[128,512]{1,0:T(8,128)(2,1)S(1)} %gate.1), channel_id=1, source_target_pairs={{0,1},{1,2},{2,3},{3,0},{4,5},{5,6},{6,7},{7,4},{8,9},{9,10},{10,1... | collective-permute-start | bytes 393224 | tf_op jit(solution)/shard_map/ppermute | solution.py:22
  (7 other events, 285.1 us)
Sparse Core Ops, SparseCore 0:
  19.6 43.7 all-gather.4
  105.6 52.1 all-gather.6
